TPU v7x, 512 devices: a whole 4x4x16 slice. The times are simulated.
512 devices in a mesh: row: 8 (over x, z_hi), col: 64 (over y, z_lo, core).
Axes of the slice: x: 4, y: 4, z: 16 (z_hi: 2, z_lo: 8; z = z_hi * 8 + z_lo), core: 2. Of those that a mesh axis runs over, the one named last changes fastest.
Arguments:
- features: bfloat16 [64, 1024, 128], P('col', 'row'), may hold values from -6 to 6
- weight: bfloat16 [128, 256], replicated, may hold values from -0.5 to 0.5
- upstream: bfloat16 [64, 1024, 256], P('col', 'row'), may hold values from -6 to 6
- tile_rows: int32 [8, 64, 64], P('row', 'col'), may hold values from 0 to 63
- tile_cols: int32 [8, 64, 64], P('row', 'col'), may hold values from 0 to 7
- tile_count: int32 [8, 64], P('row', 'col'), may hold values from 8 to 64, as said below
- edge_rows: int32 [8, 64, 64, 192], P('row', 'col'), may hold values from 0 to 127
- edge_cols: int32 [8, 64, 64, 192], P('row', 'col'), may hold values from 0 to 127
- edge_weight: bfloat16 [8, 64, 64, 192], P('row', 'col'), may hold values from 0.029907227 to 0.29882812
Outputs:
- out_act: bfloat16 [64, 1024, 256], P('col', 'row')
- grad_features: bfloat16 [64, 1024, 128], P('col', 'row')
- grad_weight: float32 [128, 256], replicated
Inputs may be any that keep to these rules, and one draw needn't show every extreme that they name: `tile_count`: live slots of each block; exactly one block has all 64 slots live, the others at most half of them.
All inputs are finite; a program needn't handle non-finite values.
Results may differ from a plain program's by a relative error of at most 0.0061.
Values may be sent and summed in bfloat16 or wider, within the bound.
No kernel may reach another device: no remote copies, remote signals or barrier semaphores. Data moves between devices by JAX's collectives and lax.ppermute only.
A program may use at most 64 MiB of HBM per device.

v0:
```python
import math

import jax
import jax.numpy as jnp
from jax import lax
from jax.sharding import PartitionSpec as P

TILE = 128


group_len = 4


def local(
    features, weight, upstream, tile_rows, tile_cols, tile_count, edge_rows, edge_cols, edge_weight
):
    feat_width = features.shape[2]
    slots_total = tile_rows.shape[2]
    row_tiles = tile_rows[0, 0]
    col_tiles = tile_cols[0, 0]
    rows_all = edge_rows[0, 0]
    cols_all = edge_cols[0, 0]
    weights_all = edge_weight[0, 0]
    live_count = tile_count[0, 0]
    group_count = (live_count + group_len - 1) // group_len
    positions = jnp.arange(TILE, dtype=jnp.int32)
    block_rows = lax.axis_size("col") * features.shape[1]
    column = lax.all_gather(features, "row", axis=1, tiled=True)
    column = column.reshape(-1, TILE, feat_width)
    col_rows = column.shape[0] * TILE

    def build_tiles(group_id):
        first_slot = group_id * group_len
        rows_now = lax.dynamic_slice_in_dim(rows_all, first_slot, group_len, 0)
        cols_now = lax.dynamic_slice_in_dim(cols_all, first_slot, group_len, 0)
        weights_now = lax.dynamic_slice_in_dim(weights_all, first_slot, group_len, 0)
        is_live = first_slot + jnp.arange(group_len, dtype=jnp.int32) < live_count
        live_weight = jnp.where(is_live[:, None], weights_now, jnp.zeros_like(weights_now))
        row_hot = (rows_now[:, :, None] == positions).astype(jnp.bfloat16)
        col_hot = jnp.where(
            cols_now[:, :, None] == positions, live_weight[:, :, None], jnp.zeros((), jnp.bfloat16)
        )
        built = jnp.einsum("kea,keb->kab", row_hot, col_hot, preferred_element_type=jnp.float32)
        return built.astype(jnp.bfloat16)

    def forward_group(group_id, state_pair):
        partial_value, dense_tiles = state_pair
        built = build_tiles(group_id)
        dense_tiles = lax.dynamic_update_slice_in_dim(dense_tiles, built, group_id * group_len, 0)
        for slot_id in range(group_len):
            slot_index = group_id * group_len + slot_id
            source = lax.dynamic_index_in_dim(column, col_tiles[slot_index], 0, keepdims=False)
            products = jnp.dot(built[slot_id], source, preferred_element_type=jnp.float32)
            row_start = row_tiles[slot_index] * TILE
            current = lax.dynamic_slice_in_dim(partial_value, row_start, TILE, 0)
            partial_value = lax.dynamic_update_slice_in_dim(
                partial_value, current + products, row_start, 0
            )
        return (partial_value, dense_tiles)

    start_pair = (
        jnp.zeros((block_rows, feat_width), jnp.float32),
        jnp.zeros((slots_total, TILE, TILE), jnp.bfloat16),
    )
    partial_value, dense_tiles = lax.fori_loop(0, group_count, forward_group, start_pair)
    partial_value = partial_value.reshape(lax.axis_size("col"), features.shape[1], feat_width)
    full_sum = lax.psum(partial_value, "col")
    own_part = lax.dynamic_slice_in_dim(full_sum, lax.axis_index("col"), 1, 0)
    aggregated = own_part[0].astype(jnp.bfloat16)
    pre_act = jnp.dot(aggregated, weight, preferred_element_type=jnp.float32)
    sigmoid_pre = jax.nn.sigmoid(pre_act)
    out_act = (pre_act * sigmoid_pre).astype(jnp.bfloat16)
    grad_pre = (
        upstream[0].astype(jnp.float32) * sigmoid_pre * (1.0 + pre_act * (1.0 - sigmoid_pre))
    ).astype(jnp.bfloat16)
    grad_agg = lax.dot_general(
        grad_pre, weight, (((1,), (1,)), ((), ())), preferred_element_type=jnp.float32
    ).astype(jnp.bfloat16)
    local_weight = lax.dot_general(
        aggregated, grad_pre, (((0,), (0,)), ((), ())), preferred_element_type=jnp.float32
    )
    node_total = features.shape[1] * lax.axis_size("row") * lax.axis_size("col")
    grad_scale = jnp.float32(1.0 / math.sqrt(node_total))
    gathered = lax.all_gather(grad_agg[None], "col", axis=0, tiled=True)
    gathered = gathered.reshape(block_rows, feat_width)

    def backward_group(group_id, accum):
        for slot_id in range(group_len):
            slot_index = group_id * group_len + slot_id
            tile_now = lax.dynamic_index_in_dim(dense_tiles, slot_index, 0, keepdims=False)
            source = lax.dynamic_slice_in_dim(gathered, row_tiles[slot_index] * TILE, TILE, 0)
            products = lax.dot_general(
                tile_now, source, (((0,), (0,)), ((), ())), preferred_element_type=jnp.float32
            )
            col_start = col_tiles[slot_index] * TILE
            current = lax.dynamic_slice_in_dim(accum, col_start, TILE, 0)
            accum = lax.dynamic_update_slice_in_dim(accum, current + products, col_start, 0)
        return accum

    col_partial = lax.fori_loop(
        0, group_count, backward_group, jnp.zeros((col_rows, feat_width), jnp.float32)
    )
    col_partial = col_partial[None]
    summed_weight = lax.psum(local_weight, ("row", "col"))
    grad_weight = summed_weight * grad_scale
    back_full = lax.psum(col_partial, "row")
    back_own = lax.dynamic_slice_in_dim(
        back_full, lax.axis_index("row") * features.shape[1], features.shape[1], 1
    )
    grad_features = back_own.astype(jnp.bfloat16)
    return (out_act[None], grad_features, grad_weight)


def solution(mesh):
    in_specs = (
        P("col", "row", None),
        P(),
        P("col", "row", None),
        P("row", "col", None),
        P("row", "col", None),
        P("row", "col"),
        P("row", "col", None, None),
        P("row", "col", None, None),
        P("row", "col", None, None),
    )
    out_specs = (P("col", "row", None), P("col", "row", None), P())
    return jax.shard_map(local, mesh=mesh, in_specs=in_specs, out_specs=out_specs, check_vma=False)
```

profile of v0, /device:TPU:185, one launch (start us, length us, event | category | flops | bytes accessed | tf_op | source)
XLA Modules:
  0.0 1526.6 jit_solution(1179104203921485720)
XLA Ops:
  8.7 58.4 %all_gather.6 = bf16[1,1024,128]{2,1,0:T(8,128)(2,1)S(1)} all-gather(bf16[1,128,128]{2,1,0:T(8,128)(2,1)} %param.13), channel_id=1, replica_groups=mesh['row'=8,'col'=64] {'row'}, dimensions={1}, use_global_device_ids=true | all-gather | bytes 294912 | tf_op jit(solution)/shard_map/all_gather | solution.py:28
  67.1 2.2 broadcast_in_dim.54
  70.0 81.8 %while.29 = (s32[]{:T(128)}, f32[8192,128]{1,0:T(8,128)}, bf16[64,128,128]{2,1,0:T(8,128)(2,1)S(1)}, s32[]{:T(128)}, s32[64]{0:T(128)S(1)}, /*index=5*/s32[64,19...) while((s32[]{:T(128)}, f32[8192,128]{1,0:T(8,128)}, ...), condition=%wide.region_1.2_spmd.clone.clone, body=%wide.region_0.1_spmd.clone.clone.sunk | while | flops 42369820 | bytes 1075025 | solution.py:65
  70.6 0.8 fusion.107
  76.3 1.6 fusion.108
  80.5 1.6 fusion.109
  84.6 1.6 fusion.110
  88.8 1.6 fusion.111
  91.1 0.8 fusion.107
  91.8 0.7 constant_dynamic-slice_fusion.4
  96.7 1.6 fusion.108
  100.9 1.6 fusion.109
  105.1 1.6 fusion.110
  109.2 1.6 fusion.111
  111.5 0.8 fusion.107
  117.2 1.6 fusion.108
  121.4 1.6 fusion.109
  125.5 1.6 fusion.110
  129.7 1.6 fusion.111
  132.0 0.8 fusion.107
  137.6 1.6 fusion.108
  141.8 1.6 fusion.109
  146.0 1.6 fusion.110
  150.1 1.6 fusion.111
  151.8 515.4 %all-reduce.5 = bf16[64,128,128]{2,1,0:T(8,128)(2,1)} all-reduce(f32[64,128,128]{2,1,0:T(8,128)} %bitcast.133), channel_id=1, replica_groups=mesh['row'=8,'col'=64] {'col'}, use_global_device_ids=true, to_apply=%region_2.3 | all-reduce | flops 1048576 | bytes 6291456 | tf_op jit(solution)/shard_map/psum | solution.py:67
  667.2 1.6 fusion.47
  668.8 1.6 fusion.50
  670.5 0.8 convolution_convert_fusion.1
  671.3 615.6 %all-reduce.4.cloned.1.call-done = f32[128,256]{1,0:T(8,128)} async-done(((f32[128,256]{1,0:T(8,128)}), f32[128,256]{1,0:T(8,128)}) %all-reduce.4.cloned.1.call-update) | async-done | bytes 131088 | tf_op jit(solution)/shard_map/psum | solution.py:104
  1286.9 1.6 broadcast_multiply_fusion
  1288.5 38.6 %while.28 = (s32[]{:T(128)}, f32[1024,128]{1,0:T(8,128)S(1)}, s32[]{:T(128)}, s32[64]{0:T(128)S(1)}, bf16[64,128,128]{2,1,0:T(8,128)(2,1)S(1)}, /*index=5*/s32[6...) while((s32[]{:T(128)}, f32[1024,128]{1,0:T(8,128)S(1)}, ...), condition=%wide.region_4.5_spmd, body=%wide.region_3.4_spmd.sunk | while | flops 16842800 | bytes 787285 | solution.py:100
  1290.5 1.0 fusion.98
  1292.7 1.0 fusion.99
  1294.9 1.0 fusion.100
  1297.2 1.0 fusion.101
  1300.1 1.0 fusion.98
  1302.3 1.0 fusion.99
  1304.6 1.0 fusion.100
  1306.8 1.0 fusion.101
  1309.8 1.0 fusion.98
  1311.9 1.0 fusion.99
  1314.2 1.0 fusion.100
  1316.5 1.0 fusion.101
  1319.4 1.0 fusion.98
  1321.6 1.0 fusion.99
  1323.8 1.0 fusion.100
  1326.1 1.0 fusion.101
  1327.1 191.5 %all-reduce.6 = bf16[1,1024,128]{2,1,0:T(8,128)(2,1)S(1)} all-reduce(f32[1,1024,128]{2,1,0:T(8,128)S(1)} %bitcast.134), channel_id=1, replica_groups=mesh['row'=8,'col'=64] {'row'}, use_global_device_ids=true, to_apply=%region_5.6 | all-reduce | flops 131072 | bytes 786432 | tf_op jit(solution)/shard_map/psum | solution.py:106
  (35 shorter events, 14.6 us)
Async XLA Ops:
  8.0 659.2 %copy-start = (bf16[128,256]{1,0:T(8,128)(2,1)S(1)}, bf16[128,256]{1,0:T(8,128)(2,1)}, u32[]{:S(2)}) copy-start(bf16[128,256]{1,0:T(8,128)(2,1)} %param.14) | copy-start | bytes 196612
  8.0 1278.9 %all-reduce.4.cloned.1.call-start = ((), (), s32[]{:S(2)}) async-start(), calls=%async_computation | async-start | bytes 262144 | tf_op jit(solution)/shard_map/psum | solution.py:104
  69.3 0.7 copy-start.1
  69.3 0.7 copy-start.2
  151.8 515.4 %copy-start.3 = (bf16[1,128,256]{2,1,0:T(8,128)(2,1)S(1)}, bf16[1,128,256]{2,1,0:T(8,128)(2,1)}, u32[]{:S(2)}) copy-start(bf16[1,128,256]{2,1,0:T(8,128)(2,1)} %param.15) | copy-start | bytes 196612
  670.4 618.0 %all-gather.3.cloned.1.call-start = ((), (), s32[]{:S(2)}) async-start(), calls=%async_computation.1 | async-start | bytes 2129920 | tf_op jit(solution)/shard_map/all_gather | solution.py:84
Sparse Core Ops, SparseCore 0:
  670.5 616.2 all-reduce.3
Sparse Core Ops, SparseCore 1:
  673.6 291.1 all-gather.2
where the time goes:
time: 1540 us; the launch traced here: 1530 us
  blocking collectives  765 us (50%)
  waiting for transfers between devices  616 us (40%)
  loops' own time  62.4 us (4%)
  matrix products  47.9 us (3%)
  between operations  16.2 us (1%)
    psum x1, waiting for transfers between devices, local(): summed_weight = lax.psum(local_weight, ('row', 'col'))  616 us
    psum x1, blocking collectives, local(): full_sum = lax.psum(partial_value, 'col')  515 us
    psum x1, blocking collectives, local(): back_full = lax.psum(col_partial, 'row')  191 us
    all_gather x1, blocking collectives, local(): column = lax.all_gather(features, 'row', axis=1, tiled=True)  58.4 us
    another operation x1, loops' own time, local(): lax.fori_loop(0, group_count, forward_group, start_pair)  41.8 us
  transfers between devices with their start and end apart: 2, of which 1 were waited for; matrix products, arithmetic and copies ran while one was open for 0% of the time, Pallas kernels for 0%

commit v1 on v0

v1 whole, which is shorter than its diff:
```python
import math

import jax
import jax.numpy as jnp
from jax import lax
from jax.experimental import pallas as pl
from jax.experimental.pallas import tpu as pltpu
from jax.sharding import Mesh
from jax.sharding import PartitionSpec as P

TILE = 128
GROUP = 4
FINE = (("x", 4), ("zh", 2), ("y", 4), ("zl", 8), ("core", 2))
N_X, N_ZH, N_Y, N_ZL, N_CORE = (size for _, size in FINE)
ROW = ("x", "zh")
COL = ("y", "zl", "core")
W_ROWS = 32
VMEM_LIMIT = 48 * 1024 * 1024
BF16 = jnp.bfloat16
F32 = jnp.float32

vmem = pl.BlockSpec(memory_space=pltpu.VMEM)
smem = pl.BlockSpec(memory_space=pltpu.SMEM)
hbm = pl.BlockSpec(memory_space=pl.ANY)


def call(body, outs, in_specs, scratch=(), flops=0, moved=0):
    return pl.pallas_call(
        body,
        out_shape=outs,
        in_specs=in_specs,
        out_specs=jax.tree.map(lambda _: vmem, outs),
        scratch_shapes=list(scratch),
        compiler_params=pltpu.CompilerParams(vmem_limit_bytes=VMEM_LIMIT),
        cost_estimate=pl.CostEstimate(flops=flops, bytes_accessed=moved, transcendentals=0),
    )


def halves(value):
    high = value.astype(BF16)
    return high, (value - high.astype(F32)).astype(BF16)


def group_total(count_ref):
    return (count_ref[0, 0] + GROUP - 1) // GROUP


def build_body(count_ref, rows_ref, cols_ref, weight_ref, tiles_ref, live_ref):
    slots, edges = rows_ref.shape
    slot_ids = lax.broadcasted_iota(jnp.int32, (slots, edges), 0)
    live_ref[...] = jnp.where(slot_ids < count_ref[0, 0], weight_ref[...].astype(F32), 0.0)
    positions = lax.broadcasted_iota(jnp.int32, (TILE, edges), 0)

    def step(group, carry):
        for i in range(GROUP):
            slot = group * GROUP + i
            row_hot = jnp.where(positions == rows_ref[pl.ds(slot, 1), :], 1.0, 0.0).astype(BF16)
            col_hot = jnp.where(
                positions == cols_ref[pl.ds(slot, 1), :], live_ref[pl.ds(slot, 1), :], 0.0
            ).astype(BF16)
            built = lax.dot_general(
                row_hot, col_hot, (((1,), (1,)), ((), ())), preferred_element_type=F32
            )
            tiles_ref[slot] = built.astype(BF16)
        return carry

    lax.fori_loop(0, group_total(count_ref), step, 0)


def forward_body(count_ref, row_ref, col_ref, tiles_ref, feats_ref, out_ref, acc_ref):
    acc_ref[...] = jnp.zeros_like(acc_ref)
    half = acc_ref.shape[0] // N_CORE

    def step(group, carry):
        products = []
        for i in range(GROUP):
            slot = group * GROUP + i
            products.append(
                jnp.dot(tiles_ref[slot], feats_ref[col_ref[0, slot]], preferred_element_type=F32)
            )
        for i in range(GROUP):
            row = row_ref[0, group * GROUP + i]
            place = (row % N_CORE) * half + row // N_CORE
            acc_ref[place] += products[i]
        return carry

    lax.fori_loop(0, group_total(count_ref), step, 0)
    out_ref[...] = acc_ref[...].astype(BF16)


def dense_body(parts_ref, weight_ref, up_ref, act_ref, send_ref, *, scale):
    aggregated = jnp.sum(parts_ref[...].astype(F32), axis=0).astype(BF16)
    weight = weight_ref[...]
    pre_act = jnp.dot(aggregated, weight, preferred_element_type=F32)
    gate = jax.nn.sigmoid(pre_act)
    act_ref[...] = (pre_act * gate).astype(BF16)
    grad_pre = (up_ref[...].astype(F32) * gate * (1.0 + pre_act * (1.0 - gate))).astype(BF16)
    grad_agg = lax.dot_general(
        weight, grad_pre, (((1,), (1,)), ((), ())), preferred_element_type=F32
    ).astype(BF16)
    local_weight = (
        lax.dot_general(aggregated, grad_pre, (((0,), (0,)), ((), ())), preferred_element_type=F32)
        * scale
    )
    deep = TILE // N_ZL
    high, low = halves(local_weight)
    for peer in range(N_ZL):
        send_ref[peer, 0:TILE, :] = grad_agg
        here = slice(peer * deep, (peer + 1) * deep)
        for k, part in enumerate(
            (high[here, :TILE], high[here, TILE:], low[here, :TILE], low[here, TILE:])
        ):
            send_ref[peer, TILE + k * deep : TILE + (k + 1) * deep, :] = part


def spread_body(got_ref, send_ref):
    terms = jnp.sum(got_ref[:, TILE:, :].astype(F32), axis=0)
    high, low = halves(terms[:W_ROWS] + terms[W_ROWS:])
    for peer in range(N_Y):
        for k in range(N_ZL):
            send_ref[peer, k * TILE : (k + 1) * TILE, :] = got_ref[k, 0:TILE, :]
        send_ref[peer, N_ZL * TILE : N_ZL * TILE + W_ROWS, :] = high
        send_ref[peer, N_ZL * TILE + W_ROWS :, :] = low


def backward_body(
    count_ref, core_ref, row_ref, col_ref, tiles_ref, own_ref, other_ref, send_ref, grads_ref, acc_ref, sems
):
    core = core_ref[0]
    copies = [
        pltpu.make_async_copy(own_ref, grads_ref.at[core], sems.at[0]),
        pltpu.make_async_copy(other_ref, grads_ref.at[1 - core], sems.at[1]),
    ]
    for copy in copies:
        copy.start()
    acc_ref[...] = jnp.zeros_like(acc_ref)
    for copy in copies:
        copy.wait()

    def step(group, carry):
        products = []
        for i in range(GROUP):
            slot = group * GROUP + i
            row = row_ref[0, slot]
            start = pl.multiple_of(row // N_CORE % N_ZL * TILE, TILE)
            grad = grads_ref[row % N_CORE, row // (N_CORE * N_ZL), pl.ds(start, TILE), :]
            products.append(jnp.dot(grad, tiles_ref[slot], preferred_element_type=F32))
        for i in range(GROUP):
            acc_ref[col_ref[0, group * GROUP + i]] += products[i]
        return carry

    lax.fori_loop(0, group_total(count_ref), step, 0)
    terms = jnp.sum(grads_ref[:, :, N_ZL * TILE :, :].astype(F32), axis=(0, 1))
    high, low = halves(terms[:W_ROWS] + terms[W_ROWS:])
    for x in range(N_X):
        for zh in range(N_ZH):
            send_ref[x, zh * TILE : (zh + 1) * TILE, :] = acc_ref[x * N_ZH + zh].astype(BF16)
        send_ref[x, N_ZH * TILE : N_ZH * TILE + W_ROWS, :] = high
        send_ref[x, N_ZH * TILE + W_ROWS :, :] = low


def halfway_body(zh_ref, got_ref, send_ref, keep_ref, keep_weight_ref):
    zh = zh_ref[0]
    total = jnp.sum(got_ref[...].astype(F32), axis=0)
    first, second = total[:TILE], total[TILE : 2 * TILE]
    mine = zh == 0
    keep_ref[...] = jnp.where(mine, first, second)
    terms = total[2 * TILE :]
    weight_sum = terms[:W_ROWS] + terms[W_ROWS:]
    keep_weight_ref[...] = weight_sum
    high, low = halves(weight_sum)
    send_ref[0:TILE, :] = jnp.where(mine, second, first).astype(BF16)
    send_ref[TILE : TILE + W_ROWS, :] = high
    send_ref[TILE + W_ROWS :, :] = low


def finish_body(got_ref, keep_ref, keep_weight_ref, grad_ref, send_ref):
    grad_ref[...] = (keep_ref[...] + got_ref[0:TILE, :].astype(F32)).T.astype(BF16)
    terms = got_ref[TILE:, :].astype(F32)
    total = keep_weight_ref[...] + (terms[:W_ROWS] + terms[W_ROWS:])
    for peer in range(N_ZL):
        send_ref[peer] = total


def swap(value, axis):
    return lax.ppermute(value, axis, [(0, 1), (1, 0)])


def exchange(value, axis):
    return lax.all_to_all(value, axis, 0, 0, tiled=True)


def local(
    features, weight, upstream, tile_rows, tile_cols, tile_count, edge_rows, edge_cols, edge_weight
):
    width = features.shape[2]
    hidden = weight.shape[1]
    slots, edges = edge_rows.shape[2:]
    row_tiles, col_tiles = tile_rows[0], tile_cols[0]
    blocks = N_Y * N_ZL * N_CORE
    shape = jax.ShapeDtypeStruct

    zh = lax.axis_index("zh")
    own = features[0]
    other = swap(own, "zh")
    pair = jnp.where(zh == 0, jnp.stack([own, other]), jnp.stack([other, own]))
    column = lax.all_gather(pair, "x", axis=0, tiled=True)

    tiles = call(
        build_body,
        shape((slots, TILE, TILE), BF16),
        [smem, vmem, vmem, vmem],
        [pltpu.VMEM((slots, edges), F32)],
        flops=slots * TILE * TILE * edges * 8,
        moved=slots * TILE * TILE * 2,
    )(tile_count, edge_rows[0, 0], edge_cols[0, 0], edge_weight[0, 0])

    partial = call(
        forward_body,
        shape((blocks, TILE, width), BF16),
        [smem, smem, smem, vmem, vmem],
        [pltpu.VMEM((blocks, TILE, width), F32)],
        flops=slots * TILE * TILE * width * 2,
        moved=slots * TILE * TILE * 4,
    )(tile_count, row_tiles, col_tiles, tiles, column)

    for axis, size in (("core", N_CORE), ("y", N_Y)):
        got = exchange(partial, axis)
        got = got.reshape((size, -1) + got.shape[1:])
        partial = jnp.sum(got.astype(F32), axis=0).astype(BF16)
    parts = exchange(partial, "zl")

    node_total = features.shape[1] * N_X * N_ZH * blocks
    scale = 1.0 / math.sqrt(node_total)

    def dense(*refs):
        dense_body(*refs, scale=scale)

    out_act, send = call(
        dense,
        (shape((TILE, hidden), BF16), shape((N_ZL, TILE + 2 * W_ROWS, TILE), BF16)),
        [vmem] * 3,
    )(parts, weight, upstream[0])

    got = exchange(send, "zl")
    send = call(spread_body, shape((N_Y, N_ZL * TILE + 2 * W_ROWS, TILE), BF16), [vmem])(got)
    mine = exchange(send, "y")
    theirs = swap(mine, "core")
    send = call(
        backward_body,
        shape((N_X, N_ZH * TILE + 2 * W_ROWS, TILE), BF16),
        [smem, smem, smem, smem, vmem, hbm, hbm],
        [
            pltpu.VMEM((N_CORE,) + mine.shape, BF16),
            pltpu.VMEM((N_X * N_ZH, width, TILE), F32),
            pltpu.SemaphoreType.DMA((2,)),
        ],
    )(
        tile_count,
        lax.axis_index("core").astype(jnp.int32)[None],
        row_tiles,
        col_tiles,
        tiles,
        mine,
        theirs,
    )

    got = exchange(send, "x")
    send, keep, keep_weight = call(
        halfway_body,
        (
            shape((TILE + 2 * W_ROWS, TILE), BF16),
            shape((TILE, TILE), F32),
            shape((W_ROWS, TILE), F32),
        ),
        [smem, vmem],
    )(zh.astype(jnp.int32)[None], got)
    got = swap(send, "zh")
    grad_features, send = call(
        finish_body,
        (shape((TILE, width), BF16), shape((N_ZL, W_ROWS, TILE), F32)),
        [vmem] * 3,
    )(got, keep, keep_weight)
    got = exchange(send, "zl")
    grad_weight = got.reshape(N_ZL, hidden // TILE, -1, TILE).transpose(0, 2, 1, 3)
    grad_weight = grad_weight.reshape(width, hidden)
    return (out_act[None], grad_features[None], grad_weight)


def solution(mesh):
    fine = Mesh(mesh.devices.reshape([size for _, size in FINE]), [name for name, _ in FINE])
    in_specs = (
        P(COL, ROW, None),
        P(),
        P(COL, ROW, None),
        P(ROW, COL, None),
        P(ROW, COL, None),
        P(ROW, COL),
        P(ROW, COL, None, None),
        P(ROW, COL, None, None),
        P(ROW, COL, None, None),
    )
    out_specs = (P(COL, ROW, None), P(COL, ROW, None), P())
    return jax.shard_map(local, mesh=fine, in_specs=in_specs, out_specs=out_specs, check_vma=False)
```

time: 1540 us -> 185 us (0.12)
  the two profiles are of different devices: /device:TPU:185 before, /device:TPU:1 now
where the time goes in v1:
time: 185 us; the launch traced here: 182 us
  blocking collectives  124 us (67%)
  starting transfers between devices  32.9 us (18%)
  Pallas kernels  9.72 us (5%)
  waiting for transfers between devices  7.15 us (4%)
  other arithmetic  3.54 us (2%)
  local copies, waits for them, and re-layouts  3.18 us (2%)
    all_to_all x7, blocking collectives, exchange(): return lax.all_to_all(value, axis, 0, 0, tiled=True)  115 us
    ppermute x3, starting transfers between devices, swap(): return lax.ppermute(value, axis, [(0, 1), (1, 0)])  32.9 us
    all_gather x1, blocking collectives, local(): column = lax.all_gather(pair, 'x', axis=0, tiled=True)  9.71 us
    ppermute x3, waiting for transfers between devices, swap(): return lax.ppermute(value, axis, [(0, 1), (1, 0)])  7.15 us
  transfers between devices with their start and end apart: 3, of which 2 were waited for; matrix products, arithmetic and copies ran while one was open for 0% of the time, Pallas kernels for 1%

profile of v1, /device:TPU:1, one launch (start us, length us, event | category | flops | bytes accessed | tf_op | source)
XLA Modules:
  0.0 182.2 jit_solution(5963010848419382893)
XLA Ops:
  0.6 16.3 %collective-permute-start = (bf16[128,128]{1,0:T(8,128)(2,1)}, bf16[128,128]{1,0:T(8,128)(2,1)S(1)}, u32[]{:S(2)}, u32[]{:S(2)}) collective-permute-start(bf16[128,128]{1,0:T(8,128)(2,1)} %bitcast.35), channel_id=1, source_target_pairs={{0,64},{64,0},{1,65},{65,1},{2,66},{66,2},{3,67},{67,3},{4,68},{68... | collective-permute-start | bytes 98312 | tf_op jit(solution)/shard_map/ppermute | solution.py:186
  17.6 0.0 copy-start.4
  17.6 0.8 copy-done.4
  18.4 0.0 copy-start.5
  18.4 0.8 copy-done.5
  19.2 0.0 copy-start.6
  19.2 0.8 copy-done.6
  20.0 0.0 copy-start.7
  20.0 0.0 copy-start.2
  20.0 0.0 copy-start.3
  20.0 2.0 %shard_map.112.tiles_ref = bf16[64,128,128]{2,1,0:T(8,128)(2,1)S(1)} custom-call(s32[1,1]{1,0:T(1,128)S(6)} %copy.18.count_ref, s32[64,192]{1,0:T(8,128)S(1)} %bitcast.27, s32[64,192]{1,0:T(8,128)S(1)} %bitcast.28, bf16[64,192]{1,0:T(8,128)(2,1)S(1)} %bitcast.29), custom_call_target="tpu_custom_call" | custom-call | flops 1610612736 | bytes 2097152 | tf_op jit(solution)/shard_map/pallas_call | solution.py:209
  22.0 0.0 collective-permute-done
  22.0 0.0 copy-done.7
  22.0 9.7 %all_gather.3.feats_ref = bf16[8,128,128]{2,1,0:T(8,128)(2,1)S(1)} all-gather(bf16[2,128,128]{2,1,0:T(8,128)(2,1)S(1)} %maximum_select_fusion), channel_id=1, replica_groups=mesh['x'=4,'zh'=2,'y'=4,'zl'=8,'core'=2] {'x'}, dimensions={0}, use_global_device_ids=true | all-gather | bytes 327680 | tf_op jit(solution)/shard_map/all_gather | solution.py:207
  31.7 0.0 copy-done.2
  31.7 0.0 copy-done.3
  31.7 2.5 %shard_map.113 = bf16[64,128,128]{2,1,0:T(8,128)(2,1)S(1)} custom-call(s32[1,1]{1,0:T(1,128)S(6)} %copy.18.count_ref, s32[1,64]{1,0:T(1,128)S(1)} %bitcast.23, s32[1,64]{1,0:T(1,128)S(1)} %bitcast.25, bf16[64,128,128]{2,1,0:T(8,128)(2,1)S(1)} %shard_map.112.tiles_ref, bf16[8,128,128]{2,1,0:T(8,128)(2,1)S(1)} %all_gather.3.feats_ref), custom_call_target="tpu_custom_call" | custom-call | flops 268435456 | bytes 4194304 | tf_op jit(solution)/shard_map/pallas_call | solution.py:218
  34.2 9.6 %all_to_all.35 = bf16[64,128,128]{2,1,0:T(8,128)(2,1)} all-to-all(bf16[64,128,128]{2,1,0:T(8,128)(2,1)S(1)} %shard_map.113), channel_id=1, replica_groups=mesh['x'=4,'zh'=2,'y'=4,'zl'=8,'core'=2] {'core'}, dimensions={0} | all-to-all | bytes 4194304 | tf_op jit(solution)/shard_map/all_to_all | solution.py:190
  43.8 3.3 %reduce_sum.24 = bf16[32,128,128]{2,1,0:T(8,128)(2,1)} reduce(bf16[2,32,128,128]{3,2,1,0:T(8,128)(2,1)} %bitcast.30, bf16[]{:T(256)} %constant.13.clone.1), dimensions={0}, to_apply=%region_0.1 | reduce | flops 524288 | bytes 3145730 | tf_op jit(solution)/shard_map/reduce_sum | solution.py:230
  47.2 0.0 copy-start
  47.2 0.0 copy-start.1
  47.2 18.5 %all_to_all.36 = bf16[32,128,128]{2,1,0:T(8,128)(2,1)S(1)} all-to-all(bf16[32,128,128]{2,1,0:T(8,128)(2,1)} %reduce_sum.24), channel_id=1, replica_groups=mesh['x'=4,'zh'=2,'y'=4,'zl'=8,'core'=2] {'y'}, dimensions={0} | all-to-all | bytes 2097152 | tf_op jit(solution)/shard_map/all_to_all | solution.py:190
  65.6 0.2 reduce_sum.25
  65.8 18.1 %all_to_all.37.refs_0_ = bf16[8,128,128]{2,1,0:T(8,128)(2,1)S(1)} all-to-all(bf16[8,128,128]{2,1,0:T(8,128)(2,1)S(1)} %reduce_sum.25), channel_id=1, replica_groups=mesh['x'=4,'zh'=2,'y'=4,'zl'=8,'core'=2] {'zl'}, dimensions={0} | all-to-all | bytes 524288 | tf_op jit(solution)/shard_map/all_to_all | solution.py:190
  83.9 0.0 copy-done
  83.9 0.0 copy-done.1
  83.9 0.8 shard_map.114
  84.8 28.4 %all_to_all.38.got_ref = bf16[8,192,128]{2,1,0:T(8,128)(2,1)S(1)} all-to-all(bf16[8,192,128]{2,1,0:T(8,128)(2,1)S(1)} %get-tuple-element.11), channel_id=1, replica_groups=mesh['x'=4,'zh'=2,'y'=4,'zl'=8,'core'=2] {'zl'}, dimensions={0} | all-to-all | bytes 786432 | tf_op jit(solution)/shard_map/all_to_all | solution.py:190
  113.1 0.1 shard_map.115
  113.3 13.4 %all_to_all.39.own_ref = bf16[4,1088,128]{2,1,0:T(8,128)(2,1)S(1)} all-to-all(bf16[4,1088,128]{2,1,0:T(8,128)(2,1)S(1)} %shard_map.115), channel_id=1, replica_groups=mesh['x'=4,'zh'=2,'y'=4,'zl'=8,'core'=2] {'y'}, dimensions={0} | all-to-all | bytes 2228224 | tf_op jit(solution)/shard_map/all_to_all | solution.py:190
  126.7 7.7 %collective-permute-start.1 = (bf16[4,1088,128]{2,1,0:T(8,128)(2,1)S(1)}, bf16[4,1088,128]{2,1,0:T(8,128)(2,1)}, u32[]{:S(2)}, u32[]{:S(2)}) collective-permute-start(bf16[4,1088,128]{2,1,0:T(8,128)(2,1)S(1)} %all_to_all.39.own_ref), channel_id=1, source_target_pairs={{0,1},{1,0},{2,3},{3,2},{4,5},{5,4},{6,7},{7,6},{8,9},{9,8},{10,11... | collective-permute-start | bytes 3342344 | tf_op jit(solution)/shard_map/ppermute | solution.py:186
  134.4 2.5 %collective-permute-done.1.other_ref = bf16[4,1088,128]{2,1,0:T(8,128)(2,1)} collective-permute-done((bf16[4,1088,128]{2,1,0:T(8,128)(2,1)S(1)}, bf16[4,1088,128]{2,1,0:T(8,128)(2,1)}, u32[]{:S(2)}, u32[]{:S(2)}) %collective-permute-start.1) | collective-permute-done | bytes 1114144 | tf_op jit(solution)/shard_map/ppermute | solution.py:186
  136.8 3.5 %shard_map.116 = bf16[4,320,128]{2,1,0:T(8,128)(2,1)S(1)} custom-call(s32[1,1]{1,0:T(1,128)S(6)} %copy.18.count_ref, s32[1]{0:T(128)} %bitcast.12.core_ref, s32[1,64]{1,0:T(1,128)S(1)} %bitcast.24, s32[1,64]{1,0:T(1,128)S(1)} %bitcast.26, bf16[64,128,128]{2,1,0:T(8,128)(2,1)S(1)} %shard_map.112.tiles_ref, bf16[4,1088,128]{2,1,0:T(8,128)(2,1)S(1)} %all_to_all.39.own_ref, ...), custom_call_target="tpu_custom_call" | custom-call | tf_op jit(solution)/shard_map/pallas_call | solution.py:249
  140.4 9.7 %all_to_all.40.got_ref = bf16[4,320,128]{2,1,0:T(8,128)(2,1)S(1)} all-to-all(bf16[4,320,128]{2,1,0:T(8,128)(2,1)S(1)} %shard_map.116), channel_id=1, replica_groups=mesh['x'=4,'zh'=2,'y'=4,'zl'=8,'core'=2] {'x'}, dimensions={0} | all-to-all | bytes 655360 | tf_op jit(solution)/shard_map/all_to_all | solution.py:190
  150.1 9.0 %collective-permute-start.2 = (bf16[192,128]{1,0:T(8,128)(2,1)S(1)}, bf16[192,128]{1,0:T(8,128)(2,1)S(1)}, u32[]{:S(2)}, u32[]{:S(2)}) collective-permute-start(bf16[192,128]{1,0:T(8,128)(2,1)S(1)} %get-tuple-element.12), channel_id=1, source_target_pairs={{0,64},{64,0},{1,65},{65,1},{2,66},{66,2},{3,67},{67,3},{4,68},{68... | collective-permute-start | bytes 147464 | tf_op jit(solution)/shard_map/ppermute | solution.py:186
  159.1 4.7 %collective-permute-done.2.got_ref = bf16[192,128]{1,0:T(8,128)(2,1)S(1)} collective-permute-done((bf16[192,128]{1,0:T(8,128)(2,1)S(1)}, bf16[192,128]{1,0:T(8,128)(2,1)S(1)}, u32[]{:S(2)}, u32[]{:S(2)}) %collective-permute-start.2) | collective-permute-done | bytes 49184 | tf_op jit(solution)/shard_map/ppermute | solution.py:186
  163.8 0.7 shard_map.118
  164.5 16.9 %all_to_all.41 = f32[8,32,128]{2,1,0:T(8,128)S(1)} all-to-all(f32[8,32,128]{2,1,0:T(8,128)S(1)} %get-tuple-element.16), channel_id=1, replica_groups=mesh['x'=4,'zh'=2,'y'=4,'zl'=8,'core'=2] {'zl'}, dimensions={0} | all-to-all | bytes 262144 | tf_op jit(solution)/shard_map/all_to_all | solution.py:190
  181.5 0.1 copy.14
  181.5 0.7 copy.17
  (2 shorter events, 0.1 us)
Async XLA Ops:
  0.6 21.4 %collective-permute-start = (bf16[128,128]{1,0:T(8,128)(2,1)}, bf16[128,128]{1,0:T(8,128)(2,1)S(1)}, u32[]{:S(2)}, u32[]{:S(2)}) collective-permute-start(bf16[128,128]{1,0:T(8,128)(2,1)} %bitcast.35), channel_id=1, source_target_pairs={{0,64},{64,0},{1,65},{65,1},{2,66},{66,2},{3,67},{67,3},{4,68},{68... | collective-permute-start | bytes 98312 | tf_op jit(solution)/shard_map/ppermute | solution.py:186
  17.6 0.8 copy-start.4
  18.4 0.8 copy-start.5
  19.2 0.8 copy-start.6
  20.0 2.0 %copy-start.7 = (bf16[1,128,128]{2,1,0:T(8,128)(2,1)S(1)}, bf16[1,128,128]{2,1,0:T(8,128)(2,1)}, u32[]{:S(2)}) copy-start(bf16[1,128,128]{2,1,0:T(8,128)(2,1)} %param.9) | copy-start | bytes 98308
  20.0 11.7 %copy-start.2 = (s32[1,1,64]{2,1,0:T(1,128)S(1)}, s32[1,1,64]{2,1,0:T(1,128)}, u32[]{:S(2)}) copy-start(s32[1,1,64]{2,1,0:T(1,128)} %param.12) | copy-start | bytes 772
  20.0 11.7 %copy-start.3 = (s32[1,1,64]{2,1,0:T(1,128)S(1)}, s32[1,1,64]{2,1,0:T(1,128)}, u32[]{:S(2)}) copy-start(s32[1,1,64]{2,1,0:T(1,128)} %param.13) | copy-start | bytes 772
  47.2 36.8 %copy-start = (bf16[128,256]{1,0:T(8,128)(2,1)S(1)}, bf16[128,256]{1,0:T(8,128)(2,1)}, u32[]{:S(2)}) copy-start(bf16[128,256]{1,0:T(8,128)(2,1)} %refs_1_.1) | copy-start | bytes 196612
  47.2 36.8 %copy-start.1 = (bf16[1,128,256]{2,1,0:T(8,128)(2,1)S(1)}, bf16[1,128,256]{2,1,0:T(8,128)(2,1)}, u32[]{:S(2)}) copy-start(bf16[1,128,256]{2,1,0:T(8,128)(2,1)} %param.11) | copy-start | bytes 196612
  126.7 10.2 %collective-permute-start.1 = (bf16[4,1088,128]{2,1,0:T(8,128)(2,1)S(1)}, bf16[4,1088,128]{2,1,0:T(8,128)(2,1)}, u32[]{:S(2)}, u32[]{:S(2)}) collective-permute-start(bf16[4,1088,128]{2,1,0:T(8,128)(2,1)S(1)} %all_to_all.39.own_ref), channel_id=1, source_target_pairs={{0,1},{1,0},{2,3},{3,2},{4,5},{5,4},{6,7},{7,6},{8,9},{9,8},{10,11... | collective-permute-start | bytes 3342344 | tf_op jit(solution)/shard_map/ppermute | solution.py:186
  150.1 13.6 %collective-permute-start.2 = (bf16[192,128]{1,0:T(8,128)(2,1)S(1)}, bf16[192,128]{1,0:T(8,128)(2,1)S(1)}, u32[]{:S(2)}, u32[]{:S(2)}) collective-permute-start(bf16[192,128]{1,0:T(8,128)(2,1)S(1)} %get-tuple-element.12), channel_id=1, source_target_pairs={{0,64},{64,0},{1,65},{65,1},{2,66},{66,2},{3,67},{67,3},{4,68},{68... | collective-permute-start | bytes 147464 | tf_op jit(solution)/shard_map/ppermute | solution.py:186

commit v2 on v1

--- a/solution.py
+++ b/solution.py
@@ -67,9 +67,11 @@
     lax.fori_loop(0, group_total(count_ref), step, 0)
 
 
-def forward_body(count_ref, row_ref, col_ref, tiles_ref, feats_ref, out_ref, acc_ref):
+def forward_body(
+    count_ref, core_ref, row_ref, col_ref, tiles_ref, feats_ref, send_ref, keep_ref, acc_ref
+):
     acc_ref[...] = jnp.zeros_like(acc_ref)
-    half = acc_ref.shape[0] // N_CORE
+    core = core_ref[0]
 
     def step(group, carry):
         products = []
@@ -80,12 +82,16 @@
             )
         for i in range(GROUP):
             row = row_ref[0, group * GROUP + i]
-            place = (row % N_CORE) * half + row // N_CORE
-            acc_ref[place] += products[i]
+            acc_ref[row % N_CORE, row // N_CORE] += products[i]
         return carry
 
     lax.fori_loop(0, group_total(count_ref), step, 0)
-    out_ref[...] = acc_ref[...].astype(BF16)
+    send_ref[...] = acc_ref[1 - core].astype(BF16)
+    keep_ref[...] = acc_ref[core]
+
+
+def merge_body(got_ref, keep_ref, out_ref):
+    out_ref[...] = (keep_ref[...] + got_ref[...].astype(F32)).astype(BF16)
 
 
 def dense_body(parts_ref, weight_ref, up_ref, act_ref, send_ref, *, scale):
@@ -103,19 +109,16 @@
         * scale
     )
     deep = TILE // N_ZL
-    high, low = halves(local_weight)
+    local_weight = local_weight.astype(BF16)
     for peer in range(N_ZL):
         send_ref[peer, 0:TILE, :] = grad_agg
         here = slice(peer * deep, (peer + 1) * deep)
-        for k, part in enumerate(
-            (high[here, :TILE], high[here, TILE:], low[here, :TILE], low[here, TILE:])
-        ):
-            send_ref[peer, TILE + k * deep : TILE + (k + 1) * deep, :] = part
+        send_ref[peer, TILE : TILE + deep, :] = local_weight[here, :TILE]
+        send_ref[peer, TILE + deep :, :] = local_weight[here, TILE:]
 
 
 def spread_body(got_ref, send_ref):
-    terms = jnp.sum(got_ref[:, TILE:, :].astype(F32), axis=0)
-    high, low = halves(terms[:W_ROWS] + terms[W_ROWS:])
+    high, low = halves(jnp.sum(got_ref[:, TILE:, :].astype(F32), axis=0))
     for peer in range(N_Y):
         for k in range(N_ZL):
             send_ref[peer, k * TILE : (k + 1) * TILE, :] = got_ref[k, 0:TILE, :]
@@ -159,27 +162,26 @@
         send_ref[x, N_ZH * TILE + W_ROWS :, :] = low
 
 
-def halfway_body(zh_ref, got_ref, send_ref, keep_ref, keep_weight_ref):
+def halfway_body(zh_ref, got_ref, send_ref, keep_ref, send_weight_ref):
     zh = zh_ref[0]
     total = jnp.sum(got_ref[...].astype(F32), axis=0)
     first, second = total[:TILE], total[TILE : 2 * TILE]
     mine = zh == 0
     keep_ref[...] = jnp.where(mine, first, second)
+    send_ref[...] = jnp.where(mine, second, first).astype(BF16)
     terms = total[2 * TILE :]
-    weight_sum = terms[:W_ROWS] + terms[W_ROWS:]
-    keep_weight_ref[...] = weight_sum
-    high, low = halves(weight_sum)
-    send_ref[0:TILE, :] = jnp.where(mine, second, first).astype(BF16)
-    send_ref[TILE : TILE + W_ROWS, :] = high
-    send_ref[TILE + W_ROWS :, :] = low
-
-
-def finish_body(got_ref, keep_ref, keep_weight_ref, grad_ref, send_ref):
-    grad_ref[...] = (keep_ref[...] + got_ref[0:TILE, :].astype(F32)).T.astype(BF16)
-    terms = got_ref[TILE:, :].astype(F32)
-    total = keep_weight_ref[...] + (terms[:W_ROWS] + terms[W_ROWS:])
-    for peer in range(N_ZL):
-        send_ref[peer] = total
+    weight_sum = (terms[:W_ROWS] + terms[W_ROWS:]).astype(BF16)
+    for peer in range(N_ZH * N_ZL):
+        send_weight_ref[peer] = weight_sum
+
+
+def finish_body(got_ref, keep_ref, got_weight_ref, grad_ref, grad_weight_ref):
+    grad_ref[...] = (keep_ref[...] + got_ref[...].astype(F32)).T.astype(BF16)
+    deep = TILE // N_ZL
+    for k in range(N_ZL):
+        total = got_weight_ref[k].astype(F32) + got_weight_ref[N_ZL + k].astype(F32)
+        grad_weight_ref[k * deep : (k + 1) * deep, :TILE] = total[:deep]
+        grad_weight_ref[k * deep : (k + 1) * deep, TILE:] = total[deep:]
 
 
 def swap(value, axis):
@@ -204,7 +206,8 @@
     own = features[0]
     other = swap(own, "zh")
     pair = jnp.where(zh == 0, jnp.stack([own, other]), jnp.stack([other, own]))
-    column = lax.all_gather(pair, "x", axis=0, tiled=True)
+    pair = jnp.broadcast_to(pair[None], (N_X,) + pair.shape)
+    column = exchange(pair, "x").reshape(N_X * N_ZH, TILE, width)
 
     tiles = call(
         build_body,
@@ -215,19 +218,20 @@
         moved=slots * TILE * TILE * 2,
     )(tile_count, edge_rows[0, 0], edge_cols[0, 0], edge_weight[0, 0])
 
-    partial = call(
+    core = lax.axis_index("core").astype(jnp.int32)[None]
+    half = (blocks // N_CORE, TILE, width)
+    send, keep = call(
         forward_body,
-        shape((blocks, TILE, width), BF16),
-        [smem, smem, smem, vmem, vmem],
-        [pltpu.VMEM((blocks, TILE, width), F32)],
+        (shape(half, BF16), shape(half, F32)),
+        [smem, smem, smem, smem, vmem, vmem],
+        [pltpu.VMEM((N_CORE,) + half, F32)],
         flops=slots * TILE * TILE * width * 2,
         moved=slots * TILE * TILE * 4,
-    )(tile_count, row_tiles, col_tiles, tiles, column)
-
-    for axis, size in (("core", N_CORE), ("y", N_Y)):
-        got = exchange(partial, axis)
-        got = got.reshape((size, -1) + got.shape[1:])
-        partial = jnp.sum(got.astype(F32), axis=0).astype(BF16)
+    )(tile_count, core, row_tiles, col_tiles, tiles, column)
+
+    partial = call(merge_body, shape(half, BF16), [vmem, vmem])(swap(send, "core"), keep)
+    got = exchange(partial, "y").reshape((N_Y, N_ZL, TILE, width))
+    partial = jnp.sum(got.astype(F32), axis=0).astype(BF16)
     parts = exchange(partial, "zl")
 
     node_total = features.shape[1] * N_X * N_ZH * blocks
@@ -238,7 +242,7 @@
 
     out_act, send = call(
         dense,
-        (shape((TILE, hidden), BF16), shape((N_ZL, TILE + 2 * W_ROWS, TILE), BF16)),
+        (shape((TILE, hidden), BF16), shape((N_ZL, TILE + W_ROWS, TILE), BF16)),
         [vmem] * 3,
     )(parts, weight, upstream[0])
 
@@ -257,7 +261,7 @@
         ],
     )(
         tile_count,
-        lax.axis_index("core").astype(jnp.int32)[None],
+        core,
         row_tiles,
         col_tiles,
         tiles,
@@ -266,24 +270,22 @@
     )
 
     got = exchange(send, "x")
-    send, keep, keep_weight = call(
+    send, keep, send_weight = call(
         halfway_body,
         (
-            shape((TILE + 2 * W_ROWS, TILE), BF16),
+            shape((TILE, TILE), BF16),
             shape((TILE, TILE), F32),
-            shape((W_ROWS, TILE), F32),
+            shape((N_ZH * N_ZL, W_ROWS, TILE), BF16),
         ),
         [smem, vmem],
     )(zh.astype(jnp.int32)[None], got)
     got = swap(send, "zh")
-    grad_features, send = call(
+    got_weight = exchange(send_weight, ("zh", "zl"))
+    grad_features, grad_weight = call(
         finish_body,
-        (shape((TILE, width), BF16), shape((N_ZL, W_ROWS, TILE), F32)),
+        (shape((TILE, width), BF16), shape((width, hidden), F32)),
         [vmem] * 3,
-    )(got, keep, keep_weight)
-    got = exchange(send, "zl")
-    grad_weight = got.reshape(N_ZL, hidden // TILE, -1, TILE).transpose(0, 2, 1, 3)
-    grad_weight = grad_weight.reshape(width, hidden)
+    )(got, keep, got_weight)
     return (out_act[None], grad_features[None], grad_weight)
 
 

time: 185 us -> 168 us (0.908); the launches traced: 182 us -> 168 us
  blocking collectives: 124 us -> 86.4 us
  starting transfers between devices: 32.9 us -> 55.9 us
  waiting for transfers between devices: 7.15 us -> 13.1 us
  Pallas kernels: 9.72 us -> 6.4 us
  other arithmetic: 3.54 us -> 1.05 us
    all_to_all x7 -> x5, blocking collectives: 115 us -> 86.4 us  [exchange(): return lax.all_to_all(value, axis, 0, 0, tiled=True)]
    all_to_all x0 -> x2, starting transfers between devices: none -> 13.8 us  [exchange(): return lax.all_to_all(value, axis, 0, 0, tiled=True)]
    all_gather x1 -> x0, blocking collectives: 9.71 us -> none  [local(): column = lax.all_gather(pair, 'x', axis=0, tiled=True)]
    ppermute x3 -> x4, starting transfers between devices: 32.9 us -> 42.1 us  [swap(): return lax.ppermute(value, axis, [(0, 1), (1, 0)])]
    ppermute x3 -> x4, waiting for transfers between devices: 7.15 us -> 11.5 us  [swap(): return lax.ppermute(value, axis, [(0, 1), (1, 0)])]
    reduce_sum x2 -> x1, other arithmetic: 3.53 us -> 0.2 us  [local(): partial = jnp.sum(got.astype(F32), axis=0).astype(BF16)]
    pallas_call x1, Pallas kernels: 3.54 us -> 1.54 us  [local(): call(backward_body, shape((N_X, N_ZH * TILE + 2 * W_ROWS, TILE), BF16), [...]
    pallas_call x4 -> x5, Pallas kernels: 4.08 us -> 3.99 us  [the longest x1 1.61 us: local(): call(forward_body, (shape(half, BF16), shape(half, F32)), [smem, smem, sm...]
  transfers between devices with their start and end apart: 3 -> 6, of which waited for: 2 -> 5; matrix products, arithmetic and copies ran while one was open for 0% -> 0% of each run, Pallas kernels for 1% -> 0%
where the time goes in v2:
time: 168 us
  blocking collectives  86.4 us (51%)
  starting transfers between devices  55.9 us (33%)
  waiting for transfers between devices  13.1 us (8%)
  Pallas kernels  6.4 us (4%)
  local copies, waits for them, and re-layouts  3.18 us (2%)
    all_to_all x5, blocking collectives, exchange(): return lax.all_to_all(value, axis, 0, 0, tiled=True)  86.4 us
    ppermute x4, starting transfers between devices, swap(): return lax.ppermute(value, axis, [(0, 1), (1, 0)])  42.1 us
    all_to_all x2, starting transfers between devices, exchange(): return lax.all_to_all(value, axis, 0, 0, tiled=True)  13.8 us
    ppermute x4, waiting for transfers between devices, swap(): return lax.ppermute(value, axis, [(0, 1), (1, 0)])  11.5 us
  transfers between devices with their start and end apart: 6, of which 5 were waited for; matrix products, arithmetic and copies ran while one was open for 0% of the time, Pallas kernels for 0%

profile of v2, /device:TPU:1, one launch (start us, length us, event | category | flops | bytes accessed | tf_op | source)
XLA Modules:
  0.0 167.5 jit_solution(11486021109686726029)
XLA Ops:
  0.6 16.3 %collective-permute-start = (bf16[128,128]{1,0:T(8,128)(2,1)}, bf16[128,128]{1,0:T(8,128)(2,1)S(1)}, u32[]{:S(2)}, u32[]{:S(2)}) collective-permute-start(bf16[128,128]{1,0:T(8,128)(2,1)} %bitcast.24), channel_id=1, source_target_pairs={{0,64},{64,0},{1,65},{65,1},{2,66},{66,2},{3,67},{67,3},{4,68},{68... | collective-permute-start | bytes 98312 | tf_op jit(solution)/shard_map/ppermute | solution.py:188
  16.9 1.6 collective-permute-done
  18.5 0.8 maximum_select_fusion
  19.4 0.7 broadcast_in_dim.19
  20.1 4.0 %all-to-all-start = ((bf16[4,2,128,128]{3,2,1,0:T(8,128)(2,1)}), bf16[4,2,128,128]{3,2,1,0:T(8,128)(2,1)S(1)}, u32[]{:S(2)}, u32[]{:S(2)}) async-start(bf16[4,2,128,128]{3,2,1,0:T(8,128)(2,1)} %broadcast_in_dim.19), calls=%async_computation | async-start | bytes 524288 | tf_op jit(solution)/shard_map/all_to_all | solution.py:192
  24.8 0.0 copy-start.4
  24.8 0.8 copy-done.4
  25.6 0.0 copy-start.5
  25.6 0.8 copy-done.5
  26.4 0.0 copy-start.6
  26.4 0.8 copy-done.6
  27.2 0.0 copy-start.2
  27.2 0.0 copy-start.3
  27.2 0.7 shard_map.112.tiles_ref
  27.9 1.7 %all-to-all-done = bf16[4,2,128,128]{3,2,1,0:T(8,128)(2,1)S(1)} async-done(((bf16[4,2,128,128]{3,2,1,0:T(8,128)(2,1)}), bf16[4,2,128,128]{3,2,1,0:T(8,128)(2,1)S(1)}, u32[]{:S(2)}, u32[]{:S(2)}) %all-to-all-start) | async-done | bytes 262176 | tf_op jit(solution)/shard_map/all_to_all | solution.py:192
  29.6 0.0 copy-done.2
  29.6 0.0 copy-done.3
  29.6 1.6 shard_map.113
  31.3 6.9 %collective-permute-start.1 = (bf16[32,128,128]{2,1,0:T(8,128)(2,1)S(1)}, bf16[32,128,128]{2,1,0:T(8,128)(2,1)S(1)}, u32[]{:S(2)}, u32[]{:S(2)}) collective-permute-start(bf16[32,128,128]{2,1,0:T(8,128)(2,1)S(1)} %get-tuple-element.12), channel_id=1, source_target_pairs={{0,1},{1,0},{2,3},{3,2},{4,5},{5,4},{6,7},{7,6},{8,9},{9,8},{10,11... | collective-permute-start | bytes 3145736 | tf_op jit(solution)/shard_map/ppermute | solution.py:188
  38.2 2.3 %collective-permute-done.1.got_ref = bf16[32,128,128]{2,1,0:T(8,128)(2,1)S(1)} collective-permute-done((bf16[32,128,128]{2,1,0:T(8,128)(2,1)S(1)}, bf16[32,128,128]{2,1,0:T(8,128)(2,1)S(1)}, u32[]{:S(2)}, u32[]{:S(2)}) %collective-permute-start.1) | collective-permute-done | bytes 1048608 | tf_op jit(solution)/shard_map/ppermute | solution.py:188
  40.4 0.2 shard_map.114
  40.6 17.3 %all_to_all.35 = bf16[32,128,128]{2,1,0:T(8,128)(2,1)S(1)} all-to-all(bf16[32,128,128]{2,1,0:T(8,128)(2,1)S(1)} %shard_map.114), channel_id=1, replica_groups=mesh['x'=4,'zh'=2,'y'=4,'zl'=8,'core'=2] {'y'}, dimensions={0} | all-to-all | bytes 2097152 | tf_op jit(solution)/shard_map/all_to_all | solution.py:192
  57.9 0.0 copy-start
  57.9 0.0 copy-start.1
  57.9 0.2 reduce_sum.12
  58.1 20.3 %all_to_all.36.refs_0_ = bf16[8,128,128]{2,1,0:T(8,128)(2,1)S(1)} all-to-all(bf16[8,128,128]{2,1,0:T(8,128)(2,1)S(1)} %reduce_sum.12), channel_id=1, replica_groups=mesh['x'=4,'zh'=2,'y'=4,'zl'=8,'core'=2] {'zl'}, dimensions={0} | all-to-all | bytes 524288 | tf_op jit(solution)/shard_map/all_to_all | solution.py:192
  78.4 0.0 copy-done
  78.4 0.0 copy-done.1
  78.4 0.8 shard_map.115
  79.2 26.3 %all_to_all.37.got_ref = bf16[8,160,128]{2,1,0:T(8,128)(2,1)S(1)} all-to-all(bf16[8,160,128]{2,1,0:T(8,128)(2,1)S(1)} %get-tuple-element.15), channel_id=1, replica_groups=mesh['x'=4,'zh'=2,'y'=4,'zl'=8,'core'=2] {'zl'}, dimensions={0} | all-to-all | bytes 655360 | tf_op jit(solution)/shard_map/all_to_all | solution.py:192
  105.5 0.1 shard_map.116
  105.6 14.1 %all_to_all.38.own_ref = bf16[4,1088,128]{2,1,0:T(8,128)(2,1)S(1)} all-to-all(bf16[4,1088,128]{2,1,0:T(8,128)(2,1)S(1)} %shard_map.116), channel_id=1, replica_groups=mesh['x'=4,'zh'=2,'y'=4,'zl'=8,'core'=2] {'y'}, dimensions={0} | all-to-all | bytes 2228224 | tf_op jit(solution)/shard_map/all_to_all | solution.py:192
  119.7 7.0 %collective-permute-start.2 = (bf16[4,1088,128]{2,1,0:T(8,128)(2,1)S(1)}, bf16[4,1088,128]{2,1,0:T(8,128)(2,1)S(1)}, u32[]{:S(2)}, u32[]{:S(2)}) collective-permute-start(bf16[4,1088,128]{2,1,0:T(8,128)(2,1)S(1)} %all_to_all.38.own_ref), channel_id=1, source_target_pairs={{0,1},{1,0},{2,3},{3,2},{4,5},{5,4},{6,7},{7,6},{8,9},{9,8},{10,11... | collective-permute-start | bytes 3342344 | tf_op jit(solution)/shard_map/ppermute | solution.py:188
  126.7 2.4 %collective-permute-done.2.other_ref = bf16[4,1088,128]{2,1,0:T(8,128)(2,1)S(1)} collective-permute-done((bf16[4,1088,128]{2,1,0:T(8,128)(2,1)S(1)}, bf16[4,1088,128]{2,1,0:T(8,128)(2,1)S(1)}, u32[]{:S(2)}, u32[]{:S(2)}) %collective-permute-start.2) | collective-permute-done | bytes 1114144 | tf_op jit(solution)/shard_map/ppermute | solution.py:188
  129.1 1.5 shard_map.117
  130.6 8.5 %all_to_all.39.got_ref = bf16[4,320,128]{2,1,0:T(8,128)(2,1)S(1)} all-to-all(bf16[4,320,128]{2,1,0:T(8,128)(2,1)S(1)} %shard_map.117), channel_id=1, replica_groups=mesh['x'=4,'zh'=2,'y'=4,'zl'=8,'core'=2] {'x'}, dimensions={0} | all-to-all | bytes 655360 | tf_op jit(solution)/shard_map/all_to_all | solution.py:192
  139.1 0.7 shard_map.118
  139.8 9.8 %all-to-all-start.6 = ((bf16[16,32,128]{2,1,0:T(8,128)(2,1)}), bf16[16,32,128]{2,1,0:T(8,128)(2,1)S(1)}, u32[]{:S(2)}, u32[]{:S(2)}) async-start(bf16[16,32,128]{2,1,0:T(8,128)(2,1)} %get-tuple-element.18), calls=%async_computation.6 | async-start | bytes 262144 | tf_op jit(solution)/shard_map/all_to_all | solution.py:192
  149.6 12.0 %collective-permute-start.3 = (bf16[128,128]{1,0:T(8,128)(2,1)S(1)}, bf16[128,128]{1,0:T(8,128)(2,1)S(1)}, u32[]{:S(2)}, u32[]{:S(2)}) collective-permute-start(bf16[128,128]{1,0:T(8,128)(2,1)S(1)} %get-tuple-element.16), channel_id=1, source_target_pairs={{0,64},{64,0},{1,65},{65,1},{2,66},{66,2},{3,67},{67,3},{4,68},{68... | collective-permute-start | bytes 98312 | tf_op jit(solution)/shard_map/ppermute | solution.py:188
  161.5 5.2 %collective-permute-done.3.got_ref = bf16[128,128]{1,0:T(8,128)(2,1)S(1)} collective-permute-done((bf16[128,128]{1,0:T(8,128)(2,1)S(1)}, bf16[128,128]{1,0:T(8,128)(2,1)S(1)}, u32[]{:S(2)}, u32[]{:S(2)}) %collective-permute-start.3) | collective-permute-done | bytes 32800 | tf_op jit(solution)/shard_map/ppermute | solution.py:188
  166.8 0.0 all-to-all-done.6.got_weight_ref
  166.8 0.7 shard_map.119
Async XLA Ops:
  0.6 17.9 %collective-permute-start = (bf16[128,128]{1,0:T(8,128)(2,1)}, bf16[128,128]{1,0:T(8,128)(2,1)S(1)}, u32[]{:S(2)}, u32[]{:S(2)}) collective-permute-start(bf16[128,128]{1,0:T(8,128)(2,1)} %bitcast.24), channel_id=1, source_target_pairs={{0,64},{64,0},{1,65},{65,1},{2,66},{66,2},{3,67},{67,3},{4,68},{68... | collective-permute-start | bytes 98312 | tf_op jit(solution)/shard_map/ppermute | solution.py:188
  20.1 9.5 %all-to-all-start = ((bf16[4,2,128,128]{3,2,1,0:T(8,128)(2,1)}), bf16[4,2,128,128]{3,2,1,0:T(8,128)(2,1)S(1)}, u32[]{:S(2)}, u32[]{:S(2)}) async-start(bf16[4,2,128,128]{3,2,1,0:T(8,128)(2,1)} %broadcast_in_dim.19), calls=%async_computation | async-start | bytes 524288 | tf_op jit(solution)/shard_map/all_to_all | solution.py:192
  24.8 0.8 copy-start.4
  25.6 0.8 copy-start.5
  26.4 0.8 copy-start.6
  27.2 2.4 %copy-start.2 = (s32[1,1,64]{2,1,0:T(1,128)S(1)}, s32[1,1,64]{2,1,0:T(1,128)}, u32[]{:S(2)}) copy-start(s32[1,1,64]{2,1,0:T(1,128)} %param.12) | copy-start | bytes 772
  27.2 2.4 %copy-start.3 = (s32[1,1,64]{2,1,0:T(1,128)S(1)}, s32[1,1,64]{2,1,0:T(1,128)}, u32[]{:S(2)}) copy-start(s32[1,1,64]{2,1,0:T(1,128)} %param.13) | copy-start | bytes 772
  31.3 9.2 %collective-permute-start.1 = (bf16[32,128,128]{2,1,0:T(8,128)(2,1)S(1)}, bf16[32,128,128]{2,1,0:T(8,128)(2,1)S(1)}, u32[]{:S(2)}, u32[]{:S(2)}) collective-permute-start(bf16[32,128,128]{2,1,0:T(8,128)(2,1)S(1)} %get-tuple-element.12), channel_id=1, source_target_pairs={{0,1},{1,0},{2,3},{3,2},{4,5},{5,4},{6,7},{7,6},{8,9},{9,8},{10,11... | collective-permute-start | bytes 3145736 | tf_op jit(solution)/shard_map/ppermute | solution.py:188
  57.9 20.5 %copy-start = (bf16[128,256]{1,0:T(8,128)(2,1)S(1)}, bf16[128,256]{1,0:T(8,128)(2,1)}, u32[]{:S(2)}) copy-start(bf16[128,256]{1,0:T(8,128)(2,1)} %refs_1_.1) | copy-start | bytes 196612
  57.9 20.5 %copy-start.1 = (bf16[1,128,256]{2,1,0:T(8,128)(2,1)S(1)}, bf16[1,128,256]{2,1,0:T(8,128)(2,1)}, u32[]{:S(2)}) copy-start(bf16[1,128,256]{2,1,0:T(8,128)(2,1)} %param.11) | copy-start | bytes 196612
  119.7 9.4 %collective-permute-start.2 = (bf16[4,1088,128]{2,1,0:T(8,128)(2,1)S(1)}, bf16[4,1088,128]{2,1,0:T(8,128)(2,1)S(1)}, u32[]{:S(2)}, u32[]{:S(2)}) collective-permute-start(bf16[4,1088,128]{2,1,0:T(8,128)(2,1)S(1)} %all_to_all.38.own_ref), channel_id=1, source_target_pairs={{0,1},{1,0},{2,3},{3,2},{4,5},{5,4},{6,7},{7,6},{8,9},{9,8},{10,11... | collective-permute-start | bytes 3342344 | tf_op jit(solution)/shard_map/ppermute | solution.py:188
  139.8 27.0 %all-to-all-start.6 = ((bf16[16,32,128]{2,1,0:T(8,128)(2,1)}), bf16[16,32,128]{2,1,0:T(8,128)(2,1)S(1)}, u32[]{:S(2)}, u32[]{:S(2)}) async-start(bf16[16,32,128]{2,1,0:T(8,128)(2,1)} %get-tuple-element.18), calls=%async_computation.6 | async-start | bytes 262144 | tf_op jit(solution)/shard_map/all_to_all | solution.py:192
  149.6 17.2 %collective-permute-start.3 = (bf16[128,128]{1,0:T(8,128)(2,1)S(1)}, bf16[128,128]{1,0:T(8,128)(2,1)S(1)}, u32[]{:S(2)}, u32[]{:S(2)}) collective-permute-start(bf16[128,128]{1,0:T(8,128)(2,1)S(1)} %get-tuple-element.16), channel_id=1, source_target_pairs={{0,64},{64,0},{1,65},{65,1},{2,66},{66,2},{3,67},{67,3},{4,68},{68... | collective-permute-start | bytes 98312 | tf_op jit(solution)/shard_map/ppermute | solution.py:188

commit v3 on v2

v3 whole, which is shorter than its diff:
```python
import functools
import math

import jax
import jax.numpy as jnp
from jax import lax
from jax.experimental import pallas as pl
from jax.experimental.pallas import tpu as pltpu
from jax.sharding import Mesh
from jax.sharding import PartitionSpec as P

TILE = 128
GROUP = 4
FINE = (("x", 4), ("zh", 2), ("y", 4), ("zl", 8), ("core", 2))
N_X, N_ZH, N_Y, N_ZL, N_CORE = (size for _, size in FINE)
ROW = ("x", "zh")
COL = ("y", "zl", "core")
LISTS = N_Y * N_CORE
PLANE = N_X * N_Y
W_ROWS = 32
BF16 = jnp.bfloat16
F32 = jnp.float32
I32 = jnp.int32

vmem = pl.BlockSpec(memory_space=pltpu.VMEM)
smem = pl.BlockSpec(memory_space=pltpu.SMEM)
shape = jax.ShapeDtypeStruct


def call(body, outs, in_specs, out_specs=None, scratch=(), flops=0, moved=0, limit=24):
    return pl.pallas_call(
        body,
        out_shape=outs,
        in_specs=in_specs,
        out_specs=jax.tree.map(lambda _: vmem, outs) if out_specs is None else out_specs,
        scratch_shapes=list(scratch),
        compiler_params=pltpu.CompilerParams(vmem_limit_bytes=limit * 1024 * 1024),
        cost_estimate=pl.CostEstimate(flops=flops, bytes_accessed=moved, transcendentals=0),
    )


def halves(value):
    high = value.astype(BF16)
    return high, (value - high.astype(F32)).astype(BF16)


def pack_body(rows_ref, cols_ref, weight_ref, row_ref, col_ref, count_ref, send_ref):
    slots, edges = rows_ref.shape
    rows = rows_ref[...].astype(F32)
    cols = cols_ref[...].astype(F32)
    weight = weight_ref[...].astype(F32)
    line = lax.broadcasted_iota(I32, (slots, slots), 0)
    meta = jnp.where(line == 0, row_ref[...], jnp.where(line == 1, col_ref[...], count_ref[0, 0]))
    blocks = (
        rows[:, :TILE],
        cols[:, :TILE],
        weight[:, :TILE],
        jnp.concatenate([rows[:, TILE:], cols[:, TILE:]], axis=1),
        jnp.concatenate([weight[:, TILE:], meta.astype(F32)], axis=1),
    )
    for k, block in enumerate(blocks):
        block = block.astype(BF16)
        for peer in range(send_ref.shape[0]):
            send_ref[peer, k * slots : (k + 1) * slots, :] = block


def build_body(
    where_ref, got_ref, tiles_ref, zl_ref, src_ref, total_ref,
    slot_ref, edge_rows_ref, edge_cols_ref, weight_ref, meta_ref, slots_ref, sem,
):
    y, core = where_ref[0], where_ref[1]
    slots = got_ref.shape[1] // 5
    edges = edge_rows_ref.shape[1]
    rest = edges - TILE
    dummy = LISTS * slots
    for index in range(LISTS):
        meta = got_ref[index, 4 * slots : 4 * slots + 16, :].astype(F32)
        meta_ref[index * 8 : (index + 1) * 8, :] = meta[:8].astype(I32)
    copy = pltpu.make_async_copy(meta_ref, slots_ref, sem)
    copy.start()
    for index in range(LISTS):
        here = slice(index * slots, (index + 1) * slots)
        block = [got_ref[index, k * slots : (k + 1) * slots, :].astype(F32) for k in range(5)]
        edge_rows_ref[here, :TILE] = block[0]
        edge_cols_ref[here, :TILE] = block[1]
        weight_ref[here, :TILE] = block[2]
        edge_rows_ref[here, TILE:] = block[3][:, :rest]
        edge_cols_ref[here, TILE:] = block[3][:, rest:]
        weight_ref[here, TILE:] = block[4][:, :rest]
    for ref in (edge_rows_ref, edge_cols_ref, weight_ref):
        ref[dummy:, :] = jnp.zeros_like(ref[dummy:, :])
    copy.wait()

    used = jnp.int32(0)
    for part in range(N_CORE):
        column_core = core if part == 0 else 1 - core
        for column_y in range(N_Y):
            index = column_y * N_CORE + column_core

            def scan(slot, used, index=index, column_y=column_y):
                row, col = slots_ref[index * 8, rest + slot], slots_ref[index * 8 + 1, rest + slot]
                slot_ref[used] = index * slots + slot
                zl_ref[used] = row // N_CORE % N_ZL
                src_ref[used] = (col // N_ZH * N_Y + column_y) * N_ZH + col % N_ZH
                mine = (row // (N_CORE * N_ZL) == y) & (row % N_CORE == core)
                return used + mine.astype(I32)

            used = lax.fori_loop(0, slots_ref[index * 8 + 2, rest], scan, used)
        for extra in range(GROUP - 1):
            slot_ref[used + extra] = dummy
            zl_ref[used + extra] = 0
            src_ref[used + extra] = 0
        used = (used + GROUP - 1) // GROUP * GROUP
        total_ref[part] = used

    positions = lax.broadcasted_iota(I32, (TILE, edges), 0).astype(F32)

    def step(group, carry):
        for i in range(GROUP):
            entry = group * GROUP + i
            slot = slot_ref[entry]
            row_hot = jnp.where(positions == edge_rows_ref[pl.ds(slot, 1), :], 1.0, 0.0)
            col_hot = jnp.where(
                positions == edge_cols_ref[pl.ds(slot, 1), :], weight_ref[pl.ds(slot, 1), :], 0.0
            )
            built = lax.dot_general(
                row_hot.astype(BF16),
                col_hot.astype(BF16),
                (((1,), (1,)), ((), ())),
                preferred_element_type=F32,
            )
            tiles_ref[entry] = built.astype(BF16)
        return carry

    lax.fori_loop(0, used // GROUP, step, 0)


def forward_body(total_ref, zl_ref, src_ref, tiles_ref, own_ref, other_ref, send_ref, acc_ref):
    acc_ref[...] = jnp.zeros_like(acc_ref)

    def step(feats_ref, group, carry):
        products = []
        for i in range(GROUP):
            entry = group * GROUP + i
            products.append(
                jnp.dot(tiles_ref[entry], feats_ref[src_ref[entry]], preferred_element_type=F32)
            )
        for i in range(GROUP):
            acc_ref[zl_ref[group * GROUP + i]] += products[i]
        return carry

    middle, end = total_ref[0] // GROUP, total_ref[1] // GROUP
    lax.fori_loop(0, middle, functools.partial(step, own_ref), 0)
    lax.fori_loop(middle, end, functools.partial(step, other_ref), 0)
    send_ref[...] = acc_ref[...].astype(BF16)


def dense_body(parts_ref, weight_ref, up_ref, act_ref, send_ref, *, scale):
    aggregated = jnp.sum(parts_ref[...].astype(F32), axis=0).astype(BF16)
    weight = weight_ref[...]
    pre_act = jnp.dot(aggregated, weight, preferred_element_type=F32)
    gate = jax.nn.sigmoid(pre_act)
    act_ref[...] = (pre_act * gate).astype(BF16)
    grad_pre = (up_ref[...].astype(F32) * gate * (1.0 + pre_act * (1.0 - gate))).astype(BF16)
    grad_agg = lax.dot_general(
        weight, grad_pre, (((1,), (1,)), ((), ())), preferred_element_type=F32
    ).astype(BF16)
    local_weight = (
        lax.dot_general(aggregated, grad_pre, (((0,), (0,)), ((), ())), preferred_element_type=F32)
        * scale
    ).astype(BF16)
    deep = TILE // N_ZL
    for peer in range(N_ZL):
        send_ref[peer, 0:TILE, :] = grad_agg
        here = slice(peer * deep, (peer + 1) * deep)
        send_ref[peer, TILE : TILE + deep, :] = local_weight[here, :TILE]
        send_ref[peer, TILE + deep :, :] = local_weight[here, TILE:]


def backward_body(
    total_ref, zl_ref, src_ref, tiles_ref, got_ref, send_ref, keep_ref, keep_weight_ref, acc_ref
):
    acc_ref[...] = jnp.zeros_like(acc_ref)

    def step(part, group, carry):
        products = []
        for i in range(GROUP):
            entry = group * GROUP + i
            grad = got_ref[zl_ref[entry], 0:TILE, :]
            products.append(jnp.dot(grad, tiles_ref[entry], preferred_element_type=F32))
        for i in range(GROUP):
            acc_ref[part, src_ref[group * GROUP + i]] += products[i]
        return carry

    middle, end = total_ref[0] // GROUP, total_ref[1] // GROUP
    lax.fori_loop(0, middle, functools.partial(step, 0), 0)
    lax.fori_loop(middle, end, functools.partial(step, 1), 0)
    keep_ref[...] = acc_ref[0]
    tiles = acc_ref.shape[1]
    send_ref[0:tiles] = acc_ref[1].astype(BF16)
    weight_sum = jnp.sum(got_ref[:, TILE:, :].astype(F32), axis=0)
    keep_weight_ref[...] = weight_sum
    high, low = halves(weight_sum)
    send_ref[tiles, 0:W_ROWS, :] = high
    send_ref[tiles, W_ROWS : 2 * W_ROWS, :] = low
    send_ref[tiles, 2 * W_ROWS :, :] = jnp.zeros_like(send_ref[tiles, 2 * W_ROWS :, :])


def merge_body(got_ref, keep_ref, keep_weight_ref, send_ref):
    tiles = keep_ref.shape[0]
    terms = got_ref[tiles, 0 : 2 * W_ROWS, :].astype(F32)
    high, low = halves(keep_weight_ref[...] + (terms[:W_ROWS] + terms[W_ROWS:]))
    for peer in range(PLANE):
        for zh in range(N_ZH):
            tile = peer * N_ZH + zh
            send_ref[peer, zh * TILE : (zh + 1) * TILE, :] = (
                keep_ref[tile] + got_ref[tile].astype(F32)
            ).astype(BF16)
        send_ref[peer, N_ZH * TILE : N_ZH * TILE + W_ROWS, :] = high
        send_ref[peer, N_ZH * TILE + W_ROWS :, :] = low


def halfway_body(zh_ref, got_ref, send_ref, keep_ref, send_weight_ref):
    zh = zh_ref[0]
    total = jnp.sum(got_ref[...].astype(F32), axis=0)
    first, second = total[:TILE], total[TILE : 2 * TILE]
    mine = zh == 0
    keep_ref[...] = jnp.where(mine, first, second)
    send_ref[...] = jnp.where(mine, second, first).astype(BF16)
    terms = total[2 * TILE :]
    weight_sum = (terms[:W_ROWS] + terms[W_ROWS:]).astype(BF16)
    for peer in range(N_ZH * N_ZL):
        send_weight_ref[peer] = weight_sum


def finish_body(got_ref, keep_ref, got_weight_ref, grad_ref, grad_weight_ref):
    grad_ref[...] = (keep_ref[...] + got_ref[...].astype(F32)).T.astype(BF16)
    deep = TILE // N_ZL
    for k in range(N_ZL):
        total = got_weight_ref[k].astype(F32) + got_weight_ref[N_ZL + k].astype(F32)
        grad_weight_ref[k * deep : (k + 1) * deep, :TILE] = total[:deep]
        grad_weight_ref[k * deep : (k + 1) * deep, TILE:] = total[deep:]


def swap(value, axis):
    return lax.ppermute(value, axis, [(0, 1), (1, 0)])


def exchange(value, axis):
    return lax.all_to_all(value, axis, 0, 0, tiled=True)


def local(
    features, weight, upstream, tile_rows, tile_cols, tile_count, edge_rows, edge_cols, edge_weight
):
    width = features.shape[2]
    hidden = weight.shape[1]
    slots, edges = edge_rows.shape[2:]
    column_tiles = PLANE * N_ZH
    most = slots + (LISTS - 1) * slots // 2 + 2 * GROUP
    zh = lax.axis_index("zh")
    where = jnp.stack([lax.axis_index("y"), lax.axis_index("core")]).astype(I32)

    own = features[0]
    other = swap(own, "zh")

    send = call(pack_body, shape((LISTS, 5 * slots, TILE), BF16), [vmem] * 5 + [smem])(
        edge_rows[0, 0], edge_cols[0, 0], edge_weight[0, 0], tile_rows[0], tile_cols[0], tile_count
    )
    lists = exchange(send, ("y", "core"))
    other, lists = lax.optimization_barrier((other, lists))
    tiles, zl_list, src_list, total = call(
        build_body,
        (
            shape((most, TILE, TILE), BF16),
            shape((most,), I32),
            shape((most,), I32),
            shape((N_CORE,), I32),
        ),
        [smem, vmem],
        (vmem, smem, smem, smem),
        [pltpu.SMEM((most,), I32)]
        + [pltpu.VMEM((LISTS * slots + 8, edges), F32)] * 3
        + [
            pltpu.VMEM((LISTS * 8, TILE), I32),
            pltpu.SMEM((LISTS * 8, TILE), I32),
            pltpu.SemaphoreType.DMA,
        ],
        flops=slots * TILE * TILE * edges * 4,
        moved=slots * TILE * TILE * 2,
    )(where, lists)

    pair = jnp.where(zh == 0, jnp.stack([own, other]), jnp.stack([other, own]))
    pair = jnp.broadcast_to(pair[None], (PLANE,) + pair.shape)
    mine = exchange(pair, ("x", "y")).reshape(column_tiles, TILE, width)
    theirs = swap(mine, "core")

    partial = call(
        forward_body,
        shape((N_ZL, TILE, width), BF16),
        [smem] * 3 + [vmem] * 3,
        scratch=[pltpu.VMEM((N_ZL, TILE, width), F32)],
    )(total, zl_list, src_list, tiles, mine, theirs)

    parts = exchange(partial, "zl")

    node_total = features.shape[1] * N_X * N_ZH * N_Y * N_ZL * N_CORE
    out_act, send = call(
        functools.partial(dense_body, scale=1.0 / math.sqrt(node_total)),
        (shape((TILE, hidden), BF16), shape((N_ZL, TILE + W_ROWS, TILE), BF16)),
        [vmem] * 3,
    )(parts, weight, upstream[0])

    got = exchange(send, "zl")
    send, keep, keep_weight = call(
        backward_body,
        (
            shape((column_tiles + 1, width, TILE), BF16),
            shape((column_tiles, width, TILE), F32),
            shape((W_ROWS, TILE), F32),
        ),
        [smem] * 3 + [vmem] * 2,
        scratch=[pltpu.VMEM((N_CORE, column_tiles, width, TILE), F32)],
    )(total, zl_list, src_list, tiles, got)

    send = call(merge_body, shape((PLANE, N_ZH * TILE + 2 * W_ROWS, TILE), BF16), [vmem] * 3)(
        swap(send, "core"), keep, keep_weight
    )
    got = exchange(send, ("x", "y"))
    send, keep, send_weight = call(
        halfway_body,
        (
            shape((TILE, TILE), BF16),
            shape((TILE, TILE), F32),
            shape((N_ZH * N_ZL, W_ROWS, TILE), BF16),
        ),
        [smem, vmem],
    )(zh.astype(I32)[None], got)
    got = swap(send, "zh")
    got_weight = exchange(send_weight, ("zh", "zl"))
    grad_features, grad_weight = call(
        finish_body,
        (shape((TILE, width), BF16), shape((width, hidden), F32)),
        [vmem] * 3,
    )(got, keep, got_weight)
    return (out_act[None], grad_features[None], grad_weight)


def solution(mesh):
    fine = Mesh(mesh.devices.reshape([size for _, size in FINE]), [name for name, _ in FINE])
    in_specs = (
        P(COL, ROW, None),
        P(),
        P(COL, ROW, None),
        P(ROW, COL, None),
        P(ROW, COL, None),
        P(ROW, COL),
        P(ROW, COL, None, None),
        P(ROW, COL, None, None),
        P(ROW, COL, None, None),
    )
    out_specs = (P(COL, ROW, None), P(COL, ROW, None), P())
    return jax.shard_map(local, mesh=fine, in_specs=in_specs, out_specs=out_specs, check_vma=False)
```

time: 168 us -> 173 us (1.030)
  Pallas kernels: 6.4 us -> 15.6 us
  starting transfers between devices: 55.9 us -> 50.8 us
  blocking collectives: 86.4 us -> 90.7 us
  waiting for transfers between devices: 13.1 us -> 9.84 us
    pallas_call x6, Pallas kernels: 5.01 us -> 14.2 us  [the longest x1 8.66 us: local(): call(build_body, (shape((most, TILE, TILE), BF16), shape((most,), I32), s...]
    ppermute x4, starting transfers between devices: 42.1 us -> 34.8 us  [swap(): return lax.ppermute(value, axis, [(0, 1), (1, 0)])]
    all_to_all x5 -> x4, blocking collectives: 86.4 us -> 90.7 us  [exchange(): return lax.all_to_all(value, axis, 0, 0, tiled=True)]
    all_to_all x2, starting transfers between devices: 13.8 us -> 16 us  [exchange(): return lax.all_to_all(value, axis, 0, 0, tiled=True)]
    unnamed x14 -> x16, local copies, waits for them, and re-layouts: 2.45 us -> 3.75 us
  transfers between devices with their start and end apart: 6 -> 6, of which waited for: 5 -> 3; matrix products, arithmetic and copies ran while one was open for 0% -> 0% of each run, Pallas kernels for 0% -> 5%
where the time goes in v3:
time: 173 us; the launch traced here: 172 us
  blocking collectives  90.7 us (52%)
  starting transfers between devices  50.8 us (29%)
  Pallas kernels  15.6 us (9%)
  waiting for transfers between devices  9.84 us (6%)
  local copies, waits for them, and re-layouts  3.98 us (2%)
    all_to_all x4, blocking collectives, exchange(): return lax.all_to_all(value, axis, 0, 0, tiled=True)  90.7 us
    ppermute x4, starting transfers between devices, swap(): return lax.ppermute(value, axis, [(0, 1), (1, 0)])  34.8 us
    all_to_all x2, starting transfers between devices, exchange(): return lax.all_to_all(value, axis, 0, 0, tiled=True)  16 us
    ppermute x4, waiting for transfers between devices, swap(): return lax.ppermute(value, axis, [(0, 1), (1, 0)])  9.83 us
    pallas_call x1, Pallas kernels, local(): call(build_body, (shape((most, TILE, TILE), BF16), shape((most,), I32), s...  8.66 us
    unnamed x16, local copies, waits for them, and re-layouts  3.75 us
  transfers between devices with their start and end apart: 6, of which 3 were waited for; matrix products, arithmetic and copies ran while one was open for 0% of the time, Pallas kernels for 5%

profile of v3, /device:TPU:1, one launch (start us, length us, event | category | flops | bytes accessed | tf_op | source)
XLA Modules:
  0.0 172.5 jit_solution(11036495913670415031)
XLA Ops:
  1.3 0.0 copy-start.2
  1.3 0.8 copy-done.2
  2.1 0.0 copy-start.3
  2.1 0.8 copy-done.3
  3.0 0.0 copy-start.4
  3.0 0.8 copy-done.4
  3.7 0.0 copy-start.5
  3.7 0.7 copy-done.5
  4.4 0.0 copy-start.6
  4.4 0.7 copy-done.6
  5.0 0.0 copy-start.7
  5.0 0.9 shard_map.112
  6.0 10.3 %all-to-all-start = ((bf16[8,320,128]{2,1,0:T(8,128)(2,1)}), bf16[8,320,128]{2,1,0:T(8,128)(2,1)S(1)}, u32[]{:S(2)}, u32[]{:S(2)}) async-start(bf16[8,320,128]{2,1,0:T(8,128)(2,1)} %shard_map.112), calls=%async_computation | async-start | bytes 1310720 | tf_op jit(solution)/shard_map/all_to_all | solution.py:250
  16.3 0.0 copy-done.7
  16.3 11.1 %collective-permute-start = (bf16[128,128]{1,0:T(8,128)(2,1)S(1)}, bf16[128,128]{1,0:T(8,128)(2,1)S(1)}, u32[]{:S(2)}, u32[]{:S(2)}) collective-permute-start(bf16[128,128]{1,0:T(8,128)(2,1)S(1)} %bitcast.22), channel_id=1, source_target_pairs={{0,64},{64,0},{1,65},{65,1},{2,66},{66,2},{3,67},{67,3},{4,68},{68... | collective-permute-start | bytes 98312 | tf_op jit(solution)/shard_map/ppermute | solution.py:246
  27.4 2.3 %collective-permute-done = bf16[128,128]{1,0:T(8,128)(2,1)S(1)} collective-permute-done((bf16[128,128]{1,0:T(8,128)(2,1)S(1)}, bf16[128,128]{1,0:T(8,128)(2,1)S(1)}, u32[]{:S(2)}, u32[]{:S(2)}) %collective-permute-start) | collective-permute-done | bytes 32800 | tf_op jit(solution)/shard_map/ppermute | solution.py:246
  29.7 0.0 all-to-all-done.got_ref
  29.7 0.2 broadcast_in_dim.15
  29.9 20.2 %all_to_all.30 = bf16[16,2,128,128]{3,2,1,0:T(8,128)(2,1)S(1)} all-to-all(bf16[16,2,128,128]{3,2,1,0:T(8,128)(2,1)S(1)} %broadcast_in_dim.15), channel_id=1, replica_groups=mesh['x'=4,'zh'=2,'y'=4,'zl'=8,'core'=2] {'x','y'}, dimensions={0} | all-to-all | bytes 2097152 | tf_op jit(solution)/shard_map/all_to_all | solution.py:250
  50.1 5.4 %collective-permute-start.1 = (bf16[32,128,128]{2,1,0:T(8,128)(2,1)S(1)}, bf16[32,128,128]{2,1,0:T(8,128)(2,1)S(1)}, u32[]{:S(2)}, u32[]{:S(2)}) collective-permute-start(bf16[32,128,128]{2,1,0:T(8,128)(2,1)S(1)} %bitcast.14), channel_id=1, source_target_pairs={{0,1},{1,0},{2,3},{3,2},{4,5},{5,4},{6,7},{7,6},{8,9},{9,8},{10,11... | collective-permute-start | bytes 3145736 | tf_op jit(solution)/shard_map/ppermute | solution.py:246
  55.5 0.1 pad_add_fusion.where_ref
  55.6 8.7 %shard_map.113 = (bf16[296,128,128]{2,1,0:T(8,128)(2,1)S(1)}, s32[296]{0:T(512)S(1)}, s32[296]{0:T(512)S(1)}, s32[2]{0:T(128)S(1)}) custom-call(s32[2]{0:T(128)S(1)} %pad_add_fusion.where_ref, bf16[8,320,128]{2,1,0:T(8,128)(2,1)S(1)} %all-to-all-done.got_ref), custom_call_target="tpu_custom_call" | custom-call | flops 805306368 | bytes 2097152 | tf_op jit(solution)/shard_map/pallas_call | solution.py:272
  64.3 0.0 collective-permute-done.1.other_ref
  64.3 0.0 copy-start
  64.3 0.0 copy-start.1
  64.3 1.6 shard_map.114
  65.9 23.9 %all_to_all.31.parts_ref = bf16[8,128,128]{2,1,0:T(8,128)(2,1)S(1)} all-to-all(bf16[8,128,128]{2,1,0:T(8,128)(2,1)S(1)} %shard_map.114), channel_id=1, replica_groups=mesh['x'=4,'zh'=2,'y'=4,'zl'=8,'core'=2] {'zl'}, dimensions={0} | all-to-all | bytes 524288 | tf_op jit(solution)/shard_map/all_to_all | solution.py:250
  89.8 0.0 copy-done
  89.8 0.0 copy-done.1
  89.8 0.8 shard_map.115
  90.6 24.2 %all_to_all.32.got_ref = bf16[8,160,128]{2,1,0:T(8,128)(2,1)S(1)} all-to-all(bf16[8,160,128]{2,1,0:T(8,128)(2,1)S(1)} %get-tuple-element.26), channel_id=1, replica_groups=mesh['x'=4,'zh'=2,'y'=4,'zl'=8,'core'=2] {'zl'}, dimensions={0} | all-to-all | bytes 655360 | tf_op jit(solution)/shard_map/all_to_all | solution.py:250
  114.8 2.0 %shard_map.116 = (bf16[33,128,128]{2,1,0:T(8,128)(2,1)S(1)}, f32[32,128,128]{2,1,0:T(8,128)S(1)}, f32[32,128]{1,0:T(8,128)S(1)}) custom-call(s32[2]{0:T(128)S(1)} %get-tuple-element.20.total_ref, s32[296]{0:T(512)S(1)} %get-tuple-element.21.zl_ref, s32[296]{0:T(512)S(1)} %get-tuple-element.22.src_ref, ...), custom_call_target="tpu_custom_call" | custom-call | tf_op jit(solution)/shard_map/pallas_call | solution.py:315
  116.8 6.3 %collective-permute-start.2 = (bf16[33,128,128]{2,1,0:T(8,128)(2,1)S(1)}, bf16[33,128,128]{2,1,0:T(8,128)(2,1)S(1)}, u32[]{:S(2)}, u32[]{:S(2)}) collective-permute-start(bf16[33,128,128]{2,1,0:T(8,128)(2,1)S(1)} %get-tuple-element.27), channel_id=1, source_target_pairs={{0,1},{1,0},{2,3},{3,2},{4,5},{5,4},{6,7},{7,6},{8,9},{9,8},{10,11... | collective-permute-start | bytes 3244040 | tf_op jit(solution)/shard_map/ppermute | solution.py:246
  123.1 2.3 %collective-permute-done.2.got_ref = bf16[33,128,128]{2,1,0:T(8,128)(2,1)S(1)} collective-permute-done((bf16[33,128,128]{2,1,0:T(8,128)(2,1)S(1)}, bf16[33,128,128]{2,1,0:T(8,128)(2,1)S(1)}, u32[]{:S(2)}, u32[]{:S(2)}) %collective-permute-start.2) | collective-permute-done | bytes 1081376 | tf_op jit(solution)/shard_map/ppermute | solution.py:246
  125.4 0.2 shard_map.117
  125.6 22.4 %all_to_all.33.got_ref = bf16[16,320,128]{2,1,0:T(8,128)(2,1)S(1)} all-to-all(bf16[16,320,128]{2,1,0:T(8,128)(2,1)S(1)} %shard_map.117), channel_id=1, replica_groups=mesh['x'=4,'zh'=2,'y'=4,'zl'=8,'core'=2] {'x','y'}, dimensions={0} | all-to-all | bytes 2621440 | tf_op jit(solution)/shard_map/all_to_all | solution.py:250
  148.1 0.7 shard_map.118
  148.8 5.7 %all-to-all-start.5 = ((bf16[16,32,128]{2,1,0:T(8,128)(2,1)}), bf16[16,32,128]{2,1,0:T(8,128)(2,1)S(1)}, u32[]{:S(2)}, u32[]{:S(2)}) async-start(bf16[16,32,128]{2,1,0:T(8,128)(2,1)} %get-tuple-element.32), calls=%async_computation.5 | async-start | bytes 262144 | tf_op jit(solution)/shard_map/all_to_all | solution.py:250
  154.5 12.0 %collective-permute-start.3 = (bf16[128,128]{1,0:T(8,128)(2,1)S(1)}, bf16[128,128]{1,0:T(8,128)(2,1)S(1)}, u32[]{:S(2)}, u32[]{:S(2)}) collective-permute-start(bf16[128,128]{1,0:T(8,128)(2,1)S(1)} %get-tuple-element.30), channel_id=1, source_target_pairs={{0,64},{64,0},{1,65},{65,1},{2,66},{66,2},{3,67},{67,3},{4,68},{68... | collective-permute-start | bytes 98312 | tf_op jit(solution)/shard_map/ppermute | solution.py:246
  166.5 5.3 %collective-permute-done.3.got_ref = bf16[128,128]{1,0:T(8,128)(2,1)S(1)} collective-permute-done((bf16[128,128]{1,0:T(8,128)(2,1)S(1)}, bf16[128,128]{1,0:T(8,128)(2,1)S(1)}, u32[]{:S(2)}, u32[]{:S(2)}) %collective-permute-start.3) | collective-permute-done | bytes 32800 | tf_op jit(solution)/shard_map/ppermute | solution.py:246
  171.8 0.0 all-to-all-done.5.got_weight_ref
  171.8 0.7 shard_map.119
  (1 shorter events, 0.0 us)
Async XLA Ops:
  1.3 0.8 copy-start.2
  2.1 0.8 copy-start.3
  3.0 0.8 copy-start.4
  3.7 0.7 copy-start.5
  4.4 0.7 copy-start.6
  5.0 11.3 %copy-start.7 = (bf16[1,128,128]{2,1,0:T(8,128)(2,1)S(1)}, bf16[1,128,128]{2,1,0:T(8,128)(2,1)}, u32[]{:S(2)}) copy-start(bf16[1,128,128]{2,1,0:T(8,128)(2,1)} %param.9) | copy-start | bytes 98308
  6.0 23.7 %all-to-all-start = ((bf16[8,320,128]{2,1,0:T(8,128)(2,1)}), bf16[8,320,128]{2,1,0:T(8,128)(2,1)S(1)}, u32[]{:S(2)}, u32[]{:S(2)}) async-start(bf16[8,320,128]{2,1,0:T(8,128)(2,1)} %shard_map.112), calls=%async_computation | async-start | bytes 1310720 | tf_op jit(solution)/shard_map/all_to_all | solution.py:250
  16.3 13.4 %collective-permute-start = (bf16[128,128]{1,0:T(8,128)(2,1)S(1)}, bf16[128,128]{1,0:T(8,128)(2,1)S(1)}, u32[]{:S(2)}, u32[]{:S(2)}) collective-permute-start(bf16[128,128]{1,0:T(8,128)(2,1)S(1)} %bitcast.22), channel_id=1, source_target_pairs={{0,64},{64,0},{1,65},{65,1},{2,66},{66,2},{3,67},{67,3},{4,68},{68... | collective-permute-start | bytes 98312 | tf_op jit(solution)/shard_map/ppermute | solution.py:246
  50.1 14.2 %collective-permute-start.1 = (bf16[32,128,128]{2,1,0:T(8,128)(2,1)S(1)}, bf16[32,128,128]{2,1,0:T(8,128)(2,1)S(1)}, u32[]{:S(2)}, u32[]{:S(2)}) collective-permute-start(bf16[32,128,128]{2,1,0:T(8,128)(2,1)S(1)} %bitcast.14), channel_id=1, source_target_pairs={{0,1},{1,0},{2,3},{3,2},{4,5},{5,4},{6,7},{7,6},{8,9},{9,8},{10,11... | collective-permute-start | bytes 3145736 | tf_op jit(solution)/shard_map/ppermute | solution.py:246
  64.3 25.5 %copy-start = (bf16[128,256]{1,0:T(8,128)(2,1)S(1)}, bf16[128,256]{1,0:T(8,128)(2,1)}, u32[]{:S(2)}) copy-start(bf16[128,256]{1,0:T(8,128)(2,1)} %weight_ref.1) | copy-start | bytes 196612
  64.3 25.5 %copy-start.1 = (bf16[1,128,256]{2,1,0:T(8,128)(2,1)S(1)}, bf16[1,128,256]{2,1,0:T(8,128)(2,1)}, u32[]{:S(2)}) copy-start(bf16[1,128,256]{2,1,0:T(8,128)(2,1)} %param.11) | copy-start | bytes 196612
  116.8 8.7 %collective-permute-start.2 = (bf16[33,128,128]{2,1,0:T(8,128)(2,1)S(1)}, bf16[33,128,128]{2,1,0:T(8,128)(2,1)S(1)}, u32[]{:S(2)}, u32[]{:S(2)}) collective-permute-start(bf16[33,128,128]{2,1,0:T(8,128)(2,1)S(1)} %get-tuple-element.27), channel_id=1, source_target_pairs={{0,1},{1,0},{2,3},{3,2},{4,5},{5,4},{6,7},{7,6},{8,9},{9,8},{10,11... | collective-permute-start | bytes 3244040 | tf_op jit(solution)/shard_map/ppermute | solution.py:246
  148.8 22.9 %all-to-all-start.5 = ((bf16[16,32,128]{2,1,0:T(8,128)(2,1)}), bf16[16,32,128]{2,1,0:T(8,128)(2,1)S(1)}, u32[]{:S(2)}, u32[]{:S(2)}) async-start(bf16[16,32,128]{2,1,0:T(8,128)(2,1)} %get-tuple-element.32), calls=%async_computation.5 | async-start | bytes 262144 | tf_op jit(solution)/shard_map/all_to_all | solution.py:250
  154.5 17.2 %collective-permute-start.3 = (bf16[128,128]{1,0:T(8,128)(2,1)S(1)}, bf16[128,128]{1,0:T(8,128)(2,1)S(1)}, u32[]{:S(2)}, u32[]{:S(2)}) collective-permute-start(bf16[128,128]{1,0:T(8,128)(2,1)S(1)} %get-tuple-element.30), channel_id=1, source_target_pairs={{0,64},{64,0},{1,65},{65,1},{2,66},{66,2},{3,67},{67,3},{4,68},{68... | collective-permute-start | bytes 98312 | tf_op jit(solution)/shard_map/ppermute | solution.py:246

commit v4 on v3

--- a/solution.py
+++ b/solution.py
@@ -17,7 +17,7 @@
 COL = ("y", "zl", "core")
 LISTS = N_Y * N_CORE
 PLANE = N_X * N_Y
-W_ROWS = 32
+W_ROWS = 16
 BF16 = jnp.bfloat16
 F32 = jnp.float32
 I32 = jnp.int32
@@ -59,28 +59,27 @@
         jnp.concatenate([weight[:, TILE:], meta.astype(F32)], axis=1),
     )
     for k, block in enumerate(blocks):
-        block = block.astype(BF16)
-        for peer in range(send_ref.shape[0]):
-            send_ref[peer, k * slots : (k + 1) * slots, :] = block
+        send_ref[k * slots : (k + 1) * slots, :] = block.astype(BF16)
 
 
 def build_body(
-    where_ref, got_ref, tiles_ref, zl_ref, src_ref, total_ref,
+    where_ref, own_ref, other_ref, tiles_ref, zl_ref, src_ref, total_ref,
     slot_ref, edge_rows_ref, edge_cols_ref, weight_ref, meta_ref, slots_ref, sem,
 ):
     y, core = where_ref[0], where_ref[1]
-    slots = got_ref.shape[1] // 5
+    slots = own_ref.shape[1] // 5
     edges = edge_rows_ref.shape[1]
     rest = edges - TILE
     dummy = LISTS * slots
+    lists = [ref.at[k] for ref in (own_ref, other_ref) for k in range(N_Y)]
     for index in range(LISTS):
-        meta = got_ref[index, 4 * slots : 4 * slots + 16, :].astype(F32)
+        meta = lists[index][4 * slots : 4 * slots + 16, :].astype(F32)
         meta_ref[index * 8 : (index + 1) * 8, :] = meta[:8].astype(I32)
     copy = pltpu.make_async_copy(meta_ref, slots_ref, sem)
     copy.start()
     for index in range(LISTS):
         here = slice(index * slots, (index + 1) * slots)
-        block = [got_ref[index, k * slots : (k + 1) * slots, :].astype(F32) for k in range(5)]
+        block = [lists[index][k * slots : (k + 1) * slots, :].astype(F32) for k in range(5)]
         edge_rows_ref[here, :TILE] = block[0]
         edge_cols_ref[here, :TILE] = block[1]
         weight_ref[here, :TILE] = block[2]
@@ -93,9 +92,9 @@
 
     used = jnp.int32(0)
     for part in range(N_CORE):
-        column_core = core if part == 0 else 1 - core
-        for column_y in range(N_Y):
-            index = column_y * N_CORE + column_core
+        for shift in range(N_Y):
+            index = part * N_Y + shift
+            column_y = (y + N_Y - shift) % N_Y
 
             def scan(slot, used, index=index, column_y=column_y):
                 row, col = slots_ref[index * 8, rest + slot], slots_ref[index * 8 + 1, rest + slot]
@@ -155,7 +154,7 @@
     send_ref[...] = acc_ref[...].astype(BF16)
 
 
-def dense_body(parts_ref, weight_ref, up_ref, act_ref, send_ref, *, scale):
+def dense_body(parts_ref, weight_ref, up_ref, act_ref, send_ref, send_weight_ref, *, scale):
     aggregated = jnp.sum(parts_ref[...].astype(F32), axis=0).astype(BF16)
     weight = weight_ref[...]
     pre_act = jnp.dot(aggregated, weight, preferred_element_type=F32)
@@ -165,16 +164,23 @@
     grad_agg = lax.dot_general(
         weight, grad_pre, (((1,), (1,)), ((), ())), preferred_element_type=F32
     ).astype(BF16)
+    send_ref[...] = grad_agg
     local_weight = (
         lax.dot_general(aggregated, grad_pre, (((0,), (0,)), ((), ())), preferred_element_type=F32)
         * scale
-    ).astype(BF16)
-    deep = TILE // N_ZL
+    )
+    deep = TILE // PLANE
+    for peer in range(PLANE):
+        here = slice(peer * deep, (peer + 1) * deep)
+        part = jnp.concatenate([local_weight[here, :TILE], local_weight[here, TILE:]], axis=0)
+        send_weight_ref[peer] = part.astype(BF16)
+
+
+def spread_body(tile_ref, terms_ref, send_ref):
+    part = jnp.sum(terms_ref[...].astype(F32), axis=0).astype(BF16)
     for peer in range(N_ZL):
-        send_ref[peer, 0:TILE, :] = grad_agg
-        here = slice(peer * deep, (peer + 1) * deep)
-        send_ref[peer, TILE : TILE + deep, :] = local_weight[here, :TILE]
-        send_ref[peer, TILE + deep :, :] = local_weight[here, TILE:]
+        send_ref[peer, 0:TILE, :] = tile_ref[...]
+        send_ref[peer, TILE:, :] = part
 
 
 def backward_body(
@@ -209,37 +215,37 @@
 def merge_body(got_ref, keep_ref, keep_weight_ref, send_ref):
     tiles = keep_ref.shape[0]
     terms = got_ref[tiles, 0 : 2 * W_ROWS, :].astype(F32)
-    high, low = halves(keep_weight_ref[...] + (terms[:W_ROWS] + terms[W_ROWS:]))
+    part = (keep_weight_ref[...] + (terms[:W_ROWS] + terms[W_ROWS:])).astype(BF16)
     for peer in range(PLANE):
         for zh in range(N_ZH):
             tile = peer * N_ZH + zh
             send_ref[peer, zh * TILE : (zh + 1) * TILE, :] = (
                 keep_ref[tile] + got_ref[tile].astype(F32)
             ).astype(BF16)
-        send_ref[peer, N_ZH * TILE : N_ZH * TILE + W_ROWS, :] = high
-        send_ref[peer, N_ZH * TILE + W_ROWS :, :] = low
-
-
-def halfway_body(zh_ref, got_ref, send_ref, keep_ref, send_weight_ref):
+        send_ref[peer, N_ZH * TILE :, :] = part
+
+
+def halfway_body(zh_ref, got_ref, send_ref, keep_ref):
     zh = zh_ref[0]
-    total = jnp.sum(got_ref[...].astype(F32), axis=0)
-    first, second = total[:TILE], total[TILE : 2 * TILE]
+    total = jnp.sum(got_ref[:, 0 : N_ZH * TILE, :].astype(F32), axis=0)
+    first, second = total[:TILE], total[TILE:]
     mine = zh == 0
     keep_ref[...] = jnp.where(mine, first, second)
-    send_ref[...] = jnp.where(mine, second, first).astype(BF16)
-    terms = total[2 * TILE :]
-    weight_sum = (terms[:W_ROWS] + terms[W_ROWS:]).astype(BF16)
-    for peer in range(N_ZH * N_ZL):
-        send_weight_ref[peer] = weight_sum
-
-
-def finish_body(got_ref, keep_ref, got_weight_ref, grad_ref, grad_weight_ref):
-    grad_ref[...] = (keep_ref[...] + got_ref[...].astype(F32)).T.astype(BF16)
-    deep = TILE // N_ZL
-    for k in range(N_ZL):
-        total = got_weight_ref[k].astype(F32) + got_weight_ref[N_ZL + k].astype(F32)
-        grad_weight_ref[k * deep : (k + 1) * deep, :TILE] = total[:deep]
-        grad_weight_ref[k * deep : (k + 1) * deep, TILE:] = total[deep:]
+    send_ref[0:TILE, :] = jnp.where(mine, second, first).astype(BF16)
+    for peer in range(PLANE):
+        send_ref[TILE + peer * W_ROWS : TILE + (peer + 1) * W_ROWS, :] = got_ref[
+            peer, N_ZH * TILE :, :
+        ]
+
+
+def finish_body(got_ref, keep_ref, sent_ref, grad_ref, grad_weight_ref):
+    grad_ref[...] = (keep_ref[...] + got_ref[0:TILE, :].astype(F32)).T.astype(BF16)
+    deep = TILE // PLANE
+    total = got_ref[TILE:, :].astype(F32) + sent_ref[TILE:, :].astype(F32)
+    for peer in range(PLANE):
+        part = total[peer * W_ROWS : (peer + 1) * W_ROWS]
+        grad_weight_ref[peer * deep : (peer + 1) * deep, :TILE] = part[:deep]
+        grad_weight_ref[peer * deep : (peer + 1) * deep, TILE:] = part[deep:]
 
 
 def swap(value, axis):
@@ -261,15 +267,19 @@
     zh = lax.axis_index("zh")
     where = jnp.stack([lax.axis_index("y"), lax.axis_index("core")]).astype(I32)
 
-    own = features[0]
-    other = swap(own, "zh")
-
-    send = call(pack_body, shape((LISTS, 5 * slots, TILE), BF16), [vmem] * 5 + [smem])(
+    own = jnp.broadcast_to(features, (N_ZH,) + features.shape[1:])
+    pair = exchange(own, "zh")
+    packed = call(pack_body, shape((5 * slots, TILE), BF16), [vmem] * 5 + [smem])(
         edge_rows[0, 0], edge_cols[0, 0], edge_weight[0, 0], tile_rows[0], tile_cols[0], tile_count
     )
-    lists = exchange(send, ("y", "core"))
-    other, lists = lax.optimization_barrier((other, lists))
-    tiles, zl_list, src_list, total = call(
+    moved = [
+        lax.ppermute(packed, "y", [(k, (k + shift) % N_Y) for k in range(N_Y)])
+        for shift in range(1, N_Y)
+    ]
+    pair, moved = lax.optimization_barrier((pair, moved))
+    mine = exchange(jnp.broadcast_to(pair[None], (PLANE,) + pair.shape), ("x", "y"))
+    lists = jnp.stack([packed] + moved)
+    built = call(
         build_body,
         (
             shape((most, TILE, TILE), BF16),
@@ -277,7 +287,7 @@
             shape((most,), I32),
             shape((N_CORE,), I32),
         ),
-        [smem, vmem],
+        [smem, vmem, vmem],
         (vmem, smem, smem, smem),
         [pltpu.SMEM((most,), I32)]
         + [pltpu.VMEM((LISTS * slots + 8, edges), F32)] * 3
@@ -288,11 +298,9 @@
         ],
         flops=slots * TILE * TILE * edges * 4,
         moved=slots * TILE * TILE * 2,
-    )(where, lists)
-
-    pair = jnp.where(zh == 0, jnp.stack([own, other]), jnp.stack([other, own]))
-    pair = jnp.broadcast_to(pair[None], (PLANE,) + pair.shape)
-    mine = exchange(pair, ("x", "y")).reshape(column_tiles, TILE, width)
+    )(where, lists, swap(lists, "core"))
+    mine, (tiles, zl_list, src_list, total) = lax.optimization_barrier((mine, built))
+    mine = mine.reshape(column_tiles, TILE, width)
     theirs = swap(mine, "core")
 
     partial = call(
@@ -305,12 +313,19 @@
     parts = exchange(partial, "zl")
 
     node_total = features.shape[1] * N_X * N_ZH * N_Y * N_ZL * N_CORE
-    out_act, send = call(
+    out_act, tile, send_weight = call(
         functools.partial(dense_body, scale=1.0 / math.sqrt(node_total)),
-        (shape((TILE, hidden), BF16), shape((N_ZL, TILE + W_ROWS, TILE), BF16)),
+        (
+            shape((TILE, hidden), BF16),
+            shape((width, TILE), BF16),
+            shape((PLANE, W_ROWS, TILE), BF16),
+        ),
         [vmem] * 3,
     )(parts, weight, upstream[0])
 
+    send = call(spread_body, shape((N_ZL, TILE + W_ROWS, TILE), BF16), [vmem] * 2)(
+        tile, exchange(send_weight, ("x", "y"))
+    )
     got = exchange(send, "zl")
     send, keep, keep_weight = call(
         backward_body,
@@ -323,26 +338,20 @@
         scratch=[pltpu.VMEM((N_CORE, column_tiles, width, TILE), F32)],
     )(total, zl_list, src_list, tiles, got)
 
-    send = call(merge_body, shape((PLANE, N_ZH * TILE + 2 * W_ROWS, TILE), BF16), [vmem] * 3)(
+    send = call(merge_body, shape((PLANE, N_ZH * TILE + W_ROWS, TILE), BF16), [vmem] * 3)(
         swap(send, "core"), keep, keep_weight
     )
     got = exchange(send, ("x", "y"))
-    send, keep, send_weight = call(
+    send, keep = call(
         halfway_body,
-        (
-            shape((TILE, TILE), BF16),
-            shape((TILE, TILE), F32),
-            shape((N_ZH * N_ZL, W_ROWS, TILE), BF16),
-        ),
+        (shape((TILE + PLANE * W_ROWS, TILE), BF16), shape((TILE, TILE), F32)),
         [smem, vmem],
     )(zh.astype(I32)[None], got)
-    got = swap(send, "zh")
-    got_weight = exchange(send_weight, ("zh", "zl"))
     grad_features, grad_weight = call(
         finish_body,
         (shape((TILE, width), BF16), shape((width, hidden), F32)),
         [vmem] * 3,
-    )(got, keep, got_weight)
+    )(swap(send, "zh"), keep, send)
     return (out_act[None], grad_features[None], grad_weight)
 
 

time: 173 us -> 182 us (1.052)
  the two profiles are of different devices: /device:TPU:1 before, /device:TPU:32 now
where the time goes in v4:
time: 182 us; the launch traced here: 181 us
  blocking collectives  60.8 us (33%)
  starting transfers between devices  53.6 us (29%)
  waiting for transfers between devices  38.2 us (21%)
  local copies, waits for them, and re-layouts  13.8 us (8%)
  Pallas kernels  12.6 us (7%)
    all_to_all x3, blocking collectives, exchange(): return lax.all_to_all(value, axis, 0, 0, tiled=True)  60.8 us
    all_to_all x3, starting transfers between devices, exchange(): return lax.all_to_all(value, axis, 0, 0, tiled=True)  24 us
    all_to_all x3, waiting for transfers between devices, exchange(): return lax.all_to_all(value, axis, 0, 0, tiled=True)  20 us
    ppermute x4, starting transfers between devices, swap(): return lax.ppermute(value, axis, [(0, 1), (1, 0)])  19.3 us
    ppermute x4, waiting for transfers between devices, swap(): return lax.ppermute(value, axis, [(0, 1), (1, 0)])  13.6 us
    unnamed x20, local copies, waits for them, and re-layouts  11.2 us
    ppermute x3, starting transfers between devices, local(): lax.ppermute(packed, 'y', [(k, (k + shift) % N_Y) for k in range(N_Y)])  10.3 us
    pallas_call x1, Pallas kernels, local(): call(build_body, (shape((most, TILE, TILE), BF16), shape((most,), I32), s...  6.72 us
  transfers between devices with their start and end apart: 10, of which 8 were waited for; matrix products, arithmetic and copies ran while one was open for 0% of the time, Pallas kernels for 4%

profile of v4, /device:TPU:32, one launch (start us, length us, event | category | flops | bytes accessed | tf_op | source)
XLA Modules:
  0.0 180.7 jit_solution(5707955564828151520)
XLA Ops:
  0.6 1.4 broadcast_in_dim.23
  2.0 14.2 %all-to-all-start = ((bf16[2,128,128]{2,1,0:T(8,128)(2,1)}), bf16[2,128,128]{2,1,0:T(8,128)(2,1)S(1)}, u32[]{:S(2)}, u32[]{:S(2)}) async-start(bf16[2,128,128]{2,1,0:T(8,128)(2,1)} %broadcast_in_dim.23), calls=%async_computation | async-start | bytes 131072 | tf_op jit(solution)/shard_map/all_to_all | solution.py:256
  16.9 0.0 copy-start.3
  16.9 0.8 copy-done.3
  17.7 0.0 copy-start.4
  17.7 0.8 copy-done.4
  18.5 0.0 copy-start.7
  18.5 0.8 copy-done.7
  19.3 0.7 copy-done.8
  20.0 0.7 copy-done.9
  20.6 0.1 shard_map.112
  20.7 4.9 %collective-permute-start.2 = (bf16[320,128]{1,0:T(8,128)(2,1)S(1)}, bf16[320,128]{1,0:T(8,128)(2,1)S(1)}, u32[]{:S(2)}, u32[]{:S(2)}) collective-permute-start(bf16[320,128]{1,0:T(8,128)(2,1)S(1)} %shard_map.112), channel_id=1, source_target_pairs={{0,48},{16,0},{32,16},{48,32},{1,49},{17,1},{33,17},{49,33},{2,50}... | collective-permute-start | bytes 245768 | tf_op jit(solution)/shard_map/ppermute | solution.py:276
  25.6 2.5 %collective-permute-start.1 = (bf16[320,128]{1,0:T(8,128)(2,1)S(1)}, bf16[320,128]{1,0:T(8,128)(2,1)S(1)}, u32[]{:S(2)}, u32[]{:S(2)}) collective-permute-start(bf16[320,128]{1,0:T(8,128)(2,1)S(1)} %shard_map.112), channel_id=1, source_target_pairs={{0,32},{16,48},{32,0},{48,16},{1,33},{17,49},{33,1},{49,17},{2,34}... | collective-permute-start | bytes 245768 | tf_op jit(solution)/shard_map/ppermute | solution.py:276
  28.2 2.9 %collective-permute-start = (bf16[320,128]{1,0:T(8,128)(2,1)S(1)}, bf16[320,128]{1,0:T(8,128)(2,1)S(1)}, u32[]{:S(2)}, u32[]{:S(2)}) collective-permute-start(bf16[320,128]{1,0:T(8,128)(2,1)S(1)} %shard_map.112), channel_id=1, source_target_pairs={{0,16},{16,32},{32,48},{48,0},{1,17},{17,33},{33,49},{49,1},{2,18}... | collective-permute-start | bytes 245768 | tf_op jit(solution)/shard_map/ppermute | solution.py:276
  31.1 0.0 collective-permute-done.2
  31.1 3.0 %collective-permute-done.1 = bf16[320,128]{1,0:T(8,128)(2,1)S(1)} collective-permute-done((bf16[320,128]{1,0:T(8,128)(2,1)S(1)}, bf16[320,128]{1,0:T(8,128)(2,1)S(1)}, u32[]{:S(2)}, u32[]{:S(2)}) %collective-permute-start.1) | collective-permute-done | bytes 81952 | tf_op jit(solution)/shard_map/ppermute | solution.py:276
  34.1 1.6 collective-permute-done
  35.7 0.0 all-to-all-done
  35.7 1.2 broadcast_in_dim.24
  36.9 5.5 %all-to-all-start.1 = ((bf16[16,2,128,128]{3,2,1,0:T(8,128)(2,1)}), bf16[16,2,128,128]{3,2,1,0:T(8,128)(2,1)S(1)}, u32[]{:S(2)}, u32[]{:S(2)}) async-start(bf16[16,2,128,128]{3,2,1,0:T(8,128)(2,1)} %broadcast_in_dim.24), calls=%async_computation.1 | async-start | bytes 2097152 | tf_op jit(solution)/shard_map/all_to_all | solution.py:256
  42.5 1.9 %collective-permute-start.3 = (bf16[4,320,128]{2,1,0:T(8,128)(2,1)S(1)}, bf16[4,320,128]{2,1,0:T(8,128)(2,1)S(1)}, u32[]{:S(2)}, u32[]{:S(2)}) collective-permute-start(bf16[4,320,128]{2,1,0:T(8,128)(2,1)S(1)} %pad_maximum_fusion.own_ref), channel_id=1, source_target_pairs={{0,1},{1,0},{2,3},{3,2},{4,5},{5,4},{6,7},{7,6},{8,9},{9,8},{10,11... | collective-permute-start | bytes 983048 | tf_op jit(solution)/shard_map/ppermute | solution.py:252
  44.5 0.1 pad_add_fusion.where_ref
  44.5 1.5 collective-permute-done.3.other_ref
  46.1 6.7 %shard_map.113 = (bf16[296,128,128]{2,1,0:T(8,128)(2,1)S(1)}, s32[296]{0:T(512)S(1)}, s32[296]{0:T(512)S(1)}, s32[2]{0:T(128)S(1)}) custom-call(s32[2]{0:T(128)S(1)} %pad_add_fusion.where_ref, bf16[4,320,128]{2,1,0:T(8,128)(2,1)S(1)} %pad_maximum_fusion.own_ref, bf16[4,320,128]{2,1,0:T(8,128)(2,1)S(1)} %collective-permute-done.3.other_ref), custom_call_target="tpu_custom_call" | custom-call | flops 805306368 | bytes 2097152 | tf_op jit(solution)/shard_map/pallas_call | solution.py:282
  52.8 0.0 copy-start
  52.8 3.7 %copy-done = bf16[296,128,128]{2,1,0:T(8,128)(2,1)} copy-done((bf16[296,128,128]{2,1,0:T(8,128)(2,1)}, bf16[296,128,128]{2,1,0:T(8,128)(2,1)S(1)}, u32[]{:S(2)}) %copy-start) | copy-done | bytes 9699352
  56.5 1.1 all-to-all-done.1
  57.6 1.9 %collective-permute-start.4 = (bf16[32,128,128]{2,1,0:T(8,128)(2,1)S(1)}, bf16[32,128,128]{2,1,0:T(8,128)(2,1)S(1)}, u32[]{:S(2)}, u32[]{:S(2)}) collective-permute-start(bf16[32,128,128]{2,1,0:T(8,128)(2,1)S(1)} %bitcast.17), channel_id=1, source_target_pairs={{0,1},{1,0},{2,3},{3,2},{4,5},{5,4},{6,7},{7,6},{8,9},{9,8},{10,11... | collective-permute-start | bytes 3145736 | tf_op jit(solution)/shard_map/ppermute | solution.py:252
  59.5 2.6 %collective-permute-done.4.other_ref = bf16[32,128,128]{2,1,0:T(8,128)(2,1)S(1)} collective-permute-done((bf16[32,128,128]{2,1,0:T(8,128)(2,1)S(1)}, bf16[32,128,128]{2,1,0:T(8,128)(2,1)S(1)}, u32[]{:S(2)}, u32[]{:S(2)}) %collective-permute-start.4) | collective-permute-done | bytes 1048608 | tf_op jit(solution)/shard_map/ppermute | solution.py:252
  62.2 3.8 %copy-done.1 = bf16[296,128,128]{2,1,0:T(8,128)(2,1)S(1)} copy-done((bf16[296,128,128]{2,1,0:T(8,128)(2,1)S(1)}, bf16[296,128,128]{2,1,0:T(8,128)(2,1)}, u32[]{:S(2)}) %copy-start.1) | copy-done | bytes 9699352
  65.9 1.2 shard_map.114
  67.1 24.0 %all_to_all.30.parts_ref = bf16[8,128,128]{2,1,0:T(8,128)(2,1)S(1)} all-to-all(bf16[8,128,128]{2,1,0:T(8,128)(2,1)S(1)} %shard_map.114), channel_id=1, replica_groups=mesh['x'=4,'zh'=2,'y'=4,'zl'=8,'core'=2] {'zl'}, dimensions={0} | all-to-all | bytes 524288 | tf_op jit(solution)/shard_map/all_to_all | solution.py:256
  91.2 0.0 copy-done.5
  91.2 0.0 copy-done.6
  91.2 0.8 shard_map.115
  92.0 15.7 %all_to_all.31.terms_ref = bf16[16,16,128]{2,1,0:T(8,128)(2,1)S(1)} all-to-all(bf16[16,16,128]{2,1,0:T(8,128)(2,1)S(1)} %get-tuple-element.41), channel_id=1, replica_groups=mesh['x'=4,'zh'=2,'y'=4,'zl'=8,'core'=2] {'x','y'}, dimensions={0} | all-to-all | bytes 131072 | tf_op jit(solution)/shard_map/all_to_all | solution.py:256
  107.8 21.0 %all_to_all.32.got_ref = bf16[8,144,128]{2,1,0:T(8,128)(2,1)S(1)} all-to-all(bf16[8,144,128]{2,1,0:T(8,128)(2,1)S(1)} %shard_map.116), channel_id=1, replica_groups=mesh['x'=4,'zh'=2,'y'=4,'zl'=8,'core'=2] {'zl'}, dimensions={0} | all-to-all | bytes 589824 | tf_op jit(solution)/shard_map/all_to_all | solution.py:256
  128.8 0.0 copy-done.2
  128.8 1.7 shard_map.117
  130.5 1.9 %collective-permute-start.5 = (bf16[33,128,128]{2,1,0:T(8,128)(2,1)S(1)}, bf16[33,128,128]{2,1,0:T(8,128)(2,1)S(1)}, u32[]{:S(2)}, u32[]{:S(2)}) collective-permute-start(bf16[33,128,128]{2,1,0:T(8,128)(2,1)S(1)} %get-tuple-element.42), channel_id=1, source_target_pairs={{0,1},{1,0},{2,3},{3,2},{4,5},{5,4},{6,7},{7,6},{8,9},{9,8},{10,11... | collective-permute-start | bytes 3244040 | tf_op jit(solution)/shard_map/ppermute | solution.py:252
  132.4 2.7 %collective-permute-done.5.got_ref = bf16[33,128,128]{2,1,0:T(8,128)(2,1)S(1)} collective-permute-done((bf16[33,128,128]{2,1,0:T(8,128)(2,1)S(1)}, bf16[33,128,128]{2,1,0:T(8,128)(2,1)S(1)}, u32[]{:S(2)}, u32[]{:S(2)}) %collective-permute-start.5) | collective-permute-done | bytes 1081376 | tf_op jit(solution)/shard_map/ppermute | solution.py:252
  135.1 1.3 shard_map.118
  136.3 4.3 %all-to-all-start.5 = ((bf16[16,272,128]{2,1,0:T(8,128)(2,1)}), bf16[16,272,128]{2,1,0:T(8,128)(2,1)S(1)}, u32[]{:S(2)}, u32[]{:S(2)}) async-start(bf16[16,272,128]{2,1,0:T(8,128)(2,1)} %shard_map.118), calls=%async_computation.5 | async-start | bytes 2228224 | tf_op jit(solution)/shard_map/all_to_all | solution.py:256
  140.6 18.9 %all-to-all-done.5.got_ref = bf16[16,272,128]{2,1,0:T(8,128)(2,1)S(1)} async-done(((bf16[16,272,128]{2,1,0:T(8,128)(2,1)}), bf16[16,272,128]{2,1,0:T(8,128)(2,1)S(1)}, u32[]{:S(2)}, u32[]{:S(2)}) %all-to-all-start.5) | async-done | bytes 1114144 | tf_op jit(solution)/shard_map/all_to_all | solution.py:256
  159.5 0.2 shard_map.119
  159.6 13.6 %collective-permute-start.6 = (bf16[384,128]{1,0:T(8,128)(2,1)S(1)}, bf16[384,128]{1,0:T(8,128)(2,1)S(1)}, u32[]{:S(2)}, u32[]{:S(2)}) collective-permute-start(bf16[384,128]{1,0:T(8,128)(2,1)S(1)} %get-tuple-element.45.sent_ref), channel_id=1, source_target_pairs={{0,64},{64,0},{1,65},{65,1},{2,66},{66,2},{3,67},{67,3},{4,68},{68... | collective-permute-start | bytes 294920 | tf_op jit(solution)/shard_map/ppermute | solution.py:252
  173.2 6.8 %collective-permute-done.6.got_ref = bf16[384,128]{1,0:T(8,128)(2,1)S(1)} collective-permute-done((bf16[384,128]{1,0:T(8,128)(2,1)S(1)}, bf16[384,128]{1,0:T(8,128)(2,1)S(1)}, u32[]{:S(2)}, u32[]{:S(2)}) %collective-permute-start.6) | collective-permute-done | bytes 98336 | tf_op jit(solution)/shard_map/ppermute | solution.py:252
  179.9 0.7 shard_map.120
  (8 shorter events, 0.1 us)
Async XLA Ops:
  2.0 33.7 %all-to-all-start = ((bf16[2,128,128]{2,1,0:T(8,128)(2,1)}), bf16[2,128,128]{2,1,0:T(8,128)(2,1)S(1)}, u32[]{:S(2)}, u32[]{:S(2)}) async-start(bf16[2,128,128]{2,1,0:T(8,128)(2,1)} %broadcast_in_dim.23), calls=%async_computation | async-start | bytes 131072 | tf_op jit(solution)/shard_map/all_to_all | solution.py:256
  16.9 0.8 copy-start.3
  17.7 0.8 copy-start.4
  18.5 0.8 copy-start.7
  19.3 0.7 copy-start.8
  20.0 0.7 copy-start.9
  20.7 10.4 %collective-permute-start.2 = (bf16[320,128]{1,0:T(8,128)(2,1)S(1)}, bf16[320,128]{1,0:T(8,128)(2,1)S(1)}, u32[]{:S(2)}, u32[]{:S(2)}) collective-permute-start(bf16[320,128]{1,0:T(8,128)(2,1)S(1)} %shard_map.112), channel_id=1, source_target_pairs={{0,48},{16,0},{32,16},{48,32},{1,49},{17,1},{33,17},{49,33},{2,50}... | collective-permute-start | bytes 245768 | tf_op jit(solution)/shard_map/ppermute | solution.py:276
  25.6 8.5 %collective-permute-start.1 = (bf16[320,128]{1,0:T(8,128)(2,1)S(1)}, bf16[320,128]{1,0:T(8,128)(2,1)S(1)}, u32[]{:S(2)}, u32[]{:S(2)}) collective-permute-start(bf16[320,128]{1,0:T(8,128)(2,1)S(1)} %shard_map.112), channel_id=1, source_target_pairs={{0,32},{16,48},{32,0},{48,16},{1,33},{17,49},{33,1},{49,17},{2,34}... | collective-permute-start | bytes 245768 | tf_op jit(solution)/shard_map/ppermute | solution.py:276
  28.2 7.5 %collective-permute-start = (bf16[320,128]{1,0:T(8,128)(2,1)S(1)}, bf16[320,128]{1,0:T(8,128)(2,1)S(1)}, u32[]{:S(2)}, u32[]{:S(2)}) collective-permute-start(bf16[320,128]{1,0:T(8,128)(2,1)S(1)} %shard_map.112), channel_id=1, source_target_pairs={{0,16},{16,32},{32,48},{48,0},{1,17},{17,33},{33,49},{49,1},{2,18}... | collective-permute-start | bytes 245768 | tf_op jit(solution)/shard_map/ppermute | solution.py:276
  36.9 20.7 %all-to-all-start.1 = ((bf16[16,2,128,128]{3,2,1,0:T(8,128)(2,1)}), bf16[16,2,128,128]{3,2,1,0:T(8,128)(2,1)S(1)}, u32[]{:S(2)}, u32[]{:S(2)}) async-start(bf16[16,2,128,128]{3,2,1,0:T(8,128)(2,1)} %broadcast_in_dim.24), calls=%async_computation.1 | async-start | bytes 2097152 | tf_op jit(solution)/shard_map/all_to_all | solution.py:256
  42.5 3.5 %collective-permute-start.3 = (bf16[4,320,128]{2,1,0:T(8,128)(2,1)S(1)}, bf16[4,320,128]{2,1,0:T(8,128)(2,1)S(1)}, u32[]{:S(2)}, u32[]{:S(2)}) collective-permute-start(bf16[4,320,128]{2,1,0:T(8,128)(2,1)S(1)} %pad_maximum_fusion.own_ref), channel_id=1, source_target_pairs={{0,1},{1,0},{2,3},{3,2},{4,5},{5,4},{6,7},{7,6},{8,9},{9,8},{10,11... | collective-permute-start | bytes 983048 | tf_op jit(solution)/shard_map/ppermute | solution.py:252
  52.8 3.7 %copy-start = (bf16[296,128,128]{2,1,0:T(8,128)(2,1)}, bf16[296,128,128]{2,1,0:T(8,128)(2,1)S(1)}, u32[]{:S(2)}) copy-start(bf16[296,128,128]{2,1,0:T(8,128)(2,1)S(1)} %get-tuple-element.37.tiles_ref) | copy-start | bytes 29097988
  57.6 4.5 %collective-permute-start.4 = (bf16[32,128,128]{2,1,0:T(8,128)(2,1)S(1)}, bf16[32,128,128]{2,1,0:T(8,128)(2,1)S(1)}, u32[]{:S(2)}, u32[]{:S(2)}) collective-permute-start(bf16[32,128,128]{2,1,0:T(8,128)(2,1)S(1)} %bitcast.17), channel_id=1, source_target_pairs={{0,1},{1,0},{2,3},{3,2},{4,5},{5,4},{6,7},{7,6},{8,9},{9,8},{10,11... | collective-permute-start | bytes 3145736 | tf_op jit(solution)/shard_map/ppermute | solution.py:252
  62.2 3.8 %copy-start.1 = (bf16[296,128,128]{2,1,0:T(8,128)(2,1)S(1)}, bf16[296,128,128]{2,1,0:T(8,128)(2,1)}, u32[]{:S(2)}) copy-start(bf16[296,128,128]{2,1,0:T(8,128)(2,1)} %copy-done) | copy-start | bytes 29097988
  65.9 25.3 %copy-start.5 = (bf16[128,256]{1,0:T(8,128)(2,1)S(1)}, bf16[128,256]{1,0:T(8,128)(2,1)}, u32[]{:S(2)}) copy-start(bf16[128,256]{1,0:T(8,128)(2,1)} %weight_ref.1) | copy-start | bytes 196612
  65.9 25.3 %copy-start.6 = (bf16[1,128,256]{2,1,0:T(8,128)(2,1)S(1)}, bf16[1,128,256]{2,1,0:T(8,128)(2,1)}, u32[]{:S(2)}) copy-start(bf16[1,128,256]{2,1,0:T(8,128)(2,1)} %param.11) | copy-start | bytes 196612
  65.9 62.9 %copy-start.2 = (bf16[296,128,128]{2,1,0:T(8,128)(2,1)S(1)}, bf16[296,128,128]{2,1,0:T(8,128)(2,1)}, u32[]{:S(2)}) copy-start(bf16[296,128,128]{2,1,0:T(8,128)(2,1)} %copy-done) | copy-start | bytes 29097988
  130.5 4.6 %collective-permute-start.5 = (bf16[33,128,128]{2,1,0:T(8,128)(2,1)S(1)}, bf16[33,128,128]{2,1,0:T(8,128)(2,1)S(1)}, u32[]{:S(2)}, u32[]{:S(2)}) collective-permute-start(bf16[33,128,128]{2,1,0:T(8,128)(2,1)S(1)} %get-tuple-element.42), channel_id=1, source_target_pairs={{0,1},{1,0},{2,3},{3,2},{4,5},{5,4},{6,7},{7,6},{8,9},{9,8},{10,11... | collective-permute-start | bytes 3244040 | tf_op jit(solution)/shard_map/ppermute | solution.py:252
  136.3 23.1 %all-to-all-start.5 = ((bf16[16,272,128]{2,1,0:T(8,128)(2,1)}), bf16[16,272,128]{2,1,0:T(8,128)(2,1)S(1)}, u32[]{:S(2)}, u32[]{:S(2)}) async-start(bf16[16,272,128]{2,1,0:T(8,128)(2,1)} %shard_map.118), calls=%async_computation.5 | async-start | bytes 2228224 | tf_op jit(solution)/shard_map/all_to_all | solution.py:256
  159.6 20.3 %collective-permute-start.6 = (bf16[384,128]{1,0:T(8,128)(2,1)S(1)}, bf16[384,128]{1,0:T(8,128)(2,1)S(1)}, u32[]{:S(2)}, u32[]{:S(2)}) collective-permute-start(bf16[384,128]{1,0:T(8,128)(2,1)S(1)} %get-tuple-element.45.sent_ref), channel_id=1, source_target_pairs={{0,64},{64,0},{1,65},{65,1},{2,66},{66,2},{3,67},{67,3},{4,68},{68... | collective-permute-start | bytes 294920 | tf_op jit(solution)/shard_map/ppermute | solution.py:252

commit v5 on v2

--- a/solution.py
+++ b/solution.py
@@ -10,11 +10,12 @@
 
 TILE = 128
 GROUP = 4
-FINE = (("x", 4), ("zh", 2), ("y", 4), ("zl", 8), ("core", 2))
-N_X, N_ZH, N_Y, N_ZL, N_CORE = (size for _, size in FINE)
+FINE = (("x", 4), ("zh", 2), ("y", 4), ("z2", 2), ("z4", 4), ("core", 2))
+N_X, N_ZH, N_Y, N_Z2, N_Z4, N_CORE = (size for _, size in FINE)
+N_ZL = N_Z2 * N_Z4
 ROW = ("x", "zh")
-COL = ("y", "zl", "core")
-W_ROWS = 32
+COL = ("y", "z2", "z4", "core")
+W_ROWS = 64
 VMEM_LIMIT = 48 * 1024 * 1024
 BF16 = jnp.bfloat16
 F32 = jnp.float32
@@ -43,6 +44,20 @@
 
 def group_total(count_ref):
     return (count_ref[0, 0] + GROUP - 1) // GROUP
+
+
+def tile_place(row):
+    near = row // N_CORE
+    return near // N_ZL * N_ZL + near % N_Z4 * N_Z2 + near // N_Z4 % N_Z2
+
+
+def pair_body(zh_ref, own_ref, other_ref, send_ref):
+    mine = zh_ref[0] == 0
+    own, other = own_ref[...], other_ref[...]
+    first, second = jnp.where(mine, own, other), jnp.where(mine, other, own)
+    for peer in range(N_X):
+        send_ref[peer, 0] = first
+        send_ref[peer, 1] = second
 
 
 def build_body(count_ref, rows_ref, cols_ref, weight_ref, tiles_ref, live_ref):
@@ -82,7 +97,7 @@
             )
         for i in range(GROUP):
             row = row_ref[0, group * GROUP + i]
-            acc_ref[row % N_CORE, row // N_CORE] += products[i]
+            acc_ref[row % N_CORE, tile_place(row)] += products[i]
         return carry
 
     lax.fori_loop(0, group_total(count_ref), step, 0)
@@ -94,34 +109,48 @@
     out_ref[...] = (keep_ref[...] + got_ref[...].astype(F32)).astype(BF16)
 
 
-def dense_body(parts_ref, weight_ref, up_ref, act_ref, send_ref, *, scale):
-    aggregated = jnp.sum(parts_ref[...].astype(F32), axis=0).astype(BF16)
+def dense_body(
+    z2_ref, own_ref, other_ref, weight_ref, up_ref, other_up_ref, act_ref, send_ref, *, scale
+):
+    first = z2_ref[0] == 0
+    total = own_ref[...].astype(F32) + other_ref[...].astype(F32)
+    aggregated = total.reshape(N_Z2 * TILE, TILE).astype(BF16)
     weight = weight_ref[...]
+    own_up, other_up = up_ref[...], other_up_ref[...]
+    up = jnp.concatenate(
+        [jnp.where(first, own_up, other_up), jnp.where(first, other_up, own_up)], axis=0
+    )
     pre_act = jnp.dot(aggregated, weight, preferred_element_type=F32)
     gate = jax.nn.sigmoid(pre_act)
-    act_ref[...] = (pre_act * gate).astype(BF16)
-    grad_pre = (up_ref[...].astype(F32) * gate * (1.0 + pre_act * (1.0 - gate))).astype(BF16)
-    grad_agg = lax.dot_general(
-        weight, grad_pre, (((1,), (1,)), ((), ())), preferred_element_type=F32
-    ).astype(BF16)
+    act = (pre_act * gate).astype(BF16)
+    act_ref[...] = jnp.where(first, act[:TILE], act[TILE:])
+    grad_pre = (up.astype(F32) * gate * (1.0 + pre_act * (1.0 - gate))).astype(BF16)
     local_weight = (
         lax.dot_general(aggregated, grad_pre, (((0,), (0,)), ((), ())), preferred_element_type=F32)
         * scale
-    )
-    deep = TILE // N_ZL
-    local_weight = local_weight.astype(BF16)
-    for peer in range(N_ZL):
-        send_ref[peer, 0:TILE, :] = grad_agg
+    ).astype(BF16)
+    deep = TILE // N_Z4
+    for z2 in range(N_Z2):
+        grad_agg = lax.dot_general(
+            weight,
+            grad_pre[z2 * TILE : (z2 + 1) * TILE],
+            (((1,), (1,)), ((), ())),
+            preferred_element_type=F32,
+        ).astype(BF16)
+        for peer in range(N_Z4):
+            send_ref[peer, z2 * TILE : (z2 + 1) * TILE, :] = grad_agg
+    for peer in range(N_Z4):
         here = slice(peer * deep, (peer + 1) * deep)
-        send_ref[peer, TILE : TILE + deep, :] = local_weight[here, :TILE]
-        send_ref[peer, TILE + deep :, :] = local_weight[here, TILE:]
+        send_ref[peer, N_Z2 * TILE : N_Z2 * TILE + deep, :] = local_weight[here, :TILE]
+        send_ref[peer, N_Z2 * TILE + deep :, :] = local_weight[here, TILE:]
 
 
 def spread_body(got_ref, send_ref):
-    high, low = halves(jnp.sum(got_ref[:, TILE:, :].astype(F32), axis=0))
+    high, low = halves(jnp.sum(got_ref[:, N_Z2 * TILE :, :].astype(F32), axis=0))
     for peer in range(N_Y):
-        for k in range(N_ZL):
-            send_ref[peer, k * TILE : (k + 1) * TILE, :] = got_ref[k, 0:TILE, :]
+        for z4 in range(N_Z4):
+            here = slice(z4 * N_Z2 * TILE, (z4 + 1) * N_Z2 * TILE)
+            send_ref[peer, here, :] = got_ref[z4, 0 : N_Z2 * TILE, :]
         send_ref[peer, N_ZL * TILE : N_ZL * TILE + W_ROWS, :] = high
         send_ref[peer, N_ZL * TILE + W_ROWS :, :] = low
 
@@ -145,8 +174,9 @@
         for i in range(GROUP):
             slot = group * GROUP + i
             row = row_ref[0, slot]
-            start = pl.multiple_of(row // N_CORE % N_ZL * TILE, TILE)
-            grad = grads_ref[row % N_CORE, row // (N_CORE * N_ZL), pl.ds(start, TILE), :]
+            place = tile_place(row)
+            start = pl.multiple_of(place % N_ZL * TILE, TILE)
+            grad = grads_ref[row % N_CORE, place // N_ZL, pl.ds(start, TILE), :]
             products.append(jnp.dot(grad, tiles_ref[slot], preferred_element_type=F32))
         for i in range(GROUP):
             acc_ref[col_ref[0, group * GROUP + i]] += products[i]
@@ -154,32 +184,30 @@
 
     lax.fori_loop(0, group_total(count_ref), step, 0)
     terms = jnp.sum(grads_ref[:, :, N_ZL * TILE :, :].astype(F32), axis=(0, 1))
-    high, low = halves(terms[:W_ROWS] + terms[W_ROWS:])
+    weight_sum = (terms[:W_ROWS] + terms[W_ROWS:]).astype(BF16)
     for x in range(N_X):
         for zh in range(N_ZH):
             send_ref[x, zh * TILE : (zh + 1) * TILE, :] = acc_ref[x * N_ZH + zh].astype(BF16)
-        send_ref[x, N_ZH * TILE : N_ZH * TILE + W_ROWS, :] = high
-        send_ref[x, N_ZH * TILE + W_ROWS :, :] = low
+        send_ref[x, N_ZH * TILE :, :] = weight_sum
 
 
 def halfway_body(zh_ref, got_ref, send_ref, keep_ref, send_weight_ref):
     zh = zh_ref[0]
     total = jnp.sum(got_ref[...].astype(F32), axis=0)
-    first, second = total[:TILE], total[TILE : 2 * TILE]
+    first, second = total[:TILE], total[TILE : N_ZH * TILE]
     mine = zh == 0
     keep_ref[...] = jnp.where(mine, first, second)
     send_ref[...] = jnp.where(mine, second, first).astype(BF16)
-    terms = total[2 * TILE :]
-    weight_sum = (terms[:W_ROWS] + terms[W_ROWS:]).astype(BF16)
-    for peer in range(N_ZH * N_ZL):
+    weight_sum = total[N_ZH * TILE :].astype(BF16)
+    for peer in range(N_ZH * N_Z4):
         send_weight_ref[peer] = weight_sum
 
 
 def finish_body(got_ref, keep_ref, got_weight_ref, grad_ref, grad_weight_ref):
     grad_ref[...] = (keep_ref[...] + got_ref[...].astype(F32)).T.astype(BF16)
-    deep = TILE // N_ZL
-    for k in range(N_ZL):
-        total = got_weight_ref[k].astype(F32) + got_weight_ref[N_ZL + k].astype(F32)
+    deep = TILE // N_Z4
+    for k in range(N_Z4):
+        total = got_weight_ref[k].astype(F32) + got_weight_ref[N_Z4 + k].astype(F32)
         grad_weight_ref[k * deep : (k + 1) * deep, :TILE] = total[:deep]
         grad_weight_ref[k * deep : (k + 1) * deep, TILE:] = total[deep:]
 
@@ -205,8 +233,10 @@
     zh = lax.axis_index("zh")
     own = features[0]
     other = swap(own, "zh")
-    pair = jnp.where(zh == 0, jnp.stack([own, other]), jnp.stack([other, own]))
-    pair = jnp.broadcast_to(pair[None], (N_X,) + pair.shape)
+    zh_here = zh.astype(jnp.int32)[None]
+    pair = call(pair_body, shape((N_X, N_ZH, TILE, width), BF16), [smem, vmem, vmem])(
+        zh_here, own, other
+    )
     column = exchange(pair, "x").reshape(N_X * N_ZH, TILE, width)
 
     tiles = call(
@@ -230,9 +260,12 @@
     )(tile_count, core, row_tiles, col_tiles, tiles, column)
 
     partial = call(merge_body, shape(half, BF16), [vmem, vmem])(swap(send, "core"), keep)
-    got = exchange(partial, "y").reshape((N_Y, N_ZL, TILE, width))
+    partial, up = lax.optimization_barrier((partial, upstream[0]))
+    got, other_up = lax.optimization_barrier((exchange(partial, "y"), swap(up, "z2")))
+    got = got.reshape((N_Y, N_ZL, TILE, width))
     partial = jnp.sum(got.astype(F32), axis=0).astype(BF16)
-    parts = exchange(partial, "zl")
+    got = exchange(partial, "z4").reshape((N_Z4, N_Z2, TILE, width))
+    partial = jnp.sum(got.astype(F32), axis=0).astype(BF16)
 
     node_total = features.shape[1] * N_X * N_ZH * blocks
     scale = 1.0 / math.sqrt(node_total)
@@ -242,17 +275,24 @@
 
     out_act, send = call(
         dense,
-        (shape((TILE, hidden), BF16), shape((N_ZL, TILE + W_ROWS, TILE), BF16)),
-        [vmem] * 3,
-    )(parts, weight, upstream[0])
-
-    got = exchange(send, "zl")
+        (shape((TILE, hidden), BF16), shape((N_Z4, N_Z2 * TILE + W_ROWS, TILE), BF16)),
+        [smem] + [vmem] * 5,
+    )(
+        lax.axis_index("z2").astype(jnp.int32)[None],
+        partial,
+        swap(partial, "z2"),
+        weight,
+        up,
+        other_up,
+    )
+
+    got = exchange(send, "z4")
     send = call(spread_body, shape((N_Y, N_ZL * TILE + 2 * W_ROWS, TILE), BF16), [vmem])(got)
     mine = exchange(send, "y")
     theirs = swap(mine, "core")
     send = call(
         backward_body,
-        shape((N_X, N_ZH * TILE + 2 * W_ROWS, TILE), BF16),
+        shape((N_X, N_ZH * TILE + W_ROWS, TILE), BF16),
         [smem, smem, smem, smem, vmem, hbm, hbm],
         [
             pltpu.VMEM((N_CORE,) + mine.shape, BF16),
@@ -275,12 +315,12 @@
         (
             shape((TILE, TILE), BF16),
             shape((TILE, TILE), F32),
-            shape((N_ZH * N_ZL, W_ROWS, TILE), BF16),
+            shape((N_ZH * N_Z4, W_ROWS, TILE), BF16),
         ),
         [smem, vmem],
-    )(zh.astype(jnp.int32)[None], got)
+    )(zh_here, got)
     got = swap(send, "zh")
-    got_weight = exchange(send_weight, ("zh", "zl"))
+    got_weight = exchange(send_weight, ("zh", "z4"))
     grad_features, grad_weight = call(
         finish_body,
         (shape((TILE, width), BF16), shape((width, hidden), F32)),

time: 168 us -> 164 us (0.976)
  blocking collectives: 86.4 us -> 51.9 us
  starting transfers between devices: 55.9 us -> 72.4 us
  waiting for transfers between devices: 13.1 us -> 23.7 us
  Pallas kernels: 6.4 us -> 9.8 us
    all_to_all x5 -> x4, blocking collectives: 86.4 us -> 51.9 us  [exchange(): return lax.all_to_all(value, axis, 0, 0, tiled=True)]
    ppermute x4 -> x6, starting transfers between devices: 42.1 us -> 52.7 us  [swap(): return lax.ppermute(value, axis, [(0, 1), (1, 0)])]
    ppermute x4 -> x6, waiting for transfers between devices: 11.5 us -> 21.2 us  [swap(): return lax.ppermute(value, axis, [(0, 1), (1, 0)])]
    all_to_all x2 -> x3, starting transfers between devices: 13.8 us -> 19.8 us  [exchange(): return lax.all_to_all(value, axis, 0, 0, tiled=True)]
    pallas_call x2 -> x3, Pallas kernels: 2.35 us -> 3.89 us  [the longest x1 2.28 us: local(): call(backward_body, shape((N_X, N_ZH * TILE + W_ROWS, TILE), BF16), [smem...]
  transfers between devices with their start and end apart: 6 -> 9, of which waited for: 5 -> 8; matrix products, arithmetic and copies ran while one was open for 0% -> 0% of each run, Pallas kernels for 0% -> 1%
where the time goes in v5:
time: 164 us; the launch traced here: 163 us
  starting transfers between devices  72.4 us (44%)
  blocking collectives  51.9 us (32%)
  waiting for transfers between devices  23.7 us (14%)
  Pallas kernels  9.8 us (6%)
  local copies, waits for them, and re-layouts  3.21 us (2%)
    ppermute x6, starting transfers between devices, swap(): return lax.ppermute(value, axis, [(0, 1), (1, 0)])  52.7 us
    all_to_all x4, blocking collectives, exchange(): return lax.all_to_all(value, axis, 0, 0, tiled=True)  51.9 us
    ppermute x6, waiting for transfers between devices, swap(): return lax.ppermute(value, axis, [(0, 1), (1, 0)])  21.2 us
    all_to_all x3, starting transfers between devices, exchange(): return lax.all_to_all(value, axis, 0, 0, tiled=True)  19.8 us
  transfers between devices with their start and end apart: 9, of which 8 were waited for; matrix products, arithmetic and copies ran while one was open for 0% of the time, Pallas kernels for 1%

profile of v5, /device:TPU:1, one launch (start us, length us, event | category | flops | bytes accessed | tf_op | source)
XLA Modules:
  0.0 163.4 jit_solution(778719848995035120)
XLA Ops:
  0.6 16.3 %collective-permute-start = (bf16[128,128]{1,0:T(8,128)(2,1)}, bf16[128,128]{1,0:T(8,128)(2,1)S(1)}, u32[]{:S(2)}, u32[]{:S(2)}) collective-permute-start(bf16[128,128]{1,0:T(8,128)(2,1)} %bitcast.18), channel_id=1, source_target_pairs={{0,64},{64,0},{1,65},{65,1},{2,66},{66,2},{3,67},{67,3},{4,68},{68... | collective-permute-start | bytes 98312 | tf_op jit(solution)/shard_map/ppermute | solution.py:216
  16.9 1.6 collective-permute-done.other_ref
  18.5 0.0 copy-start.2
  18.5 0.8 copy-done.2
  19.3 0.7 shard_map.113
  20.0 4.0 %all-to-all-start = ((bf16[4,2,128,128]{3,2,1,0:T(8,128)(2,1)}), bf16[4,2,128,128]{3,2,1,0:T(8,128)(2,1)S(1)}, u32[]{:S(2)}, u32[]{:S(2)}) async-start(bf16[4,2,128,128]{3,2,1,0:T(8,128)(2,1)} %shard_map.113), calls=%async_computation | async-start | bytes 524288 | tf_op jit(solution)/shard_map/all_to_all | solution.py:220
  24.7 0.0 copy-start.5
  24.7 0.8 copy-done.5
  25.5 0.0 copy-start.6
  25.5 0.8 copy-done.6
  26.4 0.0 copy-start.7
  26.4 0.8 copy-done.7
  27.1 0.0 copy-start.3
  27.1 0.0 copy-start.4
  27.1 1.2 shard_map.112.tiles_ref
  28.4 1.2 all-to-all-done
  29.6 0.0 copy-done.3
  29.6 0.0 copy-done.4
  29.6 2.0 %shard_map.114 = (bf16[32,128,128]{2,1,0:T(8,128)(2,1)S(1)}, f32[32,128,128]{2,1,0:T(8,128)S(1)}) custom-call(s32[1,1]{1,0:T(1,128)S(6)} %copy.12.count_ref, s32[1]{0:T(128)} %bitcast.1.core_ref, s32[1,64]{1,0:T(1,128)S(1)} %bitcast.20, s32[1,64]{1,0:T(1,128)S(1)} %bitcast.22, bf16[64,128,128]{2,1,0:T(8,128)(2,1)S(1)} %shard_map.112.tiles_ref, ...), custom_call_target="tpu_custom_call" | custom-call | flops 268435456 | bytes 4194304 | tf_op jit(solution)/shard_map/pallas_call | solution.py:253
  31.6 6.5 %collective-permute-start.1 = (bf16[32,128,128]{2,1,0:T(8,128)(2,1)S(1)}, bf16[32,128,128]{2,1,0:T(8,128)(2,1)S(1)}, u32[]{:S(2)}, u32[]{:S(2)}) collective-permute-start(bf16[32,128,128]{2,1,0:T(8,128)(2,1)S(1)} %get-tuple-element.16), channel_id=1, source_target_pairs={{0,1},{1,0},{2,3},{3,2},{4,5},{5,4},{6,7},{7,6},{8,9},{9,8},{10,11... | collective-permute-start | bytes 3145736 | tf_op jit(solution)/shard_map/ppermute | solution.py:216
  38.1 2.3 %collective-permute-done.1.got_ref = bf16[32,128,128]{2,1,0:T(8,128)(2,1)S(1)} collective-permute-done((bf16[32,128,128]{2,1,0:T(8,128)(2,1)S(1)}, bf16[32,128,128]{2,1,0:T(8,128)(2,1)S(1)}, u32[]{:S(2)}, u32[]{:S(2)}) %collective-permute-start.1) | collective-permute-done | bytes 1048608 | tf_op jit(solution)/shard_map/ppermute | solution.py:216
  40.4 1.2 shard_map.115
  41.5 0.0 copy-start.1
  41.5 3.6 %all-to-all-start.1 = ((bf16[32,128,128]{2,1,0:T(8,128)(2,1)}), bf16[32,128,128]{2,1,0:T(8,128)(2,1)S(1)}, u32[]{:S(2)}, u32[]{:S(2)}) async-start(bf16[32,128,128]{2,1,0:T(8,128)(2,1)} %shard_map.115), calls=%async_computation.1 | async-start | bytes 2097152 | tf_op jit(solution)/shard_map/all_to_all | solution.py:220
  45.2 0.0 copy-done.1
  45.2 0.0 copy-start
  45.2 5.2 %collective-permute-start.2 = (bf16[128,256]{1,0:T(8,128)(2,1)S(1)}, bf16[128,256]{1,0:T(8,128)(2,1)S(1)}, u32[]{:S(2)}, u32[]{:S(2)}) collective-permute-start(bf16[128,256]{1,0:T(8,128)(2,1)S(1)} %bitcast.16), channel_id=1, source_target_pairs={{0,8},{8,0},{1,9},{9,1},{2,10},{10,2},{3,11},{11,3},{4,12},{12,4},... | collective-permute-start | bytes 196616 | tf_op jit(solution)/shard_map/ppermute | solution.py:216
  50.4 8.2 %collective-permute-done.2.refs_5_ = bf16[128,256]{1,0:T(8,128)(2,1)S(1)} collective-permute-done((bf16[128,256]{1,0:T(8,128)(2,1)S(1)}, bf16[128,256]{1,0:T(8,128)(2,1)S(1)}, u32[]{:S(2)}, u32[]{:S(2)}) %collective-permute-start.2) | collective-permute-done | bytes 65568 | tf_op jit(solution)/shard_map/ppermute | solution.py:216
  58.7 1.3 all-to-all-done.1
  60.0 0.9 reduce_sum.24
  60.9 9.4 %all_to_all.35 = bf16[8,128,128]{2,1,0:T(8,128)(2,1)S(1)} all-to-all(bf16[8,128,128]{2,1,0:T(8,128)(2,1)} %reduce_sum.24), channel_id=1, replica_groups=mesh['x'=4,'zh'=2,'y'=4,'z2'=2,'z4'=4,'core'=2] {'z4'}, dimensions={0} | all-to-all | bytes 524288 | tf_op jit(solution)/shard_map/all_to_all | solution.py:220
  70.4 6.8 %collective-permute-start.3 = (bf16[2,128,128]{2,1,0:T(8,128)(2,1)S(1)}, bf16[2,128,128]{2,1,0:T(8,128)(2,1)S(1)}, u32[]{:S(2)}, u32[]{:S(2)}) collective-permute-start(bf16[2,128,128]{2,1,0:T(8,128)(2,1)S(1)} %reduce_sum.25.refs_1_), channel_id=1, source_target_pairs={{0,8},{8,0},{1,9},{9,1},{2,10},{10,2},{3,11},{11,3},{4,12},{12,4},... | collective-permute-start | bytes 196616 | tf_op jit(solution)/shard_map/ppermute | solution.py:216
  77.2 2.1 %collective-permute-done.3.refs_2_ = bf16[2,128,128]{2,1,0:T(8,128)(2,1)S(1)} collective-permute-done((bf16[2,128,128]{2,1,0:T(8,128)(2,1)S(1)}, bf16[2,128,128]{2,1,0:T(8,128)(2,1)S(1)}, u32[]{:S(2)}, u32[]{:S(2)}) %collective-permute-start.3) | collective-permute-done | bytes 65568 | tf_op jit(solution)/shard_map/ppermute | solution.py:216
  79.3 0.0 copy-done
  79.3 0.9 shard_map.116
  80.2 13.4 %all_to_all.36.got_ref = bf16[4,320,128]{2,1,0:T(8,128)(2,1)S(1)} all-to-all(bf16[4,320,128]{2,1,0:T(8,128)(2,1)S(1)} %get-tuple-element.23), channel_id=1, replica_groups=mesh['x'=4,'zh'=2,'y'=4,'z2'=2,'z4'=4,'core'=2] {'z4'}, dimensions={0} | all-to-all | bytes 655360 | tf_op jit(solution)/shard_map/all_to_all | solution.py:220
  93.6 0.1 shard_map.117
  93.7 19.4 %all_to_all.37.own_ref = bf16[4,1152,128]{2,1,0:T(8,128)(2,1)S(1)} all-to-all(bf16[4,1152,128]{2,1,0:T(8,128)(2,1)S(1)} %shard_map.117), channel_id=1, replica_groups=mesh['x'=4,'zh'=2,'y'=4,'z2'=2,'z4'=4,'core'=2] {'y'}, dimensions={0} | all-to-all | bytes 2359296 | tf_op jit(solution)/shard_map/all_to_all | solution.py:220
  113.2 5.8 %collective-permute-start.4 = (bf16[4,1152,128]{2,1,0:T(8,128)(2,1)S(1)}, bf16[4,1152,128]{2,1,0:T(8,128)(2,1)S(1)}, u32[]{:S(2)}, u32[]{:S(2)}) collective-permute-start(bf16[4,1152,128]{2,1,0:T(8,128)(2,1)S(1)} %all_to_all.37.own_ref), channel_id=1, source_target_pairs={{0,1},{1,0},{2,3},{3,2},{4,5},{5,4},{6,7},{7,6},{8,9},{9,8},{10,11... | collective-permute-start | bytes 3538952 | tf_op jit(solution)/shard_map/ppermute | solution.py:216
  118.9 2.5 %collective-permute-done.4.other_ref = bf16[4,1152,128]{2,1,0:T(8,128)(2,1)S(1)} collective-permute-done((bf16[4,1152,128]{2,1,0:T(8,128)(2,1)S(1)}, bf16[4,1152,128]{2,1,0:T(8,128)(2,1)S(1)}, u32[]{:S(2)}, u32[]{:S(2)}) %collective-permute-start.4) | collective-permute-done | bytes 1179680 | tf_op jit(solution)/shard_map/ppermute | solution.py:216
  121.4 2.3 %shard_map.118 = bf16[4,320,128]{2,1,0:T(8,128)(2,1)S(1)} custom-call(s32[1,1]{1,0:T(1,128)S(6)} %copy.12.count_ref, s32[1]{0:T(128)} %bitcast.1.core_ref, s32[1,64]{1,0:T(1,128)S(1)} %bitcast.21, s32[1,64]{1,0:T(1,128)S(1)} %bitcast.23, bf16[64,128,128]{2,1,0:T(8,128)(2,1)S(1)} %shard_map.112.tiles_ref, bf16[4,1152,128]{2,1,0:T(8,128)(2,1)S(1)} %all_to_all.37.own_ref, ...), custom_call_target="tpu_custom_call" | custom-call | tf_op jit(solution)/shard_map/pallas_call | solution.py:293
  123.7 9.6 %all_to_all.38.got_ref = bf16[4,320,128]{2,1,0:T(8,128)(2,1)S(1)} all-to-all(bf16[4,320,128]{2,1,0:T(8,128)(2,1)S(1)} %shard_map.118), channel_id=1, replica_groups=mesh['x'=4,'zh'=2,'y'=4,'z2'=2,'z4'=4,'core'=2] {'x'}, dimensions={0} | all-to-all | bytes 655360 | tf_op jit(solution)/shard_map/all_to_all | solution.py:220
  133.3 0.7 shard_map.119
  134.0 12.1 %all-to-all-start.6 = ((bf16[8,64,128]{2,1,0:T(8,128)(2,1)}), bf16[8,64,128]{2,1,0:T(8,128)(2,1)S(1)}, u32[]{:S(2)}, u32[]{:S(2)}) async-start(bf16[8,64,128]{2,1,0:T(8,128)(2,1)} %get-tuple-element.26), calls=%async_computation.6 | async-start | bytes 262144 | tf_op jit(solution)/shard_map/all_to_all | solution.py:220
  146.1 12.1 %collective-permute-start.5 = (bf16[128,128]{1,0:T(8,128)(2,1)S(1)}, bf16[128,128]{1,0:T(8,128)(2,1)S(1)}, u32[]{:S(2)}, u32[]{:S(2)}) collective-permute-start(bf16[128,128]{1,0:T(8,128)(2,1)S(1)} %get-tuple-element.24), channel_id=1, source_target_pairs={{0,64},{64,0},{1,65},{65,1},{2,66},{66,2},{3,67},{67,3},{4,68},{68... | collective-permute-start | bytes 98312 | tf_op jit(solution)/shard_map/ppermute | solution.py:216
  158.1 4.5 %collective-permute-done.5.got_ref = bf16[128,128]{1,0:T(8,128)(2,1)S(1)} collective-permute-done((bf16[128,128]{1,0:T(8,128)(2,1)S(1)}, bf16[128,128]{1,0:T(8,128)(2,1)S(1)}, u32[]{:S(2)}, u32[]{:S(2)}) %collective-permute-start.5) | collective-permute-done | bytes 32800 | tf_op jit(solution)/shard_map/ppermute | solution.py:216
  162.7 0.0 all-to-all-done.6.got_weight_ref
  162.7 0.7 shard_map.120
  (1 shorter events, 0.0 us)
Async XLA Ops:
  0.6 17.9 %collective-permute-start = (bf16[128,128]{1,0:T(8,128)(2,1)}, bf16[128,128]{1,0:T(8,128)(2,1)S(1)}, u32[]{:S(2)}, u32[]{:S(2)}) collective-permute-start(bf16[128,128]{1,0:T(8,128)(2,1)} %bitcast.18), channel_id=1, source_target_pairs={{0,64},{64,0},{1,65},{65,1},{2,66},{66,2},{3,67},{67,3},{4,68},{68... | collective-permute-start | bytes 98312 | tf_op jit(solution)/shard_map/ppermute | solution.py:216
  18.5 0.8 copy-start.2
  20.0 9.5 %all-to-all-start = ((bf16[4,2,128,128]{3,2,1,0:T(8,128)(2,1)}), bf16[4,2,128,128]{3,2,1,0:T(8,128)(2,1)S(1)}, u32[]{:S(2)}, u32[]{:S(2)}) async-start(bf16[4,2,128,128]{3,2,1,0:T(8,128)(2,1)} %shard_map.113), calls=%async_computation | async-start | bytes 524288 | tf_op jit(solution)/shard_map/all_to_all | solution.py:220
  24.7 0.8 copy-start.5
  25.5 0.8 copy-start.6
  26.4 0.8 copy-start.7
  27.1 2.4 %copy-start.3 = (s32[1,1,64]{2,1,0:T(1,128)S(1)}, s32[1,1,64]{2,1,0:T(1,128)}, u32[]{:S(2)}) copy-start(s32[1,1,64]{2,1,0:T(1,128)} %param.12) | copy-start | bytes 772
  27.1 2.4 %copy-start.4 = (s32[1,1,64]{2,1,0:T(1,128)S(1)}, s32[1,1,64]{2,1,0:T(1,128)}, u32[]{:S(2)}) copy-start(s32[1,1,64]{2,1,0:T(1,128)} %param.13) | copy-start | bytes 772
  31.6 8.8 %collective-permute-start.1 = (bf16[32,128,128]{2,1,0:T(8,128)(2,1)S(1)}, bf16[32,128,128]{2,1,0:T(8,128)(2,1)S(1)}, u32[]{:S(2)}, u32[]{:S(2)}) collective-permute-start(bf16[32,128,128]{2,1,0:T(8,128)(2,1)S(1)} %get-tuple-element.16), channel_id=1, source_target_pairs={{0,1},{1,0},{2,3},{3,2},{4,5},{5,4},{6,7},{7,6},{8,9},{9,8},{10,11... | collective-permute-start | bytes 3145736 | tf_op jit(solution)/shard_map/ppermute | solution.py:216
  41.5 3.7 %copy-start.1 = (bf16[1,128,256]{2,1,0:T(8,128)(2,1)S(1)}, bf16[1,128,256]{2,1,0:T(8,128)(2,1)}, u32[]{:S(2)}) copy-start(bf16[1,128,256]{2,1,0:T(8,128)(2,1)} %param.11) | copy-start | bytes 196612
  41.5 18.5 %all-to-all-start.1 = ((bf16[32,128,128]{2,1,0:T(8,128)(2,1)}), bf16[32,128,128]{2,1,0:T(8,128)(2,1)S(1)}, u32[]{:S(2)}, u32[]{:S(2)}) async-start(bf16[32,128,128]{2,1,0:T(8,128)(2,1)} %shard_map.115), calls=%async_computation.1 | async-start | bytes 2097152 | tf_op jit(solution)/shard_map/all_to_all | solution.py:220
  45.2 34.1 %copy-start = (bf16[128,256]{1,0:T(8,128)(2,1)S(1)}, bf16[128,256]{1,0:T(8,128)(2,1)}, u32[]{:S(2)}) copy-start(bf16[128,256]{1,0:T(8,128)(2,1)} %refs_3_.1) | copy-start | bytes 196612
  45.2 13.5 %collective-permute-start.2 = (bf16[128,256]{1,0:T(8,128)(2,1)S(1)}, bf16[128,256]{1,0:T(8,128)(2,1)S(1)}, u32[]{:S(2)}, u32[]{:S(2)}) collective-permute-start(bf16[128,256]{1,0:T(8,128)(2,1)S(1)} %bitcast.16), channel_id=1, source_target_pairs={{0,8},{8,0},{1,9},{9,1},{2,10},{10,2},{3,11},{11,3},{4,12},{12,4},... | collective-permute-start | bytes 196616 | tf_op jit(solution)/shard_map/ppermute | solution.py:216
  70.4 8.9 %collective-permute-start.3 = (bf16[2,128,128]{2,1,0:T(8,128)(2,1)S(1)}, bf16[2,128,128]{2,1,0:T(8,128)(2,1)S(1)}, u32[]{:S(2)}, u32[]{:S(2)}) collective-permute-start(bf16[2,128,128]{2,1,0:T(8,128)(2,1)S(1)} %reduce_sum.25.refs_1_), channel_id=1, source_target_pairs={{0,8},{8,0},{1,9},{9,1},{2,10},{10,2},{3,11},{11,3},{4,12},{12,4},... | collective-permute-start | bytes 196616 | tf_op jit(solution)/shard_map/ppermute | solution.py:216
  113.2 8.2 %collective-permute-start.4 = (bf16[4,1152,128]{2,1,0:T(8,128)(2,1)S(1)}, bf16[4,1152,128]{2,1,0:T(8,128)(2,1)S(1)}, u32[]{:S(2)}, u32[]{:S(2)}) collective-permute-start(bf16[4,1152,128]{2,1,0:T(8,128)(2,1)S(1)} %all_to_all.37.own_ref), channel_id=1, source_target_pairs={{0,1},{1,0},{2,3},{3,2},{4,5},{5,4},{6,7},{7,6},{8,9},{9,8},{10,11... | collective-permute-start | bytes 3538952 | tf_op jit(solution)/shard_map/ppermute | solution.py:216
  134.0 28.7 %all-to-all-start.6 = ((bf16[8,64,128]{2,1,0:T(8,128)(2,1)}), bf16[8,64,128]{2,1,0:T(8,128)(2,1)S(1)}, u32[]{:S(2)}, u32[]{:S(2)}) async-start(bf16[8,64,128]{2,1,0:T(8,128)(2,1)} %get-tuple-element.26), calls=%async_computation.6 | async-start | bytes 262144 | tf_op jit(solution)/shard_map/all_to_all | solution.py:220
  146.1 16.6 %collective-permute-start.5 = (bf16[128,128]{1,0:T(8,128)(2,1)S(1)}, bf16[128,128]{1,0:T(8,128)(2,1)S(1)}, u32[]{:S(2)}, u32[]{:S(2)}) collective-permute-start(bf16[128,128]{1,0:T(8,128)(2,1)S(1)} %get-tuple-element.24), channel_id=1, source_target_pairs={{0,64},{64,0},{1,65},{65,1},{2,66},{66,2},{3,67},{67,3},{4,68},{68... | collective-permute-start | bytes 98312 | tf_op jit(solution)/shard_map/ppermute | solution.py:216

commit v6 on v5

--- a/solution.py
+++ b/solution.py
@@ -9,13 +9,13 @@
 from jax.sharding import PartitionSpec as P
 
 TILE = 128
-GROUP = 4
+GROUP = 16
 FINE = (("x", 4), ("zh", 2), ("y", 4), ("z2", 2), ("z4", 4), ("core", 2))
 N_X, N_ZH, N_Y, N_Z2, N_Z4, N_CORE = (size for _, size in FINE)
 N_ZL = N_Z2 * N_Z4
 ROW = ("x", "zh")
 COL = ("y", "z2", "z4", "core")
-W_ROWS = 64
+W_ROWS = 32
 VMEM_LIMIT = 48 * 1024 * 1024
 BF16 = jnp.bfloat16
 F32 = jnp.float32
@@ -145,8 +145,9 @@
         send_ref[peer, N_Z2 * TILE + deep :, :] = local_weight[here, TILE:]
 
 
-def spread_body(got_ref, send_ref):
-    high, low = halves(jnp.sum(got_ref[:, N_Z2 * TILE :, :].astype(F32), axis=0))
+def spread_body(z2_ref, got_ref, send_ref):
+    terms = jnp.sum(got_ref[:, N_Z2 * TILE :, :].astype(F32), axis=0)
+    high, low = halves(jnp.where(z2_ref[0] == 0, terms[:W_ROWS], terms[W_ROWS:]))
     for peer in range(N_Y):
         for z4 in range(N_Z4):
             here = slice(z4 * N_Z2 * TILE, (z4 + 1) * N_Z2 * TILE)
@@ -184,11 +185,12 @@
 
     lax.fori_loop(0, group_total(count_ref), step, 0)
     terms = jnp.sum(grads_ref[:, :, N_ZL * TILE :, :].astype(F32), axis=(0, 1))
-    weight_sum = (terms[:W_ROWS] + terms[W_ROWS:]).astype(BF16)
+    high, low = halves(terms[:W_ROWS] + terms[W_ROWS:])
     for x in range(N_X):
         for zh in range(N_ZH):
             send_ref[x, zh * TILE : (zh + 1) * TILE, :] = acc_ref[x * N_ZH + zh].astype(BF16)
-        send_ref[x, N_ZH * TILE :, :] = weight_sum
+        send_ref[x, N_ZH * TILE : N_ZH * TILE + W_ROWS, :] = high
+        send_ref[x, N_ZH * TILE + W_ROWS :, :] = low
 
 
 def halfway_body(zh_ref, got_ref, send_ref, keep_ref, send_weight_ref):
@@ -198,18 +200,20 @@
     mine = zh == 0
     keep_ref[...] = jnp.where(mine, first, second)
     send_ref[...] = jnp.where(mine, second, first).astype(BF16)
-    weight_sum = total[N_ZH * TILE :].astype(BF16)
-    for peer in range(N_ZH * N_Z4):
+    terms = total[N_ZH * TILE :]
+    weight_sum = (terms[:W_ROWS] + terms[W_ROWS:]).astype(BF16)
+    for peer in range(N_ZH * N_ZL):
         send_weight_ref[peer] = weight_sum
 
 
 def finish_body(got_ref, keep_ref, got_weight_ref, grad_ref, grad_weight_ref):
     grad_ref[...] = (keep_ref[...] + got_ref[...].astype(F32)).T.astype(BF16)
     deep = TILE // N_Z4
-    for k in range(N_Z4):
-        total = got_weight_ref[k].astype(F32) + got_weight_ref[N_Z4 + k].astype(F32)
-        grad_weight_ref[k * deep : (k + 1) * deep, :TILE] = total[:deep]
-        grad_weight_ref[k * deep : (k + 1) * deep, TILE:] = total[deep:]
+    for z2 in range(N_Z2):
+        for z4 in range(N_Z4):
+            k = z2 * N_Z4 + z4
+            total = got_weight_ref[k].astype(F32) + got_weight_ref[N_ZL + k].astype(F32)
+            grad_weight_ref[z4 * deep : (z4 + 1) * deep, z2 * TILE : (z2 + 1) * TILE] = total
 
 
 def swap(value, axis):
@@ -234,6 +238,7 @@
     own = features[0]
     other = swap(own, "zh")
     zh_here = zh.astype(jnp.int32)[None]
+    z2 = lax.axis_index("z2").astype(jnp.int32)[None]
     pair = call(pair_body, shape((N_X, N_ZH, TILE, width), BF16), [smem, vmem, vmem])(
         zh_here, own, other
     )
@@ -275,10 +280,10 @@
 
     out_act, send = call(
         dense,
-        (shape((TILE, hidden), BF16), shape((N_Z4, N_Z2 * TILE + W_ROWS, TILE), BF16)),
+        (shape((TILE, hidden), BF16), shape((N_Z4, N_Z2 * (TILE + W_ROWS), TILE), BF16)),
         [smem] + [vmem] * 5,
     )(
-        lax.axis_index("z2").astype(jnp.int32)[None],
+        z2,
         partial,
         swap(partial, "z2"),
         weight,
@@ -287,12 +292,14 @@
     )
 
     got = exchange(send, "z4")
-    send = call(spread_body, shape((N_Y, N_ZL * TILE + 2 * W_ROWS, TILE), BF16), [vmem])(got)
+    send = call(spread_body, shape((N_Y, N_ZL * TILE + 2 * W_ROWS, TILE), BF16), [smem, vmem])(
+        z2, got
+    )
     mine = exchange(send, "y")
     theirs = swap(mine, "core")
     send = call(
         backward_body,
-        shape((N_X, N_ZH * TILE + W_ROWS, TILE), BF16),
+        shape((N_X, N_ZH * TILE + 2 * W_ROWS, TILE), BF16),
         [smem, smem, smem, smem, vmem, hbm, hbm],
         [
             pltpu.VMEM((N_CORE,) + mine.shape, BF16),
@@ -315,12 +322,12 @@
         (
             shape((TILE, TILE), BF16),
             shape((TILE, TILE), F32),
-            shape((N_ZH * N_Z4, W_ROWS, TILE), BF16),
+            shape((N_ZH * N_ZL, W_ROWS, TILE), BF16),
         ),
         [smem, vmem],
     )(zh_here, got)
     got = swap(send, "zh")
-    got_weight = exchange(send_weight, ("zh", "z4"))
+    got_weight = exchange(send_weight, ("zh", "z2", "z4"))
     grad_features, grad_weight = call(
         finish_body,
         (shape((TILE, width), BF16), shape((width, hidden), F32)),

time: 164 us -> 160 us (0.976)
  starting transfers between devices: 72.4 us -> 69.4 us
    all_to_all x3, waiting for transfers between devices: 2.51 us -> 6.19 us  [exchange(): return lax.all_to_all(value, axis, 0, 0, tiled=True)]
    ppermute x6, waiting for transfers between devices: 21.2 us -> 18 us  [swap(): return lax.ppermute(value, axis, [(0, 1), (1, 0)])]
    all_to_all x3, starting transfers between devices: 19.8 us -> 17.4 us  [exchange(): return lax.all_to_all(value, axis, 0, 0, tiled=True)]
where the time goes in v6:
time: 160 us
  starting transfers between devices  69.4 us (43%)
  blocking collectives  51.2 us (32%)
  waiting for transfers between devices  24.2 us (15%)
  Pallas kernels  9.1 us (6%)
  local copies, waits for them, and re-layouts  3.21 us (2%)
    ppermute x6, starting transfers between devices, swap(): return lax.ppermute(value, axis, [(0, 1), (1, 0)])  52 us
    all_to_all x4, blocking collectives, exchange(): return lax.all_to_all(value, axis, 0, 0, tiled=True)  51.2 us
    ppermute x6, waiting for transfers between devices, swap(): return lax.ppermute(value, axis, [(0, 1), (1, 0)])  18 us
    all_to_all x3, starting transfers between devices, exchange(): return lax.all_to_all(value, axis, 0, 0, tiled=True)  17.4 us
    all_to_all x3, waiting for transfers between devices, exchange(): return lax.all_to_all(value, axis, 0, 0, tiled=True)  6.19 us
    unnamed x16, local copies, waits for them, and re-layouts  3.21 us
  transfers between devices with their start and end apart: 9, of which 8 were waited for; matrix products, arithmetic and copies ran while one was open for 0% of the time, Pallas kernels for 1%

profile of v6, /device:TPU:1, one launch (start us, length us, event | category | flops | bytes accessed | tf_op | source)
XLA Modules:
  0.0 159.5 jit_solution(2092529412085203141)
XLA Ops:
  0.6 16.3 %collective-permute-start = (bf16[128,128]{1,0:T(8,128)(2,1)}, bf16[128,128]{1,0:T(8,128)(2,1)S(1)}, u32[]{:S(2)}, u32[]{:S(2)}) collective-permute-start(bf16[128,128]{1,0:T(8,128)(2,1)} %bitcast.18), channel_id=1, source_target_pairs={{0,64},{64,0},{1,65},{65,1},{2,66},{66,2},{3,67},{67,3},{4,68},{68... | collective-permute-start | bytes 98312 | tf_op jit(solution)/shard_map/ppermute | solution.py:220
  16.9 1.6 %collective-permute-done.other_ref = bf16[128,128]{1,0:T(8,128)(2,1)S(1)} collective-permute-done((bf16[128,128]{1,0:T(8,128)(2,1)}, bf16[128,128]{1,0:T(8,128)(2,1)S(1)}, u32[]{:S(2)}, u32[]{:S(2)}) %collective-permute-start) | collective-permute-done | bytes 32800 | tf_op jit(solution)/shard_map/ppermute | solution.py:220
  18.5 0.0 copy-start.2
  18.5 0.8 copy-done.2
  19.3 0.7 shard_map.113
  20.0 4.0 %all-to-all-start = ((bf16[4,2,128,128]{3,2,1,0:T(8,128)(2,1)}), bf16[4,2,128,128]{3,2,1,0:T(8,128)(2,1)S(1)}, u32[]{:S(2)}, u32[]{:S(2)}) async-start(bf16[4,2,128,128]{3,2,1,0:T(8,128)(2,1)} %shard_map.113), calls=%async_computation | async-start | bytes 524288 | tf_op jit(solution)/shard_map/all_to_all | solution.py:224
  24.7 0.0 copy-start.5
  24.7 0.8 copy-done.5
  25.5 0.0 copy-start.6
  25.5 0.8 copy-done.6
  26.4 0.0 copy-start.7
  26.4 0.8 copy-done.7
  27.1 0.0 copy-start.3
  27.1 0.0 copy-start.4
  27.1 0.9 shard_map.112.tiles_ref
  28.1 1.5 all-to-all-done
  29.6 0.0 copy-done.3
  29.6 0.0 copy-done.4
  29.6 1.8 %shard_map.114 = (bf16[32,128,128]{2,1,0:T(8,128)(2,1)S(1)}, f32[32,128,128]{2,1,0:T(8,128)S(1)}) custom-call(s32[1,1]{1,0:T(1,128)S(6)} %copy.12.count_ref, s32[1]{0:T(128)} %bitcast.1.core_ref, s32[1,64]{1,0:T(1,128)S(1)} %bitcast.20, s32[1,64]{1,0:T(1,128)S(1)} %bitcast.22, bf16[64,128,128]{2,1,0:T(8,128)(2,1)S(1)} %shard_map.112.tiles_ref, ...), custom_call_target="tpu_custom_call" | custom-call | flops 268435456 | bytes 4194304 | tf_op jit(solution)/shard_map/pallas_call | solution.py:258
  31.4 5.8 %collective-permute-start.1 = (bf16[32,128,128]{2,1,0:T(8,128)(2,1)S(1)}, bf16[32,128,128]{2,1,0:T(8,128)(2,1)S(1)}, u32[]{:S(2)}, u32[]{:S(2)}) collective-permute-start(bf16[32,128,128]{2,1,0:T(8,128)(2,1)S(1)} %get-tuple-element.16), channel_id=1, source_target_pairs={{0,1},{1,0},{2,3},{3,2},{4,5},{5,4},{6,7},{7,6},{8,9},{9,8},{10,11... | collective-permute-start | bytes 3145736 | tf_op jit(solution)/shard_map/ppermute | solution.py:220
  37.2 2.3 %collective-permute-done.1.got_ref = bf16[32,128,128]{2,1,0:T(8,128)(2,1)S(1)} collective-permute-done((bf16[32,128,128]{2,1,0:T(8,128)(2,1)S(1)}, bf16[32,128,128]{2,1,0:T(8,128)(2,1)S(1)}, u32[]{:S(2)}, u32[]{:S(2)}) %collective-permute-start.1) | collective-permute-done | bytes 1048608 | tf_op jit(solution)/shard_map/ppermute | solution.py:220
  39.4 1.2 shard_map.115
  40.6 0.0 copy-start.1
  40.6 3.6 %all-to-all-start.1 = ((bf16[32,128,128]{2,1,0:T(8,128)(2,1)}), bf16[32,128,128]{2,1,0:T(8,128)(2,1)S(1)}, u32[]{:S(2)}, u32[]{:S(2)}) async-start(bf16[32,128,128]{2,1,0:T(8,128)(2,1)} %shard_map.115), calls=%async_computation.1 | async-start | bytes 2097152 | tf_op jit(solution)/shard_map/all_to_all | solution.py:224
  44.3 0.0 copy-done.1
  44.3 0.0 copy-start
  44.3 5.2 %collective-permute-start.2 = (bf16[128,256]{1,0:T(8,128)(2,1)S(1)}, bf16[128,256]{1,0:T(8,128)(2,1)S(1)}, u32[]{:S(2)}, u32[]{:S(2)}) collective-permute-start(bf16[128,256]{1,0:T(8,128)(2,1)S(1)} %bitcast.16), channel_id=1, source_target_pairs={{0,8},{8,0},{1,9},{9,1},{2,10},{10,2},{3,11},{11,3},{4,12},{12,4},... | collective-permute-start | bytes 196616 | tf_op jit(solution)/shard_map/ppermute | solution.py:220
  49.5 4.9 %collective-permute-done.2.refs_5_ = bf16[128,256]{1,0:T(8,128)(2,1)S(1)} collective-permute-done((bf16[128,256]{1,0:T(8,128)(2,1)S(1)}, bf16[128,256]{1,0:T(8,128)(2,1)S(1)}, u32[]{:S(2)}, u32[]{:S(2)}) %collective-permute-start.2) | collective-permute-done | bytes 65568 | tf_op jit(solution)/shard_map/ppermute | solution.py:220
  54.4 4.7 %all-to-all-done.1 = bf16[32,128,128]{2,1,0:T(8,128)(2,1)S(1)} async-done(((bf16[32,128,128]{2,1,0:T(8,128)(2,1)}), bf16[32,128,128]{2,1,0:T(8,128)(2,1)S(1)}, u32[]{:S(2)}, u32[]{:S(2)}) %all-to-all-start.1) | async-done | bytes 1048608 | tf_op jit(solution)/shard_map/all_to_all | solution.py:224
  59.1 0.9 reduce_sum.24
  60.0 9.4 %all_to_all.35 = bf16[8,128,128]{2,1,0:T(8,128)(2,1)S(1)} all-to-all(bf16[8,128,128]{2,1,0:T(8,128)(2,1)} %reduce_sum.24), channel_id=1, replica_groups=mesh['x'=4,'zh'=2,'y'=4,'z2'=2,'z4'=4,'core'=2] {'z4'}, dimensions={0} | all-to-all | bytes 524288 | tf_op jit(solution)/shard_map/all_to_all | solution.py:224
  69.5 7.2 %collective-permute-start.3 = (bf16[2,128,128]{2,1,0:T(8,128)(2,1)S(1)}, bf16[2,128,128]{2,1,0:T(8,128)(2,1)S(1)}, u32[]{:S(2)}, u32[]{:S(2)}) collective-permute-start(bf16[2,128,128]{2,1,0:T(8,128)(2,1)S(1)} %reduce_sum.25.refs_1_), channel_id=1, source_target_pairs={{0,8},{8,0},{1,9},{9,1},{2,10},{10,2},{3,11},{11,3},{4,12},{12,4},... | collective-permute-start | bytes 196616 | tf_op jit(solution)/shard_map/ppermute | solution.py:220
  76.7 1.7 %collective-permute-done.3.refs_2_ = bf16[2,128,128]{2,1,0:T(8,128)(2,1)S(1)} collective-permute-done((bf16[2,128,128]{2,1,0:T(8,128)(2,1)S(1)}, bf16[2,128,128]{2,1,0:T(8,128)(2,1)S(1)}, u32[]{:S(2)}, u32[]{:S(2)}) %collective-permute-start.3) | collective-permute-done | bytes 65568 | tf_op jit(solution)/shard_map/ppermute | solution.py:220
  78.4 0.0 copy-done
  78.4 0.9 shard_map.116
  79.3 14.1 %all_to_all.36.got_ref = bf16[4,320,128]{2,1,0:T(8,128)(2,1)S(1)} all-to-all(bf16[4,320,128]{2,1,0:T(8,128)(2,1)S(1)} %get-tuple-element.23), channel_id=1, replica_groups=mesh['x'=4,'zh'=2,'y'=4,'z2'=2,'z4'=4,'core'=2] {'z4'}, dimensions={0} | all-to-all | bytes 655360 | tf_op jit(solution)/shard_map/all_to_all | solution.py:224
  93.3 0.1 shard_map.117
  93.5 18.5 %all_to_all.37.own_ref = bf16[4,1088,128]{2,1,0:T(8,128)(2,1)S(1)} all-to-all(bf16[4,1088,128]{2,1,0:T(8,128)(2,1)S(1)} %shard_map.117), channel_id=1, replica_groups=mesh['x'=4,'zh'=2,'y'=4,'z2'=2,'z4'=4,'core'=2] {'y'}, dimensions={0} | all-to-all | bytes 2228224 | tf_op jit(solution)/shard_map/all_to_all | solution.py:224
  112.0 5.5 %collective-permute-start.4 = (bf16[4,1088,128]{2,1,0:T(8,128)(2,1)S(1)}, bf16[4,1088,128]{2,1,0:T(8,128)(2,1)S(1)}, u32[]{:S(2)}, u32[]{:S(2)}) collective-permute-start(bf16[4,1088,128]{2,1,0:T(8,128)(2,1)S(1)} %all_to_all.37.own_ref), channel_id=1, source_target_pairs={{0,1},{1,0},{2,3},{3,2},{4,5},{5,4},{6,7},{7,6},{8,9},{9,8},{10,11... | collective-permute-start | bytes 3342344 | tf_op jit(solution)/shard_map/ppermute | solution.py:220
  117.5 2.4 %collective-permute-done.4.other_ref = bf16[4,1088,128]{2,1,0:T(8,128)(2,1)S(1)} collective-permute-done((bf16[4,1088,128]{2,1,0:T(8,128)(2,1)S(1)}, bf16[4,1088,128]{2,1,0:T(8,128)(2,1)S(1)}, u32[]{:S(2)}, u32[]{:S(2)}) %collective-permute-start.4) | collective-permute-done | bytes 1114144 | tf_op jit(solution)/shard_map/ppermute | solution.py:220
  119.9 2.0 %shard_map.118 = bf16[4,320,128]{2,1,0:T(8,128)(2,1)S(1)} custom-call(s32[1,1]{1,0:T(1,128)S(6)} %copy.12.count_ref, s32[1]{0:T(128)} %bitcast.1.core_ref, s32[1,64]{1,0:T(1,128)S(1)} %bitcast.21, s32[1,64]{1,0:T(1,128)S(1)} %bitcast.23, bf16[64,128,128]{2,1,0:T(8,128)(2,1)S(1)} %shard_map.112.tiles_ref, bf16[4,1088,128]{2,1,0:T(8,128)(2,1)S(1)} %all_to_all.37.own_ref, ...), custom_call_target="tpu_custom_call" | custom-call | tf_op jit(solution)/shard_map/pallas_call | solution.py:300
  121.9 9.2 %all_to_all.38.got_ref = bf16[4,320,128]{2,1,0:T(8,128)(2,1)S(1)} all-to-all(bf16[4,320,128]{2,1,0:T(8,128)(2,1)S(1)} %shard_map.118), channel_id=1, replica_groups=mesh['x'=4,'zh'=2,'y'=4,'z2'=2,'z4'=4,'core'=2] {'x'}, dimensions={0} | all-to-all | bytes 655360 | tf_op jit(solution)/shard_map/all_to_all | solution.py:224
  131.1 0.7 shard_map.119
  131.8 9.8 %all-to-all-start.6 = ((bf16[16,32,128]{2,1,0:T(8,128)(2,1)}), bf16[16,32,128]{2,1,0:T(8,128)(2,1)S(1)}, u32[]{:S(2)}, u32[]{:S(2)}) async-start(bf16[16,32,128]{2,1,0:T(8,128)(2,1)} %get-tuple-element.26), calls=%async_computation.6 | async-start | bytes 262144 | tf_op jit(solution)/shard_map/all_to_all | solution.py:224
  141.6 12.0 %collective-permute-start.5 = (bf16[128,128]{1,0:T(8,128)(2,1)S(1)}, bf16[128,128]{1,0:T(8,128)(2,1)S(1)}, u32[]{:S(2)}, u32[]{:S(2)}) collective-permute-start(bf16[128,128]{1,0:T(8,128)(2,1)S(1)} %get-tuple-element.24), channel_id=1, source_target_pairs={{0,64},{64,0},{1,65},{65,1},{2,66},{66,2},{3,67},{67,3},{4,68},{68... | collective-permute-start | bytes 98312 | tf_op jit(solution)/shard_map/ppermute | solution.py:220
  153.5 5.2 %collective-permute-done.5.got_ref = bf16[128,128]{1,0:T(8,128)(2,1)S(1)} collective-permute-done((bf16[128,128]{1,0:T(8,128)(2,1)S(1)}, bf16[128,128]{1,0:T(8,128)(2,1)S(1)}, u32[]{:S(2)}, u32[]{:S(2)}) %collective-permute-start.5) | collective-permute-done | bytes 32800 | tf_op jit(solution)/shard_map/ppermute | solution.py:220
  158.8 0.0 all-to-all-done.6.got_weight_ref
  158.8 0.7 shard_map.120
  (1 shorter events, 0.0 us)
Async XLA Ops:
  0.6 17.9 %collective-permute-start = (bf16[128,128]{1,0:T(8,128)(2,1)}, bf16[128,128]{1,0:T(8,128)(2,1)S(1)}, u32[]{:S(2)}, u32[]{:S(2)}) collective-permute-start(bf16[128,128]{1,0:T(8,128)(2,1)} %bitcast.18), channel_id=1, source_target_pairs={{0,64},{64,0},{1,65},{65,1},{2,66},{66,2},{3,67},{67,3},{4,68},{68... | collective-permute-start | bytes 98312 | tf_op jit(solution)/shard_map/ppermute | solution.py:220
  18.5 0.8 copy-start.2
  20.0 9.5 %all-to-all-start = ((bf16[4,2,128,128]{3,2,1,0:T(8,128)(2,1)}), bf16[4,2,128,128]{3,2,1,0:T(8,128)(2,1)S(1)}, u32[]{:S(2)}, u32[]{:S(2)}) async-start(bf16[4,2,128,128]{3,2,1,0:T(8,128)(2,1)} %shard_map.113), calls=%async_computation | async-start | bytes 524288 | tf_op jit(solution)/shard_map/all_to_all | solution.py:224
  24.7 0.8 copy-start.5
  25.5 0.8 copy-start.6
  26.4 0.8 copy-start.7
  27.1 2.4 %copy-start.3 = (s32[1,1,64]{2,1,0:T(1,128)S(1)}, s32[1,1,64]{2,1,0:T(1,128)}, u32[]{:S(2)}) copy-start(s32[1,1,64]{2,1,0:T(1,128)} %param.12) | copy-start | bytes 772
  27.1 2.4 %copy-start.4 = (s32[1,1,64]{2,1,0:T(1,128)S(1)}, s32[1,1,64]{2,1,0:T(1,128)}, u32[]{:S(2)}) copy-start(s32[1,1,64]{2,1,0:T(1,128)} %param.13) | copy-start | bytes 772
  31.4 8.0 %collective-permute-start.1 = (bf16[32,128,128]{2,1,0:T(8,128)(2,1)S(1)}, bf16[32,128,128]{2,1,0:T(8,128)(2,1)S(1)}, u32[]{:S(2)}, u32[]{:S(2)}) collective-permute-start(bf16[32,128,128]{2,1,0:T(8,128)(2,1)S(1)} %get-tuple-element.16), channel_id=1, source_target_pairs={{0,1},{1,0},{2,3},{3,2},{4,5},{5,4},{6,7},{7,6},{8,9},{9,8},{10,11... | collective-permute-start | bytes 3145736 | tf_op jit(solution)/shard_map/ppermute | solution.py:220
  40.6 3.7 %copy-start.1 = (bf16[1,128,256]{2,1,0:T(8,128)(2,1)S(1)}, bf16[1,128,256]{2,1,0:T(8,128)(2,1)}, u32[]{:S(2)}) copy-start(bf16[1,128,256]{2,1,0:T(8,128)(2,1)} %param.11) | copy-start | bytes 196612
  40.6 18.5 %all-to-all-start.1 = ((bf16[32,128,128]{2,1,0:T(8,128)(2,1)}), bf16[32,128,128]{2,1,0:T(8,128)(2,1)S(1)}, u32[]{:S(2)}, u32[]{:S(2)}) async-start(bf16[32,128,128]{2,1,0:T(8,128)(2,1)} %shard_map.115), calls=%async_computation.1 | async-start | bytes 2097152 | tf_op jit(solution)/shard_map/all_to_all | solution.py:224
  44.3 34.1 %copy-start = (bf16[128,256]{1,0:T(8,128)(2,1)S(1)}, bf16[128,256]{1,0:T(8,128)(2,1)}, u32[]{:S(2)}) copy-start(bf16[128,256]{1,0:T(8,128)(2,1)} %refs_3_.1) | copy-start | bytes 196612
  44.3 10.1 %collective-permute-start.2 = (bf16[128,256]{1,0:T(8,128)(2,1)S(1)}, bf16[128,256]{1,0:T(8,128)(2,1)S(1)}, u32[]{:S(2)}, u32[]{:S(2)}) collective-permute-start(bf16[128,256]{1,0:T(8,128)(2,1)S(1)} %bitcast.16), channel_id=1, source_target_pairs={{0,8},{8,0},{1,9},{9,1},{2,10},{10,2},{3,11},{11,3},{4,12},{12,4},... | collective-permute-start | bytes 196616 | tf_op jit(solution)/shard_map/ppermute | solution.py:220
  69.5 8.9 %collective-permute-start.3 = (bf16[2,128,128]{2,1,0:T(8,128)(2,1)S(1)}, bf16[2,128,128]{2,1,0:T(8,128)(2,1)S(1)}, u32[]{:S(2)}, u32[]{:S(2)}) collective-permute-start(bf16[2,128,128]{2,1,0:T(8,128)(2,1)S(1)} %reduce_sum.25.refs_1_), channel_id=1, source_target_pairs={{0,8},{8,0},{1,9},{9,1},{2,10},{10,2},{3,11},{11,3},{4,12},{12,4},... | collective-permute-start | bytes 196616 | tf_op jit(solution)/shard_map/ppermute | solution.py:220
  112.0 7.9 %collective-permute-start.4 = (bf16[4,1088,128]{2,1,0:T(8,128)(2,1)S(1)}, bf16[4,1088,128]{2,1,0:T(8,128)(2,1)S(1)}, u32[]{:S(2)}, u32[]{:S(2)}) collective-permute-start(bf16[4,1088,128]{2,1,0:T(8,128)(2,1)S(1)} %all_to_all.37.own_ref), channel_id=1, source_target_pairs={{0,1},{1,0},{2,3},{3,2},{4,5},{5,4},{6,7},{7,6},{8,9},{9,8},{10,11... | collective-permute-start | bytes 3342344 | tf_op jit(solution)/shard_map/ppermute | solution.py:220
  131.8 27.0 %all-to-all-start.6 = ((bf16[16,32,128]{2,1,0:T(8,128)(2,1)}), bf16[16,32,128]{2,1,0:T(8,128)(2,1)S(1)}, u32[]{:S(2)}, u32[]{:S(2)}) async-start(bf16[16,32,128]{2,1,0:T(8,128)(2,1)} %get-tuple-element.26), calls=%async_computation.6 | async-start | bytes 262144 | tf_op jit(solution)/shard_map/all_to_all | solution.py:224
  141.6 17.2 %collective-permute-start.5 = (bf16[128,128]{1,0:T(8,128)(2,1)S(1)}, bf16[128,128]{1,0:T(8,128)(2,1)S(1)}, u32[]{:S(2)}, u32[]{:S(2)}) collective-permute-start(bf16[128,128]{1,0:T(8,128)(2,1)S(1)} %get-tuple-element.24), channel_id=1, source_target_pairs={{0,64},{64,0},{1,65},{65,1},{2,66},{66,2},{3,67},{67,3},{4,68},{68... | collective-permute-start | bytes 98312 | tf_op jit(solution)/shard_map/ppermute | solution.py:220

commit v7 on v5

--- a/solution.py
+++ b/solution.py
@@ -9,7 +9,7 @@
 from jax.sharding import PartitionSpec as P
 
 TILE = 128
-GROUP = 4
+GROUP = 16
 FINE = (("x", 4), ("zh", 2), ("y", 4), ("z2", 2), ("z4", 4), ("core", 2))
 N_X, N_ZH, N_Y, N_Z2, N_Z4, N_CORE = (size for _, size in FINE)
 N_ZL = N_Z2 * N_Z4
@@ -128,7 +128,8 @@
     local_weight = (
         lax.dot_general(aggregated, grad_pre, (((0,), (0,)), ((), ())), preferred_element_type=F32)
         * scale
-    ).astype(BF16)
+    )
+    high, low = halves(local_weight)
     deep = TILE // N_Z4
     for z2 in range(N_Z2):
         grad_agg = lax.dot_general(
@@ -141,12 +142,16 @@
             send_ref[peer, z2 * TILE : (z2 + 1) * TILE, :] = grad_agg
     for peer in range(N_Z4):
         here = slice(peer * deep, (peer + 1) * deep)
-        send_ref[peer, N_Z2 * TILE : N_Z2 * TILE + deep, :] = local_weight[here, :TILE]
-        send_ref[peer, N_Z2 * TILE + deep :, :] = local_weight[here, TILE:]
+        for k, part in enumerate(
+            (high[here, :TILE], high[here, TILE:], low[here, :TILE], low[here, TILE:])
+        ):
+            start = N_Z2 * TILE + k * deep
+            send_ref[peer, start : start + deep, :] = part
 
 
 def spread_body(got_ref, send_ref):
-    high, low = halves(jnp.sum(got_ref[:, N_Z2 * TILE :, :].astype(F32), axis=0))
+    terms = jnp.sum(got_ref[:, N_Z2 * TILE :, :].astype(F32), axis=0)
+    high, low = halves(terms[:W_ROWS] + terms[W_ROWS:])
     for peer in range(N_Y):
         for z4 in range(N_Z4):
             here = slice(z4 * N_Z2 * TILE, (z4 + 1) * N_Z2 * TILE)
@@ -156,8 +161,9 @@
 
 
 def backward_body(
-    count_ref, core_ref, row_ref, col_ref, tiles_ref, own_ref, other_ref, send_ref, grads_ref, acc_ref, sems
+    count_ref, core_ref, x_ref, row_ref, col_ref, tiles_ref, own_ref, other_ref, *refs
 ):
+    send_refs, (send_weight_ref, keep_ref, grads_ref, acc_ref, sems) = refs[: N_X - 1], refs[N_X - 1 :]
     core = core_ref[0]
     copies = [
         pltpu.make_async_copy(own_ref, grads_ref.at[core], sems.at[0]),
@@ -185,31 +191,41 @@
     lax.fori_loop(0, group_total(count_ref), step, 0)
     terms = jnp.sum(grads_ref[:, :, N_ZL * TILE :, :].astype(F32), axis=(0, 1))
     weight_sum = (terms[:W_ROWS] + terms[W_ROWS:]).astype(BF16)
-    for x in range(N_X):
-        for zh in range(N_ZH):
-            send_ref[x, zh * TILE : (zh + 1) * TILE, :] = acc_ref[x * N_ZH + zh].astype(BF16)
-        send_ref[x, N_ZH * TILE :, :] = weight_sum
-
-
-def halfway_body(zh_ref, got_ref, send_ref, keep_ref, send_weight_ref):
-    zh = zh_ref[0]
-    total = jnp.sum(got_ref[...].astype(F32), axis=0)
-    first, second = total[:TILE], total[TILE : N_ZH * TILE]
-    mine = zh == 0
+    for peer in range(N_X * N_Z4):
+        send_weight_ref[peer] = weight_sum
+    for shift in range(N_X):
+        peer = (x_ref[0] + shift) % N_X
+        part = acc_ref[pl.ds(peer * N_ZH, N_ZH)].reshape(N_ZH * TILE, TILE)
+        if shift == 0:
+            keep_ref[...] = part.astype(BF16)
+        else:
+            send_refs[shift - 1][...] = part.astype(BF16)
+
+
+def halfway_body(zh_ref, own_ref, *refs):
+    got_refs, (got_weight_ref, send_ref, keep_ref) = refs[: N_X - 1], refs[N_X - 1 :]
+    total = own_ref[...].astype(F32)
+    for got_ref in got_refs:
+        total += got_ref[...].astype(F32)
+    first, second = total[:TILE], total[TILE:]
+    mine = zh_ref[0] == 0
     keep_ref[...] = jnp.where(mine, first, second)
-    send_ref[...] = jnp.where(mine, second, first).astype(BF16)
-    weight_sum = total[N_ZH * TILE :].astype(BF16)
-    for peer in range(N_ZH * N_Z4):
-        send_weight_ref[peer] = weight_sum
-
-
-def finish_body(got_ref, keep_ref, got_weight_ref, grad_ref, grad_weight_ref):
-    grad_ref[...] = (keep_ref[...] + got_ref[...].astype(F32)).T.astype(BF16)
+    send_ref[0:TILE, :] = jnp.where(mine, second, first).astype(BF16)
+    for z4 in range(N_Z4):
+        terms = got_weight_ref[z4].astype(F32)
+        for x in range(1, N_X):
+            terms += got_weight_ref[x * N_Z4 + z4].astype(F32)
+        send_ref[TILE + z4 * W_ROWS : TILE + (z4 + 1) * W_ROWS, :] = terms.astype(BF16)
+
+
+def finish_body(got_ref, keep_ref, sent_ref, grad_ref, grad_weight_ref):
+    grad_ref[...] = (keep_ref[...] + got_ref[0:TILE, :].astype(F32)).T.astype(BF16)
     deep = TILE // N_Z4
-    for k in range(N_Z4):
-        total = got_weight_ref[k].astype(F32) + got_weight_ref[N_Z4 + k].astype(F32)
-        grad_weight_ref[k * deep : (k + 1) * deep, :TILE] = total[:deep]
-        grad_weight_ref[k * deep : (k + 1) * deep, TILE:] = total[deep:]
+    total = got_ref[TILE:, :].astype(F32) + sent_ref[TILE:, :].astype(F32)
+    for z4 in range(N_Z4):
+        part = total[z4 * W_ROWS : (z4 + 1) * W_ROWS]
+        grad_weight_ref[z4 * deep : (z4 + 1) * deep, :TILE] = part[:deep]
+        grad_weight_ref[z4 * deep : (z4 + 1) * deep, TILE:] = part[deep:]
 
 
 def swap(value, axis):
@@ -275,7 +291,7 @@
 
     out_act, send = call(
         dense,
-        (shape((TILE, hidden), BF16), shape((N_Z4, N_Z2 * TILE + W_ROWS, TILE), BF16)),
+        (shape((TILE, hidden), BF16), shape((N_Z4, N_Z2 * TILE + 2 * W_ROWS, TILE), BF16)),
         [smem] + [vmem] * 5,
     )(
         lax.axis_index("z2").astype(jnp.int32)[None],
@@ -290,10 +306,12 @@
     send = call(spread_body, shape((N_Y, N_ZL * TILE + 2 * W_ROWS, TILE), BF16), [vmem])(got)
     mine = exchange(send, "y")
     theirs = swap(mine, "core")
-    send = call(
+    part = (N_ZH * TILE, TILE)
+    *sends, send_weight, keep = call(
         backward_body,
-        shape((N_X, N_ZH * TILE + W_ROWS, TILE), BF16),
-        [smem, smem, smem, smem, vmem, hbm, hbm],
+        (shape(part, BF16),) * (N_X - 1)
+        + (shape((N_X * N_Z4, W_ROWS, TILE), BF16), shape(part, BF16)),
+        [smem] * 5 + [vmem, hbm, hbm],
         [
             pltpu.VMEM((N_CORE,) + mine.shape, BF16),
             pltpu.VMEM((N_X * N_ZH, width, TILE), F32),
@@ -302,6 +320,7 @@
     )(
         tile_count,
         core,
+        lax.axis_index("x").astype(jnp.int32)[None],
         row_tiles,
         col_tiles,
         tiles,
@@ -309,23 +328,21 @@
         theirs,
     )
 
-    got = exchange(send, "x")
-    send, keep, send_weight = call(
+    gots = [
+        lax.ppermute(send, "x", [(k, (k + shift + 1) % N_X) for k in range(N_X)])
+        for shift, send in enumerate(sends)
+    ]
+    got_weight = exchange(send_weight, ("x", "z4"))
+    send, keep = call(
         halfway_body,
-        (
-            shape((TILE, TILE), BF16),
-            shape((TILE, TILE), F32),
-            shape((N_ZH * N_Z4, W_ROWS, TILE), BF16),
-        ),
-        [smem, vmem],
-    )(zh_here, got)
-    got = swap(send, "zh")
-    got_weight = exchange(send_weight, ("zh", "z4"))
+        (shape((TILE + N_Z4 * W_ROWS, TILE), BF16), shape((TILE, TILE), F32)),
+        [smem] + [vmem] * (N_X + 1),
+    )(zh_here, keep, *gots, got_weight)
     grad_features, grad_weight = call(
         finish_body,
         (shape((TILE, width), BF16), shape((width, hidden), F32)),
         [vmem] * 3,
-    )(got, keep, got_weight)
+    )(swap(send, "zh"), keep, send)
     return (out_act[None], grad_features[None], grad_weight)
 
 

time: 164 us -> 165 us (level)
  the two profiles are of different devices: /device:TPU:1 before, /device:TPU:160 now
where the time goes in v7:
time: 165 us; the launch traced here: 164 us
  starting transfers between devices  56.1 us (34%)
  blocking collectives  46.2 us (28%)
  waiting for transfers between devices  45.3 us (27%)
  Pallas kernels  10.4 us (6%)
  local copies, waits for them, and re-layouts  3.2 us (2%)
    all_to_all x3, blocking collectives, exchange(): return lax.all_to_all(value, axis, 0, 0, tiled=True)  46.2 us
    ppermute x6, waiting for transfers between devices, swap(): return lax.ppermute(value, axis, [(0, 1), (1, 0)])  35.5 us
    ppermute x6, starting transfers between devices, swap(): return lax.ppermute(value, axis, [(0, 1), (1, 0)])  29.3 us
    all_to_all x3, starting transfers between devices, exchange(): return lax.all_to_all(value, axis, 0, 0, tiled=True)  15.4 us
    ppermute x3, starting transfers between devices, local(): lax.ppermute(send, 'x', [(k, (k + shift + 1) % N_X) for k in range(N_X)])  11.3 us
    all_to_all x3, waiting for transfers between devices, exchange(): return lax.all_to_all(value, axis, 0, 0, tiled=True)  7.06 us
    pallas_call x1, Pallas kernels, local(): call(backward_body, (shape(part, BF16),) * (N_X - 1) + (shape((N_X * N_Z4...  3.92 us
  transfers between devices with their start and end apart: 12, of which 9 were waited for; matrix products, arithmetic and copies ran while one was open for 0% of the time, Pallas kernels for 1%

profile of v7, /device:TPU:160, one launch (start us, length us, event | category | flops | bytes accessed | tf_op | source)
XLA Modules:
  0.0 164.0 jit_solution(3583119620103271171)
XLA Ops:
  0.6 10.0 %collective-permute-start = (bf16[128,128]{1,0:T(8,128)(2,1)}, bf16[128,128]{1,0:T(8,128)(2,1)S(1)}, u32[]{:S(2)}, u32[]{:S(2)}) collective-permute-start(bf16[128,128]{1,0:T(8,128)(2,1)} %bitcast.19), channel_id=1, source_target_pairs={{0,64},{64,0},{1,65},{65,1},{2,66},{66,2},{3,67},{67,3},{4,68},{68... | collective-permute-start | bytes 98312 | tf_op jit(solution)/shard_map/ppermute | solution.py:232
  10.7 4.7 %collective-permute-done.other_ref = bf16[128,128]{1,0:T(8,128)(2,1)S(1)} collective-permute-done((bf16[128,128]{1,0:T(8,128)(2,1)}, bf16[128,128]{1,0:T(8,128)(2,1)S(1)}, u32[]{:S(2)}, u32[]{:S(2)}) %collective-permute-start) | collective-permute-done | bytes 32800 | tf_op jit(solution)/shard_map/ppermute | solution.py:232
  15.4 0.0 copy-start.2
  15.4 0.8 copy-done.2
  16.1 0.7 shard_map.113
  16.9 4.3 %all-to-all-start = ((bf16[4,2,128,128]{3,2,1,0:T(8,128)(2,1)}), bf16[4,2,128,128]{3,2,1,0:T(8,128)(2,1)S(1)}, u32[]{:S(2)}, u32[]{:S(2)}) async-start(bf16[4,2,128,128]{3,2,1,0:T(8,128)(2,1)} %shard_map.113), calls=%async_computation | async-start | bytes 524288 | tf_op jit(solution)/shard_map/all_to_all | solution.py:236
  21.8 0.0 copy-start.5
  21.8 0.8 copy-done.5
  22.6 0.0 copy-start.6
  22.6 0.8 copy-done.6
  23.5 0.8 copy-done.7
  24.2 0.9 shard_map.112.tiles_ref
  25.2 2.7 %all-to-all-done = bf16[4,2,128,128]{3,2,1,0:T(8,128)(2,1)S(1)} async-done(((bf16[4,2,128,128]{3,2,1,0:T(8,128)(2,1)}), bf16[4,2,128,128]{3,2,1,0:T(8,128)(2,1)S(1)}, u32[]{:S(2)}, u32[]{:S(2)}) %all-to-all-start) | async-done | bytes 262176 | tf_op jit(solution)/shard_map/all_to_all | solution.py:236
  27.8 0.0 copy-done.3
  27.8 0.0 copy-done.4
  27.8 1.8 %shard_map.114 = (bf16[32,128,128]{2,1,0:T(8,128)(2,1)S(1)}, f32[32,128,128]{2,1,0:T(8,128)S(1)}) custom-call(s32[1,1]{1,0:T(1,128)S(6)} %copy.12.count_ref, s32[1]{0:T(128)} %bitcast.1.core_ref, s32[1,64]{1,0:T(1,128)S(1)} %bitcast.21, s32[1,64]{1,0:T(1,128)S(1)} %bitcast.23, bf16[64,128,128]{2,1,0:T(8,128)(2,1)S(1)} %shard_map.112.tiles_ref, ...), custom_call_target="tpu_custom_call" | custom-call | flops 268435456 | bytes 4194304 | tf_op jit(solution)/shard_map/pallas_call | solution.py:269
  29.7 1.9 %collective-permute-start.1 = (bf16[32,128,128]{2,1,0:T(8,128)(2,1)S(1)}, bf16[32,128,128]{2,1,0:T(8,128)(2,1)S(1)}, u32[]{:S(2)}, u32[]{:S(2)}) collective-permute-start(bf16[32,128,128]{2,1,0:T(8,128)(2,1)S(1)} %get-tuple-element.20), channel_id=1, source_target_pairs={{0,1},{1,0},{2,3},{3,2},{4,5},{5,4},{6,7},{7,6},{8,9},{9,8},{10,11... | collective-permute-start | bytes 3145736 | tf_op jit(solution)/shard_map/ppermute | solution.py:232
  31.6 2.6 %collective-permute-done.1.got_ref = bf16[32,128,128]{2,1,0:T(8,128)(2,1)S(1)} collective-permute-done((bf16[32,128,128]{2,1,0:T(8,128)(2,1)S(1)}, bf16[32,128,128]{2,1,0:T(8,128)(2,1)S(1)}, u32[]{:S(2)}, u32[]{:S(2)}) %collective-permute-start.1) | collective-permute-done | bytes 1048608 | tf_op jit(solution)/shard_map/ppermute | solution.py:232
  34.2 1.1 shard_map.115
  35.4 4.6 %all-to-all-start.1 = ((bf16[32,128,128]{2,1,0:T(8,128)(2,1)}), bf16[32,128,128]{2,1,0:T(8,128)(2,1)}, u32[]{:S(2)}, u32[]{:S(2)}) async-start(bf16[32,128,128]{2,1,0:T(8,128)(2,1)} %shard_map.115), calls=%async_computation.1 | async-start | bytes 2097152 | tf_op jit(solution)/shard_map/all_to_all | solution.py:236
  40.0 0.0 copy-done.1
  40.0 3.2 %collective-permute-start.2 = (bf16[128,256]{1,0:T(8,128)(2,1)S(1)}, bf16[128,256]{1,0:T(8,128)(2,1)S(1)}, u32[]{:S(2)}, u32[]{:S(2)}) collective-permute-start(bf16[128,256]{1,0:T(8,128)(2,1)S(1)} %bitcast.17), channel_id=1, source_target_pairs={{0,8},{8,0},{1,9},{9,1},{2,10},{10,2},{3,11},{11,3},{4,12},{12,4},... | collective-permute-start | bytes 196616 | tf_op jit(solution)/shard_map/ppermute | solution.py:232
  43.2 7.9 %collective-permute-done.2.refs_5_ = bf16[128,256]{1,0:T(8,128)(2,1)S(1)} collective-permute-done((bf16[128,256]{1,0:T(8,128)(2,1)S(1)}, bf16[128,256]{1,0:T(8,128)(2,1)S(1)}, u32[]{:S(2)}, u32[]{:S(2)}) %collective-permute-start.2) | collective-permute-done | bytes 65568 | tf_op jit(solution)/shard_map/ppermute | solution.py:232
  51.1 4.4 %all-to-all-done.1 = bf16[32,128,128]{2,1,0:T(8,128)(2,1)} async-done(((bf16[32,128,128]{2,1,0:T(8,128)(2,1)}), bf16[32,128,128]{2,1,0:T(8,128)(2,1)}, u32[]{:S(2)}, u32[]{:S(2)}) %all-to-all-start.1) | async-done | bytes 1048608 | tf_op jit(solution)/shard_map/all_to_all | solution.py:236
  55.5 1.4 reduce_sum.24
  56.9 11.8 %all_to_all.30 = bf16[8,128,128]{2,1,0:T(8,128)(2,1)S(1)} all-to-all(bf16[8,128,128]{2,1,0:T(8,128)(2,1)S(1)} %reduce_sum.24), channel_id=1, replica_groups=mesh['x'=4,'zh'=2,'y'=4,'z2'=2,'z4'=4,'core'=2] {'z4'}, dimensions={0} | all-to-all | bytes 524288 | tf_op jit(solution)/shard_map/all_to_all | solution.py:236
  68.8 2.6 %collective-permute-start.3 = (bf16[2,128,128]{2,1,0:T(8,128)(2,1)S(1)}, bf16[2,128,128]{2,1,0:T(8,128)(2,1)S(1)}, u32[]{:S(2)}, u32[]{:S(2)}) collective-permute-start(bf16[2,128,128]{2,1,0:T(8,128)(2,1)S(1)} %reduce_sum.25.refs_1_), channel_id=1, source_target_pairs={{0,8},{8,0},{1,9},{9,1},{2,10},{10,2},{3,11},{11,3},{4,12},{12,4},... | collective-permute-start | bytes 196616 | tf_op jit(solution)/shard_map/ppermute | solution.py:232
  71.4 7.5 %collective-permute-done.3.refs_2_ = bf16[2,128,128]{2,1,0:T(8,128)(2,1)S(1)} collective-permute-done((bf16[2,128,128]{2,1,0:T(8,128)(2,1)S(1)}, bf16[2,128,128]{2,1,0:T(8,128)(2,1)S(1)}, u32[]{:S(2)}, u32[]{:S(2)}) %collective-permute-start.3) | collective-permute-done | bytes 65568 | tf_op jit(solution)/shard_map/ppermute | solution.py:232
  78.8 0.0 copy-done
  78.8 0.9 shard_map.116
  79.7 15.4 %all_to_all.31.got_ref = bf16[4,384,128]{2,1,0:T(8,128)(2,1)S(1)} all-to-all(bf16[4,384,128]{2,1,0:T(8,128)(2,1)S(1)} %get-tuple-element.27), channel_id=1, replica_groups=mesh['x'=4,'zh'=2,'y'=4,'z2'=2,'z4'=4,'core'=2] {'z4'}, dimensions={0} | all-to-all | bytes 786432 | tf_op jit(solution)/shard_map/all_to_all | solution.py:236
  95.1 0.1 shard_map.117
  95.3 18.9 %all_to_all.32.own_ref = bf16[4,1152,128]{2,1,0:T(8,128)(2,1)S(1)} all-to-all(bf16[4,1152,128]{2,1,0:T(8,128)(2,1)S(1)} %shard_map.117), channel_id=1, replica_groups=mesh['x'=4,'zh'=2,'y'=4,'z2'=2,'z4'=4,'core'=2] {'y'}, dimensions={0} | all-to-all | bytes 2359296 | tf_op jit(solution)/shard_map/all_to_all | solution.py:236
  114.2 1.9 %collective-permute-start.4 = (bf16[4,1152,128]{2,1,0:T(8,128)(2,1)S(1)}, bf16[4,1152,128]{2,1,0:T(8,128)(2,1)}, u32[]{:S(2)}, u32[]{:S(2)}) collective-permute-start(bf16[4,1152,128]{2,1,0:T(8,128)(2,1)S(1)} %all_to_all.32.own_ref), channel_id=1, source_target_pairs={{0,1},{1,0},{2,3},{3,2},{4,5},{5,4},{6,7},{7,6},{8,9},{9,8},{10,11... | collective-permute-start | bytes 3538952 | tf_op jit(solution)/shard_map/ppermute | solution.py:232
  116.1 2.9 %collective-permute-done.4.other_ref = bf16[4,1152,128]{2,1,0:T(8,128)(2,1)} collective-permute-done((bf16[4,1152,128]{2,1,0:T(8,128)(2,1)S(1)}, bf16[4,1152,128]{2,1,0:T(8,128)(2,1)}, u32[]{:S(2)}, u32[]{:S(2)}) %collective-permute-start.4) | collective-permute-done | bytes 1179680 | tf_op jit(solution)/shard_map/ppermute | solution.py:232
  119.0 3.9 %shard_map.118 = (bf16[256,128]{1,0:T(8,128)(2,1)S(1)}, bf16[256,128]{1,0:T(8,128)(2,1)S(1)}, bf16[256,128]{1,0:T(8,128)(2,1)S(1)}, bf16[16,64,128]{2,1,0:T(8,128)(2,1)}, bf16[256,128]{1,0:T(8,128)(2,1)S(1)}) custom-call(s32[1,1]{1,0:T(1,128)S(6)} %copy.12.count_ref, s32[1]{0:T(128)} %bitcast.1.core_ref, s32[1]{0:T(128)} %bitcast.14.x_ref, ...), custom_call_target="tpu_custom_call" | custom-call | tf_op jit(solution)/shard_map/pallas_call | solution.py:310
  123.0 6.5 %all-to-all-start.5 = ((bf16[16,64,128]{2,1,0:T(8,128)(2,1)}), bf16[16,64,128]{2,1,0:T(8,128)(2,1)S(1)}, u32[]{:S(2)}, u32[]{:S(2)}) async-start(bf16[16,64,128]{2,1,0:T(8,128)(2,1)} %get-tuple-element.32), calls=%async_computation.5 | async-start | bytes 524288 | tf_op jit(solution)/shard_map/all_to_all | solution.py:236
  129.5 3.4 %collective-permute-start.5 = (bf16[256,128]{1,0:T(8,128)(2,1)S(1)}, bf16[256,128]{1,0:T(8,128)(2,1)S(1)}, u32[]{:S(2)}, u32[]{:S(2)}) collective-permute-start(bf16[256,128]{1,0:T(8,128)(2,1)S(1)} %get-tuple-element.29), channel_id=1, source_target_pairs={{0,128},{128,256},{256,384},{384,0},{1,129},{129,257},{257,385},{3... | collective-permute-start | bytes 196616 | tf_op jit(solution)/shard_map/ppermute | solution.py:332
  132.9 4.6 %collective-permute-start.6 = (bf16[256,128]{1,0:T(8,128)(2,1)S(1)}, bf16[256,128]{1,0:T(8,128)(2,1)S(1)}, u32[]{:S(2)}, u32[]{:S(2)}) collective-permute-start(bf16[256,128]{1,0:T(8,128)(2,1)S(1)} %get-tuple-element.30), channel_id=1, source_target_pairs={{0,256},{128,384},{256,0},{384,128},{1,257},{129,385},{257,1},{385... | collective-permute-start | bytes 196616 | tf_op jit(solution)/shard_map/ppermute | solution.py:332
  137.5 3.4 %collective-permute-start.7 = (bf16[256,128]{1,0:T(8,128)(2,1)S(1)}, bf16[256,128]{1,0:T(8,128)(2,1)S(1)}, u32[]{:S(2)}, u32[]{:S(2)}) collective-permute-start(bf16[256,128]{1,0:T(8,128)(2,1)S(1)} %get-tuple-element.31), channel_id=1, source_target_pairs={{0,384},{128,0},{256,128},{384,256},{1,385},{129,1},{257,129},{385... | collective-permute-start | bytes 196616 | tf_op jit(solution)/shard_map/ppermute | solution.py:332
  140.9 0.0 collective-permute-done.5.refs_0_
  140.9 0.0 collective-permute-done.6.refs_1_
  140.9 2.8 %collective-permute-done.7.refs_2_ = bf16[256,128]{1,0:T(8,128)(2,1)S(1)} collective-permute-done((bf16[256,128]{1,0:T(8,128)(2,1)S(1)}, bf16[256,128]{1,0:T(8,128)(2,1)S(1)}, u32[]{:S(2)}, u32[]{:S(2)}) %collective-permute-start.7) | collective-permute-done | bytes 65568 | tf_op jit(solution)/shard_map/ppermute | solution.py:332
  143.6 0.0 all-to-all-done.5.refs_3_
  143.6 0.1 shard_map.119
  143.7 9.7 %collective-permute-start.8 = (bf16[384,128]{1,0:T(8,128)(2,1)S(1)}, bf16[384,128]{1,0:T(8,128)(2,1)S(1)}, u32[]{:S(2)}, u32[]{:S(2)}) collective-permute-start(bf16[384,128]{1,0:T(8,128)(2,1)S(1)} %get-tuple-element.33.sent_ref), channel_id=1, source_target_pairs={{0,64},{64,0},{1,65},{65,1},{2,66},{66,2},{3,67},{67,3},{4,68},{68... | collective-permute-start | bytes 294920 | tf_op jit(solution)/shard_map/ppermute | solution.py:232
  153.4 9.9 %collective-permute-done.8.got_ref = bf16[384,128]{1,0:T(8,128)(2,1)S(1)} collective-permute-done((bf16[384,128]{1,0:T(8,128)(2,1)S(1)}, bf16[384,128]{1,0:T(8,128)(2,1)S(1)}, u32[]{:S(2)}, u32[]{:S(2)}) %collective-permute-start.8) | collective-permute-done | bytes 98336 | tf_op jit(solution)/shard_map/ppermute | solution.py:232
  163.3 0.7 shard_map.120
  (6 shorter events, 0.0 us)
Async XLA Ops:
  0.6 14.7 %collective-permute-start = (bf16[128,128]{1,0:T(8,128)(2,1)}, bf16[128,128]{1,0:T(8,128)(2,1)S(1)}, u32[]{:S(2)}, u32[]{:S(2)}) collective-permute-start(bf16[128,128]{1,0:T(8,128)(2,1)} %bitcast.19), channel_id=1, source_target_pairs={{0,64},{64,0},{1,65},{65,1},{2,66},{66,2},{3,67},{67,3},{4,68},{68... | collective-permute-start | bytes 98312 | tf_op jit(solution)/shard_map/ppermute | solution.py:232
  15.4 0.8 copy-start.2
  16.9 11.0 %all-to-all-start = ((bf16[4,2,128,128]{3,2,1,0:T(8,128)(2,1)}), bf16[4,2,128,128]{3,2,1,0:T(8,128)(2,1)S(1)}, u32[]{:S(2)}, u32[]{:S(2)}) async-start(bf16[4,2,128,128]{3,2,1,0:T(8,128)(2,1)} %shard_map.113), calls=%async_computation | async-start | bytes 524288 | tf_op jit(solution)/shard_map/all_to_all | solution.py:236
  21.8 0.8 copy-start.5
  22.6 0.8 copy-start.6
  23.5 0.8 copy-start.7
  24.2 3.6 %copy-start.3 = (s32[1,1,64]{2,1,0:T(1,128)S(1)}, s32[1,1,64]{2,1,0:T(1,128)}, u32[]{:S(2)}) copy-start(s32[1,1,64]{2,1,0:T(1,128)} %param.12) | copy-start | bytes 772
  24.2 3.6 %copy-start.4 = (s32[1,1,64]{2,1,0:T(1,128)S(1)}, s32[1,1,64]{2,1,0:T(1,128)}, u32[]{:S(2)}) copy-start(s32[1,1,64]{2,1,0:T(1,128)} %param.13) | copy-start | bytes 772
  29.7 4.6 %collective-permute-start.1 = (bf16[32,128,128]{2,1,0:T(8,128)(2,1)S(1)}, bf16[32,128,128]{2,1,0:T(8,128)(2,1)S(1)}, u32[]{:S(2)}, u32[]{:S(2)}) collective-permute-start(bf16[32,128,128]{2,1,0:T(8,128)(2,1)S(1)} %get-tuple-element.20), channel_id=1, source_target_pairs={{0,1},{1,0},{2,3},{3,2},{4,5},{5,4},{6,7},{7,6},{8,9},{9,8},{10,11... | collective-permute-start | bytes 3145736 | tf_op jit(solution)/shard_map/ppermute | solution.py:232
  35.4 4.6 %copy-start.1 = (bf16[1,128,256]{2,1,0:T(8,128)(2,1)S(1)}, bf16[1,128,256]{2,1,0:T(8,128)(2,1)}, u32[]{:S(2)}) copy-start(bf16[1,128,256]{2,1,0:T(8,128)(2,1)} %param.11) | copy-start | bytes 196612
  35.4 20.1 %all-to-all-start.1 = ((bf16[32,128,128]{2,1,0:T(8,128)(2,1)}), bf16[32,128,128]{2,1,0:T(8,128)(2,1)}, u32[]{:S(2)}, u32[]{:S(2)}) async-start(bf16[32,128,128]{2,1,0:T(8,128)(2,1)} %shard_map.115), calls=%async_computation.1 | async-start | bytes 2097152 | tf_op jit(solution)/shard_map/all_to_all | solution.py:236
  40.0 38.9 %copy-start = (bf16[128,256]{1,0:T(8,128)(2,1)S(1)}, bf16[128,256]{1,0:T(8,128)(2,1)}, u32[]{:S(2)}) copy-start(bf16[128,256]{1,0:T(8,128)(2,1)} %refs_3_.1) | copy-start | bytes 196612
  40.0 11.1 %collective-permute-start.2 = (bf16[128,256]{1,0:T(8,128)(2,1)S(1)}, bf16[128,256]{1,0:T(8,128)(2,1)S(1)}, u32[]{:S(2)}, u32[]{:S(2)}) collective-permute-start(bf16[128,256]{1,0:T(8,128)(2,1)S(1)} %bitcast.17), channel_id=1, source_target_pairs={{0,8},{8,0},{1,9},{9,1},{2,10},{10,2},{3,11},{11,3},{4,12},{12,4},... | collective-permute-start | bytes 196616 | tf_op jit(solution)/shard_map/ppermute | solution.py:232
  68.8 10.1 %collective-permute-start.3 = (bf16[2,128,128]{2,1,0:T(8,128)(2,1)S(1)}, bf16[2,128,128]{2,1,0:T(8,128)(2,1)S(1)}, u32[]{:S(2)}, u32[]{:S(2)}) collective-permute-start(bf16[2,128,128]{2,1,0:T(8,128)(2,1)S(1)} %reduce_sum.25.refs_1_), channel_id=1, source_target_pairs={{0,8},{8,0},{1,9},{9,1},{2,10},{10,2},{3,11},{11,3},{4,12},{12,4},... | collective-permute-start | bytes 196616 | tf_op jit(solution)/shard_map/ppermute | solution.py:232
  114.2 4.9 %collective-permute-start.4 = (bf16[4,1152,128]{2,1,0:T(8,128)(2,1)S(1)}, bf16[4,1152,128]{2,1,0:T(8,128)(2,1)}, u32[]{:S(2)}, u32[]{:S(2)}) collective-permute-start(bf16[4,1152,128]{2,1,0:T(8,128)(2,1)S(1)} %all_to_all.32.own_ref), channel_id=1, source_target_pairs={{0,1},{1,0},{2,3},{3,2},{4,5},{5,4},{6,7},{7,6},{8,9},{9,8},{10,11... | collective-permute-start | bytes 3538952 | tf_op jit(solution)/shard_map/ppermute | solution.py:232
  123.0 20.7 %all-to-all-start.5 = ((bf16[16,64,128]{2,1,0:T(8,128)(2,1)}), bf16[16,64,128]{2,1,0:T(8,128)(2,1)S(1)}, u32[]{:S(2)}, u32[]{:S(2)}) async-start(bf16[16,64,128]{2,1,0:T(8,128)(2,1)} %get-tuple-element.32), calls=%async_computation.5 | async-start | bytes 524288 | tf_op jit(solution)/shard_map/all_to_all | solution.py:236
  129.5 11.3 %collective-permute-start.5 = (bf16[256,128]{1,0:T(8,128)(2,1)S(1)}, bf16[256,128]{1,0:T(8,128)(2,1)S(1)}, u32[]{:S(2)}, u32[]{:S(2)}) collective-permute-start(bf16[256,128]{1,0:T(8,128)(2,1)S(1)} %get-tuple-element.29), channel_id=1, source_target_pairs={{0,128},{128,256},{256,384},{384,0},{1,129},{129,257},{257,385},{3... | collective-permute-start | bytes 196616 | tf_op jit(solution)/shard_map/ppermute | solution.py:332
  132.9 8.0 %collective-permute-start.6 = (bf16[256,128]{1,0:T(8,128)(2,1)S(1)}, bf16[256,128]{1,0:T(8,128)(2,1)S(1)}, u32[]{:S(2)}, u32[]{:S(2)}) collective-permute-start(bf16[256,128]{1,0:T(8,128)(2,1)S(1)} %get-tuple-element.30), channel_id=1, source_target_pairs={{0,256},{128,384},{256,0},{384,128},{1,257},{129,385},{257,1},{385... | collective-permute-start | bytes 196616 | tf_op jit(solution)/shard_map/ppermute | solution.py:332
  137.5 6.2 %collective-permute-start.7 = (bf16[256,128]{1,0:T(8,128)(2,1)S(1)}, bf16[256,128]{1,0:T(8,128)(2,1)S(1)}, u32[]{:S(2)}, u32[]{:S(2)}) collective-permute-start(bf16[256,128]{1,0:T(8,128)(2,1)S(1)} %get-tuple-element.31), channel_id=1, source_target_pairs={{0,384},{128,0},{256,128},{384,256},{1,385},{129,1},{257,129},{385... | collective-permute-start | bytes 196616 | tf_op jit(solution)/shard_map/ppermute | solution.py:332
  143.7 19.6 %collective-permute-start.8 = (bf16[384,128]{1,0:T(8,128)(2,1)S(1)}, bf16[384,128]{1,0:T(8,128)(2,1)S(1)}, u32[]{:S(2)}, u32[]{:S(2)}) collective-permute-start(bf16[384,128]{1,0:T(8,128)(2,1)S(1)} %get-tuple-element.33.sent_ref), channel_id=1, source_target_pairs={{0,64},{64,0},{1,65},{65,1},{2,66},{66,2},{3,67},{67,3},{4,68},{68... | collective-permute-start | bytes 294920 | tf_op jit(solution)/shard_map/ppermute | solution.py:232

commit v8 on v3

--- a/solution.py
+++ b/solution.py
@@ -10,20 +10,23 @@
 from jax.sharding import PartitionSpec as P
 
 TILE = 128
-GROUP = 4
-FINE = (("x", 4), ("zh", 2), ("y", 4), ("zl", 8), ("core", 2))
-N_X, N_ZH, N_Y, N_ZL, N_CORE = (size for _, size in FINE)
+GROUP = 16
+FINE = (("x", 4), ("zh", 2), ("y", 4), ("z2", 2), ("z4", 4), ("core", 2))
+N_X, N_ZH, N_Y, N_Z2, N_Z4, N_CORE = (size for _, size in FINE)
+N_ZL = N_Z2 * N_Z4
 ROW = ("x", "zh")
-COL = ("y", "zl", "core")
+COL = ("y", "z2", "z4", "core")
 LISTS = N_Y * N_CORE
 PLANE = N_X * N_Y
-W_ROWS = 32
+LARGE = 50
+W_ROWS = 64
 BF16 = jnp.bfloat16
 F32 = jnp.float32
 I32 = jnp.int32
 
 vmem = pl.BlockSpec(memory_space=pltpu.VMEM)
 smem = pl.BlockSpec(memory_space=pltpu.SMEM)
+hbm = pl.BlockSpec(memory_space=pltpu.HBM)
 shape = jax.ShapeDtypeStruct
 
 
@@ -44,7 +47,35 @@
     return high, (value - high.astype(F32)).astype(BF16)
 
 
-def pack_body(rows_ref, cols_ref, weight_ref, row_ref, col_ref, count_ref, send_ref):
+def pair_body(zh_ref, own_ref, other_ref, send_ref):
+    mine = zh_ref[0] == 0
+    own, other = own_ref[...], other_ref[...]
+    first, second = jnp.where(mine, own, other), jnp.where(mine, other, own)
+    for peer in range(PLANE):
+        send_ref[peer, 0] = first
+        send_ref[peer, 1] = second
+
+
+def pack_body(
+    rows_hbm, cols_hbm, weight_hbm, row_hbm, col_hbm, count_ref, send_ref,
+    rows_ref, cols_ref, weight_ref, row_ref, col_ref, sems,
+):
+    copies = [
+        pltpu.make_async_copy(source, target, sems.at[k])
+        for k, (source, target) in enumerate(
+            (
+                (rows_hbm, rows_ref),
+                (cols_hbm, cols_ref),
+                (weight_hbm, weight_ref),
+                (row_hbm, row_ref),
+                (col_hbm, col_ref),
+            )
+        )
+    ]
+    for copy in copies:
+        copy.start()
+    for copy in copies:
+        copy.wait()
     slots, edges = rows_ref.shape
     rows = rows_ref[...].astype(F32)
     cols = cols_ref[...].astype(F32)
@@ -64,9 +95,22 @@
             send_ref[peer, k * slots : (k + 1) * slots, :] = block
 
 
+def fetch(tiles_hbm, tiles_ref, sems, group):
+    here = pl.ds(group * GROUP, GROUP)
+    return pltpu.make_async_copy(tiles_hbm.at[here], tiles_ref.at[here], sems.at[group])
+
+
+def fetch_all(total_ref, tiles_hbm, tiles_ref, sems):
+    def start(group, carry):
+        fetch(tiles_hbm, tiles_ref, sems, group).start()
+        return carry
+
+    lax.fori_loop(0, total_ref[1] // GROUP, start, 0)
+
+
 def build_body(
-    where_ref, got_ref, tiles_ref, zl_ref, src_ref, total_ref,
-    slot_ref, edge_rows_ref, edge_cols_ref, weight_ref, meta_ref, slots_ref, sem,
+    where_ref, got_ref, tiles_hbm, zl_ref, src_ref, total_ref,
+    slot_ref, edge_rows_ref, edge_cols_ref, weight_ref, meta_ref, slots_ref, sem, stage_ref, sems,
 ):
     y, core = where_ref[0], where_ref[1]
     slots = got_ref.shape[1] // 5
@@ -100,7 +144,8 @@
             def scan(slot, used, index=index, column_y=column_y):
                 row, col = slots_ref[index * 8, rest + slot], slots_ref[index * 8 + 1, rest + slot]
                 slot_ref[used] = index * slots + slot
-                zl_ref[used] = row // N_CORE % N_ZL
+                near = row // N_CORE
+                zl_ref[used] = near % N_Z4 * N_Z2 + near // N_Z4 % N_Z2
                 src_ref[used] = (col // N_ZH * N_Y + column_y) * N_ZH + col % N_ZH
                 mine = (row // (N_CORE * N_ZL) == y) & (row % N_CORE == core)
                 return used + mine.astype(I32)
@@ -115,7 +160,16 @@
 
     positions = lax.broadcasted_iota(I32, (TILE, edges), 0).astype(F32)
 
+    def store(group):
+        place = group % 2
+        here = pl.ds(group * GROUP, GROUP)
+        return pltpu.make_async_copy(stage_ref.at[place], tiles_hbm.at[here], sems.at[place])
+
     def step(group, carry):
+        @pl.when(group >= 2)
+        def _():
+            store(group - 2).wait()
+
         for i in range(GROUP):
             entry = group * GROUP + i
             slot = slot_ref[entry]
@@ -129,16 +183,27 @@
                 (((1,), (1,)), ((), ())),
                 preferred_element_type=F32,
             )
-            tiles_ref[entry] = built.astype(BF16)
+            stage_ref[group % 2, i] = built.astype(BF16)
+        store(group).start()
         return carry
 
-    lax.fori_loop(0, used // GROUP, step, 0)
-
-
-def forward_body(total_ref, zl_ref, src_ref, tiles_ref, own_ref, other_ref, send_ref, acc_ref):
+    groups = used // GROUP
+    lax.fori_loop(0, groups, step, 0)
+    for back in (2, 1):
+
+        @pl.when(groups >= back)
+        def _(back=back):
+            store(groups - back).wait()
+
+
+def forward_body(
+    total_ref, zl_ref, src_ref, tiles_hbm, own_ref, other_ref, send_ref, acc_ref, tiles_ref, sems
+):
+    fetch_all(total_ref, tiles_hbm, tiles_ref, sems)
     acc_ref[...] = jnp.zeros_like(acc_ref)
 
     def step(feats_ref, group, carry):
+        fetch(tiles_hbm, tiles_ref, sems, group).wait()
         products = []
         for i in range(GROUP):
             entry = group * GROUP + i
@@ -155,38 +220,57 @@
     send_ref[...] = acc_ref[...].astype(BF16)
 
 
-def dense_body(parts_ref, weight_ref, up_ref, act_ref, send_ref, *, scale):
-    aggregated = jnp.sum(parts_ref[...].astype(F32), axis=0).astype(BF16)
+def dense_body(
+    z2_ref, own_ref, other_ref, weight_ref, up_ref, other_up_ref, act_ref, send_ref, *, scale
+):
+    first = z2_ref[0] == 0
+    total = own_ref[...].astype(F32) + other_ref[...].astype(F32)
+    aggregated = total.reshape(N_Z2 * TILE, TILE).astype(BF16)
     weight = weight_ref[...]
+    own_up, other_up = up_ref[...], other_up_ref[...]
+    up = jnp.concatenate(
+        [jnp.where(first, own_up, other_up), jnp.where(first, other_up, own_up)], axis=0
+    )
     pre_act = jnp.dot(aggregated, weight, preferred_element_type=F32)
     gate = jax.nn.sigmoid(pre_act)
-    act_ref[...] = (pre_act * gate).astype(BF16)
-    grad_pre = (up_ref[...].astype(F32) * gate * (1.0 + pre_act * (1.0 - gate))).astype(BF16)
-    grad_agg = lax.dot_general(
-        weight, grad_pre, (((1,), (1,)), ((), ())), preferred_element_type=F32
-    ).astype(BF16)
+    act = (pre_act * gate).astype(BF16)
+    act_ref[...] = jnp.where(first, act[:TILE], act[TILE:])
+    grad_pre = (up.astype(F32) * gate * (1.0 + pre_act * (1.0 - gate))).astype(BF16)
     local_weight = (
         lax.dot_general(aggregated, grad_pre, (((0,), (0,)), ((), ())), preferred_element_type=F32)
         * scale
     ).astype(BF16)
-    deep = TILE // N_ZL
-    for peer in range(N_ZL):
-        send_ref[peer, 0:TILE, :] = grad_agg
+    deep = TILE // N_Z4
+    for z2 in range(N_Z2):
+        grad_agg = lax.dot_general(
+            weight,
+            grad_pre[z2 * TILE : (z2 + 1) * TILE],
+            (((1,), (1,)), ((), ())),
+            preferred_element_type=F32,
+        ).astype(BF16)
+        for peer in range(N_Z4):
+            send_ref[peer, z2 * TILE : (z2 + 1) * TILE, :] = grad_agg
+    for peer in range(N_Z4):
         here = slice(peer * deep, (peer + 1) * deep)
-        send_ref[peer, TILE : TILE + deep, :] = local_weight[here, :TILE]
-        send_ref[peer, TILE + deep :, :] = local_weight[here, TILE:]
+        send_ref[peer, N_Z2 * TILE : N_Z2 * TILE + deep, :] = local_weight[here, :TILE]
+        send_ref[peer, N_Z2 * TILE + deep :, :] = local_weight[here, TILE:]
 
 
 def backward_body(
-    total_ref, zl_ref, src_ref, tiles_ref, got_ref, send_ref, keep_ref, keep_weight_ref, acc_ref
-):
+    total_ref, zl_ref, src_ref, tiles_hbm, got_ref, send_ref, keep_ref, keep_weight_ref,
+    acc_ref, tiles_ref, sems,
+):
+    fetch_all(total_ref, tiles_hbm, tiles_ref, sems)
     acc_ref[...] = jnp.zeros_like(acc_ref)
 
     def step(part, group, carry):
+        fetch(tiles_hbm, tiles_ref, sems, group).wait()
         products = []
         for i in range(GROUP):
             entry = group * GROUP + i
-            grad = got_ref[zl_ref[entry], 0:TILE, :]
+            place = zl_ref[entry]
+            start = pl.multiple_of(place % N_Z2 * TILE, TILE)
+            grad = got_ref[place // N_Z2, pl.ds(start, TILE), :]
             products.append(jnp.dot(grad, tiles_ref[entry], preferred_element_type=F32))
         for i in range(GROUP):
             acc_ref[part, src_ref[group * GROUP + i]] += products[i]
@@ -198,46 +282,42 @@
     keep_ref[...] = acc_ref[0]
     tiles = acc_ref.shape[1]
     send_ref[0:tiles] = acc_ref[1].astype(BF16)
-    weight_sum = jnp.sum(got_ref[:, TILE:, :].astype(F32), axis=0)
-    keep_weight_ref[...] = weight_sum
-    high, low = halves(weight_sum)
+    high, low = halves(jnp.sum(got_ref[:, N_Z2 * TILE :, :].astype(F32), axis=0))
+    keep_weight_ref[...] = high.astype(F32) + low.astype(F32)
     send_ref[tiles, 0:W_ROWS, :] = high
     send_ref[tiles, W_ROWS : 2 * W_ROWS, :] = low
-    send_ref[tiles, 2 * W_ROWS :, :] = jnp.zeros_like(send_ref[tiles, 2 * W_ROWS :, :])
 
 
 def merge_body(got_ref, keep_ref, keep_weight_ref, send_ref):
     tiles = keep_ref.shape[0]
     terms = got_ref[tiles, 0 : 2 * W_ROWS, :].astype(F32)
-    high, low = halves(keep_weight_ref[...] + (terms[:W_ROWS] + terms[W_ROWS:]))
+    part = (keep_weight_ref[...] + (terms[:W_ROWS] + terms[W_ROWS:])).astype(BF16)
     for peer in range(PLANE):
         for zh in range(N_ZH):
             tile = peer * N_ZH + zh
             send_ref[peer, zh * TILE : (zh + 1) * TILE, :] = (
                 keep_ref[tile] + got_ref[tile].astype(F32)
             ).astype(BF16)
-        send_ref[peer, N_ZH * TILE : N_ZH * TILE + W_ROWS, :] = high
-        send_ref[peer, N_ZH * TILE + W_ROWS :, :] = low
+        send_ref[peer, N_ZH * TILE :, :] = part
 
 
 def halfway_body(zh_ref, got_ref, send_ref, keep_ref, send_weight_ref):
     zh = zh_ref[0]
     total = jnp.sum(got_ref[...].astype(F32), axis=0)
-    first, second = total[:TILE], total[TILE : 2 * TILE]
+    first, second = total[:TILE], total[TILE : N_ZH * TILE]
     mine = zh == 0
     keep_ref[...] = jnp.where(mine, first, second)
     send_ref[...] = jnp.where(mine, second, first).astype(BF16)
-    terms = total[2 * TILE :]
-    weight_sum = (terms[:W_ROWS] + terms[W_ROWS:]).astype(BF16)
-    for peer in range(N_ZH * N_ZL):
+    weight_sum = total[N_ZH * TILE :].astype(BF16)
+    for peer in range(N_ZH * N_Z4):
         send_weight_ref[peer] = weight_sum
 
 
 def finish_body(got_ref, keep_ref, got_weight_ref, grad_ref, grad_weight_ref):
     grad_ref[...] = (keep_ref[...] + got_ref[...].astype(F32)).T.astype(BF16)
-    deep = TILE // N_ZL
-    for k in range(N_ZL):
-        total = got_weight_ref[k].astype(F32) + got_weight_ref[N_ZL + k].astype(F32)
+    deep = TILE // N_Z4
+    for k in range(N_Z4):
+        total = got_weight_ref[k].astype(F32) + got_weight_ref[N_Z4 + k].astype(F32)
         grad_weight_ref[k * deep : (k + 1) * deep, :TILE] = total[:deep]
         grad_weight_ref[k * deep : (k + 1) * deep, TILE:] = total[deep:]
 
@@ -258,15 +338,26 @@
     slots, edges = edge_rows.shape[2:]
     column_tiles = PLANE * N_ZH
     most = slots + (LISTS - 1) * slots // 2 + 2 * GROUP
+    tile_room = [pltpu.VMEM((most, TILE, TILE), BF16), pltpu.SemaphoreType.DMA((most // GROUP,))]
     zh = lax.axis_index("zh")
     where = jnp.stack([lax.axis_index("y"), lax.axis_index("core")]).astype(I32)
 
     own = features[0]
     other = swap(own, "zh")
 
-    send = call(pack_body, shape((LISTS, 5 * slots, TILE), BF16), [vmem] * 5 + [smem])(
-        edge_rows[0, 0], edge_cols[0, 0], edge_weight[0, 0], tile_rows[0], tile_cols[0], tile_count
-    )
+    send = call(
+        pack_body,
+        shape((LISTS, 5 * slots, TILE), BF16),
+        [hbm] * 5 + [smem],
+        scratch=[
+            pltpu.VMEM((slots, edges), I32),
+            pltpu.VMEM((slots, edges), I32),
+            pltpu.VMEM((slots, edges), BF16),
+            pltpu.VMEM((1, slots), I32),
+            pltpu.VMEM((1, slots), I32),
+            pltpu.SemaphoreType.DMA((5,)),
+        ],
+    )(edge_rows[0, 0], edge_cols[0, 0], edge_weight[0, 0], tile_rows[0], tile_cols[0], tile_count)
     lists = exchange(send, ("y", "core"))
     other, lists = lax.optimization_barrier((other, lists))
     tiles, zl_list, src_list, total = call(
@@ -278,40 +369,56 @@
             shape((N_CORE,), I32),
         ),
         [smem, vmem],
-        (vmem, smem, smem, smem),
+        (hbm, smem, smem, smem),
         [pltpu.SMEM((most,), I32)]
         + [pltpu.VMEM((LISTS * slots + 8, edges), F32)] * 3
         + [
             pltpu.VMEM((LISTS * 8, TILE), I32),
             pltpu.SMEM((LISTS * 8, TILE), I32),
             pltpu.SemaphoreType.DMA,
+            pltpu.VMEM((2, GROUP, TILE, TILE), BF16),
+            pltpu.SemaphoreType.DMA((2,)),
         ],
         flops=slots * TILE * TILE * edges * 4,
         moved=slots * TILE * TILE * 2,
+        limit=LARGE,
     )(where, lists)
 
-    pair = jnp.where(zh == 0, jnp.stack([own, other]), jnp.stack([other, own]))
-    pair = jnp.broadcast_to(pair[None], (PLANE,) + pair.shape)
+    zh_here = zh.astype(I32)[None]
+    pair = call(pair_body, shape((PLANE, N_ZH, TILE, width), BF16), [smem, vmem, vmem])(
+        zh_here, own, other
+    )
+    pair, up = lax.optimization_barrier((pair, upstream[0]))
     mine = exchange(pair, ("x", "y")).reshape(column_tiles, TILE, width)
+    mine, total, other_up = lax.optimization_barrier((mine, total, swap(up, "z2")))
     theirs = swap(mine, "core")
 
     partial = call(
         forward_body,
         shape((N_ZL, TILE, width), BF16),
-        [smem] * 3 + [vmem] * 3,
-        scratch=[pltpu.VMEM((N_ZL, TILE, width), F32)],
+        [smem] * 3 + [hbm, vmem, vmem],
+        scratch=[pltpu.VMEM((N_ZL, TILE, width), F32)] + tile_room,
+        limit=LARGE,
     )(total, zl_list, src_list, tiles, mine, theirs)
 
-    parts = exchange(partial, "zl")
+    got = exchange(partial, "z4").reshape((N_Z4, N_Z2, TILE, width))
+    partial = jnp.sum(got.astype(F32), axis=0).astype(BF16)
 
     node_total = features.shape[1] * N_X * N_ZH * N_Y * N_ZL * N_CORE
     out_act, send = call(
         functools.partial(dense_body, scale=1.0 / math.sqrt(node_total)),
-        (shape((TILE, hidden), BF16), shape((N_ZL, TILE + W_ROWS, TILE), BF16)),
-        [vmem] * 3,
-    )(parts, weight, upstream[0])
-
-    got = exchange(send, "zl")
+        (shape((TILE, hidden), BF16), shape((N_Z4, N_Z2 * TILE + W_ROWS, TILE), BF16)),
+        [smem] + [vmem] * 5,
+    )(
+        lax.axis_index("z2").astype(I32)[None],
+        partial,
+        swap(partial, "z2"),
+        weight,
+        up,
+        other_up,
+    )
+
+    got = exchange(send, "z4")
     send, keep, keep_weight = call(
         backward_body,
         (
@@ -319,11 +426,12 @@
             shape((column_tiles, width, TILE), F32),
             shape((W_ROWS, TILE), F32),
         ),
-        [smem] * 3 + [vmem] * 2,
-        scratch=[pltpu.VMEM((N_CORE, column_tiles, width, TILE), F32)],
+        [smem] * 3 + [hbm, vmem],
+        scratch=[pltpu.VMEM((N_CORE, column_tiles, width, TILE), F32)] + tile_room,
+        limit=LARGE,
     )(total, zl_list, src_list, tiles, got)
 
-    send = call(merge_body, shape((PLANE, N_ZH * TILE + 2 * W_ROWS, TILE), BF16), [vmem] * 3)(
+    send = call(merge_body, shape((PLANE, N_ZH * TILE + W_ROWS, TILE), BF16), [vmem] * 3)(
         swap(send, "core"), keep, keep_weight
     )
     got = exchange(send, ("x", "y"))
@@ -332,12 +440,12 @@
         (
             shape((TILE, TILE), BF16),
             shape((TILE, TILE), F32),
-            shape((N_ZH * N_ZL, W_ROWS, TILE), BF16),
+            shape((N_ZH * N_Z4, W_ROWS, TILE), BF16),
         ),
         [smem, vmem],
-    )(zh.astype(I32)[None], got)
+    )(zh_here, got)
     got = swap(send, "zh")
-    got_weight = exchange(send_weight, ("zh", "zl"))
+    got_weight = exchange(send_weight, ("zh", "z4"))
     grad_features, grad_weight = call(
         finish_body,
         (shape((TILE, width), BF16), shape((width, hidden), F32)),

time: 173 us -> 162 us (0.936)
  blocking collectives: 90.7 us -> 54.4 us
  starting transfers between devices: 50.8 us -> 69.1 us
  Pallas kernels: 15.6 us -> 19.5 us
  waiting for transfers between devices: 9.84 us -> 12 us
    all_to_all x4 -> x3, blocking collectives: 90.7 us -> 54.4 us  [exchange(): return lax.all_to_all(value, axis, 0, 0, tiled=True)]
    ppermute x4 -> x6, starting transfers between devices: 34.8 us -> 45.1 us  [swap(): return lax.ppermute(value, axis, [(0, 1), (1, 0)])]
    all_to_all x2 -> x3, starting transfers between devices: 16 us -> 24 us  [exchange(): return lax.all_to_all(value, axis, 0, 0, tiled=True)]
    pallas_call x3 -> x4, Pallas kernels: 2.71 us -> 5.09 us  [the longest x1 2.47 us: local(): call(forward_body, shape((N_ZL, TILE, width), BF16), [smem] * 3 + [hbm, v...]
    ppermute x4 -> x6, waiting for transfers between devices: 9.83 us -> 11.7 us  [swap(): return lax.ppermute(value, axis, [(0, 1), (1, 0)])]
  transfers between devices with their start and end apart: 6 -> 9, of which waited for: 3 -> 6; matrix products, arithmetic and copies ran while one was open for 0% -> 0% of each run, Pallas kernels for 5% -> 6%
where the time goes in v8:
time: 162 us; the launch traced here: 160 us
  starting transfers between devices  69.1 us (43%)
  blocking collectives  54.4 us (34%)
  Pallas kernels  19.5 us (12%)
  waiting for transfers between devices  12 us (7%)
  local copies, waits for them, and re-layouts  3.75 us (2%)
    all_to_all x3, blocking collectives, exchange(): return lax.all_to_all(value, axis, 0, 0, tiled=True)  54.4 us
    ppermute x6, starting transfers between devices, swap(): return lax.ppermute(value, axis, [(0, 1), (1, 0)])  45.1 us
    all_to_all x3, starting transfers between devices, exchange(): return lax.all_to_all(value, axis, 0, 0, tiled=True)  24 us
    ppermute x6, waiting for transfers between devices, swap(): return lax.ppermute(value, axis, [(0, 1), (1, 0)])  11.7 us
    pallas_call x1, Pallas kernels, local(): call(build_body, (shape((most, TILE, TILE), BF16), shape((most,), I32), s...  9.43 us
    unnamed x16, local copies, waits for them, and re-layouts  3.75 us
  transfers between devices with their start and end apart: 9, of which 6 were waited for; matrix products, arithmetic and copies ran while one was open for 0% of the time, Pallas kernels for 6%

profile of v8, /device:TPU:1, one launch (start us, length us, event | category | flops | bytes accessed | tf_op | source)
XLA Modules:
  0.0 160.2 jit_solution(15017779718588660775)
XLA Ops:
  1.3 0.0 copy-start.2
  1.3 0.8 copy-done.2
  2.1 0.0 copy-start.3
  2.1 0.8 copy-done.3
  3.0 0.0 copy-start.4
  3.0 0.8 copy-done.4
  3.7 0.0 copy-start.6
  3.7 0.7 copy-done.6
  4.4 0.0 copy-start.7
  4.4 0.7 copy-done.7
  5.0 0.0 copy-start.5
  5.0 1.2 shard_map.112
  6.2 10.3 %all-to-all-start = ((bf16[8,320,128]{2,1,0:T(8,128)(2,1)}), bf16[8,320,128]{2,1,0:T(8,128)(2,1)S(1)}, u32[]{:S(2)}, u32[]{:S(2)}) async-start(bf16[8,320,128]{2,1,0:T(8,128)(2,1)} %shard_map.112), calls=%async_computation | async-start | bytes 1310720 | tf_op jit(solution)/shard_map/all_to_all | solution.py:330
  16.6 0.0 copy-done.5
  16.6 11.1 %collective-permute-start = (bf16[128,128]{1,0:T(8,128)(2,1)S(1)}, bf16[128,128]{1,0:T(8,128)(2,1)S(1)}, u32[]{:S(2)}, u32[]{:S(2)}) collective-permute-start(bf16[128,128]{1,0:T(8,128)(2,1)S(1)} %bitcast.22), channel_id=1, source_target_pairs={{0,64},{64,0},{1,65},{65,1},{2,66},{66,2},{3,67},{67,3},{4,68},{68... | collective-permute-start | bytes 98312 | tf_op jit(solution)/shard_map/ppermute | solution.py:326
  27.7 2.3 %collective-permute-done.other_ref = bf16[128,128]{1,0:T(8,128)(2,1)S(1)} collective-permute-done((bf16[128,128]{1,0:T(8,128)(2,1)S(1)}, bf16[128,128]{1,0:T(8,128)(2,1)S(1)}, u32[]{:S(2)}, u32[]{:S(2)}) %collective-permute-start) | collective-permute-done | bytes 32800 | tf_op jit(solution)/shard_map/ppermute | solution.py:326
  29.9 0.0 all-to-all-done.got_ref
  29.9 1.2 shard_map.113
  31.1 0.0 copy-start.1
  31.1 6.0 %all-to-all-start.1 = ((bf16[16,2,128,128]{3,2,1,0:T(8,128)(2,1)}), bf16[16,2,128,128]{3,2,1,0:T(8,128)(2,1)S(1)}, u32[]{:S(2)}, u32[]{:S(2)}) async-start(bf16[16,2,128,128]{3,2,1,0:T(8,128)(2,1)} %shard_map.113), calls=%async_computation.1 | async-start | bytes 2097152 | tf_op jit(solution)/shard_map/all_to_all | solution.py:330
  37.1 0.1 pad_add_fusion.where_ref
  37.2 0.0 copy-done.1
  37.2 5.3 %collective-permute-start.1 = (bf16[128,256]{1,0:T(8,128)(2,1)S(1)}, bf16[128,256]{1,0:T(8,128)(2,1)S(1)}, u32[]{:S(2)}, u32[]{:S(2)}) collective-permute-start(bf16[128,256]{1,0:T(8,128)(2,1)S(1)} %bitcast.17), channel_id=1, source_target_pairs={{0,8},{8,0},{1,9},{9,1},{2,10},{10,2},{3,11},{11,3},{4,12},{12,4},... | collective-permute-start | bytes 196616 | tf_op jit(solution)/shard_map/ppermute | solution.py:326
  42.6 9.4 %shard_map.114 = (bf16[320,128,128]{2,1,0:T(8,128)(2,1)}, s32[320]{0:T(512)S(1)}, s32[320]{0:T(512)S(1)}, s32[2]{0:T(128)S(1)}) custom-call(s32[2]{0:T(128)S(1)} %pad_add_fusion.where_ref, bf16[8,320,128]{2,1,0:T(8,128)(2,1)S(1)} %all-to-all-done.got_ref), custom_call_target="tpu_custom_call" | custom-call | flops 805306368 | bytes 2097152 | tf_op jit(solution)/shard_map/pallas_call | solution.py:363
  52.0 0.0 collective-permute-done.1.other_up_ref
  52.0 0.3 all-to-all-done.1
  52.3 5.1 %collective-permute-start.2 = (bf16[32,128,128]{2,1,0:T(8,128)(2,1)S(1)}, bf16[32,128,128]{2,1,0:T(8,128)(2,1)S(1)}, u32[]{:S(2)}, u32[]{:S(2)}) collective-permute-start(bf16[32,128,128]{2,1,0:T(8,128)(2,1)S(1)} %bitcast.15), channel_id=1, source_target_pairs={{0,1},{1,0},{2,3},{3,2},{4,5},{5,4},{6,7},{7,6},{8,9},{9,8},{10,11... | collective-permute-start | bytes 3145736 | tf_op jit(solution)/shard_map/ppermute | solution.py:326
  57.4 2.3 %collective-permute-done.2.other_ref = bf16[32,128,128]{2,1,0:T(8,128)(2,1)S(1)} collective-permute-done((bf16[32,128,128]{2,1,0:T(8,128)(2,1)S(1)}, bf16[32,128,128]{2,1,0:T(8,128)(2,1)S(1)}, u32[]{:S(2)}, u32[]{:S(2)}) %collective-permute-start.2) | collective-permute-done | bytes 1048608 | tf_op jit(solution)/shard_map/ppermute | solution.py:326
  59.7 0.0 copy-start
  59.7 2.5 %shard_map.115 = bf16[8,128,128]{2,1,0:T(8,128)(2,1)S(1)} custom-call(s32[2]{0:T(128)S(1)} %get-tuple-element.29.total_ref, s32[320]{0:T(512)S(1)} %get-tuple-element.30.zl_ref, s32[320]{0:T(512)S(1)} %get-tuple-element.31.src_ref, bf16[320,128,128]{2,1,0:T(8,128)(2,1)} %get-tuple-element.32.tiles_hbm, bf16[32,128,128]{2,1,0:T(8,128)(2,1)S(1)} %bitcast.16, ...), custom_call_target="tpu_custom_call" | custom-call | tf_op jit(solution)/shard_map/pallas_call | solution.py:396
  62.2 11.4 %all_to_all.30 = bf16[8,128,128]{2,1,0:T(8,128)(2,1)S(1)} all-to-all(bf16[8,128,128]{2,1,0:T(8,128)(2,1)S(1)} %shard_map.115), channel_id=1, replica_groups=mesh['x'=4,'zh'=2,'y'=4,'z2'=2,'z4'=4,'core'=2] {'z4'}, dimensions={0} | all-to-all | bytes 524288 | tf_op jit(solution)/shard_map/all_to_all | solution.py:330
  73.7 7.4 %collective-permute-start.3 = (bf16[2,128,128]{2,1,0:T(8,128)(2,1)S(1)}, bf16[2,128,128]{2,1,0:T(8,128)(2,1)S(1)}, u32[]{:S(2)}, u32[]{:S(2)}) collective-permute-start(bf16[2,128,128]{2,1,0:T(8,128)(2,1)S(1)} %reduce_sum.12.own_ref), channel_id=1, source_target_pairs={{0,8},{8,0},{1,9},{9,1},{2,10},{10,2},{3,11},{11,3},{4,12},{12,4},... | collective-permute-start | bytes 196616 | tf_op jit(solution)/shard_map/ppermute | solution.py:326
  81.1 1.6 %collective-permute-done.3.other_ref = bf16[2,128,128]{2,1,0:T(8,128)(2,1)S(1)} collective-permute-done((bf16[2,128,128]{2,1,0:T(8,128)(2,1)S(1)}, bf16[2,128,128]{2,1,0:T(8,128)(2,1)S(1)}, u32[]{:S(2)}, u32[]{:S(2)}) %collective-permute-start.3) | collective-permute-done | bytes 65568 | tf_op jit(solution)/shard_map/ppermute | solution.py:326
  82.7 0.0 copy-done
  82.7 0.9 shard_map.116
  83.6 16.8 %all_to_all.31.got_ref = bf16[4,320,128]{2,1,0:T(8,128)(2,1)S(1)} all-to-all(bf16[4,320,128]{2,1,0:T(8,128)(2,1)S(1)} %get-tuple-element.36), channel_id=1, replica_groups=mesh['x'=4,'zh'=2,'y'=4,'z2'=2,'z4'=4,'core'=2] {'z4'}, dimensions={0} | all-to-all | bytes 655360 | tf_op jit(solution)/shard_map/all_to_all | solution.py:330
  100.4 2.7 %shard_map.117 = (bf16[33,128,128]{2,1,0:T(8,128)(2,1)S(1)}, f32[32,128,128]{2,1,0:T(8,128)S(1)}, f32[64,128]{1,0:T(8,128)S(1)}) custom-call(s32[2]{0:T(128)S(1)} %get-tuple-element.29.total_ref, s32[320]{0:T(512)S(1)} %get-tuple-element.30.zl_ref, s32[320]{0:T(512)S(1)} %get-tuple-element.31.src_ref, bf16[320,128,128]{2,1,0:T(8,128)(2,1)} %get-tuple-element.32.tiles_hbm, ...), custom_call_target="tpu_custom_call" | custom-call | tf_op jit(solution)/shard_map/pallas_call | solution.py:422
  103.0 4.1 %collective-permute-start.4 = (bf16[33,128,128]{2,1,0:T(8,128)(2,1)S(1)}, bf16[33,128,128]{2,1,0:T(8,128)(2,1)S(1)}, u32[]{:S(2)}, u32[]{:S(2)}) collective-permute-start(bf16[33,128,128]{2,1,0:T(8,128)(2,1)S(1)} %get-tuple-element.37), channel_id=1, source_target_pairs={{0,1},{1,0},{2,3},{3,2},{4,5},{5,4},{6,7},{7,6},{8,9},{9,8},{10,11... | collective-permute-start | bytes 3244040 | tf_op jit(solution)/shard_map/ppermute | solution.py:326
  107.2 2.3 %collective-permute-done.4.got_ref = bf16[33,128,128]{2,1,0:T(8,128)(2,1)S(1)} collective-permute-done((bf16[33,128,128]{2,1,0:T(8,128)(2,1)S(1)}, bf16[33,128,128]{2,1,0:T(8,128)(2,1)S(1)}, u32[]{:S(2)}, u32[]{:S(2)}) %collective-permute-start.4) | collective-permute-done | bytes 1081376 | tf_op jit(solution)/shard_map/ppermute | solution.py:326
  109.5 0.2 shard_map.118
  109.7 26.2 %all_to_all.32.got_ref = bf16[16,320,128]{2,1,0:T(8,128)(2,1)S(1)} all-to-all(bf16[16,320,128]{2,1,0:T(8,128)(2,1)S(1)} %shard_map.118), channel_id=1, replica_groups=mesh['x'=4,'zh'=2,'y'=4,'z2'=2,'z4'=4,'core'=2] {'x','y'}, dimensions={0} | all-to-all | bytes 2621440 | tf_op jit(solution)/shard_map/all_to_all | solution.py:330
  135.9 0.7 shard_map.119
  136.6 7.7 %all-to-all-start.5 = ((bf16[8,64,128]{2,1,0:T(8,128)(2,1)}), bf16[8,64,128]{2,1,0:T(8,128)(2,1)S(1)}, u32[]{:S(2)}, u32[]{:S(2)}) async-start(bf16[8,64,128]{2,1,0:T(8,128)(2,1)} %get-tuple-element.42), calls=%async_computation.5 | async-start | bytes 262144 | tf_op jit(solution)/shard_map/all_to_all | solution.py:330
  144.2 12.1 %collective-permute-start.5 = (bf16[128,128]{1,0:T(8,128)(2,1)S(1)}, bf16[128,128]{1,0:T(8,128)(2,1)S(1)}, u32[]{:S(2)}, u32[]{:S(2)}) collective-permute-start(bf16[128,128]{1,0:T(8,128)(2,1)S(1)} %get-tuple-element.40), channel_id=1, source_target_pairs={{0,64},{64,0},{1,65},{65,1},{2,66},{66,2},{3,67},{67,3},{4,68},{68... | collective-permute-start | bytes 98312 | tf_op jit(solution)/shard_map/ppermute | solution.py:326
  156.3 3.2 %collective-permute-done.5.got_ref = bf16[128,128]{1,0:T(8,128)(2,1)S(1)} collective-permute-done((bf16[128,128]{1,0:T(8,128)(2,1)S(1)}, bf16[128,128]{1,0:T(8,128)(2,1)S(1)}, u32[]{:S(2)}, u32[]{:S(2)}) %collective-permute-start.5) | collective-permute-done | bytes 32800 | tf_op jit(solution)/shard_map/ppermute | solution.py:326
  159.5 0.0 all-to-all-done.5.got_weight_ref
  159.5 0.7 shard_map.120
  (1 shorter events, 0.0 us)
Async XLA Ops:
  1.3 0.8 copy-start.2
  2.1 0.8 copy-start.3
  3.0 0.8 copy-start.4
  3.7 0.7 copy-start.6
  4.4 0.7 copy-start.7
  5.0 11.5 %copy-start.5 = (bf16[1,128,128]{2,1,0:T(8,128)(2,1)S(1)}, bf16[1,128,128]{2,1,0:T(8,128)(2,1)}, u32[]{:S(2)}) copy-start(bf16[1,128,128]{2,1,0:T(8,128)(2,1)} %param.9) | copy-start | bytes 98308
  6.2 23.7 %all-to-all-start = ((bf16[8,320,128]{2,1,0:T(8,128)(2,1)}), bf16[8,320,128]{2,1,0:T(8,128)(2,1)S(1)}, u32[]{:S(2)}, u32[]{:S(2)}) async-start(bf16[8,320,128]{2,1,0:T(8,128)(2,1)} %shard_map.112), calls=%async_computation | async-start | bytes 1310720 | tf_op jit(solution)/shard_map/all_to_all | solution.py:330
  16.6 13.4 %collective-permute-start = (bf16[128,128]{1,0:T(8,128)(2,1)S(1)}, bf16[128,128]{1,0:T(8,128)(2,1)S(1)}, u32[]{:S(2)}, u32[]{:S(2)}) collective-permute-start(bf16[128,128]{1,0:T(8,128)(2,1)S(1)} %bitcast.22), channel_id=1, source_target_pairs={{0,64},{64,0},{1,65},{65,1},{2,66},{66,2},{3,67},{67,3},{4,68},{68... | collective-permute-start | bytes 98312 | tf_op jit(solution)/shard_map/ppermute | solution.py:326
  31.1 6.1 %copy-start.1 = (bf16[1,128,256]{2,1,0:T(8,128)(2,1)S(1)}, bf16[1,128,256]{2,1,0:T(8,128)(2,1)}, u32[]{:S(2)}) copy-start(bf16[1,128,256]{2,1,0:T(8,128)(2,1)} %param.11) | copy-start | bytes 196612
  31.1 21.2 %all-to-all-start.1 = ((bf16[16,2,128,128]{3,2,1,0:T(8,128)(2,1)}), bf16[16,2,128,128]{3,2,1,0:T(8,128)(2,1)S(1)}, u32[]{:S(2)}, u32[]{:S(2)}) async-start(bf16[16,2,128,128]{3,2,1,0:T(8,128)(2,1)} %shard_map.113), calls=%async_computation.1 | async-start | bytes 2097152 | tf_op jit(solution)/shard_map/all_to_all | solution.py:330
  37.2 14.8 %collective-permute-start.1 = (bf16[128,256]{1,0:T(8,128)(2,1)S(1)}, bf16[128,256]{1,0:T(8,128)(2,1)S(1)}, u32[]{:S(2)}, u32[]{:S(2)}) collective-permute-start(bf16[128,256]{1,0:T(8,128)(2,1)S(1)} %bitcast.17), channel_id=1, source_target_pairs={{0,8},{8,0},{1,9},{9,1},{2,10},{10,2},{3,11},{11,3},{4,12},{12,4},... | collective-permute-start | bytes 196616 | tf_op jit(solution)/shard_map/ppermute | solution.py:326
  52.3 7.3 %collective-permute-start.2 = (bf16[32,128,128]{2,1,0:T(8,128)(2,1)S(1)}, bf16[32,128,128]{2,1,0:T(8,128)(2,1)S(1)}, u32[]{:S(2)}, u32[]{:S(2)}) collective-permute-start(bf16[32,128,128]{2,1,0:T(8,128)(2,1)S(1)} %bitcast.15), channel_id=1, source_target_pairs={{0,1},{1,0},{2,3},{3,2},{4,5},{5,4},{6,7},{7,6},{8,9},{9,8},{10,11... | collective-permute-start | bytes 3145736 | tf_op jit(solution)/shard_map/ppermute | solution.py:326
  59.7 23.0 %copy-start = (bf16[128,256]{1,0:T(8,128)(2,1)S(1)}, bf16[128,256]{1,0:T(8,128)(2,1)}, u32[]{:S(2)}) copy-start(bf16[128,256]{1,0:T(8,128)(2,1)} %weight_ref.1) | copy-start | bytes 196612
  73.7 9.1 %collective-permute-start.3 = (bf16[2,128,128]{2,1,0:T(8,128)(2,1)S(1)}, bf16[2,128,128]{2,1,0:T(8,128)(2,1)S(1)}, u32[]{:S(2)}, u32[]{:S(2)}) collective-permute-start(bf16[2,128,128]{2,1,0:T(8,128)(2,1)S(1)} %reduce_sum.12.own_ref), channel_id=1, source_target_pairs={{0,8},{8,0},{1,9},{9,1},{2,10},{10,2},{3,11},{11,3},{4,12},{12,4},... | collective-permute-start | bytes 196616 | tf_op jit(solution)/shard_map/ppermute | solution.py:326
  103.0 6.4 %collective-permute-start.4 = (bf16[33,128,128]{2,1,0:T(8,128)(2,1)S(1)}, bf16[33,128,128]{2,1,0:T(8,128)(2,1)S(1)}, u32[]{:S(2)}, u32[]{:S(2)}) collective-permute-start(bf16[33,128,128]{2,1,0:T(8,128)(2,1)S(1)} %get-tuple-element.37), channel_id=1, source_target_pairs={{0,1},{1,0},{2,3},{3,2},{4,5},{5,4},{6,7},{7,6},{8,9},{9,8},{10,11... | collective-permute-start | bytes 3244040 | tf_op jit(solution)/shard_map/ppermute | solution.py:326
  136.6 22.9 %all-to-all-start.5 = ((bf16[8,64,128]{2,1,0:T(8,128)(2,1)}), bf16[8,64,128]{2,1,0:T(8,128)(2,1)S(1)}, u32[]{:S(2)}, u32[]{:S(2)}) async-start(bf16[8,64,128]{2,1,0:T(8,128)(2,1)} %get-tuple-element.42), calls=%async_computation.5 | async-start | bytes 262144 | tf_op jit(solution)/shard_map/all_to_all | solution.py:330
  144.2 15.3 %collective-permute-start.5 = (bf16[128,128]{1,0:T(8,128)(2,1)S(1)}, bf16[128,128]{1,0:T(8,128)(2,1)S(1)}, u32[]{:S(2)}, u32[]{:S(2)}) collective-permute-start(bf16[128,128]{1,0:T(8,128)(2,1)S(1)} %get-tuple-element.40), channel_id=1, source_target_pairs={{0,64},{64,0},{1,65},{65,1},{2,66},{66,2},{3,67},{67,3},{4,68},{68... | collective-permute-start | bytes 98312 | tf_op jit(solution)/shard_map/ppermute | solution.py:326

commit v9 on v8

--- a/solution.py
+++ b/solution.py
@@ -11,6 +11,7 @@
 
 TILE = 128
 GROUP = 16
+BLOCK = 8
 FINE = (("x", 4), ("zh", 2), ("y", 4), ("z2", 2), ("z4", 4), ("core", 2))
 N_X, N_ZH, N_Y, N_Z2, N_Z4, N_CORE = (size for _, size in FINE)
 N_ZL = N_Z2 * N_Z4
@@ -18,6 +19,7 @@
 COL = ("y", "z2", "z4", "core")
 LISTS = N_Y * N_CORE
 PLANE = N_X * N_Y
+PACK = 62
 LARGE = 50
 W_ROWS = 64
 BF16 = jnp.bfloat16
@@ -141,16 +143,22 @@
         for column_y in range(N_Y):
             index = column_y * N_CORE + column_core
 
-            def scan(slot, used, index=index, column_y=column_y):
-                row, col = slots_ref[index * 8, rest + slot], slots_ref[index * 8 + 1, rest + slot]
-                slot_ref[used] = index * slots + slot
-                near = row // N_CORE
-                zl_ref[used] = near % N_Z4 * N_Z2 + near // N_Z4 % N_Z2
-                src_ref[used] = (col // N_ZH * N_Y + column_y) * N_ZH + col % N_ZH
-                mine = (row // (N_CORE * N_ZL) == y) & (row % N_CORE == core)
-                return used + mine.astype(I32)
-
-            used = lax.fori_loop(0, slots_ref[index * 8 + 2, rest], scan, used)
+            count = slots_ref[index * 8 + 2, rest]
+
+            def scan(block, used, index=index, column_y=column_y, count=count):
+                for i in range(BLOCK):
+                    slot = block * BLOCK + i
+                    row = slots_ref[index * 8, rest + slot]
+                    col = slots_ref[index * 8 + 1, rest + slot]
+                    slot_ref[used] = index * slots + slot
+                    near = row // N_CORE
+                    zl_ref[used] = near % N_Z4 * N_Z2 + near // N_Z4 % N_Z2
+                    src_ref[used] = (col // N_ZH * N_Y + column_y) * N_ZH + col % N_ZH
+                    mine = (near // N_ZL == y) & (row % N_CORE == core) & (slot < count)
+                    used = used + mine.astype(I32)
+                return used
+
+            used = lax.fori_loop(0, (count + BLOCK - 1) // BLOCK, scan, used)
         for extra in range(GROUP - 1):
             slot_ref[used + extra] = dummy
             zl_ref[used + extra] = 0
@@ -357,6 +365,7 @@
             pltpu.VMEM((1, slots), I32),
             pltpu.SemaphoreType.DMA((5,)),
         ],
+        limit=PACK,
     )(edge_rows[0, 0], edge_cols[0, 0], edge_weight[0, 0], tile_rows[0], tile_cols[0], tile_count)
     lists = exchange(send, ("y", "core"))
     other, lists = lax.optimization_barrier((other, lists))

time: 162 us -> 158 us (0.975)
  waiting for transfers between devices: 12 us -> 18.1 us
  blocking collectives: 54.4 us -> 49.3 us
  starting transfers between devices: 69.1 us -> 64.5 us
  local copies, waits for them, and re-layouts: 3.75 us -> 0.01 us
  Pallas kernels: 19.5 us -> 22.5 us
    ppermute x6, waiting for transfers between devices: 11.7 us -> 18.1 us  [swap(): return lax.ppermute(value, axis, [(0, 1), (1, 0)])]
    all_to_all x3, blocking collectives: 54.4 us -> 49.3 us  [exchange(): return lax.all_to_all(value, axis, 0, 0, tiled=True)]
    unnamed x16 -> x6, local copies, waits for them, and re-layouts: 3.75 us -> 0.01 us
    ppermute x6, starting transfers between devices: 45.1 us -> 41.9 us  [swap(): return lax.ppermute(value, axis, [(0, 1), (1, 0)])]
    pallas_call x1, Pallas kernels: 9.43 us -> 11.2 us  [local(): call(build_body, (shape((most, TILE, TILE), BF16), shape((most,), I32), s...]
  transfers between devices with their start and end apart: 9 -> 9, of which waited for: 6 -> 5; matrix products, arithmetic and copies ran while one was open for 0% -> 0% of each run, Pallas kernels for 6% -> 7%
where the time goes in v9:
time: 158 us; the launch traced here: 156 us
  starting transfers between devices  64.5 us (41%)
  blocking collectives  49.3 us (31%)
  Pallas kernels  22.5 us (14%)
  waiting for transfers between devices  18.1 us (11%)
    all_to_all x3, blocking collectives, exchange(): return lax.all_to_all(value, axis, 0, 0, tiled=True)  49.3 us
    ppermute x6, starting transfers between devices, swap(): return lax.ppermute(value, axis, [(0, 1), (1, 0)])  41.9 us
    all_to_all x3, starting transfers between devices, exchange(): return lax.all_to_all(value, axis, 0, 0, tiled=True)  22.6 us
    ppermute x6, waiting for transfers between devices, swap(): return lax.ppermute(value, axis, [(0, 1), (1, 0)])  18.1 us
    pallas_call x1, Pallas kernels, local(): call(build_body, (shape((most, TILE, TILE), BF16), shape((most,), I32), s...  11.2 us
  transfers between devices with their start and end apart: 9, of which 5 were waited for; matrix products, arithmetic and copies ran while one was open for 0% of the time, Pallas kernels for 7%

profile of v9, /device:TPU:1, one launch (start us, length us, event | category | flops | bytes accessed | tf_op | source)
XLA Modules:
  0.0 155.9 jit_solution(14469796089999963380)
XLA Ops:
  0.6 0.0 copy-start.2
  1.3 1.9 %shard_map.112 = bf16[8,320,128]{2,1,0:T(8,128)(2,1)} custom-call(s32[64,192]{1,0:T(8,128)} %bitcast.22, s32[64,192]{1,0:T(8,128)} %bitcast.23, bf16[64,192]{1,0:T(8,128)(2,1)} %bitcast.24, s32[1,64]{1,0:T(1,128)} %bitcast.25, s32[1,64]{1,0:T(1,128)} %bitcast.26, s32[1,1]{1,0:T(1,128)S(6)} %copy.12.count_ref), custom_call_target="tpu_custom_call" | custom-call | tf_op jit(solution)/shard_map/pallas_call | solution.py:356
  3.2 10.3 %all-to-all-start = ((bf16[8,320,128]{2,1,0:T(8,128)(2,1)}), bf16[8,320,128]{2,1,0:T(8,128)(2,1)S(1)}, u32[]{:S(2)}, u32[]{:S(2)}) async-start(bf16[8,320,128]{2,1,0:T(8,128)(2,1)} %shard_map.112), calls=%async_computation | async-start | bytes 1310720 | tf_op jit(solution)/shard_map/all_to_all | solution.py:338
  13.5 0.0 copy-done.2
  13.5 11.1 %collective-permute-start = (bf16[128,128]{1,0:T(8,128)(2,1)S(1)}, bf16[128,128]{1,0:T(8,128)(2,1)S(1)}, u32[]{:S(2)}, u32[]{:S(2)}) collective-permute-start(bf16[128,128]{1,0:T(8,128)(2,1)S(1)} %bitcast.19), channel_id=1, source_target_pairs={{0,64},{64,0},{1,65},{65,1},{2,66},{66,2},{3,67},{67,3},{4,68},{68... | collective-permute-start | bytes 98312 | tf_op jit(solution)/shard_map/ppermute | solution.py:334
  24.6 2.3 %collective-permute-done.other_ref = bf16[128,128]{1,0:T(8,128)(2,1)S(1)} collective-permute-done((bf16[128,128]{1,0:T(8,128)(2,1)S(1)}, bf16[128,128]{1,0:T(8,128)(2,1)S(1)}, u32[]{:S(2)}, u32[]{:S(2)}) %collective-permute-start) | collective-permute-done | bytes 32800 | tf_op jit(solution)/shard_map/ppermute | solution.py:334
  26.9 0.0 all-to-all-done.got_ref
  26.9 1.2 shard_map.113
  28.1 0.0 copy-start.1
  28.1 6.0 %all-to-all-start.1 = ((bf16[16,2,128,128]{3,2,1,0:T(8,128)(2,1)}), bf16[16,2,128,128]{3,2,1,0:T(8,128)(2,1)S(1)}, u32[]{:S(2)}, u32[]{:S(2)}) async-start(bf16[16,2,128,128]{3,2,1,0:T(8,128)(2,1)} %shard_map.113), calls=%async_computation.1 | async-start | bytes 2097152 | tf_op jit(solution)/shard_map/all_to_all | solution.py:338
  34.0 0.1 pad_add_fusion.where_ref
  34.1 0.0 copy-done.1
  34.1 5.3 %collective-permute-start.1 = (bf16[128,256]{1,0:T(8,128)(2,1)S(1)}, bf16[128,256]{1,0:T(8,128)(2,1)S(1)}, u32[]{:S(2)}, u32[]{:S(2)}) collective-permute-start(bf16[128,256]{1,0:T(8,128)(2,1)S(1)} %bitcast.17), channel_id=1, source_target_pairs={{0,8},{8,0},{1,9},{9,1},{2,10},{10,2},{3,11},{11,3},{4,12},{12,4},... | collective-permute-start | bytes 196616 | tf_op jit(solution)/shard_map/ppermute | solution.py:334
  39.5 11.2 %shard_map.114 = (bf16[320,128,128]{2,1,0:T(8,128)(2,1)}, s32[320]{0:T(512)S(1)}, s32[320]{0:T(512)S(1)}, s32[2]{0:T(128)S(1)}) custom-call(s32[2]{0:T(128)S(1)} %pad_add_fusion.where_ref, bf16[8,320,128]{2,1,0:T(8,128)(2,1)S(1)} %all-to-all-done.got_ref), custom_call_target="tpu_custom_call" | custom-call | flops 805306368 | bytes 2097152 | tf_op jit(solution)/shard_map/pallas_call | solution.py:372
  50.7 0.0 collective-permute-done.1.other_up_ref
  50.7 0.0 all-to-all-done.1
  50.7 4.3 %collective-permute-start.2 = (bf16[32,128,128]{2,1,0:T(8,128)(2,1)S(1)}, bf16[32,128,128]{2,1,0:T(8,128)(2,1)S(1)}, u32[]{:S(2)}, u32[]{:S(2)}) collective-permute-start(bf16[32,128,128]{2,1,0:T(8,128)(2,1)S(1)} %bitcast.15), channel_id=1, source_target_pairs={{0,1},{1,0},{2,3},{3,2},{4,5},{5,4},{6,7},{7,6},{8,9},{9,8},{10,11... | collective-permute-start | bytes 3145736 | tf_op jit(solution)/shard_map/ppermute | solution.py:334
  55.0 2.3 %collective-permute-done.2.other_ref = bf16[32,128,128]{2,1,0:T(8,128)(2,1)S(1)} collective-permute-done((bf16[32,128,128]{2,1,0:T(8,128)(2,1)S(1)}, bf16[32,128,128]{2,1,0:T(8,128)(2,1)S(1)}, u32[]{:S(2)}, u32[]{:S(2)}) %collective-permute-start.2) | collective-permute-done | bytes 1048608 | tf_op jit(solution)/shard_map/ppermute | solution.py:334
  57.2 0.0 copy-start
  57.2 2.8 %shard_map.115 = bf16[8,128,128]{2,1,0:T(8,128)(2,1)S(1)} custom-call(s32[2]{0:T(128)S(1)} %get-tuple-element.29.total_ref, s32[320]{0:T(512)S(1)} %get-tuple-element.30.zl_ref, s32[320]{0:T(512)S(1)} %get-tuple-element.31.src_ref, bf16[320,128,128]{2,1,0:T(8,128)(2,1)} %get-tuple-element.32.tiles_hbm, bf16[32,128,128]{2,1,0:T(8,128)(2,1)S(1)} %bitcast.16, ...), custom_call_target="tpu_custom_call" | custom-call | tf_op jit(solution)/shard_map/pallas_call | solution.py:405
  60.0 12.7 %all_to_all.30 = bf16[8,128,128]{2,1,0:T(8,128)(2,1)S(1)} all-to-all(bf16[8,128,128]{2,1,0:T(8,128)(2,1)S(1)} %shard_map.115), channel_id=1, replica_groups=mesh['x'=4,'zh'=2,'y'=4,'z2'=2,'z4'=4,'core'=2] {'z4'}, dimensions={0} | all-to-all | bytes 524288 | tf_op jit(solution)/shard_map/all_to_all | solution.py:338
  72.7 5.3 %collective-permute-start.3 = (bf16[2,128,128]{2,1,0:T(8,128)(2,1)S(1)}, bf16[2,128,128]{2,1,0:T(8,128)(2,1)S(1)}, u32[]{:S(2)}, u32[]{:S(2)}) collective-permute-start(bf16[2,128,128]{2,1,0:T(8,128)(2,1)S(1)} %reduce_sum.12.own_ref), channel_id=1, source_target_pairs={{0,8},{8,0},{1,9},{9,1},{2,10},{10,2},{3,11},{11,3},{4,12},{12,4},... | collective-permute-start | bytes 196616 | tf_op jit(solution)/shard_map/ppermute | solution.py:334
  78.0 8.0 %collective-permute-done.3.other_ref = bf16[2,128,128]{2,1,0:T(8,128)(2,1)S(1)} collective-permute-done((bf16[2,128,128]{2,1,0:T(8,128)(2,1)S(1)}, bf16[2,128,128]{2,1,0:T(8,128)(2,1)S(1)}, u32[]{:S(2)}, u32[]{:S(2)}) %collective-permute-start.3) | collective-permute-done | bytes 65568 | tf_op jit(solution)/shard_map/ppermute | solution.py:334
  86.0 0.0 copy-done
  86.0 0.9 shard_map.116
  86.8 11.3 %all_to_all.31.got_ref = bf16[4,320,128]{2,1,0:T(8,128)(2,1)S(1)} all-to-all(bf16[4,320,128]{2,1,0:T(8,128)(2,1)S(1)} %get-tuple-element.36), channel_id=1, replica_groups=mesh['x'=4,'zh'=2,'y'=4,'z2'=2,'z4'=4,'core'=2] {'z4'}, dimensions={0} | all-to-all | bytes 655360 | tf_op jit(solution)/shard_map/all_to_all | solution.py:338
  98.2 3.0 %shard_map.117 = (bf16[33,128,128]{2,1,0:T(8,128)(2,1)S(1)}, f32[32,128,128]{2,1,0:T(8,128)S(1)}, f32[64,128]{1,0:T(8,128)S(1)}) custom-call(s32[2]{0:T(128)S(1)} %get-tuple-element.29.total_ref, s32[320]{0:T(512)S(1)} %get-tuple-element.30.zl_ref, s32[320]{0:T(512)S(1)} %get-tuple-element.31.src_ref, bf16[320,128,128]{2,1,0:T(8,128)(2,1)} %get-tuple-element.32.tiles_hbm, ...), custom_call_target="tpu_custom_call" | custom-call | tf_op jit(solution)/shard_map/pallas_call | solution.py:431
  101.2 3.9 %collective-permute-start.4 = (bf16[33,128,128]{2,1,0:T(8,128)(2,1)S(1)}, bf16[33,128,128]{2,1,0:T(8,128)(2,1)S(1)}, u32[]{:S(2)}, u32[]{:S(2)}) collective-permute-start(bf16[33,128,128]{2,1,0:T(8,128)(2,1)S(1)} %get-tuple-element.37), channel_id=1, source_target_pairs={{0,1},{1,0},{2,3},{3,2},{4,5},{5,4},{6,7},{7,6},{8,9},{9,8},{10,11... | collective-permute-start | bytes 3244040 | tf_op jit(solution)/shard_map/ppermute | solution.py:334
  105.0 2.3 %collective-permute-done.4.got_ref = bf16[33,128,128]{2,1,0:T(8,128)(2,1)S(1)} collective-permute-done((bf16[33,128,128]{2,1,0:T(8,128)(2,1)S(1)}, bf16[33,128,128]{2,1,0:T(8,128)(2,1)S(1)}, u32[]{:S(2)}, u32[]{:S(2)}) %collective-permute-start.4) | collective-permute-done | bytes 1081376 | tf_op jit(solution)/shard_map/ppermute | solution.py:334
  107.3 0.2 shard_map.118
  107.5 25.3 %all_to_all.32.got_ref = bf16[16,320,128]{2,1,0:T(8,128)(2,1)S(1)} all-to-all(bf16[16,320,128]{2,1,0:T(8,128)(2,1)S(1)} %shard_map.118), channel_id=1, replica_groups=mesh['x'=4,'zh'=2,'y'=4,'z2'=2,'z4'=4,'core'=2] {'x','y'}, dimensions={0} | all-to-all | bytes 2621440 | tf_op jit(solution)/shard_map/all_to_all | solution.py:338
  132.8 0.7 shard_map.119
  133.5 6.3 %all-to-all-start.5 = ((bf16[8,64,128]{2,1,0:T(8,128)(2,1)}), bf16[8,64,128]{2,1,0:T(8,128)(2,1)S(1)}, u32[]{:S(2)}, u32[]{:S(2)}) async-start(bf16[8,64,128]{2,1,0:T(8,128)(2,1)} %get-tuple-element.42), calls=%async_computation.5 | async-start | bytes 262144 | tf_op jit(solution)/shard_map/all_to_all | solution.py:338
  139.8 12.1 %collective-permute-start.5 = (bf16[128,128]{1,0:T(8,128)(2,1)S(1)}, bf16[128,128]{1,0:T(8,128)(2,1)S(1)}, u32[]{:S(2)}, u32[]{:S(2)}) collective-permute-start(bf16[128,128]{1,0:T(8,128)(2,1)S(1)} %get-tuple-element.40), channel_id=1, source_target_pairs={{0,64},{64,0},{1,65},{65,1},{2,66},{66,2},{3,67},{67,3},{4,68},{68... | collective-permute-start | bytes 98312 | tf_op jit(solution)/shard_map/ppermute | solution.py:334
  151.9 3.3 %collective-permute-done.5.got_ref = bf16[128,128]{1,0:T(8,128)(2,1)S(1)} collective-permute-done((bf16[128,128]{1,0:T(8,128)(2,1)S(1)}, bf16[128,128]{1,0:T(8,128)(2,1)S(1)}, u32[]{:S(2)}, u32[]{:S(2)}) %collective-permute-start.5) | collective-permute-done | bytes 32800 | tf_op jit(solution)/shard_map/ppermute | solution.py:334
  155.2 0.0 all-to-all-done.5.got_weight_ref
  155.2 0.7 shard_map.120
  (1 shorter events, 0.0 us)
Async XLA Ops:
  0.6 12.9 %copy-start.2 = (bf16[1,128,128]{2,1,0:T(8,128)(2,1)S(1)}, bf16[1,128,128]{2,1,0:T(8,128)(2,1)}, u32[]{:S(2)}) copy-start(bf16[1,128,128]{2,1,0:T(8,128)(2,1)} %param.9) | copy-start | bytes 98308
  3.2 23.7 %all-to-all-start = ((bf16[8,320,128]{2,1,0:T(8,128)(2,1)}), bf16[8,320,128]{2,1,0:T(8,128)(2,1)S(1)}, u32[]{:S(2)}, u32[]{:S(2)}) async-start(bf16[8,320,128]{2,1,0:T(8,128)(2,1)} %shard_map.112), calls=%async_computation | async-start | bytes 1310720 | tf_op jit(solution)/shard_map/all_to_all | solution.py:338
  13.5 13.4 %collective-permute-start = (bf16[128,128]{1,0:T(8,128)(2,1)S(1)}, bf16[128,128]{1,0:T(8,128)(2,1)S(1)}, u32[]{:S(2)}, u32[]{:S(2)}) collective-permute-start(bf16[128,128]{1,0:T(8,128)(2,1)S(1)} %bitcast.19), channel_id=1, source_target_pairs={{0,64},{64,0},{1,65},{65,1},{2,66},{66,2},{3,67},{67,3},{4,68},{68... | collective-permute-start | bytes 98312 | tf_op jit(solution)/shard_map/ppermute | solution.py:334
  28.1 6.1 %copy-start.1 = (bf16[1,128,256]{2,1,0:T(8,128)(2,1)S(1)}, bf16[1,128,256]{2,1,0:T(8,128)(2,1)}, u32[]{:S(2)}) copy-start(bf16[1,128,256]{2,1,0:T(8,128)(2,1)} %param.11) | copy-start | bytes 196612
  28.1 22.6 %all-to-all-start.1 = ((bf16[16,2,128,128]{3,2,1,0:T(8,128)(2,1)}), bf16[16,2,128,128]{3,2,1,0:T(8,128)(2,1)S(1)}, u32[]{:S(2)}, u32[]{:S(2)}) async-start(bf16[16,2,128,128]{3,2,1,0:T(8,128)(2,1)} %shard_map.113), calls=%async_computation.1 | async-start | bytes 2097152 | tf_op jit(solution)/shard_map/all_to_all | solution.py:338
  34.1 16.5 %collective-permute-start.1 = (bf16[128,256]{1,0:T(8,128)(2,1)S(1)}, bf16[128,256]{1,0:T(8,128)(2,1)S(1)}, u32[]{:S(2)}, u32[]{:S(2)}) collective-permute-start(bf16[128,256]{1,0:T(8,128)(2,1)S(1)} %bitcast.17), channel_id=1, source_target_pairs={{0,8},{8,0},{1,9},{9,1},{2,10},{10,2},{3,11},{11,3},{4,12},{12,4},... | collective-permute-start | bytes 196616 | tf_op jit(solution)/shard_map/ppermute | solution.py:334
  50.7 6.6 %collective-permute-start.2 = (bf16[32,128,128]{2,1,0:T(8,128)(2,1)S(1)}, bf16[32,128,128]{2,1,0:T(8,128)(2,1)S(1)}, u32[]{:S(2)}, u32[]{:S(2)}) collective-permute-start(bf16[32,128,128]{2,1,0:T(8,128)(2,1)S(1)} %bitcast.15), channel_id=1, source_target_pairs={{0,1},{1,0},{2,3},{3,2},{4,5},{5,4},{6,7},{7,6},{8,9},{9,8},{10,11... | collective-permute-start | bytes 3145736 | tf_op jit(solution)/shard_map/ppermute | solution.py:334
  57.2 28.7 %copy-start = (bf16[128,256]{1,0:T(8,128)(2,1)S(1)}, bf16[128,256]{1,0:T(8,128)(2,1)}, u32[]{:S(2)}) copy-start(bf16[128,256]{1,0:T(8,128)(2,1)} %weight_ref.1) | copy-start | bytes 196612
  72.7 13.2 %collective-permute-start.3 = (bf16[2,128,128]{2,1,0:T(8,128)(2,1)S(1)}, bf16[2,128,128]{2,1,0:T(8,128)(2,1)S(1)}, u32[]{:S(2)}, u32[]{:S(2)}) collective-permute-start(bf16[2,128,128]{2,1,0:T(8,128)(2,1)S(1)} %reduce_sum.12.own_ref), channel_id=1, source_target_pairs={{0,8},{8,0},{1,9},{9,1},{2,10},{10,2},{3,11},{11,3},{4,12},{12,4},... | collective-permute-start | bytes 196616 | tf_op jit(solution)/shard_map/ppermute | solution.py:334
  101.2 6.2 %collective-permute-start.4 = (bf16[33,128,128]{2,1,0:T(8,128)(2,1)S(1)}, bf16[33,128,128]{2,1,0:T(8,128)(2,1)S(1)}, u32[]{:S(2)}, u32[]{:S(2)}) collective-permute-start(bf16[33,128,128]{2,1,0:T(8,128)(2,1)S(1)} %get-tuple-element.37), channel_id=1, source_target_pairs={{0,1},{1,0},{2,3},{3,2},{4,5},{5,4},{6,7},{7,6},{8,9},{9,8},{10,11... | collective-permute-start | bytes 3244040 | tf_op jit(solution)/shard_map/ppermute | solution.py:334
  133.5 21.7 %all-to-all-start.5 = ((bf16[8,64,128]{2,1,0:T(8,128)(2,1)}), bf16[8,64,128]{2,1,0:T(8,128)(2,1)S(1)}, u32[]{:S(2)}, u32[]{:S(2)}) async-start(bf16[8,64,128]{2,1,0:T(8,128)(2,1)} %get-tuple-element.42), calls=%async_computation.5 | async-start | bytes 262144 | tf_op jit(solution)/shard_map/all_to_all | solution.py:338
  139.8 15.4 %collective-permute-start.5 = (bf16[128,128]{1,0:T(8,128)(2,1)S(1)}, bf16[128,128]{1,0:T(8,128)(2,1)S(1)}, u32[]{:S(2)}, u32[]{:S(2)}) collective-permute-start(bf16[128,128]{1,0:T(8,128)(2,1)S(1)} %get-tuple-element.40), channel_id=1, source_target_pairs={{0,64},{64,0},{1,65},{65,1},{2,66},{66,2},{3,67},{67,3},{4,68},{68... | collective-permute-start | bytes 98312 | tf_op jit(solution)/shard_map/ppermute | solution.py:334

commit v10 on v9

--- a/solution.py
+++ b/solution.py
@@ -12,6 +12,7 @@
 TILE = 128
 GROUP = 16
 BLOCK = 8
+SRC_AT, ZL_AT, FLAG_AT = 10, 15, 18
 FINE = (("x", 4), ("zh", 2), ("y", 4), ("z2", 2), ("z4", 4), ("core", 2))
 N_X, N_ZH, N_Y, N_Z2, N_Z4, N_CORE = (size for _, size in FINE)
 N_ZL = N_Z2 * N_Z4
@@ -97,31 +98,48 @@
             send_ref[peer, k * slots : (k + 1) * slots, :] = block
 
 
+def field(code, at, until):
+    return (code >> at) & ((1 << (until - at)) - 1)
+
+
 def fetch(tiles_hbm, tiles_ref, sems, group):
     here = pl.ds(group * GROUP, GROUP)
     return pltpu.make_async_copy(tiles_hbm.at[here], tiles_ref.at[here], sems.at[group])
 
 
-def fetch_all(total_ref, tiles_hbm, tiles_ref, sems):
+def part_groups(total_ref, part):
+    first = 0 if part == 0 else total_ref[0] // GROUP
+    return first, total_ref[part] // GROUP
+
+
+def fetch_part(total_ref, part, tiles_hbm, tiles_ref, sems):
     def start(group, carry):
         fetch(tiles_hbm, tiles_ref, sems, group).start()
         return carry
 
-    lax.fori_loop(0, total_ref[1] // GROUP, start, 0)
+    lax.fori_loop(*part_groups(total_ref, part), start, 0)
 
 
 def build_body(
-    where_ref, got_ref, tiles_hbm, zl_ref, src_ref, total_ref,
-    slot_ref, edge_rows_ref, edge_cols_ref, weight_ref, meta_ref, slots_ref, sem, stage_ref, sems,
+    where_ref, got_ref, tiles_hbm, code_ref, total_ref,
+    edge_rows_ref, edge_cols_ref, weight_ref, meta_ref, slots_ref, sem, stage_ref, sems,
 ):
     y, core = where_ref[0], where_ref[1]
     slots = got_ref.shape[1] // 5
     edges = edge_rows_ref.shape[1]
     rest = edges - TILE
     dummy = LISTS * slots
+    lane = lax.broadcasted_iota(I32, (1, TILE), 1) - rest
     for index in range(LISTS):
-        meta = got_ref[index, 4 * slots : 4 * slots + 16, :].astype(F32)
-        meta_ref[index * 8 : (index + 1) * 8, :] = meta[:8].astype(I32)
+        meta = got_ref[index, 4 * slots : 4 * slots + 16, :].astype(F32).astype(I32)
+        row, col, count = meta[0:1], meta[1:2], meta[2:3]
+        near = row >> 1
+        place = (near & (N_Z4 - 1)) * N_Z2 + (near >> 2 & 1)
+        source = ((col >> 1) * N_Y + index // N_CORE) * N_ZH + (col & 1)
+        mine = (near >> 3 == y) & (row & 1 == core) & (lane < count)
+        code = (index * slots + lane) + (source << SRC_AT) + (place << ZL_AT)
+        meta_ref[index * 8 : index * 8 + 1, :] = code + jnp.where(mine, 1 << FLAG_AT, 0)
+        meta_ref[index * 8 + 1 : index * 8 + 2, :] = count
     copy = pltpu.make_async_copy(meta_ref, slots_ref, sem)
     copy.start()
     for index in range(LISTS):
@@ -143,26 +161,18 @@
         for column_y in range(N_Y):
             index = column_y * N_CORE + column_core
 
-            count = slots_ref[index * 8 + 2, rest]
-
-            def scan(block, used, index=index, column_y=column_y, count=count):
+            count = slots_ref[index * 8 + 1, rest]
+
+            def scan(block, used, index=index):
                 for i in range(BLOCK):
-                    slot = block * BLOCK + i
-                    row = slots_ref[index * 8, rest + slot]
-                    col = slots_ref[index * 8 + 1, rest + slot]
-                    slot_ref[used] = index * slots + slot
-                    near = row // N_CORE
-                    zl_ref[used] = near % N_Z4 * N_Z2 + near // N_Z4 % N_Z2
-                    src_ref[used] = (col // N_ZH * N_Y + column_y) * N_ZH + col % N_ZH
-                    mine = (near // N_ZL == y) & (row % N_CORE == core) & (slot < count)
-                    used = used + mine.astype(I32)
+                    code = slots_ref[index * 8, rest + block * BLOCK + i]
+                    code_ref[used] = code
+                    used = used + (code >> FLAG_AT)
                 return used
 
             used = lax.fori_loop(0, (count + BLOCK - 1) // BLOCK, scan, used)
         for extra in range(GROUP - 1):
-            slot_ref[used + extra] = dummy
-            zl_ref[used + extra] = 0
-            src_ref[used + extra] = 0
+            code_ref[used + extra] = dummy
         used = (used + GROUP - 1) // GROUP * GROUP
         total_ref[part] = used
 
@@ -180,7 +190,7 @@
 
         for i in range(GROUP):
             entry = group * GROUP + i
-            slot = slot_ref[entry]
+            slot = field(code_ref[entry], 0, SRC_AT)
             row_hot = jnp.where(positions == edge_rows_ref[pl.ds(slot, 1), :], 1.0, 0.0)
             col_hot = jnp.where(
                 positions == edge_cols_ref[pl.ds(slot, 1), :], weight_ref[pl.ds(slot, 1), :], 0.0
@@ -204,28 +214,26 @@
             store(groups - back).wait()
 
 
-def forward_body(
-    total_ref, zl_ref, src_ref, tiles_hbm, own_ref, other_ref, send_ref, acc_ref, tiles_ref, sems
-):
-    fetch_all(total_ref, tiles_hbm, tiles_ref, sems)
-    acc_ref[...] = jnp.zeros_like(acc_ref)
-
-    def step(feats_ref, group, carry):
+def forward_body(part, total_ref, code_ref, tiles_hbm, feats_ref, *refs):
+    *start_refs, out_ref, acc_ref, tiles_ref, sems = refs
+    fetch_part(total_ref, part, tiles_hbm, tiles_ref, sems)
+    acc_ref[...] = start_refs[0][...] if start_refs else jnp.zeros_like(acc_ref)
+
+    def step(group, carry):
         fetch(tiles_hbm, tiles_ref, sems, group).wait()
         products = []
         for i in range(GROUP):
             entry = group * GROUP + i
+            source = field(code_ref[entry], SRC_AT, ZL_AT)
             products.append(
-                jnp.dot(tiles_ref[entry], feats_ref[src_ref[entry]], preferred_element_type=F32)
+                jnp.dot(tiles_ref[entry], feats_ref[source], preferred_element_type=F32)
             )
         for i in range(GROUP):
-            acc_ref[zl_ref[group * GROUP + i]] += products[i]
+            acc_ref[field(code_ref[group * GROUP + i], ZL_AT, FLAG_AT)] += products[i]
         return carry
 
-    middle, end = total_ref[0] // GROUP, total_ref[1] // GROUP
-    lax.fori_loop(0, middle, functools.partial(step, own_ref), 0)
-    lax.fori_loop(middle, end, functools.partial(step, other_ref), 0)
-    send_ref[...] = acc_ref[...].astype(BF16)
+    lax.fori_loop(*part_groups(total_ref, part), step, 0)
+    out_ref[...] = acc_ref[...].astype(out_ref.dtype)
 
 
 def dense_body(
@@ -264,36 +272,47 @@
         send_ref[peer, N_Z2 * TILE + deep :, :] = local_weight[here, TILE:]
 
 
-def backward_body(
-    total_ref, zl_ref, src_ref, tiles_hbm, got_ref, send_ref, keep_ref, keep_weight_ref,
-    acc_ref, tiles_ref, sems,
-):
-    fetch_all(total_ref, tiles_hbm, tiles_ref, sems)
+def backward_tiles(part, total_ref, code_ref, tiles_hbm, got_ref, acc_ref, tiles_ref, sems):
+    fetch_part(total_ref, part, tiles_hbm, tiles_ref, sems)
     acc_ref[...] = jnp.zeros_like(acc_ref)
 
-    def step(part, group, carry):
+    def step(group, carry):
         fetch(tiles_hbm, tiles_ref, sems, group).wait()
         products = []
         for i in range(GROUP):
             entry = group * GROUP + i
-            place = zl_ref[entry]
+            place = field(code_ref[entry], ZL_AT, FLAG_AT)
             start = pl.multiple_of(place % N_Z2 * TILE, TILE)
             grad = got_ref[place // N_Z2, pl.ds(start, TILE), :]
             products.append(jnp.dot(grad, tiles_ref[entry], preferred_element_type=F32))
         for i in range(GROUP):
-            acc_ref[part, src_ref[group * GROUP + i]] += products[i]
+            acc_ref[field(code_ref[group * GROUP + i], SRC_AT, ZL_AT)] += products[i]
         return carry
 
-    middle, end = total_ref[0] // GROUP, total_ref[1] // GROUP
-    lax.fori_loop(0, middle, functools.partial(step, 0), 0)
-    lax.fori_loop(middle, end, functools.partial(step, 1), 0)
-    keep_ref[...] = acc_ref[0]
-    tiles = acc_ref.shape[1]
-    send_ref[0:tiles] = acc_ref[1].astype(BF16)
-    high, low = halves(jnp.sum(got_ref[:, N_Z2 * TILE :, :].astype(F32), axis=0))
+    lax.fori_loop(*part_groups(total_ref, part), step, 0)
+
+
+def weight_terms(got_ref):
+    return halves(jnp.sum(got_ref[:, N_Z2 * TILE :, :].astype(F32), axis=0))
+
+
+def backward_other_body(
+    total_ref, code_ref, tiles_hbm, got_ref, send_ref, acc_ref, tiles_ref, sems
+):
+    backward_tiles(1, total_ref, code_ref, tiles_hbm, got_ref, acc_ref, tiles_ref, sems)
+    tiles = acc_ref.shape[0]
+    send_ref[0:tiles] = acc_ref[...].astype(BF16)
+    high, low = weight_terms(got_ref)
+    send_ref[tiles, 0:W_ROWS, :] = high
+    send_ref[tiles, W_ROWS:, :] = low
+
+
+def backward_own_body(
+    total_ref, code_ref, tiles_hbm, got_ref, keep_ref, keep_weight_ref, tiles_ref, sems
+):
+    backward_tiles(0, total_ref, code_ref, tiles_hbm, got_ref, keep_ref, tiles_ref, sems)
+    high, low = weight_terms(got_ref)
     keep_weight_ref[...] = high.astype(F32) + low.astype(F32)
-    send_ref[tiles, 0:W_ROWS, :] = high
-    send_ref[tiles, W_ROWS : 2 * W_ROWS, :] = low
 
 
 def merge_body(got_ref, keep_ref, keep_weight_ref, send_ref):
@@ -369,18 +388,12 @@
     )(edge_rows[0, 0], edge_cols[0, 0], edge_weight[0, 0], tile_rows[0], tile_cols[0], tile_count)
     lists = exchange(send, ("y", "core"))
     other, lists = lax.optimization_barrier((other, lists))
-    tiles, zl_list, src_list, total = call(
+    tiles, codes, total = call(
         build_body,
-        (
-            shape((most, TILE, TILE), BF16),
-            shape((most,), I32),
-            shape((most,), I32),
-            shape((N_CORE,), I32),
-        ),
+        (shape((most, TILE, TILE), BF16), shape((most,), I32), shape((N_CORE,), I32)),
         [smem, vmem],
-        (hbm, smem, smem, smem),
-        [pltpu.SMEM((most,), I32)]
-        + [pltpu.VMEM((LISTS * slots + 8, edges), F32)] * 3
+        (hbm, smem, smem),
+        [pltpu.VMEM((LISTS * slots + 8, edges), F32)] * 3
         + [
             pltpu.VMEM((LISTS * 8, TILE), I32),
             pltpu.SMEM((LISTS * 8, TILE), I32),
@@ -402,13 +415,22 @@
     mine, total, other_up = lax.optimization_barrier((mine, total, swap(up, "z2")))
     theirs = swap(mine, "core")
 
+    work = dict(flops=slots * TILE * TILE * width, moved=slots * TILE * TILE, limit=LARGE)
+    sums = (N_ZL, TILE, width)
     partial = call(
-        forward_body,
-        shape((N_ZL, TILE, width), BF16),
-        [smem] * 3 + [hbm, vmem, vmem],
-        scratch=[pltpu.VMEM((N_ZL, TILE, width), F32)] + tile_room,
-        limit=LARGE,
-    )(total, zl_list, src_list, tiles, mine, theirs)
+        functools.partial(forward_body, 0),
+        shape(sums, F32),
+        [smem] * 2 + [hbm, vmem],
+        scratch=[pltpu.VMEM(sums, F32)] + tile_room,
+        **work,
+    )(total, codes, tiles, mine)
+    partial = call(
+        functools.partial(forward_body, 1),
+        shape(sums, BF16),
+        [smem] * 2 + [hbm, vmem, vmem],
+        scratch=[pltpu.VMEM(sums, F32)] + tile_room,
+        **work,
+    )(total, codes, tiles, theirs, partial)
 
     got = exchange(partial, "z4").reshape((N_Z4, N_Z2, TILE, width))
     partial = jnp.sum(got.astype(F32), axis=0).astype(BF16)
@@ -428,17 +450,21 @@
     )
 
     got = exchange(send, "z4")
-    send, keep, keep_weight = call(
-        backward_body,
-        (
-            shape((column_tiles + 1, width, TILE), BF16),
-            shape((column_tiles, width, TILE), F32),
-            shape((W_ROWS, TILE), F32),
-        ),
-        [smem] * 3 + [hbm, vmem],
-        scratch=[pltpu.VMEM((N_CORE, column_tiles, width, TILE), F32)] + tile_room,
-        limit=LARGE,
-    )(total, zl_list, src_list, tiles, got)
+    sums = (column_tiles, width, TILE)
+    send = call(
+        backward_other_body,
+        shape((column_tiles + 1, width, TILE), BF16),
+        [smem] * 2 + [hbm, vmem],
+        scratch=[pltpu.VMEM(sums, F32)] + tile_room,
+        **work,
+    )(total, codes, tiles, got)
+    keep, keep_weight = call(
+        backward_own_body,
+        (shape(sums, F32), shape((W_ROWS, TILE), F32)),
+        [smem] * 2 + [hbm, vmem],
+        scratch=tile_room,
+        **work,
+    )(total, codes, tiles, got)
 
     send = call(merge_body, shape((PLANE, N_ZH * TILE + W_ROWS, TILE), BF16), [vmem] * 3)(
         swap(send, "core"), keep, keep_weight

time: 158 us -> 159 us (level)
  the two profiles are of different devices: /device:TPU:1 before, /device:TPU:32 now
where the time goes in v10:
time: 159 us; the launch traced here: 158 us
  starting transfers between devices  70.2 us (44%)
  blocking collectives  47.9 us (30%)
  Pallas kernels  19.3 us (12%)
  waiting for transfers between devices  18.7 us (12%)
    all_to_all x3, blocking collectives, exchange(): return lax.all_to_all(value, axis, 0, 0, tiled=True)  47.9 us
    ppermute x6, starting transfers between devices, swap(): return lax.ppermute(value, axis, [(0, 1), (1, 0)])  46.3 us
    all_to_all x3, starting transfers between devices, exchange(): return lax.all_to_all(value, axis, 0, 0, tiled=True)  23.9 us
    ppermute x6, waiting for transfers between devices, swap(): return lax.ppermute(value, axis, [(0, 1), (1, 0)])  14.7 us
    pallas_call x1, Pallas kernels, local(): call(build_body, (shape((most, TILE, TILE), BF16), shape((most,), I32), s...  4.9 us
    all_to_all x3, waiting for transfers between devices, exchange(): return lax.all_to_all(value, axis, 0, 0, tiled=True)  4.09 us
  transfers between devices with their start and end apart: 9, of which 7 were waited for; matrix products, arithmetic and copies ran while one was open for 0% of the time, Pallas kernels for 6%

profile of v10, /device:TPU:32, one launch (start us, length us, event | category | flops | bytes accessed | tf_op | source)
XLA Modules:
  0.0 157.8 jit_solution(17878073877523511420)
XLA Ops:
  0.6 0.0 copy-start.2
  1.3 1.9 %shard_map.112 = bf16[8,320,128]{2,1,0:T(8,128)(2,1)} custom-call(s32[64,192]{1,0:T(8,128)} %bitcast.22, s32[64,192]{1,0:T(8,128)} %bitcast.23, bf16[64,192]{1,0:T(8,128)(2,1)} %bitcast.24, s32[1,64]{1,0:T(1,128)} %bitcast.25, s32[1,64]{1,0:T(1,128)} %bitcast.26, s32[1,1]{1,0:T(1,128)S(6)} %copy.12.count_ref), custom_call_target="tpu_custom_call" | custom-call | tf_op jit(solution)/shard_map/pallas_call | solution.py:375
  3.2 4.5 %all-to-all-start = ((bf16[8,320,128]{2,1,0:T(8,128)(2,1)}), bf16[8,320,128]{2,1,0:T(8,128)(2,1)S(1)}, u32[]{:S(2)}, u32[]{:S(2)}) async-start(bf16[8,320,128]{2,1,0:T(8,128)(2,1)} %shard_map.112), calls=%async_computation | async-start | bytes 1310720 | tf_op jit(solution)/shard_map/all_to_all | solution.py:357
  7.6 0.0 copy-done.2
  7.6 14.8 %collective-permute-start = (bf16[128,128]{1,0:T(8,128)(2,1)S(1)}, bf16[128,128]{1,0:T(8,128)(2,1)S(1)}, u32[]{:S(2)}, u32[]{:S(2)}) collective-permute-start(bf16[128,128]{1,0:T(8,128)(2,1)S(1)} %bitcast.19), channel_id=1, source_target_pairs={{0,64},{64,0},{1,65},{65,1},{2,66},{66,2},{3,67},{67,3},{4,68},{68... | collective-permute-start | bytes 98312 | tf_op jit(solution)/shard_map/ppermute | solution.py:353
  22.5 2.0 %collective-permute-done.other_ref = bf16[128,128]{1,0:T(8,128)(2,1)S(1)} collective-permute-done((bf16[128,128]{1,0:T(8,128)(2,1)S(1)}, bf16[128,128]{1,0:T(8,128)(2,1)S(1)}, u32[]{:S(2)}, u32[]{:S(2)}) %collective-permute-start) | collective-permute-done | bytes 32800 | tf_op jit(solution)/shard_map/ppermute | solution.py:353
  24.5 0.0 all-to-all-done.got_ref
  24.5 1.2 shard_map.113
  25.7 0.0 copy-start.1
  25.7 7.3 %all-to-all-start.1 = ((bf16[16,2,128,128]{3,2,1,0:T(8,128)(2,1)}), bf16[16,2,128,128]{3,2,1,0:T(8,128)(2,1)S(1)}, u32[]{:S(2)}, u32[]{:S(2)}) async-start(bf16[16,2,128,128]{3,2,1,0:T(8,128)(2,1)} %shard_map.113), calls=%async_computation.1 | async-start | bytes 2097152 | tf_op jit(solution)/shard_map/all_to_all | solution.py:357
  33.1 0.1 pad_add_fusion.where_ref
  33.1 0.0 copy-done.1
  33.1 6.9 %collective-permute-start.1 = (bf16[128,256]{1,0:T(8,128)(2,1)S(1)}, bf16[128,256]{1,0:T(8,128)(2,1)S(1)}, u32[]{:S(2)}, u32[]{:S(2)}) collective-permute-start(bf16[128,256]{1,0:T(8,128)(2,1)S(1)} %bitcast.17), channel_id=1, source_target_pairs={{0,8},{8,0},{1,9},{9,1},{2,10},{10,2},{3,11},{11,3},{4,12},{12,4},... | collective-permute-start | bytes 196616 | tf_op jit(solution)/shard_map/ppermute | solution.py:353
  40.0 4.9 %shard_map.114 = (bf16[320,128,128]{2,1,0:T(8,128)(2,1)}, s32[320]{0:T(512)S(1)}, s32[2]{0:T(128)S(1)}) custom-call(s32[2]{0:T(128)S(1)} %pad_add_fusion.where_ref, bf16[8,320,128]{2,1,0:T(8,128)(2,1)S(1)} %all-to-all-done.got_ref), custom_call_target="tpu_custom_call" | custom-call | flops 805306368 | bytes 2097152 | tf_op jit(solution)/shard_map/pallas_call | solution.py:391
  44.9 0.9 collective-permute-done.1.other_up_ref
  45.8 4.1 %all-to-all-done.1 = bf16[16,2,128,128]{3,2,1,0:T(8,128)(2,1)S(1)} async-done(((bf16[16,2,128,128]{3,2,1,0:T(8,128)(2,1)}), bf16[16,2,128,128]{3,2,1,0:T(8,128)(2,1)S(1)}, u32[]{:S(2)}, u32[]{:S(2)}) %all-to-all-start.1) | async-done | bytes 1048608 | tf_op jit(solution)/shard_map/all_to_all | solution.py:357
  49.9 1.9 %collective-permute-start.2 = (bf16[32,128,128]{2,1,0:T(8,128)(2,1)S(1)}, bf16[32,128,128]{2,1,0:T(8,128)(2,1)S(1)}, u32[]{:S(2)}, u32[]{:S(2)}) collective-permute-start(bf16[32,128,128]{2,1,0:T(8,128)(2,1)S(1)} %bitcast.15), channel_id=1, source_target_pairs={{0,1},{1,0},{2,3},{3,2},{4,5},{5,4},{6,7},{7,6},{8,9},{9,8},{10,11... | collective-permute-start | bytes 3145736 | tf_op jit(solution)/shard_map/ppermute | solution.py:353
  51.8 2.3 %shard_map.115.refs_0_ = f32[8,128,128]{2,1,0:T(8,128)S(1)} custom-call(s32[2]{0:T(128)S(1)} %get-tuple-element.27.total_ref, s32[320]{0:T(512)S(1)} %get-tuple-element.28.code_ref, bf16[320,128,128]{2,1,0:T(8,128)(2,1)} %get-tuple-element.29.tiles_hbm, bf16[32,128,128]{2,1,0:T(8,128)(2,1)S(1)} %bitcast.16), custom_call_target="tpu_custom_call" | custom-call | flops 134217728 | bytes 1048576 | tf_op jit(solution)/shard_map/pallas_call | solution.py:420
  54.1 0.0 copy-start
  54.1 0.3 collective-permute-done.2.feats_ref
  54.4 2.3 %shard_map.116 = bf16[8,128,128]{2,1,0:T(8,128)(2,1)S(1)} custom-call(s32[2]{0:T(128)S(1)} %get-tuple-element.27.total_ref, s32[320]{0:T(512)S(1)} %get-tuple-element.28.code_ref, bf16[320,128,128]{2,1,0:T(8,128)(2,1)} %get-tuple-element.29.tiles_hbm, bf16[32,128,128]{2,1,0:T(8,128)(2,1)S(1)} %collective-permute-done.2.feats_ref, ...), custom_call_target="tpu_custom_call" | custom-call | flops 134217728 | bytes 1048576 | tf_op jit(solution)/shard_map/pallas_call | solution.py:427
  56.7 11.4 %all_to_all.30 = bf16[8,128,128]{2,1,0:T(8,128)(2,1)S(1)} all-to-all(bf16[8,128,128]{2,1,0:T(8,128)(2,1)S(1)} %shard_map.116), channel_id=1, replica_groups=mesh['x'=4,'zh'=2,'y'=4,'z2'=2,'z4'=4,'core'=2] {'z4'}, dimensions={0} | all-to-all | bytes 524288 | tf_op jit(solution)/shard_map/all_to_all | solution.py:357
  68.2 9.5 %collective-permute-start.3 = (bf16[2,128,128]{2,1,0:T(8,128)(2,1)S(1)}, bf16[2,128,128]{2,1,0:T(8,128)(2,1)S(1)}, u32[]{:S(2)}, u32[]{:S(2)}) collective-permute-start(bf16[2,128,128]{2,1,0:T(8,128)(2,1)S(1)} %reduce_sum.12.own_ref), channel_id=1, source_target_pairs={{0,8},{8,0},{1,9},{9,1},{2,10},{10,2},{3,11},{11,3},{4,12},{12,4},... | collective-permute-start | bytes 196616 | tf_op jit(solution)/shard_map/ppermute | solution.py:353
  77.7 4.4 %collective-permute-done.3.other_ref = bf16[2,128,128]{2,1,0:T(8,128)(2,1)S(1)} collective-permute-done((bf16[2,128,128]{2,1,0:T(8,128)(2,1)S(1)}, bf16[2,128,128]{2,1,0:T(8,128)(2,1)S(1)}, u32[]{:S(2)}, u32[]{:S(2)}) %collective-permute-start.3) | collective-permute-done | bytes 65568 | tf_op jit(solution)/shard_map/ppermute | solution.py:353
  82.2 0.0 copy-done
  82.2 0.9 shard_map.117
  83.0 13.3 %all_to_all.31.got_ref = bf16[4,320,128]{2,1,0:T(8,128)(2,1)S(1)} all-to-all(bf16[4,320,128]{2,1,0:T(8,128)(2,1)S(1)} %get-tuple-element.33), channel_id=1, replica_groups=mesh['x'=4,'zh'=2,'y'=4,'z2'=2,'z4'=4,'core'=2] {'z4'}, dimensions={0} | all-to-all | bytes 655360 | tf_op jit(solution)/shard_map/all_to_all | solution.py:357
  96.4 2.2 %shard_map.118 = bf16[33,128,128]{2,1,0:T(8,128)(2,1)S(1)} custom-call(s32[2]{0:T(128)S(1)} %get-tuple-element.27.total_ref, s32[320]{0:T(512)S(1)} %get-tuple-element.28.code_ref, bf16[320,128,128]{2,1,0:T(8,128)(2,1)} %get-tuple-element.29.tiles_hbm, bf16[4,320,128]{2,1,0:T(8,128)(2,1)S(1)} %all_to_all.31.got_ref), custom_call_target="tpu_custom_call" | custom-call | flops 134217728 | bytes 1048576 | tf_op jit(solution)/shard_map/pallas_call | solution.py:454
  98.6 1.9 %collective-permute-start.4 = (bf16[33,128,128]{2,1,0:T(8,128)(2,1)S(1)}, bf16[33,128,128]{2,1,0:T(8,128)(2,1)S(1)}, u32[]{:S(2)}, u32[]{:S(2)}) collective-permute-start(bf16[33,128,128]{2,1,0:T(8,128)(2,1)S(1)} %shard_map.118), channel_id=1, source_target_pairs={{0,1},{1,0},{2,3},{3,2},{4,5},{5,4},{6,7},{7,6},{8,9},{9,8},{10,11... | collective-permute-start | bytes 3244040 | tf_op jit(solution)/shard_map/ppermute | solution.py:353
  100.5 2.1 %shard_map.119 = (f32[32,128,128]{2,1,0:T(8,128)S(1)}, f32[64,128]{1,0:T(8,128)S(1)}) custom-call(s32[2]{0:T(128)S(1)} %get-tuple-element.27.total_ref, s32[320]{0:T(512)S(1)} %get-tuple-element.28.code_ref, bf16[320,128,128]{2,1,0:T(8,128)(2,1)} %get-tuple-element.29.tiles_hbm, bf16[4,320,128]{2,1,0:T(8,128)(2,1)S(1)} %all_to_all.31.got_ref), custom_call_target="tpu_custom_call" | custom-call | flops 134217728 | bytes 1048576 | tf_op jit(solution)/shard_map/pallas_call | solution.py:461
  102.7 0.5 collective-permute-done.4.got_ref
  103.2 0.2 shard_map.120
  103.4 23.2 %all_to_all.32.got_ref = bf16[16,320,128]{2,1,0:T(8,128)(2,1)S(1)} all-to-all(bf16[16,320,128]{2,1,0:T(8,128)(2,1)S(1)} %shard_map.120), channel_id=1, replica_groups=mesh['x'=4,'zh'=2,'y'=4,'z2'=2,'z4'=4,'core'=2] {'x','y'}, dimensions={0} | all-to-all | bytes 2621440 | tf_op jit(solution)/shard_map/all_to_all | solution.py:357
  126.6 0.7 shard_map.121
  127.3 12.1 %all-to-all-start.5 = ((bf16[8,64,128]{2,1,0:T(8,128)(2,1)}), bf16[8,64,128]{2,1,0:T(8,128)(2,1)S(1)}, u32[]{:S(2)}, u32[]{:S(2)}) async-start(bf16[8,64,128]{2,1,0:T(8,128)(2,1)} %get-tuple-element.38), calls=%async_computation.5 | async-start | bytes 262144 | tf_op jit(solution)/shard_map/all_to_all | solution.py:357
  139.4 11.2 %collective-permute-start.5 = (bf16[128,128]{1,0:T(8,128)(2,1)S(1)}, bf16[128,128]{1,0:T(8,128)(2,1)S(1)}, u32[]{:S(2)}, u32[]{:S(2)}) collective-permute-start(bf16[128,128]{1,0:T(8,128)(2,1)S(1)} %get-tuple-element.36), channel_id=1, source_target_pairs={{0,64},{64,0},{1,65},{65,1},{2,66},{66,2},{3,67},{67,3},{4,68},{68... | collective-permute-start | bytes 98312 | tf_op jit(solution)/shard_map/ppermute | solution.py:353
  150.6 6.5 %collective-permute-done.5.got_ref = bf16[128,128]{1,0:T(8,128)(2,1)S(1)} collective-permute-done((bf16[128,128]{1,0:T(8,128)(2,1)S(1)}, bf16[128,128]{1,0:T(8,128)(2,1)S(1)}, u32[]{:S(2)}, u32[]{:S(2)}) %collective-permute-start.5) | collective-permute-done | bytes 32800 | tf_op jit(solution)/shard_map/ppermute | solution.py:353
  157.1 0.0 all-to-all-done.5.got_weight_ref
  157.1 0.7 shard_map.122
  (1 shorter events, 0.0 us)
Async XLA Ops:
  0.6 7.0 %copy-start.2 = (bf16[1,128,128]{2,1,0:T(8,128)(2,1)S(1)}, bf16[1,128,128]{2,1,0:T(8,128)(2,1)}, u32[]{:S(2)}) copy-start(bf16[1,128,128]{2,1,0:T(8,128)(2,1)} %param.9) | copy-start | bytes 98308
  3.2 21.4 %all-to-all-start = ((bf16[8,320,128]{2,1,0:T(8,128)(2,1)}), bf16[8,320,128]{2,1,0:T(8,128)(2,1)S(1)}, u32[]{:S(2)}, u32[]{:S(2)}) async-start(bf16[8,320,128]{2,1,0:T(8,128)(2,1)} %shard_map.112), calls=%async_computation | async-start | bytes 1310720 | tf_op jit(solution)/shard_map/all_to_all | solution.py:357
  7.6 16.9 %collective-permute-start = (bf16[128,128]{1,0:T(8,128)(2,1)S(1)}, bf16[128,128]{1,0:T(8,128)(2,1)S(1)}, u32[]{:S(2)}, u32[]{:S(2)}) collective-permute-start(bf16[128,128]{1,0:T(8,128)(2,1)S(1)} %bitcast.19), channel_id=1, source_target_pairs={{0,64},{64,0},{1,65},{65,1},{2,66},{66,2},{3,67},{67,3},{4,68},{68... | collective-permute-start | bytes 98312 | tf_op jit(solution)/shard_map/ppermute | solution.py:353
  25.7 7.4 %copy-start.1 = (bf16[1,128,256]{2,1,0:T(8,128)(2,1)S(1)}, bf16[1,128,256]{2,1,0:T(8,128)(2,1)}, u32[]{:S(2)}) copy-start(bf16[1,128,256]{2,1,0:T(8,128)(2,1)} %param.11) | copy-start | bytes 196612
  25.7 24.2 %all-to-all-start.1 = ((bf16[16,2,128,128]{3,2,1,0:T(8,128)(2,1)}), bf16[16,2,128,128]{3,2,1,0:T(8,128)(2,1)S(1)}, u32[]{:S(2)}, u32[]{:S(2)}) async-start(bf16[16,2,128,128]{3,2,1,0:T(8,128)(2,1)} %shard_map.113), calls=%async_computation.1 | async-start | bytes 2097152 | tf_op jit(solution)/shard_map/all_to_all | solution.py:357
  33.1 12.7 %collective-permute-start.1 = (bf16[128,256]{1,0:T(8,128)(2,1)S(1)}, bf16[128,256]{1,0:T(8,128)(2,1)S(1)}, u32[]{:S(2)}, u32[]{:S(2)}) collective-permute-start(bf16[128,256]{1,0:T(8,128)(2,1)S(1)} %bitcast.17), channel_id=1, source_target_pairs={{0,8},{8,0},{1,9},{9,1},{2,10},{10,2},{3,11},{11,3},{4,12},{12,4},... | collective-permute-start | bytes 196616 | tf_op jit(solution)/shard_map/ppermute | solution.py:353
  49.9 4.5 %collective-permute-start.2 = (bf16[32,128,128]{2,1,0:T(8,128)(2,1)S(1)}, bf16[32,128,128]{2,1,0:T(8,128)(2,1)S(1)}, u32[]{:S(2)}, u32[]{:S(2)}) collective-permute-start(bf16[32,128,128]{2,1,0:T(8,128)(2,1)S(1)} %bitcast.15), channel_id=1, source_target_pairs={{0,1},{1,0},{2,3},{3,2},{4,5},{5,4},{6,7},{7,6},{8,9},{9,8},{10,11... | collective-permute-start | bytes 3145736 | tf_op jit(solution)/shard_map/ppermute | solution.py:353
  54.1 28.1 %copy-start = (bf16[128,256]{1,0:T(8,128)(2,1)S(1)}, bf16[128,256]{1,0:T(8,128)(2,1)}, u32[]{:S(2)}) copy-start(bf16[128,256]{1,0:T(8,128)(2,1)} %weight_ref.1) | copy-start | bytes 196612
  68.2 14.0 %collective-permute-start.3 = (bf16[2,128,128]{2,1,0:T(8,128)(2,1)S(1)}, bf16[2,128,128]{2,1,0:T(8,128)(2,1)S(1)}, u32[]{:S(2)}, u32[]{:S(2)}) collective-permute-start(bf16[2,128,128]{2,1,0:T(8,128)(2,1)S(1)} %reduce_sum.12.own_ref), channel_id=1, source_target_pairs={{0,8},{8,0},{1,9},{9,1},{2,10},{10,2},{3,11},{11,3},{4,12},{12,4},... | collective-permute-start | bytes 196616 | tf_op jit(solution)/shard_map/ppermute | solution.py:353
  98.6 4.6 %collective-permute-start.4 = (bf16[33,128,128]{2,1,0:T(8,128)(2,1)S(1)}, bf16[33,128,128]{2,1,0:T(8,128)(2,1)S(1)}, u32[]{:S(2)}, u32[]{:S(2)}) collective-permute-start(bf16[33,128,128]{2,1,0:T(8,128)(2,1)S(1)} %shard_map.118), channel_id=1, source_target_pairs={{0,1},{1,0},{2,3},{3,2},{4,5},{5,4},{6,7},{7,6},{8,9},{9,8},{10,11... | collective-permute-start | bytes 3244040 | tf_op jit(solution)/shard_map/ppermute | solution.py:353
  127.3 29.7 %all-to-all-start.5 = ((bf16[8,64,128]{2,1,0:T(8,128)(2,1)}), bf16[8,64,128]{2,1,0:T(8,128)(2,1)S(1)}, u32[]{:S(2)}, u32[]{:S(2)}) async-start(bf16[8,64,128]{2,1,0:T(8,128)(2,1)} %get-tuple-element.38), calls=%async_computation.5 | async-start | bytes 262144 | tf_op jit(solution)/shard_map/all_to_all | solution.py:357
  139.4 17.6 %collective-permute-start.5 = (bf16[128,128]{1,0:T(8,128)(2,1)S(1)}, bf16[128,128]{1,0:T(8,128)(2,1)S(1)}, u32[]{:S(2)}, u32[]{:S(2)}) collective-permute-start(bf16[128,128]{1,0:T(8,128)(2,1)S(1)} %get-tuple-element.36), channel_id=1, source_target_pairs={{0,64},{64,0},{1,65},{65,1},{2,66},{66,2},{3,67},{67,3},{4,68},{68... | collective-permute-start | bytes 98312 | tf_op jit(solution)/shard_map/ppermute | solution.py:353

commit v11 on v10

--- a/solution.py
+++ b/solution.py
@@ -23,6 +23,7 @@
 PACK = 62
 LARGE = 50
 W_ROWS = 64
+W_HALF = W_ROWS // N_CORE
 BF16 = jnp.bfloat16
 F32 = jnp.float32
 I32 = jnp.int32
@@ -292,33 +293,34 @@
     lax.fori_loop(*part_groups(total_ref, part), step, 0)
 
 
-def weight_terms(got_ref):
-    return halves(jnp.sum(got_ref[:, N_Z2 * TILE :, :].astype(F32), axis=0))
+def weight_half(got_ref, core):
+    terms = jnp.sum(got_ref[:, N_Z2 * TILE :, :].astype(F32), axis=0)
+    return jnp.where(core == 0, terms[:W_HALF], terms[W_HALF:])
 
 
 def backward_other_body(
-    total_ref, code_ref, tiles_hbm, got_ref, send_ref, acc_ref, tiles_ref, sems
+    core_ref, total_ref, code_ref, tiles_hbm, got_ref, send_ref, acc_ref, tiles_ref, sems
 ):
     backward_tiles(1, total_ref, code_ref, tiles_hbm, got_ref, acc_ref, tiles_ref, sems)
     tiles = acc_ref.shape[0]
     send_ref[0:tiles] = acc_ref[...].astype(BF16)
-    high, low = weight_terms(got_ref)
-    send_ref[tiles, 0:W_ROWS, :] = high
-    send_ref[tiles, W_ROWS:, :] = low
+    high, low = halves(weight_half(got_ref, 1 - core_ref[0]))
+    send_ref[tiles, 0:W_HALF, :] = high
+    send_ref[tiles, W_HALF : 2 * W_HALF, :] = low
+    send_ref[tiles, 2 * W_HALF :, :] = jnp.zeros_like(send_ref[tiles, 2 * W_HALF :, :])
 
 
 def backward_own_body(
-    total_ref, code_ref, tiles_hbm, got_ref, keep_ref, keep_weight_ref, tiles_ref, sems
+    core_ref, total_ref, code_ref, tiles_hbm, got_ref, keep_ref, keep_weight_ref, tiles_ref, sems
 ):
     backward_tiles(0, total_ref, code_ref, tiles_hbm, got_ref, keep_ref, tiles_ref, sems)
-    high, low = weight_terms(got_ref)
-    keep_weight_ref[...] = high.astype(F32) + low.astype(F32)
+    keep_weight_ref[...] = weight_half(got_ref, core_ref[0])
 
 
 def merge_body(got_ref, keep_ref, keep_weight_ref, send_ref):
     tiles = keep_ref.shape[0]
-    terms = got_ref[tiles, 0 : 2 * W_ROWS, :].astype(F32)
-    part = (keep_weight_ref[...] + (terms[:W_ROWS] + terms[W_ROWS:])).astype(BF16)
+    terms = got_ref[tiles, 0 : 2 * W_HALF, :].astype(F32)
+    part = (keep_weight_ref[...] + (terms[:W_HALF] + terms[W_HALF:])).astype(BF16)
     for peer in range(PLANE):
         for zh in range(N_ZH):
             tile = peer * N_ZH + zh
@@ -328,25 +330,35 @@
         send_ref[peer, N_ZH * TILE :, :] = part
 
 
-def halfway_body(zh_ref, got_ref, send_ref, keep_ref, send_weight_ref):
+def halfway_body(zh_ref, got_ref, send_ref, keep_ref):
     zh = zh_ref[0]
     total = jnp.sum(got_ref[...].astype(F32), axis=0)
     first, second = total[:TILE], total[TILE : N_ZH * TILE]
     mine = zh == 0
     keep_ref[...] = jnp.where(mine, first, second)
-    send_ref[...] = jnp.where(mine, second, first).astype(BF16)
-    weight_sum = total[N_ZH * TILE :].astype(BF16)
-    for peer in range(N_ZH * N_Z4):
-        send_weight_ref[peer] = weight_sum
-
-
-def finish_body(got_ref, keep_ref, got_weight_ref, grad_ref, grad_weight_ref):
-    grad_ref[...] = (keep_ref[...] + got_ref[...].astype(F32)).T.astype(BF16)
-    deep = TILE // N_Z4
-    for k in range(N_Z4):
-        total = got_weight_ref[k].astype(F32) + got_weight_ref[N_Z4 + k].astype(F32)
-        grad_weight_ref[k * deep : (k + 1) * deep, :TILE] = total[:deep]
-        grad_weight_ref[k * deep : (k + 1) * deep, TILE:] = total[deep:]
+    send_ref[0:TILE, :] = jnp.where(mine, second, first).astype(BF16)
+    high, low = halves(total[N_ZH * TILE :])
+    send_ref[TILE : TILE + W_HALF, :] = high
+    send_ref[TILE + W_HALF :, :] = low
+
+
+def last_sum_body(got_ref, sent_ref, send_ref):
+    terms = got_ref[TILE:, :].astype(F32), sent_ref[TILE:, :].astype(F32)
+    total = (terms[0][:W_HALF] + terms[0][W_HALF:]) + (terms[1][:W_HALF] + terms[1][W_HALF:])
+    for peer in range(N_Z4 * N_CORE):
+        send_ref[peer] = total
+
+
+def finish_body(got_ref, keep_ref, grad_ref):
+    grad_ref[...] = (keep_ref[...] + got_ref[0:TILE, :].astype(F32)).T.astype(BF16)
+
+
+def place_body(got_ref, grad_weight_ref):
+    for z4 in range(N_Z4):
+        for core in range(N_CORE):
+            grad_weight_ref[
+                z4 * W_HALF : (z4 + 1) * W_HALF, core * TILE : (core + 1) * TILE
+            ] = got_ref[z4 * N_CORE + core]
 
 
 def swap(value, axis):
@@ -454,38 +466,34 @@
     send = call(
         backward_other_body,
         shape((column_tiles + 1, width, TILE), BF16),
-        [smem] * 2 + [hbm, vmem],
+        [smem] * 3 + [hbm, vmem],
         scratch=[pltpu.VMEM(sums, F32)] + tile_room,
         **work,
-    )(total, codes, tiles, got)
+    )(where[1:], total, codes, tiles, got)
     keep, keep_weight = call(
         backward_own_body,
-        (shape(sums, F32), shape((W_ROWS, TILE), F32)),
-        [smem] * 2 + [hbm, vmem],
+        (shape(sums, F32), shape((W_HALF, TILE), F32)),
+        [smem] * 3 + [hbm, vmem],
         scratch=tile_room,
         **work,
-    )(total, codes, tiles, got)
-
-    send = call(merge_body, shape((PLANE, N_ZH * TILE + W_ROWS, TILE), BF16), [vmem] * 3)(
+    )(where[1:], total, codes, tiles, got)
+
+    send = call(merge_body, shape((PLANE, N_ZH * TILE + W_HALF, TILE), BF16), [vmem] * 3)(
         swap(send, "core"), keep, keep_weight
     )
     got = exchange(send, ("x", "y"))
-    send, keep, send_weight = call(
+    send, keep = call(
         halfway_body,
-        (
-            shape((TILE, TILE), BF16),
-            shape((TILE, TILE), F32),
-            shape((N_ZH * N_Z4, W_ROWS, TILE), BF16),
-        ),
+        (shape((TILE + 2 * W_HALF, TILE), BF16), shape((TILE, TILE), F32)),
         [smem, vmem],
     )(zh_here, got)
     got = swap(send, "zh")
-    got_weight = exchange(send_weight, ("zh", "z4"))
-    grad_features, grad_weight = call(
-        finish_body,
-        (shape((TILE, width), BF16), shape((width, hidden), F32)),
-        [vmem] * 3,
-    )(got, keep, got_weight)
+    send_weight = call(last_sum_body, shape((N_Z4 * N_CORE, W_HALF, TILE), F32), [vmem] * 2)(
+        got, send
+    )
+    got_weight = exchange(send_weight, ("z4", "core"))
+    grad_features = call(finish_body, shape((TILE, width), BF16), [vmem] * 2)(got, keep)
+    grad_weight = call(place_body, shape((width, hidden), F32), [vmem])(got_weight)
     return (out_act[None], grad_features[None], grad_weight)
 
 

time: 159 us -> 155 us (0.975)
  the two profiles are of different devices: /device:TPU:32 before, /device:TPU:1 now
where the time goes in v11:
time: 155 us; the launch traced here: 154 us
  starting transfers between devices  67.2 us (43%)
  blocking collectives  46.9 us (30%)
  Pallas kernels  20 us (13%)
  waiting for transfers between devices  18 us (12%)
    all_to_all x3, blocking collectives, exchange(): return lax.all_to_all(value, axis, 0, 0, tiled=True)  46.9 us
    ppermute x6, starting transfers between devices, swap(): return lax.ppermute(value, axis, [(0, 1), (1, 0)])  44.7 us
    all_to_all x3, starting transfers between devices, exchange(): return lax.all_to_all(value, axis, 0, 0, tiled=True)  22.5 us
    all_to_all x3, waiting for transfers between devices, exchange(): return lax.all_to_all(value, axis, 0, 0, tiled=True)  10.1 us
    ppermute x6, waiting for transfers between devices, swap(): return lax.ppermute(value, axis, [(0, 1), (1, 0)])  7.82 us
    pallas_call x1, Pallas kernels, local(): call(build_body, (shape((most, TILE, TILE), BF16), shape((most,), I32), s...  4.76 us
  transfers between devices with their start and end apart: 9, of which 6 were waited for; matrix products, arithmetic and copies ran while one was open for 0% of the time, Pallas kernels for 6%

profile of v11, /device:TPU:1, one launch (start us, length us, event | category | flops | bytes accessed | tf_op | source)
XLA Modules:
  0.0 153.6 jit_solution(10215450036079856845)
XLA Ops:
  0.6 0.0 copy-start.2
  1.3 1.9 %shard_map.112 = bf16[8,320,128]{2,1,0:T(8,128)(2,1)} custom-call(s32[64,192]{1,0:T(8,128)} %bitcast.22, s32[64,192]{1,0:T(8,128)} %bitcast.23, bf16[64,192]{1,0:T(8,128)(2,1)} %bitcast.24, s32[1,64]{1,0:T(1,128)} %bitcast.26, s32[1,64]{1,0:T(1,128)} %bitcast.27, s32[1,1]{1,0:T(1,128)S(6)} %copy.12.count_ref), custom_call_target="tpu_custom_call" | custom-call | tf_op jit(solution)/shard_map/pallas_call | solution.py:387
  3.2 10.3 %all-to-all-start = ((bf16[8,320,128]{2,1,0:T(8,128)(2,1)}), bf16[8,320,128]{2,1,0:T(8,128)(2,1)S(1)}, u32[]{:S(2)}, u32[]{:S(2)}) async-start(bf16[8,320,128]{2,1,0:T(8,128)(2,1)} %shard_map.112), calls=%async_computation | async-start | bytes 1310720 | tf_op jit(solution)/shard_map/all_to_all | solution.py:369
  13.5 0.0 copy-done.2
  13.5 11.1 %collective-permute-start = (bf16[128,128]{1,0:T(8,128)(2,1)S(1)}, bf16[128,128]{1,0:T(8,128)(2,1)S(1)}, u32[]{:S(2)}, u32[]{:S(2)}) collective-permute-start(bf16[128,128]{1,0:T(8,128)(2,1)S(1)} %bitcast.19), channel_id=1, source_target_pairs={{0,64},{64,0},{1,65},{65,1},{2,66},{66,2},{3,67},{67,3},{4,68},{68... | collective-permute-start | bytes 98312 | tf_op jit(solution)/shard_map/ppermute | solution.py:365
  24.6 2.3 %collective-permute-done.other_ref = bf16[128,128]{1,0:T(8,128)(2,1)S(1)} collective-permute-done((bf16[128,128]{1,0:T(8,128)(2,1)S(1)}, bf16[128,128]{1,0:T(8,128)(2,1)S(1)}, u32[]{:S(2)}, u32[]{:S(2)}) %collective-permute-start) | collective-permute-done | bytes 32800 | tf_op jit(solution)/shard_map/ppermute | solution.py:365
  26.9 0.0 all-to-all-done.got_ref
  26.9 1.2 shard_map.113
  28.1 0.0 copy-start.1
  28.1 6.0 %all-to-all-start.1 = ((bf16[16,2,128,128]{3,2,1,0:T(8,128)(2,1)}), bf16[16,2,128,128]{3,2,1,0:T(8,128)(2,1)S(1)}, u32[]{:S(2)}, u32[]{:S(2)}) async-start(bf16[16,2,128,128]{3,2,1,0:T(8,128)(2,1)} %shard_map.113), calls=%async_computation.1 | async-start | bytes 2097152 | tf_op jit(solution)/shard_map/all_to_all | solution.py:369
  34.0 0.1 pad_add_fusion.where_ref
  34.1 0.0 copy-done.1
  34.1 5.3 %collective-permute-start.1 = (bf16[128,256]{1,0:T(8,128)(2,1)S(1)}, bf16[128,256]{1,0:T(8,128)(2,1)S(1)}, u32[]{:S(2)}, u32[]{:S(2)}) collective-permute-start(bf16[128,256]{1,0:T(8,128)(2,1)S(1)} %bitcast.17), channel_id=1, source_target_pairs={{0,8},{8,0},{1,9},{9,1},{2,10},{10,2},{3,11},{11,3},{4,12},{12,4},... | collective-permute-start | bytes 196616 | tf_op jit(solution)/shard_map/ppermute | solution.py:365
  39.5 4.8 %shard_map.114 = (bf16[320,128,128]{2,1,0:T(8,128)(2,1)}, s32[320]{0:T(512)S(1)}, s32[2]{0:T(128)S(1)}) custom-call(s32[2]{0:T(128)S(1)} %pad_add_fusion.where_ref, bf16[8,320,128]{2,1,0:T(8,128)(2,1)S(1)} %all-to-all-done.got_ref), custom_call_target="tpu_custom_call" | custom-call | flops 805306368 | bytes 2097152 | tf_op jit(solution)/shard_map/pallas_call | solution.py:403
  44.2 0.0 collective-permute-done.1.other_up_ref
  44.2 5.0 %all-to-all-done.1 = bf16[16,2,128,128]{3,2,1,0:T(8,128)(2,1)S(1)} async-done(((bf16[16,2,128,128]{3,2,1,0:T(8,128)(2,1)}), bf16[16,2,128,128]{3,2,1,0:T(8,128)(2,1)S(1)}, u32[]{:S(2)}, u32[]{:S(2)}) %all-to-all-start.1) | async-done | bytes 1048608 | tf_op jit(solution)/shard_map/all_to_all | solution.py:369
  49.3 5.1 %collective-permute-start.2 = (bf16[32,128,128]{2,1,0:T(8,128)(2,1)S(1)}, bf16[32,128,128]{2,1,0:T(8,128)(2,1)S(1)}, u32[]{:S(2)}, u32[]{:S(2)}) collective-permute-start(bf16[32,128,128]{2,1,0:T(8,128)(2,1)S(1)} %bitcast.15), channel_id=1, source_target_pairs={{0,1},{1,0},{2,3},{3,2},{4,5},{5,4},{6,7},{7,6},{8,9},{9,8},{10,11... | collective-permute-start | bytes 3145736 | tf_op jit(solution)/shard_map/ppermute | solution.py:365
  54.3 2.3 %shard_map.115.refs_0_ = f32[8,128,128]{2,1,0:T(8,128)S(1)} custom-call(s32[2]{0:T(128)S(1)} %get-tuple-element.24.total_ref, s32[320]{0:T(512)S(1)} %get-tuple-element.25.code_ref, bf16[320,128,128]{2,1,0:T(8,128)(2,1)} %get-tuple-element.26.tiles_hbm, bf16[32,128,128]{2,1,0:T(8,128)(2,1)S(1)} %bitcast.16), custom_call_target="tpu_custom_call" | custom-call | flops 134217728 | bytes 1048576 | tf_op jit(solution)/shard_map/pallas_call | solution.py:432
  56.6 0.0 copy-start
  56.6 0.0 collective-permute-done.2.feats_ref
  56.6 2.3 %shard_map.116 = bf16[8,128,128]{2,1,0:T(8,128)(2,1)S(1)} custom-call(s32[2]{0:T(128)S(1)} %get-tuple-element.24.total_ref, s32[320]{0:T(512)S(1)} %get-tuple-element.25.code_ref, bf16[320,128,128]{2,1,0:T(8,128)(2,1)} %get-tuple-element.26.tiles_hbm, bf16[32,128,128]{2,1,0:T(8,128)(2,1)S(1)} %collective-permute-done.2.feats_ref, ...), custom_call_target="tpu_custom_call" | custom-call | flops 134217728 | bytes 1048576 | tf_op jit(solution)/shard_map/pallas_call | solution.py:439
  58.9 9.6 %all_to_all.30 = bf16[8,128,128]{2,1,0:T(8,128)(2,1)S(1)} all-to-all(bf16[8,128,128]{2,1,0:T(8,128)(2,1)S(1)} %shard_map.116), channel_id=1, replica_groups=mesh['x'=4,'zh'=2,'y'=4,'z2'=2,'z4'=4,'core'=2] {'z4'}, dimensions={0} | all-to-all | bytes 524288 | tf_op jit(solution)/shard_map/all_to_all | solution.py:369
  68.6 9.3 %collective-permute-start.3 = (bf16[2,128,128]{2,1,0:T(8,128)(2,1)S(1)}, bf16[2,128,128]{2,1,0:T(8,128)(2,1)S(1)}, u32[]{:S(2)}, u32[]{:S(2)}) collective-permute-start(bf16[2,128,128]{2,1,0:T(8,128)(2,1)S(1)} %reduce_sum.12.own_ref), channel_id=1, source_target_pairs={{0,8},{8,0},{1,9},{9,1},{2,10},{10,2},{3,11},{11,3},{4,12},{12,4},... | collective-permute-start | bytes 196616 | tf_op jit(solution)/shard_map/ppermute | solution.py:365
  77.9 1.6 %collective-permute-done.3.other_ref = bf16[2,128,128]{2,1,0:T(8,128)(2,1)S(1)} collective-permute-done((bf16[2,128,128]{2,1,0:T(8,128)(2,1)S(1)}, bf16[2,128,128]{2,1,0:T(8,128)(2,1)S(1)}, u32[]{:S(2)}, u32[]{:S(2)}) %collective-permute-start.3) | collective-permute-done | bytes 65568 | tf_op jit(solution)/shard_map/ppermute | solution.py:365
  79.5 0.0 copy-done
  79.5 0.9 shard_map.117
  80.4 16.8 %all_to_all.31.got_ref = bf16[4,320,128]{2,1,0:T(8,128)(2,1)S(1)} all-to-all(bf16[4,320,128]{2,1,0:T(8,128)(2,1)S(1)} %get-tuple-element.30), channel_id=1, replica_groups=mesh['x'=4,'zh'=2,'y'=4,'z2'=2,'z4'=4,'core'=2] {'z4'}, dimensions={0} | all-to-all | bytes 655360 | tf_op jit(solution)/shard_map/all_to_all | solution.py:369
  97.2 2.2 %shard_map.118 = bf16[33,128,128]{2,1,0:T(8,128)(2,1)S(1)} custom-call(s32[1]{0:T(128)} %bitcast.11.core_ref, s32[2]{0:T(128)S(1)} %get-tuple-element.24.total_ref, s32[320]{0:T(512)S(1)} %get-tuple-element.25.code_ref, bf16[320,128,128]{2,1,0:T(8,128)(2,1)} %get-tuple-element.26.tiles_hbm, bf16[4,320,128]{2,1,0:T(8,128)(2,1)S(1)} %all_to_all.31.got_ref), custom_call_target="tpu_custom_call" | custom-call | flops 134217728 | bytes 1048576 | tf_op jit(solution)/shard_map/pallas_call | solution.py:466
  99.4 4.1 %collective-permute-start.4 = (bf16[33,128,128]{2,1,0:T(8,128)(2,1)S(1)}, bf16[33,128,128]{2,1,0:T(8,128)(2,1)S(1)}, u32[]{:S(2)}, u32[]{:S(2)}) collective-permute-start(bf16[33,128,128]{2,1,0:T(8,128)(2,1)S(1)} %shard_map.118), channel_id=1, source_target_pairs={{0,1},{1,0},{2,3},{3,2},{4,5},{5,4},{6,7},{7,6},{8,9},{9,8},{10,11... | collective-permute-start | bytes 3244040 | tf_op jit(solution)/shard_map/ppermute | solution.py:365
  103.5 2.1 %shard_map.119 = (f32[32,128,128]{2,1,0:T(8,128)S(1)}, f32[32,128]{1,0:T(8,128)S(1)}) custom-call(s32[1]{0:T(128)} %bitcast.11.core_ref, s32[2]{0:T(128)S(1)} %get-tuple-element.24.total_ref, s32[320]{0:T(512)S(1)} %get-tuple-element.25.code_ref, bf16[320,128,128]{2,1,0:T(8,128)(2,1)} %get-tuple-element.26.tiles_hbm, bf16[4,320,128]{2,1,0:T(8,128)(2,1)S(1)} %all_to_all.31.got_ref), custom_call_target="tpu_custom_call" | custom-call | flops 134217728 | bytes 1048576 | tf_op jit(solution)/shard_map/pallas_call | solution.py:473
  105.7 0.2 collective-permute-done.4.got_ref
  105.8 0.2 shard_map.120
  106.0 20.5 %all_to_all.32.got_ref = bf16[16,288,128]{2,1,0:T(8,128)(2,1)S(1)} all-to-all(bf16[16,288,128]{2,1,0:T(8,128)(2,1)S(1)} %shard_map.120), channel_id=1, replica_groups=mesh['x'=4,'zh'=2,'y'=4,'z2'=2,'z4'=4,'core'=2] {'x','y'}, dimensions={0} | all-to-all | bytes 2359296 | tf_op jit(solution)/shard_map/all_to_all | solution.py:369
  126.5 0.2 shard_map.121
  126.7 9.8 %collective-permute-start.5 = (bf16[192,128]{1,0:T(8,128)(2,1)S(1)}, bf16[192,128]{1,0:T(8,128)(2,1)S(1)}, u32[]{:S(2)}, u32[]{:S(2)}) collective-permute-start(bf16[192,128]{1,0:T(8,128)(2,1)S(1)} %get-tuple-element.33.sent_ref), channel_id=1, source_target_pairs={{0,64},{64,0},{1,65},{65,1},{2,66},{66,2},{3,67},{67,3},{4,68},{68... | collective-permute-start | bytes 147464 | tf_op jit(solution)/shard_map/ppermute | solution.py:365
  136.5 3.7 %collective-permute-done.5.got_ref = bf16[192,128]{1,0:T(8,128)(2,1)S(1)} collective-permute-done((bf16[192,128]{1,0:T(8,128)(2,1)S(1)}, bf16[192,128]{1,0:T(8,128)(2,1)S(1)}, u32[]{:S(2)}, u32[]{:S(2)}) %collective-permute-start.5) | collective-permute-done | bytes 49184 | tf_op jit(solution)/shard_map/ppermute | solution.py:365
  140.3 0.7 shard_map.123
  140.9 6.1 %all-to-all-start.5 = ((f32[8,32,128]{2,1,0:T(8,128)}), f32[8,32,128]{2,1,0:T(8,128)S(1)}, u32[]{:S(2)}, u32[]{:S(2)}) async-start(f32[8,32,128]{2,1,0:T(8,128)} %shard_map.123), calls=%async_computation.5 | async-start | bytes 262144 | tf_op jit(solution)/shard_map/all_to_all | solution.py:369
  147.1 0.7 shard_map.122
  147.8 5.1 %all-to-all-done.5.got_ref = f32[8,32,128]{2,1,0:T(8,128)S(1)} async-done(((f32[8,32,128]{2,1,0:T(8,128)}), f32[8,32,128]{2,1,0:T(8,128)S(1)}, u32[]{:S(2)}, u32[]{:S(2)}) %all-to-all-start.5) | async-done | bytes 131104 | tf_op jit(solution)/shard_map/all_to_all | solution.py:369
  152.9 0.7 shard_map.124
  (1 shorter events, 0.0 us)
Async XLA Ops:
  0.6 12.9 %copy-start.2 = (bf16[1,128,128]{2,1,0:T(8,128)(2,1)S(1)}, bf16[1,128,128]{2,1,0:T(8,128)(2,1)}, u32[]{:S(2)}) copy-start(bf16[1,128,128]{2,1,0:T(8,128)(2,1)} %param.9) | copy-start | bytes 98308
  3.2 23.7 %all-to-all-start = ((bf16[8,320,128]{2,1,0:T(8,128)(2,1)}), bf16[8,320,128]{2,1,0:T(8,128)(2,1)S(1)}, u32[]{:S(2)}, u32[]{:S(2)}) async-start(bf16[8,320,128]{2,1,0:T(8,128)(2,1)} %shard_map.112), calls=%async_computation | async-start | bytes 1310720 | tf_op jit(solution)/shard_map/all_to_all | solution.py:369
  13.5 13.4 %collective-permute-start = (bf16[128,128]{1,0:T(8,128)(2,1)S(1)}, bf16[128,128]{1,0:T(8,128)(2,1)S(1)}, u32[]{:S(2)}, u32[]{:S(2)}) collective-permute-start(bf16[128,128]{1,0:T(8,128)(2,1)S(1)} %bitcast.19), channel_id=1, source_target_pairs={{0,64},{64,0},{1,65},{65,1},{2,66},{66,2},{3,67},{67,3},{4,68},{68... | collective-permute-start | bytes 98312 | tf_op jit(solution)/shard_map/ppermute | solution.py:365
  28.1 6.1 %copy-start.1 = (bf16[1,128,256]{2,1,0:T(8,128)(2,1)S(1)}, bf16[1,128,256]{2,1,0:T(8,128)(2,1)}, u32[]{:S(2)}) copy-start(bf16[1,128,256]{2,1,0:T(8,128)(2,1)} %param.11) | copy-start | bytes 196612
  28.1 21.2 %all-to-all-start.1 = ((bf16[16,2,128,128]{3,2,1,0:T(8,128)(2,1)}), bf16[16,2,128,128]{3,2,1,0:T(8,128)(2,1)S(1)}, u32[]{:S(2)}, u32[]{:S(2)}) async-start(bf16[16,2,128,128]{3,2,1,0:T(8,128)(2,1)} %shard_map.113), calls=%async_computation.1 | async-start | bytes 2097152 | tf_op jit(solution)/shard_map/all_to_all | solution.py:369
  34.1 10.1 %collective-permute-start.1 = (bf16[128,256]{1,0:T(8,128)(2,1)S(1)}, bf16[128,256]{1,0:T(8,128)(2,1)S(1)}, u32[]{:S(2)}, u32[]{:S(2)}) collective-permute-start(bf16[128,256]{1,0:T(8,128)(2,1)S(1)} %bitcast.17), channel_id=1, source_target_pairs={{0,8},{8,0},{1,9},{9,1},{2,10},{10,2},{3,11},{11,3},{4,12},{12,4},... | collective-permute-start | bytes 196616 | tf_op jit(solution)/shard_map/ppermute | solution.py:365
  49.3 7.4 %collective-permute-start.2 = (bf16[32,128,128]{2,1,0:T(8,128)(2,1)S(1)}, bf16[32,128,128]{2,1,0:T(8,128)(2,1)S(1)}, u32[]{:S(2)}, u32[]{:S(2)}) collective-permute-start(bf16[32,128,128]{2,1,0:T(8,128)(2,1)S(1)} %bitcast.15), channel_id=1, source_target_pairs={{0,1},{1,0},{2,3},{3,2},{4,5},{5,4},{6,7},{7,6},{8,9},{9,8},{10,11... | collective-permute-start | bytes 3145736 | tf_op jit(solution)/shard_map/ppermute | solution.py:365
  56.6 22.9 %copy-start = (bf16[128,256]{1,0:T(8,128)(2,1)S(1)}, bf16[128,256]{1,0:T(8,128)(2,1)}, u32[]{:S(2)}) copy-start(bf16[128,256]{1,0:T(8,128)(2,1)} %weight_ref.1) | copy-start | bytes 196612
  68.6 10.9 %collective-permute-start.3 = (bf16[2,128,128]{2,1,0:T(8,128)(2,1)S(1)}, bf16[2,128,128]{2,1,0:T(8,128)(2,1)S(1)}, u32[]{:S(2)}, u32[]{:S(2)}) collective-permute-start(bf16[2,128,128]{2,1,0:T(8,128)(2,1)S(1)} %reduce_sum.12.own_ref), channel_id=1, source_target_pairs={{0,8},{8,0},{1,9},{9,1},{2,10},{10,2},{3,11},{11,3},{4,12},{12,4},... | collective-permute-start | bytes 196616 | tf_op jit(solution)/shard_map/ppermute | solution.py:365
  99.4 6.4 %collective-permute-start.4 = (bf16[33,128,128]{2,1,0:T(8,128)(2,1)S(1)}, bf16[33,128,128]{2,1,0:T(8,128)(2,1)S(1)}, u32[]{:S(2)}, u32[]{:S(2)}) collective-permute-start(bf16[33,128,128]{2,1,0:T(8,128)(2,1)S(1)} %shard_map.118), channel_id=1, source_target_pairs={{0,1},{1,0},{2,3},{3,2},{4,5},{5,4},{6,7},{7,6},{8,9},{9,8},{10,11... | collective-permute-start | bytes 3244040 | tf_op jit(solution)/shard_map/ppermute | solution.py:365
  126.7 13.6 %collective-permute-start.5 = (bf16[192,128]{1,0:T(8,128)(2,1)S(1)}, bf16[192,128]{1,0:T(8,128)(2,1)S(1)}, u32[]{:S(2)}, u32[]{:S(2)}) collective-permute-start(bf16[192,128]{1,0:T(8,128)(2,1)S(1)} %get-tuple-element.33.sent_ref), channel_id=1, source_target_pairs={{0,64},{64,0},{1,65},{65,1},{2,66},{66,2},{3,67},{67,3},{4,68},{68... | collective-permute-start | bytes 147464 | tf_op jit(solution)/shard_map/ppermute | solution.py:365
  140.9 12.0 %all-to-all-start.5 = ((f32[8,32,128]{2,1,0:T(8,128)}), f32[8,32,128]{2,1,0:T(8,128)S(1)}, u32[]{:S(2)}, u32[]{:S(2)}) async-start(f32[8,32,128]{2,1,0:T(8,128)} %shard_map.123), calls=%async_computation.5 | async-start | bytes 262144 | tf_op jit(solution)/shard_map/all_to_all | solution.py:369

commit v12 on v11

--- a/solution.py
+++ b/solution.py
@@ -13,6 +13,7 @@
 GROUP = 16
 BLOCK = 8
 SRC_AT, ZL_AT, FLAG_AT = 10, 15, 18
+EXTRA = 8
 FINE = (("x", 4), ("zh", 2), ("y", 4), ("z2", 2), ("z4", 4), ("core", 2))
 N_X, N_ZH, N_Y, N_Z2, N_Z4, N_CORE = (size for _, size in FINE)
 N_ZL = N_Z2 * N_Z4
@@ -108,21 +109,22 @@
     return pltpu.make_async_copy(tiles_hbm.at[here], tiles_ref.at[here], sems.at[group])
 
 
-def part_groups(total_ref, part):
-    first = 0 if part == 0 else total_ref[0] // GROUP
-    return first, total_ref[part] // GROUP
-
-
-def fetch_part(total_ref, part, tiles_hbm, tiles_ref, sems):
+def part_groups(code_ref, part):
+    ends = code_ref.shape[0] - EXTRA
+    first = 0 if part == 0 else code_ref[ends] // GROUP
+    return first, code_ref[ends + part] // GROUP
+
+
+def fetch_part(code_ref, part, tiles_hbm, tiles_ref, sems):
     def start(group, carry):
         fetch(tiles_hbm, tiles_ref, sems, group).start()
         return carry
 
-    lax.fori_loop(*part_groups(total_ref, part), start, 0)
+    lax.fori_loop(*part_groups(code_ref, part), start, 0)
 
 
 def build_body(
-    where_ref, got_ref, tiles_hbm, code_ref, total_ref,
+    where_ref, got_ref, tiles_hbm, code_ref,
     edge_rows_ref, edge_cols_ref, weight_ref, meta_ref, slots_ref, sem, stage_ref, sems,
 ):
     y, core = where_ref[0], where_ref[1]
@@ -156,6 +158,7 @@
         ref[dummy:, :] = jnp.zeros_like(ref[dummy:, :])
     copy.wait()
 
+    code_ref[code_ref.shape[0] - EXTRA + N_CORE] = core
     used = jnp.int32(0)
     for part in range(N_CORE):
         column_core = core if part == 0 else 1 - core
@@ -175,7 +178,7 @@
         for extra in range(GROUP - 1):
             code_ref[used + extra] = dummy
         used = (used + GROUP - 1) // GROUP * GROUP
-        total_ref[part] = used
+        code_ref[code_ref.shape[0] - EXTRA + part] = used
 
     positions = lax.broadcasted_iota(I32, (TILE, edges), 0).astype(F32)
 
@@ -215,9 +218,9 @@
             store(groups - back).wait()
 
 
-def forward_body(part, total_ref, code_ref, tiles_hbm, feats_ref, *refs):
+def forward_body(part, code_ref, tiles_hbm, feats_ref, *refs):
     *start_refs, out_ref, acc_ref, tiles_ref, sems = refs
-    fetch_part(total_ref, part, tiles_hbm, tiles_ref, sems)
+    fetch_part(code_ref, part, tiles_hbm, tiles_ref, sems)
     acc_ref[...] = start_refs[0][...] if start_refs else jnp.zeros_like(acc_ref)
 
     def step(group, carry):
@@ -233,7 +236,7 @@
             acc_ref[field(code_ref[group * GROUP + i], ZL_AT, FLAG_AT)] += products[i]
         return carry
 
-    lax.fori_loop(*part_groups(total_ref, part), step, 0)
+    lax.fori_loop(*part_groups(code_ref, part), step, 0)
     out_ref[...] = acc_ref[...].astype(out_ref.dtype)
 
 
@@ -273,8 +276,8 @@
         send_ref[peer, N_Z2 * TILE + deep :, :] = local_weight[here, TILE:]
 
 
-def backward_tiles(part, total_ref, code_ref, tiles_hbm, got_ref, acc_ref, tiles_ref, sems):
-    fetch_part(total_ref, part, tiles_hbm, tiles_ref, sems)
+def backward_tiles(part, code_ref, tiles_hbm, got_ref, acc_ref, tiles_ref, sems):
+    fetch_part(code_ref, part, tiles_hbm, tiles_ref, sems)
     acc_ref[...] = jnp.zeros_like(acc_ref)
 
     def step(group, carry):
@@ -290,7 +293,11 @@
             acc_ref[field(code_ref[group * GROUP + i], SRC_AT, ZL_AT)] += products[i]
         return carry
 
-    lax.fori_loop(*part_groups(total_ref, part), step, 0)
+    lax.fori_loop(*part_groups(code_ref, part), step, 0)
+
+
+def own_core(code_ref):
+    return code_ref[code_ref.shape[0] - EXTRA + N_CORE]
 
 
 def weight_half(got_ref, core):
@@ -299,45 +306,40 @@
 
 
 def backward_other_body(
-    core_ref, total_ref, code_ref, tiles_hbm, got_ref, send_ref, acc_ref, tiles_ref, sems
+    code_ref, tiles_hbm, got_ref, send_ref, acc_ref, tiles_ref, sems
 ):
-    backward_tiles(1, total_ref, code_ref, tiles_hbm, got_ref, acc_ref, tiles_ref, sems)
+    backward_tiles(1, code_ref, tiles_hbm, got_ref, acc_ref, tiles_ref, sems)
     tiles = acc_ref.shape[0]
     send_ref[0:tiles] = acc_ref[...].astype(BF16)
-    high, low = halves(weight_half(got_ref, 1 - core_ref[0]))
+    high, low = halves(weight_half(got_ref, 1 - own_core(code_ref)))
     send_ref[tiles, 0:W_HALF, :] = high
     send_ref[tiles, W_HALF : 2 * W_HALF, :] = low
     send_ref[tiles, 2 * W_HALF :, :] = jnp.zeros_like(send_ref[tiles, 2 * W_HALF :, :])
 
 
 def backward_own_body(
-    core_ref, total_ref, code_ref, tiles_hbm, got_ref, keep_ref, keep_weight_ref, tiles_ref, sems
+    code_ref, tiles_hbm, got_ref, keep_ref, keep_weight_ref, tiles_ref, sems
 ):
-    backward_tiles(0, total_ref, code_ref, tiles_hbm, got_ref, keep_ref, tiles_ref, sems)
-    keep_weight_ref[...] = weight_half(got_ref, core_ref[0])
-
-
-def merge_body(got_ref, keep_ref, keep_weight_ref, send_ref):
+    backward_tiles(0, code_ref, tiles_hbm, got_ref, keep_ref, tiles_ref, sems)
+    keep_weight_ref[...] = weight_half(got_ref, own_core(code_ref))
+
+
+def merge_body(zh_ref, got_ref, keep_ref, keep_weight_ref, send_ref, send_own_ref):
+    zh = zh_ref[0]
     tiles = keep_ref.shape[0]
     terms = got_ref[tiles, 0 : 2 * W_HALF, :].astype(F32)
     part = (keep_weight_ref[...] + (terms[:W_HALF] + terms[W_HALF:])).astype(BF16)
     for peer in range(PLANE):
-        for zh in range(N_ZH):
-            tile = peer * N_ZH + zh
-            send_ref[peer, zh * TILE : (zh + 1) * TILE, :] = (
-                keep_ref[tile] + got_ref[tile].astype(F32)
-            ).astype(BF16)
-        send_ref[peer, N_ZH * TILE :, :] = part
-
-
-def halfway_body(zh_ref, got_ref, send_ref, keep_ref):
-    zh = zh_ref[0]
+        own, other = peer * N_ZH + zh, peer * N_ZH + 1 - zh
+        send_ref[peer, 0:TILE, :] = (keep_ref[other] + got_ref[other].astype(F32)).astype(BF16)
+        send_ref[peer, TILE:, :] = part
+        send_own_ref[peer] = (keep_ref[own] + got_ref[own].astype(F32)).astype(BF16)
+
+
+def halfway_body(got_ref, send_ref):
     total = jnp.sum(got_ref[...].astype(F32), axis=0)
-    first, second = total[:TILE], total[TILE : N_ZH * TILE]
-    mine = zh == 0
-    keep_ref[...] = jnp.where(mine, first, second)
-    send_ref[0:TILE, :] = jnp.where(mine, second, first).astype(BF16)
-    high, low = halves(total[N_ZH * TILE :])
+    send_ref[0:TILE, :] = total[:TILE].astype(BF16)
+    high, low = halves(total[TILE:])
     send_ref[TILE : TILE + W_HALF, :] = high
     send_ref[TILE + W_HALF :, :] = low
 
@@ -349,8 +351,9 @@
         send_ref[peer] = total
 
 
-def finish_body(got_ref, keep_ref, grad_ref):
-    grad_ref[...] = (keep_ref[...] + got_ref[0:TILE, :].astype(F32)).T.astype(BF16)
+def finish_body(got_ref, got_own_ref, grad_ref):
+    total = jnp.sum(got_own_ref[...].astype(F32), axis=0)
+    grad_ref[...] = (total + got_ref[0:TILE, :].astype(F32)).T.astype(BF16)
 
 
 def place_body(got_ref, grad_weight_ref):
@@ -400,11 +403,11 @@
     )(edge_rows[0, 0], edge_cols[0, 0], edge_weight[0, 0], tile_rows[0], tile_cols[0], tile_count)
     lists = exchange(send, ("y", "core"))
     other, lists = lax.optimization_barrier((other, lists))
-    tiles, codes, total = call(
+    tiles, codes = call(
         build_body,
-        (shape((most, TILE, TILE), BF16), shape((most,), I32), shape((N_CORE,), I32)),
+        (shape((most, TILE, TILE), BF16), shape((most + EXTRA,), I32)),
         [smem, vmem],
-        (hbm, smem, smem),
+        (hbm, smem),
         [pltpu.VMEM((LISTS * slots + 8, edges), F32)] * 3
         + [
             pltpu.VMEM((LISTS * 8, TILE), I32),
@@ -424,7 +427,7 @@
     )
     pair, up = lax.optimization_barrier((pair, upstream[0]))
     mine = exchange(pair, ("x", "y")).reshape(column_tiles, TILE, width)
-    mine, total, other_up = lax.optimization_barrier((mine, total, swap(up, "z2")))
+    mine, codes, other_up = lax.optimization_barrier((mine, codes, swap(up, "z2")))
     theirs = swap(mine, "core")
 
     work = dict(flops=slots * TILE * TILE * width, moved=slots * TILE * TILE, limit=LARGE)
@@ -432,17 +435,17 @@
     partial = call(
         functools.partial(forward_body, 0),
         shape(sums, F32),
-        [smem] * 2 + [hbm, vmem],
+        [smem, hbm, vmem],
         scratch=[pltpu.VMEM(sums, F32)] + tile_room,
         **work,
-    )(total, codes, tiles, mine)
+    )(codes, tiles, mine)
     partial = call(
         functools.partial(forward_body, 1),
         shape(sums, BF16),
-        [smem] * 2 + [hbm, vmem, vmem],
+        [smem, hbm, vmem, vmem],
         scratch=[pltpu.VMEM(sums, F32)] + tile_room,
         **work,
-    )(total, codes, tiles, theirs, partial)
+    )(codes, tiles, theirs, partial)
 
     got = exchange(partial, "z4").reshape((N_Z4, N_Z2, TILE, width))
     partial = jnp.sum(got.astype(F32), axis=0).astype(BF16)
@@ -466,33 +469,33 @@
     send = call(
         backward_other_body,
         shape((column_tiles + 1, width, TILE), BF16),
-        [smem] * 3 + [hbm, vmem],
+        [smem, hbm, vmem],
         scratch=[pltpu.VMEM(sums, F32)] + tile_room,
         **work,
-    )(where[1:], total, codes, tiles, got)
+    )(codes, tiles, got)
     keep, keep_weight = call(
         backward_own_body,
         (shape(sums, F32), shape((W_HALF, TILE), F32)),
-        [smem] * 3 + [hbm, vmem],
+        [smem, hbm, vmem],
         scratch=tile_room,
         **work,
-    )(where[1:], total, codes, tiles, got)
-
-    send = call(merge_body, shape((PLANE, N_ZH * TILE + W_HALF, TILE), BF16), [vmem] * 3)(
-        swap(send, "core"), keep, keep_weight
-    )
+    )(codes, tiles, got)
+
+    send, send_own = call(
+        merge_body,
+        (shape((PLANE, TILE + W_HALF, TILE), BF16), shape((PLANE, TILE, TILE), BF16)),
+        [smem] + [vmem] * 3,
+    )(zh_here, swap(send, "core"), keep, keep_weight)
     got = exchange(send, ("x", "y"))
-    send, keep = call(
-        halfway_body,
-        (shape((TILE + 2 * W_HALF, TILE), BF16), shape((TILE, TILE), F32)),
-        [smem, vmem],
-    )(zh_here, got)
+    got, send_own = lax.optimization_barrier((got, send_own))
+    got_own = exchange(send_own, ("x", "y"))
+    send = call(halfway_body, shape((TILE + 2 * W_HALF, TILE), BF16), [vmem])(got)
     got = swap(send, "zh")
     send_weight = call(last_sum_body, shape((N_Z4 * N_CORE, W_HALF, TILE), F32), [vmem] * 2)(
         got, send
     )
     got_weight = exchange(send_weight, ("z4", "core"))
-    grad_features = call(finish_body, shape((TILE, width), BF16), [vmem] * 2)(got, keep)
+    grad_features = call(finish_body, shape((TILE, width), BF16), [vmem] * 2)(got, got_own)
     grad_weight = call(place_body, shape((width, hidden), F32), [vmem])(got_weight)
     return (out_act[None], grad_features[None], grad_weight)
 

time: 155 us -> 154 us (level)
  blocking collectives: 46.9 us -> 41.3 us
  starting transfers between devices: 67.2 us -> 71.4 us
    all_to_all x3, blocking collectives: 46.9 us -> 41.3 us  [exchange(): return lax.all_to_all(value, axis, 0, 0, tiled=True)]
    all_to_all x3 -> x4, starting transfers between devices: 22.5 us -> 26 us  [exchange(): return lax.all_to_all(value, axis, 0, 0, tiled=True)]
    all_to_all x3 -> x4, waiting for transfers between devices: 10.1 us -> 10.1 us  [exchange(): return lax.all_to_all(value, axis, 0, 0, tiled=True)]
  transfers between devices with their start and end apart: 9 -> 10, of which waited for: 6 -> 6; matrix products, arithmetic and copies ran while one was open for 0% -> 0% of each run, Pallas kernels for 6% -> 7%
where the time goes in v12:
time: 154 us; the launch traced here: 152 us
  starting transfers between devices  71.4 us (46%)
  blocking collectives  41.3 us (27%)
  Pallas kernels  20.7 us (13%)
  waiting for transfers between devices  17.3 us (11%)
    ppermute x6, starting transfers between devices, swap(): return lax.ppermute(value, axis, [(0, 1), (1, 0)])  45.4 us
    all_to_all x3, blocking collectives, exchange(): return lax.all_to_all(value, axis, 0, 0, tiled=True)  41.3 us
    all_to_all x4, starting transfers between devices, exchange(): return lax.all_to_all(value, axis, 0, 0, tiled=True)  26 us
    all_to_all x4, waiting for transfers between devices, exchange(): return lax.all_to_all(value, axis, 0, 0, tiled=True)  10.1 us
    ppermute x6, waiting for transfers between devices, swap(): return lax.ppermute(value, axis, [(0, 1), (1, 0)])  7.15 us
    pallas_call x1, Pallas kernels, local(): call(build_body, (shape((most, TILE, TILE), BF16), shape((most + EXTRA,),...  4.73 us
  transfers between devices with their start and end apart: 10, of which 6 were waited for; matrix products, arithmetic and copies ran while one was open for 0% of the time, Pallas kernels for 7%

profile of v12, /device:TPU:1, one launch (start us, length us, event | category | flops | bytes accessed | tf_op | source)
XLA Modules:
  0.0 152.2 jit_solution(15523348887266665517)
XLA Ops:
  0.6 0.0 copy-start.2
  1.3 1.8 %shard_map.112 = bf16[8,320,128]{2,1,0:T(8,128)(2,1)} custom-call(s32[64,192]{1,0:T(8,128)} %bitcast.22, s32[64,192]{1,0:T(8,128)} %bitcast.23, bf16[64,192]{1,0:T(8,128)(2,1)} %bitcast.24, s32[1,64]{1,0:T(1,128)} %bitcast.26, s32[1,64]{1,0:T(1,128)} %bitcast.27, s32[1,1]{1,0:T(1,128)S(6)} %copy.12.count_ref), custom_call_target="tpu_custom_call" | custom-call | tf_op jit(solution)/shard_map/pallas_call | solution.py:390
  3.1 0.0 copy-start.1
  3.2 10.5 %all-to-all-start = ((bf16[8,320,128]{2,1,0:T(8,128)(2,1)}), bf16[8,320,128]{2,1,0:T(8,128)(2,1)S(1)}, u32[]{:S(2)}, u32[]{:S(2)}) async-start(bf16[8,320,128]{2,1,0:T(8,128)(2,1)} %shard_map.112), calls=%async_computation | async-start | bytes 1310720 | tf_op jit(solution)/shard_map/all_to_all | solution.py:372
  13.6 0.0 copy-done.2
  13.6 11.1 %collective-permute-start = (bf16[128,128]{1,0:T(8,128)(2,1)S(1)}, bf16[128,128]{1,0:T(8,128)(2,1)S(1)}, u32[]{:S(2)}, u32[]{:S(2)}) collective-permute-start(bf16[128,128]{1,0:T(8,128)(2,1)S(1)} %bitcast.19), channel_id=1, source_target_pairs={{0,64},{64,0},{1,65},{65,1},{2,66},{66,2},{3,67},{67,3},{4,68},{68... | collective-permute-start | bytes 98312 | tf_op jit(solution)/shard_map/ppermute | solution.py:368
  24.7 2.3 %collective-permute-done.other_ref = bf16[128,128]{1,0:T(8,128)(2,1)S(1)} collective-permute-done((bf16[128,128]{1,0:T(8,128)(2,1)S(1)}, bf16[128,128]{1,0:T(8,128)(2,1)S(1)}, u32[]{:S(2)}, u32[]{:S(2)}) %collective-permute-start) | collective-permute-done | bytes 32800 | tf_op jit(solution)/shard_map/ppermute | solution.py:368
  27.0 0.0 all-to-all-done.got_ref
  27.0 1.2 shard_map.113
  28.2 5.9 %all-to-all-start.1 = ((bf16[16,2,128,128]{3,2,1,0:T(8,128)(2,1)}), bf16[16,2,128,128]{3,2,1,0:T(8,128)(2,1)S(1)}, u32[]{:S(2)}, u32[]{:S(2)}) async-start(bf16[16,2,128,128]{3,2,1,0:T(8,128)(2,1)} %shard_map.113), calls=%async_computation.1 | async-start | bytes 2097152 | tf_op jit(solution)/shard_map/all_to_all | solution.py:372
  34.1 0.1 pad_add_fusion.where_ref
  34.1 0.0 copy-done.1
  34.1 5.3 %collective-permute-start.1 = (bf16[128,256]{1,0:T(8,128)(2,1)S(1)}, bf16[128,256]{1,0:T(8,128)(2,1)S(1)}, u32[]{:S(2)}, u32[]{:S(2)}) collective-permute-start(bf16[128,256]{1,0:T(8,128)(2,1)S(1)} %bitcast.17), channel_id=1, source_target_pairs={{0,8},{8,0},{1,9},{9,1},{2,10},{10,2},{3,11},{11,3},{4,12},{12,4},... | collective-permute-start | bytes 196616 | tf_op jit(solution)/shard_map/ppermute | solution.py:368
  39.5 4.7 %shard_map.114 = (bf16[320,128,128]{2,1,0:T(8,128)(2,1)}, s32[328]{0:T(512)S(1)}) custom-call(s32[2]{0:T(128)S(1)} %pad_add_fusion.where_ref, bf16[8,320,128]{2,1,0:T(8,128)(2,1)S(1)} %all-to-all-done.got_ref), custom_call_target="tpu_custom_call" | custom-call | flops 805306368 | bytes 2097152 | tf_op jit(solution)/shard_map/pallas_call | solution.py:406
  44.2 0.0 collective-permute-done.1.other_up_ref
  44.2 5.0 %all-to-all-done.1 = bf16[16,2,128,128]{3,2,1,0:T(8,128)(2,1)S(1)} async-done(((bf16[16,2,128,128]{3,2,1,0:T(8,128)(2,1)}), bf16[16,2,128,128]{3,2,1,0:T(8,128)(2,1)S(1)}, u32[]{:S(2)}, u32[]{:S(2)}) %all-to-all-start.1) | async-done | bytes 1048608 | tf_op jit(solution)/shard_map/all_to_all | solution.py:372
  49.3 5.1 %collective-permute-start.2 = (bf16[32,128,128]{2,1,0:T(8,128)(2,1)S(1)}, bf16[32,128,128]{2,1,0:T(8,128)(2,1)S(1)}, u32[]{:S(2)}, u32[]{:S(2)}) collective-permute-start(bf16[32,128,128]{2,1,0:T(8,128)(2,1)S(1)} %bitcast.15), channel_id=1, source_target_pairs={{0,1},{1,0},{2,3},{3,2},{4,5},{5,4},{6,7},{7,6},{8,9},{9,8},{10,11... | collective-permute-start | bytes 3145736 | tf_op jit(solution)/shard_map/ppermute | solution.py:368
  54.3 2.3 %shard_map.115.refs_0_ = f32[8,128,128]{2,1,0:T(8,128)S(1)} custom-call(s32[328]{0:T(512)S(1)} %get-tuple-element.25.code_ref, bf16[320,128,128]{2,1,0:T(8,128)(2,1)} %get-tuple-element.26.tiles_hbm, bf16[32,128,128]{2,1,0:T(8,128)(2,1)S(1)} %bitcast.16), custom_call_target="tpu_custom_call" | custom-call | flops 134217728 | bytes 1048576 | tf_op jit(solution)/shard_map/pallas_call | solution.py:435
  56.6 0.0 copy-start
  56.6 0.0 collective-permute-done.2.feats_ref
  56.6 2.3 %shard_map.116 = bf16[8,128,128]{2,1,0:T(8,128)(2,1)S(1)} custom-call(s32[328]{0:T(512)S(1)} %get-tuple-element.25.code_ref, bf16[320,128,128]{2,1,0:T(8,128)(2,1)} %get-tuple-element.26.tiles_hbm, bf16[32,128,128]{2,1,0:T(8,128)(2,1)S(1)} %collective-permute-done.2.feats_ref, f32[8,128,128]{2,1,0:T(8,128)S(1)} %shard_map.115.refs_0_), custom_call_target="tpu_custom_call" | custom-call | flops 134217728 | bytes 1048576 | tf_op jit(solution)/shard_map/pallas_call | solution.py:442
  58.9 9.6 %all_to_all.35 = bf16[8,128,128]{2,1,0:T(8,128)(2,1)S(1)} all-to-all(bf16[8,128,128]{2,1,0:T(8,128)(2,1)S(1)} %shard_map.116), channel_id=1, replica_groups=mesh['x'=4,'zh'=2,'y'=4,'z2'=2,'z4'=4,'core'=2] {'z4'}, dimensions={0} | all-to-all | bytes 524288 | tf_op jit(solution)/shard_map/all_to_all | solution.py:372
  68.6 9.3 %collective-permute-start.3 = (bf16[2,128,128]{2,1,0:T(8,128)(2,1)S(1)}, bf16[2,128,128]{2,1,0:T(8,128)(2,1)S(1)}, u32[]{:S(2)}, u32[]{:S(2)}) collective-permute-start(bf16[2,128,128]{2,1,0:T(8,128)(2,1)S(1)} %reduce_sum.12.own_ref), channel_id=1, source_target_pairs={{0,8},{8,0},{1,9},{9,1},{2,10},{10,2},{3,11},{11,3},{4,12},{12,4},... | collective-permute-start | bytes 196616 | tf_op jit(solution)/shard_map/ppermute | solution.py:368
  77.8 1.6 %collective-permute-done.3.other_ref = bf16[2,128,128]{2,1,0:T(8,128)(2,1)S(1)} collective-permute-done((bf16[2,128,128]{2,1,0:T(8,128)(2,1)S(1)}, bf16[2,128,128]{2,1,0:T(8,128)(2,1)S(1)}, u32[]{:S(2)}, u32[]{:S(2)}) %collective-permute-start.3) | collective-permute-done | bytes 65568 | tf_op jit(solution)/shard_map/ppermute | solution.py:368
  79.5 0.0 copy-done
  79.5 0.9 shard_map.117
  80.3 16.8 %all_to_all.36.got_ref = bf16[4,320,128]{2,1,0:T(8,128)(2,1)S(1)} all-to-all(bf16[4,320,128]{2,1,0:T(8,128)(2,1)S(1)} %get-tuple-element.30), channel_id=1, replica_groups=mesh['x'=4,'zh'=2,'y'=4,'z2'=2,'z4'=4,'core'=2] {'z4'}, dimensions={0} | all-to-all | bytes 655360 | tf_op jit(solution)/shard_map/all_to_all | solution.py:372
  97.2 2.2 %shard_map.118 = bf16[33,128,128]{2,1,0:T(8,128)(2,1)S(1)} custom-call(s32[328]{0:T(512)S(1)} %get-tuple-element.25.code_ref, bf16[320,128,128]{2,1,0:T(8,128)(2,1)} %get-tuple-element.26.tiles_hbm, bf16[4,320,128]{2,1,0:T(8,128)(2,1)S(1)} %all_to_all.36.got_ref), custom_call_target="tpu_custom_call" | custom-call | flops 134217728 | bytes 1048576 | tf_op jit(solution)/shard_map/pallas_call | solution.py:469
  99.4 4.1 %collective-permute-start.4 = (bf16[33,128,128]{2,1,0:T(8,128)(2,1)S(1)}, bf16[33,128,128]{2,1,0:T(8,128)(2,1)S(1)}, u32[]{:S(2)}, u32[]{:S(2)}) collective-permute-start(bf16[33,128,128]{2,1,0:T(8,128)(2,1)S(1)} %shard_map.118), channel_id=1, source_target_pairs={{0,1},{1,0},{2,3},{3,2},{4,5},{5,4},{6,7},{7,6},{8,9},{9,8},{10,11... | collective-permute-start | bytes 3244040 | tf_op jit(solution)/shard_map/ppermute | solution.py:368
  103.5 2.1 %shard_map.119 = (f32[32,128,128]{2,1,0:T(8,128)S(1)}, f32[32,128]{1,0:T(8,128)S(1)}) custom-call(s32[328]{0:T(512)S(1)} %get-tuple-element.25.code_ref, bf16[320,128,128]{2,1,0:T(8,128)(2,1)} %get-tuple-element.26.tiles_hbm, bf16[4,320,128]{2,1,0:T(8,128)(2,1)S(1)} %all_to_all.36.got_ref), custom_call_target="tpu_custom_call" | custom-call | flops 134217728 | bytes 1048576 | tf_op jit(solution)/shard_map/pallas_call | solution.py:476
  105.7 0.2 collective-permute-done.4.got_ref
  105.8 0.9 shard_map.120
  106.8 14.8 %all_to_all.37.got_ref = bf16[16,160,128]{2,1,0:T(8,128)(2,1)S(1)} all-to-all(bf16[16,160,128]{2,1,0:T(8,128)(2,1)S(1)} %get-tuple-element.33), channel_id=1, replica_groups=mesh['x'=4,'zh'=2,'y'=4,'z2'=2,'z4'=4,'core'=2] {'x','y'}, dimensions={0} | all-to-all | bytes 1310720 | tf_op jit(solution)/shard_map/all_to_all | solution.py:372
  121.6 3.6 %all-to-all-start.5 = ((bf16[16,128,128]{2,1,0:T(8,128)(2,1)}), bf16[16,128,128]{2,1,0:T(8,128)(2,1)S(1)}, u32[]{:S(2)}, u32[]{:S(2)}) async-start(bf16[16,128,128]{2,1,0:T(8,128)(2,1)} %get-tuple-element.36), calls=%async_computation.5 | async-start | bytes 1048576 | tf_op jit(solution)/shard_map/all_to_all | solution.py:372
  125.2 0.1 shard_map.121.sent_ref
  125.3 10.5 %collective-permute-start.5 = (bf16[192,128]{1,0:T(8,128)(2,1)S(1)}, bf16[192,128]{1,0:T(8,128)(2,1)S(1)}, u32[]{:S(2)}, u32[]{:S(2)}) collective-permute-start(bf16[192,128]{1,0:T(8,128)(2,1)S(1)} %shard_map.121.sent_ref), channel_id=1, source_target_pairs={{0,64},{64,0},{1,65},{65,1},{2,66},{66,2},{3,67},{67,3},{4,68},{68... | collective-permute-start | bytes 147464 | tf_op jit(solution)/shard_map/ppermute | solution.py:368
  135.8 3.1 %collective-permute-done.5.got_ref = bf16[192,128]{1,0:T(8,128)(2,1)S(1)} collective-permute-done((bf16[192,128]{1,0:T(8,128)(2,1)S(1)}, bf16[192,128]{1,0:T(8,128)(2,1)S(1)}, u32[]{:S(2)}, u32[]{:S(2)}) %collective-permute-start.5) | collective-permute-done | bytes 49184 | tf_op jit(solution)/shard_map/ppermute | solution.py:368
  138.9 0.7 shard_map.123
  139.5 0.0 all-to-all-done.5.got_own_ref
  139.5 6.2 %all-to-all-start.6 = ((f32[8,32,128]{2,1,0:T(8,128)}), f32[8,32,128]{2,1,0:T(8,128)S(1)}, u32[]{:S(2)}, u32[]{:S(2)}) async-start(f32[8,32,128]{2,1,0:T(8,128)} %shard_map.123), calls=%async_computation.6 | async-start | bytes 262144 | tf_op jit(solution)/shard_map/all_to_all | solution.py:372
  145.7 0.8 shard_map.122
  146.5 5.1 %all-to-all-done.6.got_ref = f32[8,32,128]{2,1,0:T(8,128)S(1)} async-done(((f32[8,32,128]{2,1,0:T(8,128)}), f32[8,32,128]{2,1,0:T(8,128)S(1)}, u32[]{:S(2)}, u32[]{:S(2)}) %all-to-all-start.6) | async-done | bytes 131104 | tf_op jit(solution)/shard_map/all_to_all | solution.py:372
  151.5 0.7 shard_map.124
  (1 shorter events, 0.0 us)
Async XLA Ops:
  0.6 13.0 %copy-start.2 = (bf16[1,128,128]{2,1,0:T(8,128)(2,1)S(1)}, bf16[1,128,128]{2,1,0:T(8,128)(2,1)}, u32[]{:S(2)}) copy-start(bf16[1,128,128]{2,1,0:T(8,128)(2,1)} %param.9) | copy-start | bytes 98308
  3.1 31.0 %copy-start.1 = (bf16[1,128,256]{2,1,0:T(8,128)(2,1)S(1)}, bf16[1,128,256]{2,1,0:T(8,128)(2,1)}, u32[]{:S(2)}) copy-start(bf16[1,128,256]{2,1,0:T(8,128)(2,1)} %param.11) | copy-start | bytes 196612
  3.2 23.8 %all-to-all-start = ((bf16[8,320,128]{2,1,0:T(8,128)(2,1)}), bf16[8,320,128]{2,1,0:T(8,128)(2,1)S(1)}, u32[]{:S(2)}, u32[]{:S(2)}) async-start(bf16[8,320,128]{2,1,0:T(8,128)(2,1)} %shard_map.112), calls=%async_computation | async-start | bytes 1310720 | tf_op jit(solution)/shard_map/all_to_all | solution.py:372
  13.6 13.4 %collective-permute-start = (bf16[128,128]{1,0:T(8,128)(2,1)S(1)}, bf16[128,128]{1,0:T(8,128)(2,1)S(1)}, u32[]{:S(2)}, u32[]{:S(2)}) collective-permute-start(bf16[128,128]{1,0:T(8,128)(2,1)S(1)} %bitcast.19), channel_id=1, source_target_pairs={{0,64},{64,0},{1,65},{65,1},{2,66},{66,2},{3,67},{67,3},{4,68},{68... | collective-permute-start | bytes 98312 | tf_op jit(solution)/shard_map/ppermute | solution.py:368
  28.2 21.1 %all-to-all-start.1 = ((bf16[16,2,128,128]{3,2,1,0:T(8,128)(2,1)}), bf16[16,2,128,128]{3,2,1,0:T(8,128)(2,1)S(1)}, u32[]{:S(2)}, u32[]{:S(2)}) async-start(bf16[16,2,128,128]{3,2,1,0:T(8,128)(2,1)} %shard_map.113), calls=%async_computation.1 | async-start | bytes 2097152 | tf_op jit(solution)/shard_map/all_to_all | solution.py:372
  34.1 10.1 %collective-permute-start.1 = (bf16[128,256]{1,0:T(8,128)(2,1)S(1)}, bf16[128,256]{1,0:T(8,128)(2,1)S(1)}, u32[]{:S(2)}, u32[]{:S(2)}) collective-permute-start(bf16[128,256]{1,0:T(8,128)(2,1)S(1)} %bitcast.17), channel_id=1, source_target_pairs={{0,8},{8,0},{1,9},{9,1},{2,10},{10,2},{3,11},{11,3},{4,12},{12,4},... | collective-permute-start | bytes 196616 | tf_op jit(solution)/shard_map/ppermute | solution.py:368
  49.3 7.4 %collective-permute-start.2 = (bf16[32,128,128]{2,1,0:T(8,128)(2,1)S(1)}, bf16[32,128,128]{2,1,0:T(8,128)(2,1)S(1)}, u32[]{:S(2)}, u32[]{:S(2)}) collective-permute-start(bf16[32,128,128]{2,1,0:T(8,128)(2,1)S(1)} %bitcast.15), channel_id=1, source_target_pairs={{0,1},{1,0},{2,3},{3,2},{4,5},{5,4},{6,7},{7,6},{8,9},{9,8},{10,11... | collective-permute-start | bytes 3145736 | tf_op jit(solution)/shard_map/ppermute | solution.py:368
  56.6 22.9 %copy-start = (bf16[128,256]{1,0:T(8,128)(2,1)S(1)}, bf16[128,256]{1,0:T(8,128)(2,1)}, u32[]{:S(2)}) copy-start(bf16[128,256]{1,0:T(8,128)(2,1)} %weight_ref.1) | copy-start | bytes 196612
  68.6 10.9 %collective-permute-start.3 = (bf16[2,128,128]{2,1,0:T(8,128)(2,1)S(1)}, bf16[2,128,128]{2,1,0:T(8,128)(2,1)S(1)}, u32[]{:S(2)}, u32[]{:S(2)}) collective-permute-start(bf16[2,128,128]{2,1,0:T(8,128)(2,1)S(1)} %reduce_sum.12.own_ref), channel_id=1, source_target_pairs={{0,8},{8,0},{1,9},{9,1},{2,10},{10,2},{3,11},{11,3},{4,12},{12,4},... | collective-permute-start | bytes 196616 | tf_op jit(solution)/shard_map/ppermute | solution.py:368
  99.4 6.4 %collective-permute-start.4 = (bf16[33,128,128]{2,1,0:T(8,128)(2,1)S(1)}, bf16[33,128,128]{2,1,0:T(8,128)(2,1)S(1)}, u32[]{:S(2)}, u32[]{:S(2)}) collective-permute-start(bf16[33,128,128]{2,1,0:T(8,128)(2,1)S(1)} %shard_map.118), channel_id=1, source_target_pairs={{0,1},{1,0},{2,3},{3,2},{4,5},{5,4},{6,7},{7,6},{8,9},{9,8},{10,11... | collective-permute-start | bytes 3244040 | tf_op jit(solution)/shard_map/ppermute | solution.py:368
  121.6 17.9 %all-to-all-start.5 = ((bf16[16,128,128]{2,1,0:T(8,128)(2,1)}), bf16[16,128,128]{2,1,0:T(8,128)(2,1)S(1)}, u32[]{:S(2)}, u32[]{:S(2)}) async-start(bf16[16,128,128]{2,1,0:T(8,128)(2,1)} %get-tuple-element.36), calls=%async_computation.5 | async-start | bytes 1048576 | tf_op jit(solution)/shard_map/all_to_all | solution.py:372
  125.3 13.6 %collective-permute-start.5 = (bf16[192,128]{1,0:T(8,128)(2,1)S(1)}, bf16[192,128]{1,0:T(8,128)(2,1)S(1)}, u32[]{:S(2)}, u32[]{:S(2)}) collective-permute-start(bf16[192,128]{1,0:T(8,128)(2,1)S(1)} %shard_map.121.sent_ref), channel_id=1, source_target_pairs={{0,64},{64,0},{1,65},{65,1},{2,66},{66,2},{3,67},{67,3},{4,68},{68... | collective-permute-start | bytes 147464 | tf_op jit(solution)/shard_map/ppermute | solution.py:368
  139.5 12.0 %all-to-all-start.6 = ((f32[8,32,128]{2,1,0:T(8,128)}), f32[8,32,128]{2,1,0:T(8,128)S(1)}, u32[]{:S(2)}, u32[]{:S(2)}) async-start(f32[8,32,128]{2,1,0:T(8,128)} %shard_map.123), calls=%async_computation.6 | async-start | bytes 262144 | tf_op jit(solution)/shard_map/all_to_all | solution.py:372

commit v13 on v12

--- a/solution.py
+++ b/solution.py
@@ -13,6 +13,7 @@
 GROUP = 16
 BLOCK = 8
 SRC_AT, ZL_AT, FLAG_AT = 10, 15, 18
+NEAR = 4
 EXTRA = 8
 FINE = (("x", 4), ("zh", 2), ("y", 4), ("z2", 2), ("z4", 4), ("core", 2))
 N_X, N_ZH, N_Y, N_Z2, N_Z4, N_CORE = (size for _, size in FINE)
@@ -22,7 +23,7 @@
 LISTS = N_Y * N_CORE
 PLANE = N_X * N_Y
 PACK = 62
-LARGE = 50
+LARGE = 46
 W_ROWS = 64
 W_HALF = W_ROWS // N_CORE
 BF16 = jnp.bfloat16
@@ -115,16 +116,29 @@
     return first, code_ref[ends + part] // GROUP
 
 
-def fetch_part(code_ref, part, tiles_hbm, tiles_ref, sems):
+def split_loops(first, last, near_step, far_step):
+    lax.fori_loop(jnp.minimum(first, NEAR), jnp.minimum(last, NEAR), near_step, 0)
+    lax.fori_loop(jnp.maximum(first, NEAR), jnp.maximum(last, NEAR), far_step, 0)
+
+
+def part_loops(code_ref, part, near_ref, tiles_hbm, tiles_ref, sems, prepare, step):
+    first, last = part_groups(code_ref, part)
+
     def start(group, carry):
         fetch(tiles_hbm, tiles_ref, sems, group).start()
         return carry
 
-    lax.fori_loop(*part_groups(code_ref, part), start, 0)
+    def far_step(group, carry):
+        fetch(tiles_hbm, tiles_ref, sems, group).wait()
+        return step(tiles_ref, group, carry)
+
+    lax.fori_loop(jnp.maximum(first, NEAR), jnp.maximum(last, NEAR), start, 0)
+    prepare()
+    split_loops(first, last, functools.partial(step, near_ref), far_step)
 
 
 def build_body(
-    where_ref, got_ref, tiles_hbm, code_ref,
+    where_ref, got_ref, near_ref, tiles_hbm, code_ref,
     edge_rows_ref, edge_cols_ref, weight_ref, meta_ref, slots_ref, sem, stage_ref, sems,
 ):
     y, core = where_ref[0], where_ref[1]
@@ -187,56 +201,61 @@
         here = pl.ds(group * GROUP, GROUP)
         return pltpu.make_async_copy(stage_ref.at[place], tiles_hbm.at[here], sems.at[place])
 
-    def step(group, carry):
-        @pl.when(group >= 2)
+    def make(entry):
+        slot = field(code_ref[entry], 0, SRC_AT)
+        row_hot = jnp.where(positions == edge_rows_ref[pl.ds(slot, 1), :], 1.0, 0.0)
+        col_hot = jnp.where(
+            positions == edge_cols_ref[pl.ds(slot, 1), :], weight_ref[pl.ds(slot, 1), :], 0.0
+        )
+        built = lax.dot_general(
+            row_hot.astype(BF16),
+            col_hot.astype(BF16),
+            (((1,), (1,)), ((), ())),
+            preferred_element_type=F32,
+        )
+        return built.astype(BF16)
+
+    def near_step(group, carry):
+        for i in range(GROUP):
+            near_ref[group * GROUP + i] = make(group * GROUP + i)
+        return carry
+
+    def far_step(group, carry):
+        @pl.when(group >= NEAR + 2)
         def _():
             store(group - 2).wait()
 
         for i in range(GROUP):
-            entry = group * GROUP + i
-            slot = field(code_ref[entry], 0, SRC_AT)
-            row_hot = jnp.where(positions == edge_rows_ref[pl.ds(slot, 1), :], 1.0, 0.0)
-            col_hot = jnp.where(
-                positions == edge_cols_ref[pl.ds(slot, 1), :], weight_ref[pl.ds(slot, 1), :], 0.0
-            )
-            built = lax.dot_general(
-                row_hot.astype(BF16),
-                col_hot.astype(BF16),
-                (((1,), (1,)), ((), ())),
-                preferred_element_type=F32,
-            )
-            stage_ref[group % 2, i] = built.astype(BF16)
+            stage_ref[group % 2, i] = make(group * GROUP + i)
         store(group).start()
         return carry
 
     groups = used // GROUP
-    lax.fori_loop(0, groups, step, 0)
+    split_loops(0, groups, near_step, far_step)
     for back in (2, 1):
 
-        @pl.when(groups >= back)
+        @pl.when(groups >= NEAR + back)
         def _(back=back):
             store(groups - back).wait()
 
 
-def forward_body(part, code_ref, tiles_hbm, feats_ref, *refs):
+def forward_body(part, code_ref, near_ref, tiles_hbm, feats_ref, *refs):
     *start_refs, out_ref, acc_ref, tiles_ref, sems = refs
-    fetch_part(code_ref, part, tiles_hbm, tiles_ref, sems)
-    acc_ref[...] = start_refs[0][...] if start_refs else jnp.zeros_like(acc_ref)
-
-    def step(group, carry):
-        fetch(tiles_hbm, tiles_ref, sems, group).wait()
+
+    def prepare():
+        acc_ref[...] = start_refs[0][...] if start_refs else jnp.zeros_like(acc_ref)
+
+    def step(from_ref, group, carry):
         products = []
         for i in range(GROUP):
             entry = group * GROUP + i
             source = field(code_ref[entry], SRC_AT, ZL_AT)
-            products.append(
-                jnp.dot(tiles_ref[entry], feats_ref[source], preferred_element_type=F32)
-            )
+            products.append(jnp.dot(from_ref[entry], feats_ref[source], preferred_element_type=F32))
         for i in range(GROUP):
             acc_ref[field(code_ref[group * GROUP + i], ZL_AT, FLAG_AT)] += products[i]
         return carry
 
-    lax.fori_loop(*part_groups(code_ref, part), step, 0)
+    part_loops(code_ref, part, near_ref, tiles_hbm, tiles_ref, sems, prepare, step)
     out_ref[...] = acc_ref[...].astype(out_ref.dtype)
 
 
@@ -276,24 +295,23 @@
         send_ref[peer, N_Z2 * TILE + deep :, :] = local_weight[here, TILE:]
 
 
-def backward_tiles(part, code_ref, tiles_hbm, got_ref, acc_ref, tiles_ref, sems):
-    fetch_part(code_ref, part, tiles_hbm, tiles_ref, sems)
-    acc_ref[...] = jnp.zeros_like(acc_ref)
-
-    def step(group, carry):
-        fetch(tiles_hbm, tiles_ref, sems, group).wait()
+def backward_tiles(part, code_ref, near_ref, tiles_hbm, got_ref, acc_ref, tiles_ref, sems):
+    def prepare():
+        acc_ref[...] = jnp.zeros_like(acc_ref)
+
+    def step(from_ref, group, carry):
         products = []
         for i in range(GROUP):
             entry = group * GROUP + i
             place = field(code_ref[entry], ZL_AT, FLAG_AT)
             start = pl.multiple_of(place % N_Z2 * TILE, TILE)
             grad = got_ref[place // N_Z2, pl.ds(start, TILE), :]
-            products.append(jnp.dot(grad, tiles_ref[entry], preferred_element_type=F32))
+            products.append(jnp.dot(grad, from_ref[entry], preferred_element_type=F32))
         for i in range(GROUP):
             acc_ref[field(code_ref[group * GROUP + i], SRC_AT, ZL_AT)] += products[i]
         return carry
 
-    lax.fori_loop(*part_groups(code_ref, part), step, 0)
+    part_loops(code_ref, part, near_ref, tiles_hbm, tiles_ref, sems, prepare, step)
 
 
 def own_core(code_ref):
@@ -306,9 +324,9 @@
 
 
 def backward_other_body(
-    code_ref, tiles_hbm, got_ref, send_ref, acc_ref, tiles_ref, sems
+    code_ref, near_ref, tiles_hbm, got_ref, send_ref, acc_ref, tiles_ref, sems
 ):
-    backward_tiles(1, code_ref, tiles_hbm, got_ref, acc_ref, tiles_ref, sems)
+    backward_tiles(1, code_ref, near_ref, tiles_hbm, got_ref, acc_ref, tiles_ref, sems)
     tiles = acc_ref.shape[0]
     send_ref[0:tiles] = acc_ref[...].astype(BF16)
     high, low = halves(weight_half(got_ref, 1 - own_core(code_ref)))
@@ -318,9 +336,9 @@
 
 
 def backward_own_body(
-    code_ref, tiles_hbm, got_ref, keep_ref, keep_weight_ref, tiles_ref, sems
+    code_ref, near_ref, tiles_hbm, got_ref, keep_ref, keep_weight_ref, tiles_ref, sems
 ):
-    backward_tiles(0, code_ref, tiles_hbm, got_ref, keep_ref, tiles_ref, sems)
+    backward_tiles(0, code_ref, near_ref, tiles_hbm, got_ref, keep_ref, tiles_ref, sems)
     keep_weight_ref[...] = weight_half(got_ref, own_core(code_ref))
 
 
@@ -403,11 +421,15 @@
     )(edge_rows[0, 0], edge_cols[0, 0], edge_weight[0, 0], tile_rows[0], tile_cols[0], tile_count)
     lists = exchange(send, ("y", "core"))
     other, lists = lax.optimization_barrier((other, lists))
-    tiles, codes = call(
+    near, tiles, codes = call(
         build_body,
-        (shape((most, TILE, TILE), BF16), shape((most + EXTRA,), I32)),
+        (
+            shape((NEAR * GROUP, TILE, TILE), BF16),
+            shape((2 * most, TILE, TILE), BF16),
+            shape((most + EXTRA,), I32),
+        ),
         [smem, vmem],
-        (hbm, smem),
+        (vmem, hbm, smem),
         [pltpu.VMEM((LISTS * slots + 8, edges), F32)] * 3
         + [
             pltpu.VMEM((LISTS * 8, TILE), I32),
@@ -435,17 +457,17 @@
     partial = call(
         functools.partial(forward_body, 0),
         shape(sums, F32),
-        [smem, hbm, vmem],
+        [smem, vmem, hbm, vmem],
         scratch=[pltpu.VMEM(sums, F32)] + tile_room,
         **work,
-    )(codes, tiles, mine)
+    )(codes, near, tiles, mine)
     partial = call(
         functools.partial(forward_body, 1),
         shape(sums, BF16),
-        [smem, hbm, vmem, vmem],
+        [smem, vmem, hbm, vmem, vmem],
         scratch=[pltpu.VMEM(sums, F32)] + tile_room,
         **work,
-    )(codes, tiles, theirs, partial)
+    )(codes, near, tiles, theirs, partial)
 
     got = exchange(partial, "z4").reshape((N_Z4, N_Z2, TILE, width))
     partial = jnp.sum(got.astype(F32), axis=0).astype(BF16)
@@ -469,17 +491,17 @@
     send = call(
         backward_other_body,
         shape((column_tiles + 1, width, TILE), BF16),
-        [smem, hbm, vmem],
+        [smem, vmem, hbm, vmem],
         scratch=[pltpu.VMEM(sums, F32)] + tile_room,
         **work,
-    )(codes, tiles, got)
+    )(codes, near, tiles, got)
     keep, keep_weight = call(
         backward_own_body,
         (shape(sums, F32), shape((W_HALF, TILE), F32)),
-        [smem, hbm, vmem],
+        [smem, vmem, hbm, vmem],
         scratch=tile_room,
         **work,
-    )(codes, tiles, got)
+    )(codes, near, tiles, got)
 
     send, send_own = call(
         merge_body,

time: 154 us -> 151 us (0.981)
  Pallas kernels: 20.7 us -> 16.1 us
  waiting for transfers between devices: 17.3 us -> 19.4 us
    pallas_call x3, Pallas kernels: 9.27 us -> 6.55 us  [the longest x1 4 us: local(): call(build_body, (shape((NEAR * GROUP, TILE, TILE), BF16), shape((2 * mos...]
    ppermute x6, waiting for transfers between devices: 7.15 us -> 9.65 us  [swap(): return lax.ppermute(value, axis, [(0, 1), (1, 0)])]
  transfers between devices with their start and end apart: 10 -> 10, of which waited for: 6 -> 7; matrix products, arithmetic and copies ran while one was open for 0% -> 0% of each run, Pallas kernels for 7% -> 5%
where the time goes in v13:
time: 151 us; the launch traced here: 150 us
  starting transfers between devices  70.8 us (47%)
  blocking collectives  41.2 us (27%)
  waiting for transfers between devices  19.4 us (13%)
  Pallas kernels  16.1 us (11%)
    ppermute x6, starting transfers between devices, swap(): return lax.ppermute(value, axis, [(0, 1), (1, 0)])  44.7 us
    all_to_all x3, blocking collectives, exchange(): return lax.all_to_all(value, axis, 0, 0, tiled=True)  41.2 us
    all_to_all x4, starting transfers between devices, exchange(): return lax.all_to_all(value, axis, 0, 0, tiled=True)  26 us
    all_to_all x4, waiting for transfers between devices, exchange(): return lax.all_to_all(value, axis, 0, 0, tiled=True)  9.75 us
    ppermute x6, waiting for transfers between devices, swap(): return lax.ppermute(value, axis, [(0, 1), (1, 0)])  9.65 us
    pallas_call x1, Pallas kernels, local(): call(build_body, (shape((NEAR * GROUP, TILE, TILE), BF16), shape((2 * mos...  4 us
  transfers between devices with their start and end apart: 10, of which 7 were waited for; matrix products, arithmetic and copies ran while one was open for 0% of the time, Pallas kernels for 5%

profile of v13, /device:TPU:1, one launch (start us, length us, event | category | flops | bytes accessed | tf_op | source)
XLA Modules:
  0.0 150.2 jit_solution(10311771147375993283)
XLA Ops:
  0.6 0.0 copy-start.4
  1.3 1.9 %shard_map.112 = bf16[8,320,128]{2,1,0:T(8,128)(2,1)} custom-call(s32[64,192]{1,0:T(8,128)} %bitcast.22, s32[64,192]{1,0:T(8,128)} %bitcast.23, bf16[64,192]{1,0:T(8,128)(2,1)} %bitcast.24, s32[1,64]{1,0:T(1,128)} %bitcast.26, s32[1,64]{1,0:T(1,128)} %bitcast.27, s32[1,1]{1,0:T(1,128)S(6)} %copy.12.count_ref), custom_call_target="tpu_custom_call" | custom-call | tf_op jit(solution)/shard_map/pallas_call | solution.py:408
  3.2 0.0 copy-start.3
  3.2 10.5 %all-to-all-start = ((bf16[8,320,128]{2,1,0:T(8,128)(2,1)}), bf16[8,320,128]{2,1,0:T(8,128)(2,1)S(1)}, u32[]{:S(2)}, u32[]{:S(2)}) async-start(bf16[8,320,128]{2,1,0:T(8,128)(2,1)} %shard_map.112), calls=%async_computation | async-start | bytes 1310720 | tf_op jit(solution)/shard_map/all_to_all | solution.py:390
  13.6 0.0 copy-done.4
  13.6 11.1 %collective-permute-start = (bf16[128,128]{1,0:T(8,128)(2,1)S(1)}, bf16[128,128]{1,0:T(8,128)(2,1)S(1)}, u32[]{:S(2)}, u32[]{:S(2)}) collective-permute-start(bf16[128,128]{1,0:T(8,128)(2,1)S(1)} %bitcast.19), channel_id=1, source_target_pairs={{0,64},{64,0},{1,65},{65,1},{2,66},{66,2},{3,67},{67,3},{4,68},{68... | collective-permute-start | bytes 98312 | tf_op jit(solution)/shard_map/ppermute | solution.py:386
  24.7 2.3 %collective-permute-done.other_ref = bf16[128,128]{1,0:T(8,128)(2,1)S(1)} collective-permute-done((bf16[128,128]{1,0:T(8,128)(2,1)S(1)}, bf16[128,128]{1,0:T(8,128)(2,1)S(1)}, u32[]{:S(2)}, u32[]{:S(2)}) %collective-permute-start) | collective-permute-done | bytes 32800 | tf_op jit(solution)/shard_map/ppermute | solution.py:386
  27.0 0.0 all-to-all-done.got_ref
  27.0 0.0 copy-start
  27.0 1.2 shard_map.113
  28.2 5.9 %all-to-all-start.1 = ((bf16[16,2,128,128]{3,2,1,0:T(8,128)(2,1)}), bf16[16,2,128,128]{3,2,1,0:T(8,128)(2,1)S(1)}, u32[]{:S(2)}, u32[]{:S(2)}) async-start(bf16[16,2,128,128]{3,2,1,0:T(8,128)(2,1)} %shard_map.113), calls=%async_computation.1 | async-start | bytes 2097152 | tf_op jit(solution)/shard_map/all_to_all | solution.py:390
  34.1 0.1 pad_add_fusion.where_ref
  34.1 0.0 copy-done
  34.1 0.0 copy-done.3
  34.1 5.3 %collective-permute-start.1 = (bf16[128,256]{1,0:T(8,128)(2,1)S(1)}, bf16[128,256]{1,0:T(8,128)(2,1)S(1)}, u32[]{:S(2)}, u32[]{:S(2)}) collective-permute-start(bf16[128,256]{1,0:T(8,128)(2,1)S(1)} %bitcast.17), channel_id=1, source_target_pairs={{0,8},{8,0},{1,9},{9,1},{2,10},{10,2},{3,11},{11,3},{4,12},{12,4},... | collective-permute-start | bytes 196616 | tf_op jit(solution)/shard_map/ppermute | solution.py:386
  39.5 0.0 copy-start.1
  39.5 1.1 copy-done.1
  40.6 4.0 %shard_map.114 = (bf16[64,128,128]{2,1,0:T(8,128)(2,1)S(1)}, bf16[640,128,128]{2,1,0:T(8,128)(2,1)}, s32[328]{0:T(512)S(1)}) custom-call(s32[2]{0:T(128)S(1)} %pad_add_fusion.where_ref, bf16[8,320,128]{2,1,0:T(8,128)(2,1)S(1)} %copy-done.1), custom_call_target="tpu_custom_call" | custom-call | flops 805306368 | bytes 2097152 | tf_op jit(solution)/shard_map/pallas_call | solution.py:424
  44.6 0.0 collective-permute-done.1.other_up_ref
  44.6 4.7 %all-to-all-done.1 = bf16[16,2,128,128]{3,2,1,0:T(8,128)(2,1)S(1)} async-done(((bf16[16,2,128,128]{3,2,1,0:T(8,128)(2,1)}), bf16[16,2,128,128]{3,2,1,0:T(8,128)(2,1)S(1)}, u32[]{:S(2)}, u32[]{:S(2)}) %all-to-all-start.1) | async-done | bytes 1048608 | tf_op jit(solution)/shard_map/all_to_all | solution.py:390
  49.3 5.1 %collective-permute-start.2 = (bf16[32,128,128]{2,1,0:T(8,128)(2,1)S(1)}, bf16[32,128,128]{2,1,0:T(8,128)(2,1)S(1)}, u32[]{:S(2)}, u32[]{:S(2)}) collective-permute-start(bf16[32,128,128]{2,1,0:T(8,128)(2,1)S(1)} %bitcast.15), channel_id=1, source_target_pairs={{0,1},{1,0},{2,3},{3,2},{4,5},{5,4},{6,7},{7,6},{8,9},{9,8},{10,11... | collective-permute-start | bytes 3145736 | tf_op jit(solution)/shard_map/ppermute | solution.py:386
  54.3 1.3 shard_map.115.refs_0_
  55.6 0.0 copy-start.2
  55.6 1.0 collective-permute-done.2.feats_ref
  56.6 1.3 shard_map.116
  57.9 9.6 %all_to_all.35 = bf16[8,128,128]{2,1,0:T(8,128)(2,1)S(1)} all-to-all(bf16[8,128,128]{2,1,0:T(8,128)(2,1)S(1)} %shard_map.116), channel_id=1, replica_groups=mesh['x'=4,'zh'=2,'y'=4,'z2'=2,'z4'=4,'core'=2] {'z4'}, dimensions={0} | all-to-all | bytes 524288 | tf_op jit(solution)/shard_map/all_to_all | solution.py:390
  67.6 9.3 %collective-permute-start.3 = (bf16[2,128,128]{2,1,0:T(8,128)(2,1)S(1)}, bf16[2,128,128]{2,1,0:T(8,128)(2,1)S(1)}, u32[]{:S(2)}, u32[]{:S(2)}) collective-permute-start(bf16[2,128,128]{2,1,0:T(8,128)(2,1)S(1)} %reduce_sum.12.own_ref), channel_id=1, source_target_pairs={{0,8},{8,0},{1,9},{9,1},{2,10},{10,2},{3,11},{11,3},{4,12},{12,4},... | collective-permute-start | bytes 196616 | tf_op jit(solution)/shard_map/ppermute | solution.py:386
  76.8 1.6 %collective-permute-done.3.other_ref = bf16[2,128,128]{2,1,0:T(8,128)(2,1)S(1)} collective-permute-done((bf16[2,128,128]{2,1,0:T(8,128)(2,1)S(1)}, bf16[2,128,128]{2,1,0:T(8,128)(2,1)S(1)}, u32[]{:S(2)}, u32[]{:S(2)}) %collective-permute-start.3) | collective-permute-done | bytes 65568 | tf_op jit(solution)/shard_map/ppermute | solution.py:386
  78.5 0.0 copy-done.2
  78.5 0.9 shard_map.117
  79.3 16.8 %all_to_all.36.got_ref = bf16[4,320,128]{2,1,0:T(8,128)(2,1)S(1)} all-to-all(bf16[4,320,128]{2,1,0:T(8,128)(2,1)S(1)} %get-tuple-element.32), channel_id=1, replica_groups=mesh['x'=4,'zh'=2,'y'=4,'z2'=2,'z4'=4,'core'=2] {'z4'}, dimensions={0} | all-to-all | bytes 655360 | tf_op jit(solution)/shard_map/all_to_all | solution.py:390
  96.1 1.3 shard_map.118
  97.4 4.1 %collective-permute-start.4 = (bf16[33,128,128]{2,1,0:T(8,128)(2,1)S(1)}, bf16[33,128,128]{2,1,0:T(8,128)(2,1)S(1)}, u32[]{:S(2)}, u32[]{:S(2)}) collective-permute-start(bf16[33,128,128]{2,1,0:T(8,128)(2,1)S(1)} %shard_map.118), channel_id=1, source_target_pairs={{0,1},{1,0},{2,3},{3,2},{4,5},{5,4},{6,7},{7,6},{8,9},{9,8},{10,11... | collective-permute-start | bytes 3244040 | tf_op jit(solution)/shard_map/ppermute | solution.py:386
  101.6 1.2 shard_map.119
  102.8 1.1 collective-permute-done.4.got_ref
  103.9 0.9 shard_map.120
  104.8 14.8 %all_to_all.37.got_ref = bf16[16,160,128]{2,1,0:T(8,128)(2,1)S(1)} all-to-all(bf16[16,160,128]{2,1,0:T(8,128)(2,1)S(1)} %get-tuple-element.35), channel_id=1, replica_groups=mesh['x'=4,'zh'=2,'y'=4,'z2'=2,'z4'=4,'core'=2] {'x','y'}, dimensions={0} | all-to-all | bytes 1310720 | tf_op jit(solution)/shard_map/all_to_all | solution.py:390
  119.6 3.6 %all-to-all-start.5 = ((bf16[16,128,128]{2,1,0:T(8,128)(2,1)}), bf16[16,128,128]{2,1,0:T(8,128)(2,1)S(1)}, u32[]{:S(2)}, u32[]{:S(2)}) async-start(bf16[16,128,128]{2,1,0:T(8,128)(2,1)} %get-tuple-element.38), calls=%async_computation.5 | async-start | bytes 1048576 | tf_op jit(solution)/shard_map/all_to_all | solution.py:390
  123.2 0.1 shard_map.121.sent_ref
  123.3 9.9 %collective-permute-start.5 = (bf16[192,128]{1,0:T(8,128)(2,1)S(1)}, bf16[192,128]{1,0:T(8,128)(2,1)S(1)}, u32[]{:S(2)}, u32[]{:S(2)}) collective-permute-start(bf16[192,128]{1,0:T(8,128)(2,1)S(1)} %shard_map.121.sent_ref), channel_id=1, source_target_pairs={{0,64},{64,0},{1,65},{65,1},{2,66},{66,2},{3,67},{67,3},{4,68},{68... | collective-permute-start | bytes 147464 | tf_op jit(solution)/shard_map/ppermute | solution.py:386
  133.2 3.7 %collective-permute-done.5.got_ref = bf16[192,128]{1,0:T(8,128)(2,1)S(1)} collective-permute-done((bf16[192,128]{1,0:T(8,128)(2,1)S(1)}, bf16[192,128]{1,0:T(8,128)(2,1)S(1)}, u32[]{:S(2)}, u32[]{:S(2)}) %collective-permute-start.5) | collective-permute-done | bytes 49184 | tf_op jit(solution)/shard_map/ppermute | solution.py:386
  136.9 0.7 shard_map.123
  137.5 0.0 all-to-all-done.5.got_own_ref
  137.6 6.2 %all-to-all-start.6 = ((f32[8,32,128]{2,1,0:T(8,128)}), f32[8,32,128]{2,1,0:T(8,128)S(1)}, u32[]{:S(2)}, u32[]{:S(2)}) async-start(f32[8,32,128]{2,1,0:T(8,128)} %shard_map.123), calls=%async_computation.6 | async-start | bytes 262144 | tf_op jit(solution)/shard_map/all_to_all | solution.py:390
  143.7 0.8 shard_map.122
  144.5 5.1 %all-to-all-done.6.got_ref = f32[8,32,128]{2,1,0:T(8,128)S(1)} async-done(((f32[8,32,128]{2,1,0:T(8,128)}), f32[8,32,128]{2,1,0:T(8,128)S(1)}, u32[]{:S(2)}, u32[]{:S(2)}) %all-to-all-start.6) | async-done | bytes 131104 | tf_op jit(solution)/shard_map/all_to_all | solution.py:390
  149.5 0.7 shard_map.124
  (1 shorter events, 0.0 us)
Async XLA Ops:
  0.6 13.0 %copy-start.4 = (bf16[1,128,128]{2,1,0:T(8,128)(2,1)S(1)}, bf16[1,128,128]{2,1,0:T(8,128)(2,1)}, u32[]{:S(2)}) copy-start(bf16[1,128,128]{2,1,0:T(8,128)(2,1)} %param.9) | copy-start | bytes 98308
  3.2 31.0 %copy-start.3 = (bf16[1,128,256]{2,1,0:T(8,128)(2,1)S(1)}, bf16[1,128,256]{2,1,0:T(8,128)(2,1)}, u32[]{:S(2)}) copy-start(bf16[1,128,256]{2,1,0:T(8,128)(2,1)} %param.11) | copy-start | bytes 196612
  3.2 23.8 %all-to-all-start = ((bf16[8,320,128]{2,1,0:T(8,128)(2,1)}), bf16[8,320,128]{2,1,0:T(8,128)(2,1)S(1)}, u32[]{:S(2)}, u32[]{:S(2)}) async-start(bf16[8,320,128]{2,1,0:T(8,128)(2,1)} %shard_map.112), calls=%async_computation | async-start | bytes 1310720 | tf_op jit(solution)/shard_map/all_to_all | solution.py:390
  13.6 13.4 %collective-permute-start = (bf16[128,128]{1,0:T(8,128)(2,1)S(1)}, bf16[128,128]{1,0:T(8,128)(2,1)S(1)}, u32[]{:S(2)}, u32[]{:S(2)}) collective-permute-start(bf16[128,128]{1,0:T(8,128)(2,1)S(1)} %bitcast.19), channel_id=1, source_target_pairs={{0,64},{64,0},{1,65},{65,1},{2,66},{66,2},{3,67},{67,3},{4,68},{68... | collective-permute-start | bytes 98312 | tf_op jit(solution)/shard_map/ppermute | solution.py:386
  27.0 7.1 %copy-start = (bf16[8,320,128]{2,1,0:T(8,128)(2,1)}, bf16[8,320,128]{2,1,0:T(8,128)(2,1)S(1)}, u32[]{:S(2)}) copy-start(bf16[8,320,128]{2,1,0:T(8,128)(2,1)S(1)} %all-to-all-done.got_ref) | copy-start | bytes 1966084
  28.2 21.1 %all-to-all-start.1 = ((bf16[16,2,128,128]{3,2,1,0:T(8,128)(2,1)}), bf16[16,2,128,128]{3,2,1,0:T(8,128)(2,1)S(1)}, u32[]{:S(2)}, u32[]{:S(2)}) async-start(bf16[16,2,128,128]{3,2,1,0:T(8,128)(2,1)} %shard_map.113), calls=%async_computation.1 | async-start | bytes 2097152 | tf_op jit(solution)/shard_map/all_to_all | solution.py:390
  34.1 10.4 %collective-permute-start.1 = (bf16[128,256]{1,0:T(8,128)(2,1)S(1)}, bf16[128,256]{1,0:T(8,128)(2,1)S(1)}, u32[]{:S(2)}, u32[]{:S(2)}) collective-permute-start(bf16[128,256]{1,0:T(8,128)(2,1)S(1)} %bitcast.17), channel_id=1, source_target_pairs={{0,8},{8,0},{1,9},{9,1},{2,10},{10,2},{3,11},{11,3},{4,12},{12,4},... | collective-permute-start | bytes 196616 | tf_op jit(solution)/shard_map/ppermute | solution.py:386
  39.5 1.1 copy-start.1
  49.3 7.3 %collective-permute-start.2 = (bf16[32,128,128]{2,1,0:T(8,128)(2,1)S(1)}, bf16[32,128,128]{2,1,0:T(8,128)(2,1)S(1)}, u32[]{:S(2)}, u32[]{:S(2)}) collective-permute-start(bf16[32,128,128]{2,1,0:T(8,128)(2,1)S(1)} %bitcast.15), channel_id=1, source_target_pairs={{0,1},{1,0},{2,3},{3,2},{4,5},{5,4},{6,7},{7,6},{8,9},{9,8},{10,11... | collective-permute-start | bytes 3145736 | tf_op jit(solution)/shard_map/ppermute | solution.py:386
  55.6 22.8 %copy-start.2 = (bf16[128,256]{1,0:T(8,128)(2,1)S(1)}, bf16[128,256]{1,0:T(8,128)(2,1)}, u32[]{:S(2)}) copy-start(bf16[128,256]{1,0:T(8,128)(2,1)} %weight_ref.1) | copy-start | bytes 196612
  67.6 10.9 %collective-permute-start.3 = (bf16[2,128,128]{2,1,0:T(8,128)(2,1)S(1)}, bf16[2,128,128]{2,1,0:T(8,128)(2,1)S(1)}, u32[]{:S(2)}, u32[]{:S(2)}) collective-permute-start(bf16[2,128,128]{2,1,0:T(8,128)(2,1)S(1)} %reduce_sum.12.own_ref), channel_id=1, source_target_pairs={{0,8},{8,0},{1,9},{9,1},{2,10},{10,2},{3,11},{11,3},{4,12},{12,4},... | collective-permute-start | bytes 196616 | tf_op jit(solution)/shard_map/ppermute | solution.py:386
  97.4 6.4 %collective-permute-start.4 = (bf16[33,128,128]{2,1,0:T(8,128)(2,1)S(1)}, bf16[33,128,128]{2,1,0:T(8,128)(2,1)S(1)}, u32[]{:S(2)}, u32[]{:S(2)}) collective-permute-start(bf16[33,128,128]{2,1,0:T(8,128)(2,1)S(1)} %shard_map.118), channel_id=1, source_target_pairs={{0,1},{1,0},{2,3},{3,2},{4,5},{5,4},{6,7},{7,6},{8,9},{9,8},{10,11... | collective-permute-start | bytes 3244040 | tf_op jit(solution)/shard_map/ppermute | solution.py:386
  119.6 17.9 %all-to-all-start.5 = ((bf16[16,128,128]{2,1,0:T(8,128)(2,1)}), bf16[16,128,128]{2,1,0:T(8,128)(2,1)S(1)}, u32[]{:S(2)}, u32[]{:S(2)}) async-start(bf16[16,128,128]{2,1,0:T(8,128)(2,1)} %get-tuple-element.38), calls=%async_computation.5 | async-start | bytes 1048576 | tf_op jit(solution)/shard_map/all_to_all | solution.py:390
  123.3 13.6 %collective-permute-start.5 = (bf16[192,128]{1,0:T(8,128)(2,1)S(1)}, bf16[192,128]{1,0:T(8,128)(2,1)S(1)}, u32[]{:S(2)}, u32[]{:S(2)}) collective-permute-start(bf16[192,128]{1,0:T(8,128)(2,1)S(1)} %shard_map.121.sent_ref), channel_id=1, source_target_pairs={{0,64},{64,0},{1,65},{65,1},{2,66},{66,2},{3,67},{67,3},{4,68},{68... | collective-permute-start | bytes 147464 | tf_op jit(solution)/shard_map/ppermute | solution.py:386
  137.6 12.0 %all-to-all-start.6 = ((f32[8,32,128]{2,1,0:T(8,128)}), f32[8,32,128]{2,1,0:T(8,128)S(1)}, u32[]{:S(2)}, u32[]{:S(2)}) async-start(f32[8,32,128]{2,1,0:T(8,128)} %shard_map.123), calls=%async_computation.6 | async-start | bytes 262144 | tf_op jit(solution)/shard_map/all_to_all | solution.py:390

commit v14 on v13

--- a/solution.py
+++ b/solution.py
@@ -355,23 +355,18 @@
 
 
 def halfway_body(got_ref, send_ref):
-    total = jnp.sum(got_ref[...].astype(F32), axis=0)
-    send_ref[0:TILE, :] = total[:TILE].astype(BF16)
-    high, low = halves(total[TILE:])
-    send_ref[TILE : TILE + W_HALF, :] = high
-    send_ref[TILE + W_HALF :, :] = low
+    send_ref[...] = jnp.sum(got_ref[...].astype(F32), axis=0)
 
 
 def last_sum_body(got_ref, sent_ref, send_ref):
-    terms = got_ref[TILE:, :].astype(F32), sent_ref[TILE:, :].astype(F32)
-    total = (terms[0][:W_HALF] + terms[0][W_HALF:]) + (terms[1][:W_HALF] + terms[1][W_HALF:])
+    total = got_ref[TILE:, :] + sent_ref[TILE:, :]
     for peer in range(N_Z4 * N_CORE):
         send_ref[peer] = total
 
 
 def finish_body(got_ref, got_own_ref, grad_ref):
     total = jnp.sum(got_own_ref[...].astype(F32), axis=0)
-    grad_ref[...] = (total + got_ref[0:TILE, :].astype(F32)).T.astype(BF16)
+    grad_ref[...] = (total + got_ref[0:TILE, :]).T.astype(BF16)
 
 
 def place_body(got_ref, grad_weight_ref):
@@ -511,7 +506,7 @@
     got = exchange(send, ("x", "y"))
     got, send_own = lax.optimization_barrier((got, send_own))
     got_own = exchange(send_own, ("x", "y"))
-    send = call(halfway_body, shape((TILE + 2 * W_HALF, TILE), BF16), [vmem])(got)
+    send = call(halfway_body, shape((TILE + W_HALF, TILE), F32), [vmem])(got)
     got = swap(send, "zh")
     send_weight = call(last_sum_body, shape((N_Z4 * N_CORE, W_HALF, TILE), F32), [vmem] * 2)(
         got, send

time: 151 us -> 154 us (1.020); the launches traced: 150 us -> 151 us
  no operation moved by 1% of the time
where the time goes in v14:
time: 154 us; the launch traced here: 151 us
  starting transfers between devices  70.2 us (46%)
  blocking collectives  41.2 us (27%)
  waiting for transfers between devices  20.4 us (13%)
  Pallas kernels  16.1 us (10%)
    ppermute x6, starting transfers between devices, swap(): return lax.ppermute(value, axis, [(0, 1), (1, 0)])  44.1 us
    all_to_all x3, blocking collectives, exchange(): return lax.all_to_all(value, axis, 0, 0, tiled=True)  41.2 us
    all_to_all x4, starting transfers between devices, exchange(): return lax.all_to_all(value, axis, 0, 0, tiled=True)  26.1 us
    ppermute x6, waiting for transfers between devices, swap(): return lax.ppermute(value, axis, [(0, 1), (1, 0)])  10.7 us
    all_to_all x4, waiting for transfers between devices, exchange(): return lax.all_to_all(value, axis, 0, 0, tiled=True)  9.73 us
    pallas_call x1, Pallas kernels, local(): call(build_body, (shape((NEAR * GROUP, TILE, TILE), BF16), shape((2 * mos...  4.03 us
  transfers between devices with their start and end apart: 10, of which 7 were waited for; matrix products, arithmetic and copies ran while one was open for 0% of the time, Pallas kernels for 5%

profile of v14, /device:TPU:1, one launch (start us, length us, event | category | flops | bytes accessed | tf_op | source)
XLA Modules:
  0.0 150.7 jit_solution(15683216481129763334)
XLA Ops:
  0.6 0.0 copy-start.4
  1.3 1.9 %shard_map.112 = bf16[8,320,128]{2,1,0:T(8,128)(2,1)} custom-call(s32[64,192]{1,0:T(8,128)} %bitcast.22, s32[64,192]{1,0:T(8,128)} %bitcast.23, bf16[64,192]{1,0:T(8,128)(2,1)} %bitcast.24, s32[1,64]{1,0:T(1,128)} %bitcast.26, s32[1,64]{1,0:T(1,128)} %bitcast.27, s32[1,1]{1,0:T(1,128)S(6)} %copy.12.count_ref), custom_call_target="tpu_custom_call" | custom-call | tf_op jit(solution)/shard_map/pallas_call | solution.py:403
  3.2 0.0 copy-start.3
  3.2 10.5 %all-to-all-start = ((bf16[8,320,128]{2,1,0:T(8,128)(2,1)}), bf16[8,320,128]{2,1,0:T(8,128)(2,1)S(1)}, u32[]{:S(2)}, u32[]{:S(2)}) async-start(bf16[8,320,128]{2,1,0:T(8,128)(2,1)} %shard_map.112), calls=%async_computation | async-start | bytes 1310720 | tf_op jit(solution)/shard_map/all_to_all | solution.py:385
  13.6 0.0 copy-done.4
  13.6 11.1 %collective-permute-start = (bf16[128,128]{1,0:T(8,128)(2,1)S(1)}, bf16[128,128]{1,0:T(8,128)(2,1)S(1)}, u32[]{:S(2)}, u32[]{:S(2)}) collective-permute-start(bf16[128,128]{1,0:T(8,128)(2,1)S(1)} %bitcast.19), channel_id=1, source_target_pairs={{0,64},{64,0},{1,65},{65,1},{2,66},{66,2},{3,67},{67,3},{4,68},{68... | collective-permute-start | bytes 98312 | tf_op jit(solution)/shard_map/ppermute | solution.py:381
  24.7 2.3 %collective-permute-done.other_ref = bf16[128,128]{1,0:T(8,128)(2,1)S(1)} collective-permute-done((bf16[128,128]{1,0:T(8,128)(2,1)S(1)}, bf16[128,128]{1,0:T(8,128)(2,1)S(1)}, u32[]{:S(2)}, u32[]{:S(2)}) %collective-permute-start) | collective-permute-done | bytes 32800 | tf_op jit(solution)/shard_map/ppermute | solution.py:381
  27.0 0.0 all-to-all-done.got_ref
  27.0 0.0 copy-start
  27.0 1.2 shard_map.113
  28.2 5.9 %all-to-all-start.1 = ((bf16[16,2,128,128]{3,2,1,0:T(8,128)(2,1)}), bf16[16,2,128,128]{3,2,1,0:T(8,128)(2,1)S(1)}, u32[]{:S(2)}, u32[]{:S(2)}) async-start(bf16[16,2,128,128]{3,2,1,0:T(8,128)(2,1)} %shard_map.113), calls=%async_computation.1 | async-start | bytes 2097152 | tf_op jit(solution)/shard_map/all_to_all | solution.py:385
  34.1 0.1 pad_add_fusion.where_ref
  34.1 0.0 copy-done
  34.1 0.0 copy-done.3
  34.1 5.3 %collective-permute-start.1 = (bf16[128,256]{1,0:T(8,128)(2,1)S(1)}, bf16[128,256]{1,0:T(8,128)(2,1)S(1)}, u32[]{:S(2)}, u32[]{:S(2)}) collective-permute-start(bf16[128,256]{1,0:T(8,128)(2,1)S(1)} %bitcast.17), channel_id=1, source_target_pairs={{0,8},{8,0},{1,9},{9,1},{2,10},{10,2},{3,11},{11,3},{4,12},{12,4},... | collective-permute-start | bytes 196616 | tf_op jit(solution)/shard_map/ppermute | solution.py:381
  39.5 0.0 copy-start.1
  39.5 1.1 copy-done.1
  40.6 4.0 %shard_map.114 = (bf16[64,128,128]{2,1,0:T(8,128)(2,1)S(1)}, bf16[640,128,128]{2,1,0:T(8,128)(2,1)}, s32[328]{0:T(512)S(1)}) custom-call(s32[2]{0:T(128)S(1)} %pad_add_fusion.where_ref, bf16[8,320,128]{2,1,0:T(8,128)(2,1)S(1)} %copy-done.1), custom_call_target="tpu_custom_call" | custom-call | flops 805306368 | bytes 2097152 | tf_op jit(solution)/shard_map/pallas_call | solution.py:419
  44.6 0.0 collective-permute-done.1.other_up_ref
  44.6 4.6 %all-to-all-done.1 = bf16[16,2,128,128]{3,2,1,0:T(8,128)(2,1)S(1)} async-done(((bf16[16,2,128,128]{3,2,1,0:T(8,128)(2,1)}), bf16[16,2,128,128]{3,2,1,0:T(8,128)(2,1)S(1)}, u32[]{:S(2)}, u32[]{:S(2)}) %all-to-all-start.1) | async-done | bytes 1048608 | tf_op jit(solution)/shard_map/all_to_all | solution.py:385
  49.3 5.1 %collective-permute-start.2 = (bf16[32,128,128]{2,1,0:T(8,128)(2,1)S(1)}, bf16[32,128,128]{2,1,0:T(8,128)(2,1)S(1)}, u32[]{:S(2)}, u32[]{:S(2)}) collective-permute-start(bf16[32,128,128]{2,1,0:T(8,128)(2,1)S(1)} %bitcast.15), channel_id=1, source_target_pairs={{0,1},{1,0},{2,3},{3,2},{4,5},{5,4},{6,7},{7,6},{8,9},{9,8},{10,11... | collective-permute-start | bytes 3145736 | tf_op jit(solution)/shard_map/ppermute | solution.py:381
  54.3 1.3 shard_map.115.refs_0_
  55.6 0.0 copy-start.2
  55.6 1.0 collective-permute-done.2.feats_ref
  56.6 1.3 shard_map.116
  57.9 9.6 %all_to_all.35 = bf16[8,128,128]{2,1,0:T(8,128)(2,1)S(1)} all-to-all(bf16[8,128,128]{2,1,0:T(8,128)(2,1)S(1)} %shard_map.116), channel_id=1, replica_groups=mesh['x'=4,'zh'=2,'y'=4,'z2'=2,'z4'=4,'core'=2] {'z4'}, dimensions={0} | all-to-all | bytes 524288 | tf_op jit(solution)/shard_map/all_to_all | solution.py:385
  67.6 9.3 %collective-permute-start.3 = (bf16[2,128,128]{2,1,0:T(8,128)(2,1)S(1)}, bf16[2,128,128]{2,1,0:T(8,128)(2,1)S(1)}, u32[]{:S(2)}, u32[]{:S(2)}) collective-permute-start(bf16[2,128,128]{2,1,0:T(8,128)(2,1)S(1)} %reduce_sum.12.own_ref), channel_id=1, source_target_pairs={{0,8},{8,0},{1,9},{9,1},{2,10},{10,2},{3,11},{11,3},{4,12},{12,4},... | collective-permute-start | bytes 196616 | tf_op jit(solution)/shard_map/ppermute | solution.py:381
  76.8 1.6 %collective-permute-done.3.other_ref = bf16[2,128,128]{2,1,0:T(8,128)(2,1)S(1)} collective-permute-done((bf16[2,128,128]{2,1,0:T(8,128)(2,1)S(1)}, bf16[2,128,128]{2,1,0:T(8,128)(2,1)S(1)}, u32[]{:S(2)}, u32[]{:S(2)}) %collective-permute-start.3) | collective-permute-done | bytes 65568 | tf_op jit(solution)/shard_map/ppermute | solution.py:381
  78.5 0.0 copy-done.2
  78.5 0.9 shard_map.117
  79.3 16.8 %all_to_all.36.got_ref = bf16[4,320,128]{2,1,0:T(8,128)(2,1)S(1)} all-to-all(bf16[4,320,128]{2,1,0:T(8,128)(2,1)S(1)} %get-tuple-element.32), channel_id=1, replica_groups=mesh['x'=4,'zh'=2,'y'=4,'z2'=2,'z4'=4,'core'=2] {'z4'}, dimensions={0} | all-to-all | bytes 655360 | tf_op jit(solution)/shard_map/all_to_all | solution.py:385
  96.1 1.3 shard_map.118
  97.4 4.1 %collective-permute-start.4 = (bf16[33,128,128]{2,1,0:T(8,128)(2,1)S(1)}, bf16[33,128,128]{2,1,0:T(8,128)(2,1)S(1)}, u32[]{:S(2)}, u32[]{:S(2)}) collective-permute-start(bf16[33,128,128]{2,1,0:T(8,128)(2,1)S(1)} %shard_map.118), channel_id=1, source_target_pairs={{0,1},{1,0},{2,3},{3,2},{4,5},{5,4},{6,7},{7,6},{8,9},{9,8},{10,11... | collective-permute-start | bytes 3244040 | tf_op jit(solution)/shard_map/ppermute | solution.py:381
  101.6 1.2 shard_map.119
  102.8 1.1 collective-permute-done.4.got_ref
  103.9 0.9 shard_map.120
  104.8 14.8 %all_to_all.37.got_ref = bf16[16,160,128]{2,1,0:T(8,128)(2,1)S(1)} all-to-all(bf16[16,160,128]{2,1,0:T(8,128)(2,1)S(1)} %get-tuple-element.35), channel_id=1, replica_groups=mesh['x'=4,'zh'=2,'y'=4,'z2'=2,'z4'=4,'core'=2] {'x','y'}, dimensions={0} | all-to-all | bytes 1310720 | tf_op jit(solution)/shard_map/all_to_all | solution.py:385
  119.6 3.6 %all-to-all-start.5 = ((bf16[16,128,128]{2,1,0:T(8,128)(2,1)}), bf16[16,128,128]{2,1,0:T(8,128)(2,1)S(1)}, u32[]{:S(2)}, u32[]{:S(2)}) async-start(bf16[16,128,128]{2,1,0:T(8,128)(2,1)} %get-tuple-element.38), calls=%async_computation.5 | async-start | bytes 1048576 | tf_op jit(solution)/shard_map/all_to_all | solution.py:385
  123.2 0.1 shard_map.121.sent_ref
  123.3 9.3 %collective-permute-start.5 = (f32[160,128]{1,0:T(8,128)S(1)}, f32[160,128]{1,0:T(8,128)S(1)}, u32[]{:S(2)}, u32[]{:S(2)}) collective-permute-start(f32[160,128]{1,0:T(8,128)S(1)} %shard_map.121.sent_ref), channel_id=1, source_target_pairs={{0,64},{64,0},{1,65},{65,1},{2,66},{66,2},{3,67},{67,3},{4,68},{68... | collective-permute-start | bytes 245768 | tf_op jit(solution)/shard_map/ppermute | solution.py:381
  132.6 4.7 %collective-permute-done.5.got_ref = f32[160,128]{1,0:T(8,128)S(1)} collective-permute-done((f32[160,128]{1,0:T(8,128)S(1)}, f32[160,128]{1,0:T(8,128)S(1)}, u32[]{:S(2)}, u32[]{:S(2)}) %collective-permute-start.5) | collective-permute-done | bytes 81952 | tf_op jit(solution)/shard_map/ppermute | solution.py:381
  137.3 0.7 shard_map.123
  138.0 0.0 all-to-all-done.5.got_own_ref
  138.0 6.2 %all-to-all-start.6 = ((f32[8,32,128]{2,1,0:T(8,128)}), f32[8,32,128]{2,1,0:T(8,128)S(1)}, u32[]{:S(2)}, u32[]{:S(2)}) async-start(f32[8,32,128]{2,1,0:T(8,128)} %shard_map.123), calls=%async_computation.6 | async-start | bytes 262144 | tf_op jit(solution)/shard_map/all_to_all | solution.py:385
  144.2 0.8 shard_map.122
  144.9 5.1 %all-to-all-done.6.got_ref = f32[8,32,128]{2,1,0:T(8,128)S(1)} async-done(((f32[8,32,128]{2,1,0:T(8,128)}), f32[8,32,128]{2,1,0:T(8,128)S(1)}, u32[]{:S(2)}, u32[]{:S(2)}) %all-to-all-start.6) | async-done | bytes 131104 | tf_op jit(solution)/shard_map/all_to_all | solution.py:385
  150.0 0.7 shard_map.124
  (1 shorter events, 0.0 us)
Async XLA Ops:
  0.6 13.0 %copy-start.4 = (bf16[1,128,128]{2,1,0:T(8,128)(2,1)S(1)}, bf16[1,128,128]{2,1,0:T(8,128)(2,1)}, u32[]{:S(2)}) copy-start(bf16[1,128,128]{2,1,0:T(8,128)(2,1)} %param.9) | copy-start | bytes 98308
  3.2 31.0 %copy-start.3 = (bf16[1,128,256]{2,1,0:T(8,128)(2,1)S(1)}, bf16[1,128,256]{2,1,0:T(8,128)(2,1)}, u32[]{:S(2)}) copy-start(bf16[1,128,256]{2,1,0:T(8,128)(2,1)} %param.11) | copy-start | bytes 196612
  3.2 23.8 %all-to-all-start = ((bf16[8,320,128]{2,1,0:T(8,128)(2,1)}), bf16[8,320,128]{2,1,0:T(8,128)(2,1)S(1)}, u32[]{:S(2)}, u32[]{:S(2)}) async-start(bf16[8,320,128]{2,1,0:T(8,128)(2,1)} %shard_map.112), calls=%async_computation | async-start | bytes 1310720 | tf_op jit(solution)/shard_map/all_to_all | solution.py:385
  13.6 13.4 %collective-permute-start = (bf16[128,128]{1,0:T(8,128)(2,1)S(1)}, bf16[128,128]{1,0:T(8,128)(2,1)S(1)}, u32[]{:S(2)}, u32[]{:S(2)}) collective-permute-start(bf16[128,128]{1,0:T(8,128)(2,1)S(1)} %bitcast.19), channel_id=1, source_target_pairs={{0,64},{64,0},{1,65},{65,1},{2,66},{66,2},{3,67},{67,3},{4,68},{68... | collective-permute-start | bytes 98312 | tf_op jit(solution)/shard_map/ppermute | solution.py:381
  27.0 7.1 %copy-start = (bf16[8,320,128]{2,1,0:T(8,128)(2,1)}, bf16[8,320,128]{2,1,0:T(8,128)(2,1)S(1)}, u32[]{:S(2)}) copy-start(bf16[8,320,128]{2,1,0:T(8,128)(2,1)S(1)} %all-to-all-done.got_ref) | copy-start | bytes 1966084
  28.2 21.1 %all-to-all-start.1 = ((bf16[16,2,128,128]{3,2,1,0:T(8,128)(2,1)}), bf16[16,2,128,128]{3,2,1,0:T(8,128)(2,1)S(1)}, u32[]{:S(2)}, u32[]{:S(2)}) async-start(bf16[16,2,128,128]{3,2,1,0:T(8,128)(2,1)} %shard_map.113), calls=%async_computation.1 | async-start | bytes 2097152 | tf_op jit(solution)/shard_map/all_to_all | solution.py:385
  34.1 10.5 %collective-permute-start.1 = (bf16[128,256]{1,0:T(8,128)(2,1)S(1)}, bf16[128,256]{1,0:T(8,128)(2,1)S(1)}, u32[]{:S(2)}, u32[]{:S(2)}) collective-permute-start(bf16[128,256]{1,0:T(8,128)(2,1)S(1)} %bitcast.17), channel_id=1, source_target_pairs={{0,8},{8,0},{1,9},{9,1},{2,10},{10,2},{3,11},{11,3},{4,12},{12,4},... | collective-permute-start | bytes 196616 | tf_op jit(solution)/shard_map/ppermute | solution.py:381
  39.5 1.1 copy-start.1
  49.3 7.3 %collective-permute-start.2 = (bf16[32,128,128]{2,1,0:T(8,128)(2,1)S(1)}, bf16[32,128,128]{2,1,0:T(8,128)(2,1)S(1)}, u32[]{:S(2)}, u32[]{:S(2)}) collective-permute-start(bf16[32,128,128]{2,1,0:T(8,128)(2,1)S(1)} %bitcast.15), channel_id=1, source_target_pairs={{0,1},{1,0},{2,3},{3,2},{4,5},{5,4},{6,7},{7,6},{8,9},{9,8},{10,11... | collective-permute-start | bytes 3145736 | tf_op jit(solution)/shard_map/ppermute | solution.py:381
  55.6 22.8 %copy-start.2 = (bf16[128,256]{1,0:T(8,128)(2,1)S(1)}, bf16[128,256]{1,0:T(8,128)(2,1)}, u32[]{:S(2)}) copy-start(bf16[128,256]{1,0:T(8,128)(2,1)} %weight_ref.1) | copy-start | bytes 196612
  67.6 10.9 %collective-permute-start.3 = (bf16[2,128,128]{2,1,0:T(8,128)(2,1)S(1)}, bf16[2,128,128]{2,1,0:T(8,128)(2,1)S(1)}, u32[]{:S(2)}, u32[]{:S(2)}) collective-permute-start(bf16[2,128,128]{2,1,0:T(8,128)(2,1)S(1)} %reduce_sum.12.own_ref), channel_id=1, source_target_pairs={{0,8},{8,0},{1,9},{9,1},{2,10},{10,2},{3,11},{11,3},{4,12},{12,4},... | collective-permute-start | bytes 196616 | tf_op jit(solution)/shard_map/ppermute | solution.py:381
  97.4 6.4 %collective-permute-start.4 = (bf16[33,128,128]{2,1,0:T(8,128)(2,1)S(1)}, bf16[33,128,128]{2,1,0:T(8,128)(2,1)S(1)}, u32[]{:S(2)}, u32[]{:S(2)}) collective-permute-start(bf16[33,128,128]{2,1,0:T(8,128)(2,1)S(1)} %shard_map.118), channel_id=1, source_target_pairs={{0,1},{1,0},{2,3},{3,2},{4,5},{5,4},{6,7},{7,6},{8,9},{9,8},{10,11... | collective-permute-start | bytes 3244040 | tf_op jit(solution)/shard_map/ppermute | solution.py:381
  119.6 18.4 %all-to-all-start.5 = ((bf16[16,128,128]{2,1,0:T(8,128)(2,1)}), bf16[16,128,128]{2,1,0:T(8,128)(2,1)S(1)}, u32[]{:S(2)}, u32[]{:S(2)}) async-start(bf16[16,128,128]{2,1,0:T(8,128)(2,1)} %get-tuple-element.38), calls=%async_computation.5 | async-start | bytes 1048576 | tf_op jit(solution)/shard_map/all_to_all | solution.py:385
  123.3 14.0 %collective-permute-start.5 = (f32[160,128]{1,0:T(8,128)S(1)}, f32[160,128]{1,0:T(8,128)S(1)}, u32[]{:S(2)}, u32[]{:S(2)}) collective-permute-start(f32[160,128]{1,0:T(8,128)S(1)} %shard_map.121.sent_ref), channel_id=1, source_target_pairs={{0,64},{64,0},{1,65},{65,1},{2,66},{66,2},{3,67},{67,3},{4,68},{68... | collective-permute-start | bytes 245768 | tf_op jit(solution)/shard_map/ppermute | solution.py:381
  138.0 12.0 %all-to-all-start.6 = ((f32[8,32,128]{2,1,0:T(8,128)}), f32[8,32,128]{2,1,0:T(8,128)S(1)}, u32[]{:S(2)}, u32[]{:S(2)}) async-start(f32[8,32,128]{2,1,0:T(8,128)} %shard_map.123), calls=%async_computation.6 | async-start | bytes 262144 | tf_op jit(solution)/shard_map/all_to_all | solution.py:385
